TPU v7x, 32 devices: a whole 2x2x4 slice. The times are simulated.
32 devices in a mesh: seq: 16 (over z, y, core), fsdp: 2 (over x).
Axes of the slice: x: 2, y: 2, z: 4, core: 2. Of those that a mesh axis runs over, the one named last changes fastest.
Arguments:
- tokens: bfloat16 [2, 4096, 2048], P('fsdp', 'seq'), may hold values from -6 to 6
- seq_lengths: int32 [2, 4], P('fsdp'), may hold values from 1 to 4009, as said below
- norm_gain: bfloat16 [2048], P(('seq', 'fsdp')), may hold values from 0.25 to 1.75
- w_query: bfloat16 [2048, 256], P(('seq', 'fsdp')), may hold values from -0.125 to 0.125
- w_key: bfloat16 [2048, 256], P(('seq', 'fsdp')), may hold values from -0.125 to 0.125
- w_value: bfloat16 [2048, 2048], P(('seq', 'fsdp')), may hold values from -0.125 to 0.125
- w_out: bfloat16 [2048, 2048], P(('seq', 'fsdp')), may hold values from -4 to 4
- mlp_gain: bfloat16 [2048], P(('seq', 'fsdp')), may hold values from 0.25 to 1.75
- w_gate: bfloat16 [2048, 5632], P(('seq', 'fsdp')), may hold values from -0.125 to 0.125
- w_up: bfloat16 [2048, 5632], P(('seq', 'fsdp')), may hold values from -0.125 to 0.125
- w_down: bfloat16 [5632, 2048], P(('seq', 'fsdp')), may hold values from -0.078125 to 0.078125
- cotangent: bfloat16 [2, 4096, 2048], P('fsdp', 'seq'), may hold values from -6 to 6
Outputs:
- block_out: float32 [2, 4096, 2048], P('fsdp', 'seq')
- input_grad: float32 [2, 4096, 2048], P('fsdp', 'seq')
- norm_gain_grad: float32 [2048], P(('seq', 'fsdp'))
- w_query_grad: float32 [2048, 256], P(('seq', 'fsdp'))
- w_key_grad: float32 [2048, 256], P(('seq', 'fsdp'))
- w_value_grad: float32 [2048, 2048], P(('seq', 'fsdp'))
- w_out_grad: float32 [2048, 2048], P(('seq', 'fsdp'))
- mlp_gain_grad: float32 [2048], P(('seq', 'fsdp'))
- w_gate_grad: float32 [2048, 5632], P(('seq', 'fsdp'))
- w_up_grad: float32 [2048, 5632], P(('seq', 'fsdp'))
- w_down_grad: float32 [5632, 2048], P(('seq', 'fsdp'))
Inputs may be any that keep to these rules, and one draw needn't show every extreme that they name: `seq_lengths`: each row sums to 4096. In each row all entries but one lie between 1 and (255) // 3, and one of them equals that bound. In some row of every draw all entries but two equal 1.
All inputs are finite; a program needn't handle non-finite values.
Results may differ from a plain program's by a relative error of at most 0.017.
Values may be sent and summed in bfloat16 or wider, within the bound.
No kernel may reach another device: no remote copies, remote signals or barrier semaphores. Data moves between devices by JAX's collectives and lax.ppermute only.
A program may use at most 512 MiB of HBM per device.

v0:
```python
import math

import jax
import jax.numpy as jnp
from jax import lax
from jax.sharding import PartitionSpec as P

H = 16
FD = 16
DV = 128
PHI = 273


def entering(shard, axis, combine, identity, reverse):
    length, position = (lax.axis_size(axis), lax.axis_index(axis))
    everything = jax.tree.map(
        lambda part, kind: lax.all_gather(part.astype(kind), axis),
        shard,
        (jnp.bfloat16, jnp.bfloat16, jnp.bfloat16),
    )
    start = jax.tree.map(
        lambda part, zero: jnp.broadcast_to(jnp.asarray(zero, part.dtype), part.shape),
        shard,
        identity,
    )

    def lap(k, before):
        at = length - 1 - k if reverse else k
        reached = at > position if reverse else at < position
        new = combine(
            before, jax.tree.map(lambda part, own: part[at].astype(own.dtype), everything, shard)
        )
        return jax.tree.map(lambda a, b: jnp.where(reached, a, b), new, before)

    return lax.fori_loop(0, length, lap, start)


def rms_scale(values, gain_vec):
    return values * lax.rsqrt(jnp.mean(values * values, axis=-1, keepdims=True) + 1e-05) * gain_vec


def taylor(values):
    feat_width = values.shape[-1]
    outer_prod = (values[..., :, None] * values[..., None, :]).reshape(
        values.shape[:-1] + (feat_width * feat_width,)
    )
    ones_col = jnp.ones(values.shape[:-1] + (1,), values.dtype)
    return jnp.concatenate(
        [
            ones_col,
            values / math.sqrt(math.sqrt(feat_width)),
            outer_prod / (math.sqrt(2.0) * math.sqrt(feat_width)),
        ],
        axis=-1,
    )


def compose(earlier, latter):
    keep_early, state_early, den_early = earlier
    keep_late, state_late, den_late = latter
    return (
        keep_early * keep_late,
        state_late + keep_late * state_early,
        den_late + keep_late * den_early,
    )


def on_device(
    tokens,
    seq_lengths,
    norm_gain,
    w_query,
    w_key,
    w_value,
    w_out,
    mlp_gain,
    w_gate,
    w_up,
    w_down,
    cotangent,
):
    hidden_in = tokens[0].astype(jnp.float32)
    row_count = hidden_in.shape[0]
    lengths = seq_lengths[0]
    seq_ends = jnp.cumsum(lengths)
    first_row = lax.axis_index("seq") * row_count
    places = first_row + jnp.arange(row_count, dtype=jnp.int32)
    segment = jnp.sum((places[:, None] >= seq_ends[None, :]).astype(jnp.int32), axis=1)
    before = jnp.where(first_row > 0, jnp.sum((first_row - 1 >= seq_ends).astype(jnp.int32)), -1)
    continues = (segment == before).astype(jnp.float32)
    tail_rows = (segment == segment[-1]).astype(jnp.float32)
    carry_on = continues[-1]
    index_row = jnp.arange(row_count)
    pair_mask = (
        (segment[:, None] == segment[None, :]) & (index_row[:, None] >= index_row[None, :])
    ).astype(jnp.float32)
    cont_low = continues.astype(jnp.bfloat16)
    tail_low = tail_rows.astype(jnp.bfloat16)
    gain_one, full_query, full_key, full_value, full_out = (
        lax.all_gather(norm_gain, ("seq", "fsdp"), axis=0, tiled=True),
        lax.all_gather(w_query, ("seq", "fsdp"), axis=0, tiled=True),
        lax.all_gather(w_key, ("seq", "fsdp"), axis=0, tiled=True),
        lax.all_gather(w_value, ("seq", "fsdp"), axis=0, tiled=True),
        lax.all_gather(w_out, ("seq", "fsdp"), axis=0, tiled=True),
    )
    gain_one = gain_one.astype(jnp.float32)
    normed = rms_scale(hidden_in, gain_one).astype(jnp.bfloat16)
    queries = jnp.dot(normed, full_query, preferred_element_type=jnp.float32).reshape(
        row_count, H, FD
    )
    key_rows = jnp.dot(normed, full_key, preferred_element_type=jnp.float32).reshape(
        row_count, H, FD
    )
    value_rows = jnp.dot(normed, full_value, preferred_element_type=jnp.float32)
    feat_query = taylor(queries).astype(jnp.bfloat16)
    feat_key = taylor(key_rows).astype(jnp.bfloat16)
    values_low = value_rows.reshape(row_count, H, DV).astype(jnp.bfloat16)
    scores = (
        jnp.einsum("thp,shp->hts", feat_query, feat_key, preferred_element_type=jnp.float32)
        * pair_mask[None]
    )
    scores_low = scores.astype(jnp.bfloat16)
    added_state = jnp.einsum(
        "thp,thv->hpv",
        feat_key,
        values_low * tail_low[:, None, None],
        preferred_element_type=jnp.float32,
    )
    added_den = jnp.einsum("thp,t->hp", feat_key, tail_low, preferred_element_type=jnp.float32)
    identity = (
        jnp.ones((), jnp.float32),
        jnp.zeros((H, PHI, DV), jnp.float32),
        jnp.zeros((H, PHI), jnp.float32),
    )
    incoming = entering((carry_on, added_state, added_den), "seq", compose, identity, False)
    state_low = incoming[1].astype(jnp.bfloat16)
    den_in = incoming[2]
    feat_query_wide = feat_query.astype(jnp.float32)
    numerator = jnp.einsum(
        "hts,shv->thv", scores_low, values_low, preferred_element_type=jnp.float32
    )
    numerator = numerator + continues[:, None, None] * jnp.einsum(
        "thp,hpv->thv", feat_query, state_low, preferred_element_type=jnp.float32
    )
    denominator = jnp.sum(scores, axis=2).T + continues[:, None] * jnp.einsum(
        "thp,hp->th", feat_query_wide, den_in, precision=lax.Precision.HIGHEST
    )
    attn_heads = numerator / denominator[:, :, None]
    mixed_heads = attn_heads.reshape(row_count, H * DV).astype(jnp.bfloat16)
    residual = hidden_in + jnp.dot(mixed_heads, full_out, preferred_element_type=jnp.float32)
    gain_two, full_gate, full_up, full_down = (
        lax.all_gather(mlp_gain, ("seq", "fsdp"), axis=0, tiled=True),
        lax.all_gather(w_gate, ("seq", "fsdp"), axis=0, tiled=True),
        lax.all_gather(w_up, ("seq", "fsdp"), axis=0, tiled=True),
        lax.all_gather(w_down, ("seq", "fsdp"), axis=0, tiled=True),
    )
    gain_two = gain_two.astype(jnp.float32)
    normed_two = rms_scale(residual, gain_two).astype(jnp.bfloat16)
    gate_rows = jnp.dot(normed_two, full_gate, preferred_element_type=jnp.float32)
    up_rows = jnp.dot(normed_two, full_up, preferred_element_type=jnp.float32)
    sigmoid_gate = jax.nn.sigmoid(gate_rows)
    silu_gate = gate_rows * sigmoid_gate
    hidden = (silu_gate * up_rows).astype(jnp.bfloat16)
    block_out = residual + jnp.dot(hidden, full_down, preferred_element_type=jnp.float32)
    grad_out = cotangent[0].astype(jnp.float32)
    grad_low = grad_out.astype(jnp.bfloat16)
    gain_two, full_gate, full_up, full_down = (
        lax.all_gather(mlp_gain, ("seq", "fsdp"), axis=0, tiled=True),
        lax.all_gather(w_gate, ("seq", "fsdp"), axis=0, tiled=True),
        lax.all_gather(w_up, ("seq", "fsdp"), axis=0, tiled=True),
        lax.all_gather(w_down, ("seq", "fsdp"), axis=0, tiled=True),
    )
    gain_two = gain_two.astype(jnp.float32)
    grad_w_down = jnp.einsum("tf,td->fd", hidden, grad_low, preferred_element_type=jnp.float32)
    grad_hidden = jnp.einsum("td,fd->tf", grad_low, full_down, preferred_element_type=jnp.float32)
    grad_gate = (
        grad_hidden * up_rows * sigmoid_gate * (1.0 + gate_rows * (1.0 - sigmoid_gate))
    ).astype(jnp.bfloat16)
    grad_up = (grad_hidden * silu_gate).astype(jnp.bfloat16)
    grad_w_gate = jnp.einsum("td,tf->df", normed_two, grad_gate, preferred_element_type=jnp.float32)
    grad_w_up = jnp.einsum("td,tf->df", normed_two, grad_up, preferred_element_type=jnp.float32)
    grad_normed_two = jnp.einsum(
        "tf,df->td", grad_gate, full_gate, preferred_element_type=jnp.float32
    )
    grad_normed_two = grad_normed_two + jnp.einsum(
        "tf,df->td", grad_up, full_up, preferred_element_type=jnp.float32
    )
    _, pull_two = jax.vjp(rms_scale, residual, gain_two)
    grad_resid_part, grad_gain_two = pull_two(grad_normed_two)
    mlp_sums = (
        lax.psum_scatter(grad_gain_two, ("seq", "fsdp"), scatter_dimension=0, tiled=True),
        lax.psum_scatter(grad_w_gate, ("seq", "fsdp"), scatter_dimension=0, tiled=True),
        lax.psum_scatter(grad_w_up, ("seq", "fsdp"), scatter_dimension=0, tiled=True),
        lax.psum_scatter(grad_w_down, ("seq", "fsdp"), scatter_dimension=0, tiled=True),
    )
    grad_resid = grad_out + grad_resid_part
    gain_one, full_query, full_key, full_value, full_out = (
        lax.all_gather(norm_gain, ("seq", "fsdp"), axis=0, tiled=True),
        lax.all_gather(w_query, ("seq", "fsdp"), axis=0, tiled=True),
        lax.all_gather(w_key, ("seq", "fsdp"), axis=0, tiled=True),
        lax.all_gather(w_value, ("seq", "fsdp"), axis=0, tiled=True),
        lax.all_gather(w_out, ("seq", "fsdp"), axis=0, tiled=True),
    )
    gain_one = gain_one.astype(jnp.float32)
    grad_branch = grad_resid.astype(jnp.bfloat16)
    grad_w_out = jnp.einsum(
        "tk,td->kd", mixed_heads, grad_branch, preferred_element_type=jnp.float32
    )
    grad_heads = jnp.einsum(
        "td,kd->tk", grad_branch, full_out, preferred_element_type=jnp.float32
    ).reshape(row_count, H, DV)
    grad_numer = (grad_heads / denominator[:, :, None]).astype(jnp.bfloat16)
    grad_denom = -jnp.sum(grad_heads * attn_heads, axis=2) / denominator
    use_state = jnp.einsum(
        "thp,thv->hpv",
        feat_query,
        grad_numer * cont_low[:, None, None],
        preferred_element_type=jnp.float32,
    )
    use_den = jnp.einsum(
        "thp,th->hp",
        feat_query_wide,
        grad_denom * continues[:, None],
        precision=lax.Precision.HIGHEST,
    )
    outgoing = entering((carry_on, use_state, use_den), "seq", compose, identity, True)
    back_low = outgoing[1].astype(jnp.bfloat16)
    back_den = outgoing[2]
    incoming = entering((carry_on, added_state, added_den), "seq", compose, identity, False)
    state_low = incoming[1].astype(jnp.bfloat16)
    den_in = incoming[2]
    grad_scores = jnp.einsum(
        "thv,shv->hts", grad_numer, values_low, preferred_element_type=jnp.float32
    )
    grad_scores_low = ((grad_scores + grad_denom.T[:, :, None]) * pair_mask[None]).astype(
        jnp.bfloat16
    )
    grad_feat_query = jnp.einsum(
        "hts,shp->thp", grad_scores_low, feat_key, preferred_element_type=jnp.float32
    )
    grad_feat_query = grad_feat_query + continues[:, None, None] * (
        jnp.einsum("thv,hpv->thp", grad_numer, state_low, preferred_element_type=jnp.float32)
        + grad_denom[:, :, None] * den_in[None]
    )
    grad_feat_key = jnp.einsum(
        "hts,thp->shp", grad_scores_low, feat_query, preferred_element_type=jnp.float32
    )
    grad_feat_key = grad_feat_key + tail_rows[:, None, None] * (
        jnp.einsum("thv,hpv->thp", values_low, back_low, preferred_element_type=jnp.float32)
        + back_den[None]
    )
    grad_values = jnp.einsum(
        "hts,thv->shv", scores_low, grad_numer, preferred_element_type=jnp.float32
    )
    grad_values = grad_values + tail_rows[:, None, None] * jnp.einsum(
        "thp,hpv->thv", feat_key, back_low, preferred_element_type=jnp.float32
    )
    _, pull_query = jax.vjp(taylor, queries)
    grad_query = pull_query(grad_feat_query)[0].reshape(row_count, H * FD).astype(jnp.bfloat16)
    _, pull_key = jax.vjp(taylor, key_rows)
    grad_key = pull_key(grad_feat_key)[0].reshape(row_count, H * FD).astype(jnp.bfloat16)
    grad_value = grad_values.reshape(row_count, H * DV).astype(jnp.bfloat16)
    grad_w_query = jnp.einsum("td,tk->dk", normed, grad_query, preferred_element_type=jnp.float32)
    grad_w_key = jnp.einsum("td,tk->dk", normed, grad_key, preferred_element_type=jnp.float32)
    grad_w_value = jnp.einsum("td,tk->dk", normed, grad_value, preferred_element_type=jnp.float32)
    grad_normed = jnp.einsum(
        "tk,dk->td", grad_query, full_query, preferred_element_type=jnp.float32
    )
    grad_normed = grad_normed + jnp.einsum(
        "tk,dk->td", grad_key, full_key, preferred_element_type=jnp.float32
    )
    grad_normed = grad_normed + jnp.einsum(
        "tk,dk->td", grad_value, full_value, preferred_element_type=jnp.float32
    )
    _, pull_one = jax.vjp(rms_scale, hidden_in, gain_one)
    grad_in_part, grad_gain_one = pull_one(grad_normed)
    attn_sums = (
        lax.psum_scatter(grad_gain_one, ("seq", "fsdp"), scatter_dimension=0, tiled=True),
        lax.psum_scatter(grad_w_query, ("seq", "fsdp"), scatter_dimension=0, tiled=True),
        lax.psum_scatter(grad_w_key, ("seq", "fsdp"), scatter_dimension=0, tiled=True),
        lax.psum_scatter(grad_w_value, ("seq", "fsdp"), scatter_dimension=0, tiled=True),
        lax.psum_scatter(grad_w_out, ("seq", "fsdp"), scatter_dimension=0, tiled=True),
    )
    input_grad = grad_resid + grad_in_part
    return (
        block_out[None],
        input_grad[None],
        attn_sums[0],
        attn_sums[1],
        attn_sums[2],
        attn_sums[3],
        attn_sums[4],
        mlp_sums[0],
        mlp_sums[1],
        mlp_sums[2],
        mlp_sums[3],
    )


def solution(mesh):
    placed = (
        P("fsdp", "seq", None),
        P("fsdp", None),
        P(("seq", "fsdp")),
        P(("seq", "fsdp"), None),
        P(("seq", "fsdp"), None),
        P(("seq", "fsdp"), None),
        P(("seq", "fsdp"), None),
        P(("seq", "fsdp")),
        P(("seq", "fsdp"), None),
        P(("seq", "fsdp"), None),
        P(("seq", "fsdp"), None),
        P("fsdp", "seq", None),
    )
    return jax.shard_map(
        on_device,
        mesh=mesh,
        in_specs=placed,
        out_specs=(
            P("fsdp", "seq", None),
            P("fsdp", "seq", None),
            P(("seq", "fsdp")),
            P(("seq", "fsdp"), None),
            P(("seq", "fsdp"), None),
            P(("seq", "fsdp"), None),
            P(("seq", "fsdp"), None),
            P(("seq", "fsdp")),
            P(("seq", "fsdp"), None),
            P(("seq", "fsdp"), None),
            P(("seq", "fsdp"), None),
        ),
        check_vma=False,
    )
```

profile of v0, /device:TPU:0, one launch (start us, length us, event | category | flops | bytes accessed | tf_op | source)
XLA Modules:
  0.0 4903.7 jit_solution(11184636253892135811)
XLA Ops:
  12.0 42.2 all-reduce.6
  58.9 8.5 all-gather.18.cloned.1.call-done
  70.9 75.9 %all-gather.14.cloned.1.call-done = bf16[2048,2048]{1,0:T(8,128)(2,1)} async-done(((bf16[64,2048]{1,0:T(8,128)(2,1)}), bf16[2048,2048]{1,0:T(8,128)(2,1)}) %all-gather.14.cloned.1.call-update) | async-done | bytes 8388624 | tf_op jit(solution)/shard_map/all_gather | solution.py:103
  146.7 12.3 copy.53
  159.1 5.0 convolution_convert_fusion.2
  171.6 32.2 all-reduce.1
  206.9 2.6 fusion.77
  209.5 20.5 all-gather.1
  233.0 3.8 multiply_reduce_fusion.4
  236.8 4.2 fusion.41
  241.0 65.5 %all-gather.28.cloned.1.call-done = bf16[256,273,128]{2,0,1:T(8,128)(2,1)} async-done(((bf16[16,273,128]{2,0,1:T(8,128)(2,1)}), bf16[256,273,128]{2,0,1:T(8,128)(2,1)}) %all-gather.28.cloned.1.call-update) | async-done | bytes 17891344 | tf_op jit(solution)/shard_map/all_gather | solution.py:17
  306.6 76.0 %while.40 = (s32[]{:T(128)}, f32[16,273,128]{2,1,0:T(8,128)S(1)}, f32[16,273]{1,0:T(8,128)S(1)}, s32[]{:T(128)}, bf16[16,16,273,128]{3,1,0,2:T(8,128)(2,1)}, /*i...) while((s32[]{:T(128)}, f32[16,273,128]{2,1,0:T(8,128)S(1)}, ...), condition=%wide.region_5.6_spmd.clone, body=%wide.region_4.5_spmd.clone.sunk | while | flops 2817365 | bytes 7871289 | solution.py:35
  382.5 3.3 fusion.61
  385.9 3.0 fusion.81
  388.9 7.4 multiply_reduce_fusion.8
  396.4 3.0 multiply_convert_fusion.7
  399.4 132.4 %all-gather.22.cloned.1.call-done = bf16[2048,5632]{1,0:T(8,128)(2,1)} async-done(((bf16[64,5632]{1,0:T(8,128)(2,1)}), bf16[2048,5632]{1,0:T(8,128)(2,1)}) %all-gather.22.cloned.1.call-update) | async-done | bytes 23068688 | tf_op jit(solution)/shard_map/all_gather | solution.py:153
  531.8 12.5 fusion.82
  544.3 133.2 %all-gather.24.cloned.1.call-done = bf16[2048,5632]{1,0:T(8,128)(2,1)} async-done(((bf16[64,5632]{1,0:T(8,128)(2,1)}), bf16[2048,5632]{1,0:T(8,128)(2,1)}) %all-gather.24.cloned.1.call-update) | async-done | bytes 23068688 | tf_op jit(solution)/shard_map/all_gather | solution.py:154
  677.5 12.8 fusion.83
  690.3 132.9 %all-gather.26.cloned.1.call-done = bf16[5632,2048]{1,0:T(8,128)(2,1)} async-done(((bf16[176,2048]{1,0:T(8,128)(2,1)}), bf16[5632,2048]{1,0:T(8,128)(2,1)}) %all-gather.26.cloned.1.call-update) | async-done | bytes 23068688 | tf_op jit(solution)/shard_map/all_gather | solution.py:155
  823.2 18.6 multiply_convert_fusion
  841.9 12.6 fusion.84
  854.4 14.9 multiply_reduce_fusion.5
  869.3 3.2 fusion.20
  872.6 6.8 multiply_reduce_fusion.6
  883.7 2.4 multiply_convert_fusion.3
  896.2 8.4 fusion.48
  905.5 3.6 fusion.64
  909.2 22.0 all-gather.3
  931.2 54.2 %all-gather.30.cloned.1.call-done = bf16[256,273,128]{2,0,1:T(8,128)(2,1)} async-done(((bf16[16,273,128]{2,0,1:T(8,128)(2,1)}), bf16[256,273,128]{2,0,1:T(8,128)(2,1)}) %all-gather.30.cloned.1.call-update) | async-done | bytes 17891344 | tf_op jit(solution)/shard_map/all_gather | solution.py:17
  985.4 75.9 %while.41 = (s32[]{:T(128)}, f32[16,273,128]{2,1,0:T(8,128)S(1)}, f32[16,273]{1,0:T(8,128)S(1)}, s32[]{:T(128)}, bf16[16,16,273,128]{3,1,0,2:T(8,128)(2,1)}, /*i...) while((s32[]{:T(128)}, f32[16,273,128]{2,1,0:T(8,128)S(1)}, ...), condition=%wide.region_13.14_spmd.clone, body=%wide.region_12.13_spmd.clone.sunk | while | flops 2817369 | bytes 7871351 | solution.py:35
  1071.1 3.5 fusion.40
  1076.9 8.3 fusion.34
  1086.5 19.7 fusion.87
  1106.2 19.7 fusion.88
  1127.1 19.9 fusion.23
  1150.1 13.2 fusion.13
  1163.3 5.9 fusion.86
  1169.3 2.4 fusion.17
  1171.7 40.1 all-reduce.5
  1213.0 3.4 fusion.22
  1216.5 265.2 %reduce-scatter.14.cloned.1.call-done = f32[64,2048]{1,0:T(8,128)} async-done(((f32[2048,2048]{1,0:T(8,128)}), f32[64,2048]{1,0:T(8,128)}) %reduce-scatter.14.cloned.1.call-update) | async-done | bytes 524304 | tf_op jit(solution)/shard_map/reduce_scatter | solution.py:282
  1481.7 141.4 %reduce-scatter.10.cloned.1.call-done = f32[64,256]{1,0:T(8,128)} async-done(((f32[2048,256]{1,0:T(8,128)}), f32[64,256]{1,0:T(8,128)}) %reduce-scatter.10.cloned.1.call-update) | async-done | bytes 65552 | tf_op jit(solution)/shard_map/reduce_scatter | solution.py:280
  1623.1 356.1 %reduce-scatter.12.cloned.1.call-done = f32[64,2048]{1,0:T(8,128)} async-done(((f32[2048,2048]{1,0:T(8,128)}), f32[64,2048]{1,0:T(8,128)}) %reduce-scatter.12.cloned.1.call-update) | async-done | bytes 524304 | tf_op jit(solution)/shard_map/reduce_scatter | solution.py:281
  1979.3 971.4 %reduce-scatter.16.cloned.1.call-done = f32[64,5632]{1,0:T(8,128)} async-done(((f32[2048,5632]{1,0:T(8,128)}), f32[64,5632]{1,0:T(8,128)}) %reduce-scatter.16.cloned.1.call-update) | async-done | bytes 1441808 | tf_op jit(solution)/shard_map/reduce_scatter | solution.py:192
  2950.7 973.0 %reduce-scatter.18.cloned.1.call-done = f32[64,5632]{1,0:T(8,128)} async-done(((f32[2048,5632]{1,0:T(8,128)}), f32[64,5632]{1,0:T(8,128)}) %reduce-scatter.18.cloned.1.call-update) | async-done | bytes 1441808 | tf_op jit(solution)/shard_map/reduce_scatter | solution.py:193
  3923.7 973.0 %reduce-scatter.20.cloned.1.call-done = f32[176,2048]{1,0:T(8,128)} async-done(((f32[5632,2048]{1,0:T(8,128)}), f32[176,2048]{1,0:T(8,128)}) %reduce-scatter.20.cloned.1.call-update) | async-done | bytes 1441808 | tf_op jit(solution)/shard_map/reduce_scatter | solution.py:194
  (327 shorter events, 189.7 us)
Async XLA Ops:
  7.2 61.8 %copy-start = (bf16[1,256,2048]{2,1,0:T(8,128)(2,1)S(1)}, bf16[1,256,2048]{2,1,0:T(8,128)(2,1)}, u32[]{:S(2)}) copy-start(bf16[1,256,2048]{2,1,0:T(8,128)(2,1)} %param.16) | copy-start | bytes 3145732
  7.2 60.2 %all-gather.18.cloned.1.call-start = ((), (), s32[]{:S(2)}) async-start(), calls=%async_computation.9 | async-start | bytes 1081344 | tf_op jit(solution)/shard_map/all_gather | solution.py:102
  7.9 138.8 %all-gather.14.cloned.1.call-start = ((), (), s32[]{:S(2)}) async-start(), calls=%async_computation.7 | async-start | bytes 8650752 | tf_op jit(solution)/shard_map/all_gather | solution.py:103
  8.7 196.0 %all-gather.16.cloned.1.call-start = ((), (), s32[]{:S(2)}) async-start(), calls=%async_computation.8 | async-start | bytes 1081344 | tf_op jit(solution)/shard_map/all_gather | solution.py:101
  9.4 297.2 %all-gather.28.cloned.1.call-start = ((), (), s32[]{:S(2)}) async-start(), calls=%async_computation.21 | async-start | bytes 19009536 | tf_op jit(solution)/shard_map/all_gather | solution.py:17
  55.7 2.0 copy-start.47
  69.5 94.6 %copy-start.37 = (bf16[256,16,16]{0,2,1:T(8,128)(2,1)}, bf16[256,16,16]{0,2,1:T(8,128)(2,1)S(1)}, u32[]{:S(2)}) copy-start(bf16[256,16,16]{0,2,1:T(8,128)(2,1)S(1)} %get-tuple-element.460) | copy-start | bytes 393220
  70.8 93.3 %copy-start.8 = (bf16[256,16,16,16]{0,3,2,1:T(8,128)(2,1)}, bf16[256,16,16,16]{0,3,2,1:T(8,128)(2,1)S(1)}, u32[]{:S(2)}) copy-start(bf16[256,16,16,16]{0,3,2,1:T(8,128)(2,1)S(1)} %multiply_convert_fusion.4) | copy-start | bytes 6291460
  166.3 3.3 copy-start.50
  166.3 222.6 %all-gather.20.cloned.1.call-start = ((), (), s32[]{:S(2)}) async-start(), calls=%async_computation.10 | async-start | bytes 8650752 | tf_op jit(solution)/shard_map/all_gather | solution.py:104
  166.9 364.8 %all-gather.22.cloned.1.call-start = ((), (), s32[]{:S(2)}) async-start(), calls=%async_computation.11 | async-start | bytes 23789568 | tf_op jit(solution)/shard_map/all_gather | solution.py:153
  167.5 510.0 %all-gather.24.cloned.1.call-start = ((), (), s32[]{:S(2)}) async-start(), calls=%async_computation.12 | async-start | bytes 23789568 | tf_op jit(solution)/shard_map/all_gather | solution.py:154
  168.2 655.0 %all-gather.26.cloned.1.call-start = ((), (), s32[]{:S(2)}) async-start(), calls=%async_computation.13 | async-start | bytes 23789568 | tf_op jit(solution)/shard_map/all_gather | solution.py:155
  169.0 816.4 %all-gather.30.cloned.1.call-start = ((), (), s32[]{:S(2)}) async-start(), calls=%async_computation.22 | async-start | bytes 19009536 | tf_op jit(solution)/shard_map/all_gather | solution.py:17
  206.9 23.2 copy-start.36
  230.7 6.1 copy-start.41
  230.7 2.2 copy-start.32
  230.7 2.3 copy-start.38
  231.3 5.5 copy-start.17
  233.0 3.8 copy-start.16
  382.5 3.3 copy-start.18
  382.5 3.3 copy-start.33
  382.5 3.3 copy-start.42
  385.9 3.1 copy-start.1
  869.3 3.3 copy-start.51
  872.6 6.8 copy-start.3
  883.6 332.9 %reduce-scatter.8.cloned.1.call-start = ((), (), s32[]{:S(2)}) async-start(), calls=%async_computation.14 | async-start | bytes 2162688 | tf_op jit(solution)/shard_map/reduce_scatter | solution.py:279
  883.6 2.5 copy-start.10
  883.6 2.5 copy-start.39
  893.1 2.2 copy-start.4
  895.0 586.7 %reduce-scatter.14.cloned.1.call-start = ((), (), s32[]{:S(2)}) async-start(), calls=%async_computation.17 | async-start | bytes 17301504 | tf_op jit(solution)/shard_map/reduce_scatter | solution.py:282
  904.6 718.5 %reduce-scatter.10.cloned.1.call-start = ((), (), s32[]{:S(2)}) async-start(), calls=%async_computation.15 | async-start | bytes 2162688 | tf_op jit(solution)/shard_map/reduce_scatter | solution.py:280
  1061.3 2.2 copy-start.7
  1061.3 2.5 copy-start.20
  1061.3 2.5 copy-start.45
  1061.3 2.5 copy-start.46
  1066.4 2.3 copy-start.2
  1070.8 908.4 %reduce-scatter.12.cloned.1.call-start = ((), (), s32[]{:S(2)}) async-start(), calls=%async_computation.16 | async-start | bytes 17301504 | tf_op jit(solution)/shard_map/reduce_scatter | solution.py:281
  1071.1 3.5 copy-start.11
  1071.1 3.5 copy-start.40
  1085.3 1865.4 %reduce-scatter.16.cloned.1.call-start = ((), (), s32[]{:S(2)}) async-start(), calls=%async_computation.18 | async-start | bytes 47579136 | tf_op jit(solution)/shard_map/reduce_scatter | solution.py:192
  1106.2 2817.5 %reduce-scatter.18.cloned.1.call-start = ((), (), s32[]{:S(2)}) async-start(), calls=%async_computation.19 | async-start | bytes 47579136 | tf_op jit(solution)/shard_map/reduce_scatter | solution.py:193
  1125.9 3770.8 %reduce-scatter.20.cloned.1.call-start = ((), (), s32[]{:S(2)}) async-start(), calls=%async_computation.20 | async-start | bytes 47579136 | tf_op jit(solution)/shard_map/reduce_scatter | solution.py:194
  1150.1 13.2 copy-start.30
  1163.3 6.0 copy-start.27
  1169.3 2.4 copy-start.49
  1169.3 43.7 copy-start.48
  1169.3 43.7 copy-start.5
  (20 other events, 25.2 us)
Sparse Core Ops, SparseCore 0:
  10.9 56.4 all-gather.17
  70.4 76.2 all-gather.13
  149.6 52.2 all-gather.15
  203.9 102.6 all-gather.27
  309.4 76.2 all-gather.19
  388.4 143.2 all-gather.21
  534.6 142.8 all-gather.23
  680.4 142.7 all-gather.25
  883.7 101.6 all-gather.29
  988.1 135.8 reduce-scatter.7
  1127.0 354.6 reduce-scatter.13
  1484.5 138.5 reduce-scatter.9
  1626.0 353.2 reduce-scatter.11
  1982.0 968.6 reduce-scatter.15
  2953.4 970.2 reduce-scatter.17
  3926.4 970.2 reduce-scatter.19
where the time goes:
time: 4920 us; the launch traced here: 4900 us
  waiting for transfers between devices  4290 us (87%)
  matrix products  229 us (5%)
  blocking collectives  157 us (3%)
  local copies, waits for them, and re-layouts  105 us (2%)
  other arithmetic  86.1 us (2%)
    reduce_scatter x1, waiting for transfers between devices, on_device(): lax.psum_scatter(grad_w_down, ('seq', 'fsdp'), scatter_dimension=0, tiled...  973 us
    reduce_scatter x1, waiting for transfers between devices, on_device(): lax.psum_scatter(grad_w_up, ('seq', 'fsdp'), scatter_dimension=0, tiled=T...  973 us
    reduce_scatter x1, waiting for transfers between devices, on_device(): lax.psum_scatter(grad_w_gate, ('seq', 'fsdp'), scatter_dimension=0, tiled...  971 us
    reduce_scatter x1, waiting for transfers between devices, on_device(): lax.psum_scatter(grad_w_value, ('seq', 'fsdp'), scatter_dimension=0, tile...  356 us
    reduce_scatter x1, waiting for transfers between devices, on_device(): lax.psum_scatter(grad_w_out, ('seq', 'fsdp'), scatter_dimension=0, tiled=...  265 us
    reduce_scatter x1, waiting for transfers between devices, on_device(): lax.psum_scatter(grad_w_key, ('seq', 'fsdp'), scatter_dimension=0, tiled=...  141 us
    all_gather x1, waiting for transfers between devices, on_device(): lax.all_gather(w_up, ('seq', 'fsdp'), axis=0, tiled=True)  133 us
    all_gather x1, waiting for transfers between devices, on_device(): lax.all_gather(w_down, ('seq', 'fsdp'), axis=0, tiled=True)  133 us
  transfers between devices with their start and end apart: 16, of which 13 were waited for; matrix products, arithmetic and copies ran while one was open for 7% of the time, Pallas kernels for 0%

commit v1 on v0

v1 whole, which is shorter than its diff:
```python
import jax
import jax.numpy as jnp
import numpy as np
from jax import lax
from jax.sharding import Mesh
from jax.sharding import PartitionSpec as P

H = 16
FD = 16
DV = 128
HP = 2
TP = ("l", "y", "c")
DP = ("h", "x")
EPS = 1e-5
F32, BF16 = jnp.float32, jnp.bfloat16
HIGH = lax.Precision.HIGHEST


def dot(a, b, dims):
    return lax.dot_general(a, b, (dims, ((), ())), preferred_element_type=F32)


def mm(a, b):
    return dot(a, b, ((1,), (0,)))


def mm_nt(a, b):
    return dot(a, b, ((1,), (1,)))


def mm_tn(a, b):
    return dot(a, b, ((0,), (0,)))


def swap(a, axis):
    return lax.ppermute(a, axis, [(0, 1), (1, 0)])


def gather_tokens(own):
    half = own.shape[0] // 2
    from_l, from_y = swap(own, "l"), swap(own, "y")
    far = jnp.concatenate([swap(from_y[:half], "l"), swap(from_l[half:], "y")], 0)
    same = [own, from_y, from_l, far]
    return [b for s in same for b in (s, swap(s, "c"))]


def scatter_tokens(parts):
    half = parts[0].shape[0] // 2
    pair = lambda r: parts[r].astype(F32) + swap(parts[r ^ 1], "c").astype(F32)
    far = pair(6).astype(BF16)
    via_l, via_y = swap(far[:half], "l").astype(F32), swap(far[half:], "y").astype(F32)
    for_y, for_l = pair(2), pair(4)
    for_y = jnp.concatenate([for_y[:half] + via_l, for_y[half:]], 0).astype(BF16)
    for_l = jnp.concatenate([for_l[:half], for_l[half:] + via_y], 0).astype(BF16)
    return pair(0) + swap(for_l, "l").astype(F32) + swap(for_y, "y").astype(F32)


def reorder(blocks):
    me = lax.axis_index(TP)
    return jnp.stack([lax.dynamic_index_in_dim(blocks, p ^ me, 0, keepdims=False) for p in range(8)])


def flips(a):
    a = jnp.where(lax.axis_index("h") == 0, a, a[::-1])
    return jnp.where(lax.axis_index("x") == 0, a, a[:, ::-1])


def gather_weights(a):
    if lax.axis_size("h") == 2 and lax.axis_size("x") == 2:
        over_h = swap(a, "h")
        rel = jnp.stack([jnp.stack([a, swap(a, "x")]), jnp.stack([over_h, swap(over_h, "x")])])
        return flips(rel)
    full = lax.all_gather(a, DP)
    return full.reshape((lax.axis_size("h"), lax.axis_size("x")) + a.shape)


def scatter_weights(parts):
    if parts.shape[:2] == (2, 2):
        rel = flips(parts)
        near = rel[0, 0].astype(F32) + swap(rel[0, 1], "x").astype(F32)
        over = rel[1, 0].astype(F32) + swap(rel[1, 1], "x").astype(F32)
        return near + swap(over.astype(BF16), "h").astype(F32)
    flat = parts.reshape((-1,) + parts.shape[2:])
    return lax.psum_scatter(flat, DP, scatter_dimension=0, tiled=False).astype(F32)


def sub_head():
    return lax.axis_size(DP + TP) // H == 2 * lax.axis_size("x")


def split_heads(w, width):
    rows = w.shape[0]
    if sub_head():
        w = w.reshape(rows, 2, HP, 2, 2, width).transpose(3, 4, 1, 0, 2, 5)
    else:
        w = w.reshape(rows, HP, 8, width).transpose(2, 0, 1, 3)
    return w.reshape(8, rows, HP * width)


def join_heads(w, width):
    rows = w.shape[1]
    if sub_head():
        w = w.reshape(2, 2, 2, rows, HP, width).transpose(3, 2, 4, 0, 1, 5)
    else:
        w = w.reshape(8, rows, HP, width).transpose(1, 2, 0, 3)
    return w.reshape(rows, H * width)


def split_hidden(w):
    h, x = lax.axis_size("h"), lax.axis_size("x")
    rows = w.shape[0]
    w = w.reshape(rows, h, 8, x, -1).transpose(2, 0, 1, 3, 4)
    return w.reshape(8, rows, -1)


def join_hidden(w):
    h, x = lax.axis_size("h"), lax.axis_size("x")
    rows = w.shape[1]
    w = w.reshape(8, rows, h, x, -1).transpose(1, 2, 0, 3, 4)
    return w.reshape(rows, -1)


def columns_in(w):
    rows, n = w.shape[1:]
    mine = lax.all_to_all(w, TP, 0, 0, tiled=True)
    full = gather_weights(mine.reshape(8 * rows, n))
    h, x = full.shape[:2]
    return full.reshape(h, x, 8, rows, n).transpose(0, 2, 1, 3, 4).reshape(-1, n)


def columns_out(grad):
    h, x = lax.axis_size("h"), lax.axis_size("x")
    n = grad.shape[1]
    parts = grad.reshape(h, 8, x, -1, n).transpose(0, 2, 1, 3, 4)
    mine = scatter_weights(parts).astype(BF16)
    return lax.all_to_all(mine, TP, 0, 0, tiled=True)


def out_rows_in(w):
    full = gather_weights(w)
    if sub_head():
        h, x, rows, d = full.shape
        full = lax.all_to_all(full.reshape(2, h // 2, x, rows, d), "c", 0, 0, tiled=True)
        full = full.transpose(1, 0, 2, 3, 4)
    return full.reshape(HP * DV, -1)


def out_rows_out(grad):
    h, x = lax.axis_size("h"), lax.axis_size("x")
    d = grad.shape[1]
    if sub_head():
        grad = grad.reshape(HP, 2, x, -1, d).transpose(1, 0, 2, 3, 4)
        grad = lax.all_to_all(grad, "c", 0, 0, tiled=True)
    return scatter_weights(grad.reshape(h, x, -1, d))


def entering(total, reverse):
    n = lax.axis_size("h")
    low = total.astype(BF16)
    got = jnp.zeros_like(total)
    for s in range(1, n):
        route = [(i + s, i) if reverse else (i, i + s) for i in range(n - s)]
        got = got + lax.ppermute(low, "h", route).astype(F32)
    return got


PAIRS = [(i, j) for i in range(FD + 1) for j in range(i, FD + 1)]
LEFT = np.zeros((FD + 1, len(PAIRS)), np.float32)
RIGHT = np.zeros((FD + 1, len(PAIRS)), np.float32)
for col, (i, j) in enumerate(PAIRS):
    LEFT[i, col] = 1.0
    RIGHT[j, col] = 2.0**-0.5 if i == j < FD else 1.0


def features(u):
    wide = jnp.concatenate([u * 0.5, jnp.ones(u.shape[:-1] + (1,), u.dtype)], -1)
    return jnp.dot(wide, LEFT, precision=HIGH) * jnp.dot(wide, RIGHT, precision=HIGH)


def ein(spec, a, b):
    return jnp.einsum(spec, a, b, preferred_element_type=F32)


def masks(lengths, tokens, chunk):
    ends = jnp.cumsum(lengths)
    places = lax.axis_index("h") * tokens + jnp.arange(tokens, dtype=jnp.int32)
    segment = jnp.sum((places[:, None] >= ends[None, :]).astype(jnp.int32), 1).reshape(-1, chunk)
    crosses = (segment == jnp.argmax(lengths)).astype(F32)
    row = jnp.arange(chunk)
    pairs = (segment[:, :, None] == segment[:, None, :]) & (row[:, None] >= row[None, :])
    return crosses, pairs.astype(F32)


def attention(queries, keys, values, crosses, pairs):
    taylor_q, pull_q = jax.vjp(features, queries)
    taylor_k, pull_k = jax.vjp(features, keys)
    feat_q = (taylor_q * crosses[:, :, None, None]).astype(BF16)
    feat_k = (taylor_k * crosses[:, :, None, None]).astype(BF16)
    flat = jnp.einsum("cthe,cshe->chts", queries, keys, precision=HIGH) * 0.25
    scores = (1.0 + flat + 0.5 * flat * flat) * pairs[:, None]
    low = scores.astype(BF16)
    added = ein("cshf,cshv->chfv", feat_k, values)
    added_den = jnp.sum(feat_k.astype(F32), 1)
    both = jnp.concatenate([added, added_den[..., None]], -1)
    state = entering(jnp.sum(both, 0), False) + jnp.cumsum(both, 0) - both
    state_low, den_state = state[..., :DV].astype(BF16), state[..., DV].astype(BF16)
    numer = ein("chts,cshv->cthv", low, values) + ein("cthf,chfv->cthv", feat_q, state_low)
    denom = jnp.sum(scores, -1).transpose(0, 2, 1) + ein("cthf,chf->cth", feat_q, den_state)
    attn = numer / denom[..., None]

    def back(d_attn):
        d_numer = (d_attn / denom[..., None]).astype(BF16)
        d_denom = -jnp.sum(d_attn * attn, -1) / denom
        use = ein("cthf,cthv->chfv", feat_q, d_numer)
        use_den = ein("cthf,cth->chf", feat_q, d_denom.astype(BF16))
        both = jnp.concatenate([use, use_den[..., None]], -1)
        total = jnp.sum(both, 0)
        later = entering(total, True) + total - jnp.cumsum(both, 0)
        back_low, back_den = later[..., :DV].astype(BF16), later[..., DV]
        d_scores = ein("cthv,cshv->chts", d_numer, values) + d_denom.transpose(0, 2, 1)[..., None]
        d_flat = (d_scores * pairs[:, None] * (1.0 + flat) * 0.25).astype(BF16)
        d_feat_q = ein("cthv,chfv->cthf", d_numer, state_low) + d_denom[..., None] * den_state.astype(F32)[:, None]
        d_feat_k = ein("cshv,chfv->cshf", values, back_low) + back_den[:, None]
        d_q = ein("chts,cshe->cthe", d_flat, keys.astype(BF16)) + pull_q(d_feat_q * crosses[:, :, None, None])[0]
        d_k = ein("chts,cthe->cshe", d_flat, queries.astype(BF16)) + pull_k(d_feat_k * crosses[:, :, None, None])[0]
        d_v = ein("chts,cthv->cshv", low, d_numer) + ein("cshf,chfv->cshv", feat_k, back_low)
        return d_q, d_k, d_v

    return attn, back


def stack(blocks):
    return jnp.concatenate(blocks, 0)


def unstack(rows):
    return list(rows.reshape(8, -1, rows.shape[-1]))


def on_device(
    tokens, seq_lengths, norm_gain, w_query, w_key, w_value, w_out, mlp_gain, w_gate, w_up, w_down, cotangent
):
    x_low = tokens[0]
    x_own, dy_own = x_low.astype(F32), cotangent[0].astype(F32)
    size, d_model = x_own.shape
    gain_one = norm_gain.astype(F32)[:, None]
    gain_two = mlp_gain.astype(F32)[:, None]
    crosses, pairs = masks(seq_lengths[0], 8 * size, size)

    gained = lambda gain, w: (gain * w.astype(F32)).astype(BF16)
    w_qkv = columns_in(
        jnp.concatenate(
            [
                split_heads(gained(gain_one, w_value), DV),
                split_heads(gained(gain_one, w_query), FD),
                split_heads(gained(gain_one, w_key), FD),
            ],
            -1,
        )
    )
    x_all = stack(gather_tokens(x_low))
    w_out_mine = out_rows_in(w_out)
    w_gu = columns_in(
        jnp.concatenate([split_hidden(gained(gain_two, w_gate)), split_hidden(gained(gain_two, w_up))], -1)
    )
    w_down_mine = gather_weights(w_down).reshape(-1, d_model)
    ff = w_down_mine.shape[0]

    r_all = lax.rsqrt(jnp.mean(jnp.square(x_all.astype(F32)), -1, keepdims=True) + EPS)
    qkv = reorder((mm(x_all, w_qkv) * r_all).reshape(8, size, -1))
    nv, nq = HP * DV, HP * FD
    values = qkv[..., :nv].astype(BF16).reshape(8, size, HP, DV)
    queries = qkv[..., nv : nv + nq].reshape(8, size, HP, FD)
    keys = qkv[..., nv + nq :].reshape(8, size, HP, FD)
    attn, attention_back = attention(queries, keys, values, crosses, pairs)
    mixed = reorder(attn.astype(BF16).reshape(8, size, nv)).reshape(8 * size, nv)
    branch = scatter_tokens(unstack(mm(mixed, w_out_mine).astype(BF16)))
    resid = x_own + branch
    r_two = lax.rsqrt(jnp.mean(resid * resid, -1, keepdims=True) + EPS)
    n_two = resid * r_two

    n_all = stack(gather_tokens(n_two.astype(BF16)))
    dy_all = stack(gather_tokens(cotangent[0]))
    gu = mm(n_all, w_gu)
    gate, up = gu[:, :ff], gu[:, ff:]
    sig = jax.nn.sigmoid(gate)
    silu = gate * sig
    hidden = (silu * up).astype(BF16)
    d_hidden = mm_nt(dy_all, w_down_mine)
    d_gate = d_hidden * up * sig * (1.0 + gate * (1.0 - sig))
    d_gu = jnp.concatenate([d_gate, d_hidden * silu], 1).astype(BF16)
    d_n_two = scatter_tokens(unstack(mm_nt(d_gu, w_gu).astype(BF16)))
    block_out = resid + scatter_tokens(unstack(mm(hidden, w_down_mine).astype(BF16)))
    g_gu = columns_out(mm_tn(n_all, d_gu).astype(BF16))
    g_down = scatter_weights(
        mm_tn(hidden, dy_all).astype(BF16).reshape(lax.axis_size("h"), lax.axis_size("x"), -1, d_model)
    )
    d_resid = dy_own + r_two * (d_n_two - n_two * jnp.mean(d_n_two * n_two, -1, keepdims=True))

    db_all = stack(gather_tokens(d_resid.astype(BF16)))
    d_attn = reorder(mm_nt(db_all, w_out_mine).reshape(8, size, nv)).reshape(8, size, HP, DV)
    g_out = out_rows_out(mm_tn(mixed, db_all).astype(BF16))
    d_q, d_k, d_v = attention_back(d_attn)
    d_qkv = jnp.concatenate([t.reshape(8, size, -1) for t in (d_v, d_q, d_k)], -1)
    d_qkv = (reorder(d_qkv).reshape(8 * size, -1) * r_all).astype(BF16)
    d_x = scatter_tokens(unstack(mm_nt(d_qkv, w_qkv).astype(BF16)))
    g_qkv = columns_out(mm_tn(x_all, d_qkv).astype(BF16)).astype(F32)
    n_one = x_own * lax.rsqrt(jnp.mean(x_own * x_own, -1, keepdims=True) + EPS)
    input_grad = d_resid + d_x - n_one * jnp.mean(d_x * n_one, -1, keepdims=True)

    g_gu = g_gu.astype(F32)
    g_gate, g_up = join_hidden(g_gu[..., :ff]), join_hidden(g_gu[..., ff:])
    g_value = join_heads(g_qkv[..., :nv], DV)
    g_query = join_heads(g_qkv[..., nv : nv + nq], FD)
    g_key = join_heads(g_qkv[..., nv + nq :], FD)
    along = lambda w, g: jnp.sum(w.astype(F32) * g, -1)
    g_gain_one = along(w_query, g_query) + along(w_key, g_key) + along(w_value, g_value)
    g_gain_two = along(w_gate, g_gate) + along(w_up, g_up)
    return (
        block_out[None],
        input_grad[None],
        g_gain_one,
        gain_one * g_query,
        gain_one * g_key,
        gain_one * g_value,
        g_out,
        g_gain_two,
        gain_two * g_gate,
        gain_two * g_up,
        g_down,
    )


def solution(mesh):
    seq, fsdp = mesh.shape["seq"], mesh.shape["fsdp"]
    fine = Mesh(mesh.devices.reshape(seq // 8, 2, 2, 2, fsdp), ("h", "l", "y", "c", "x"))
    along = ("h", "l", "y", "c")
    token, vec, mat = P("x", along, None), P(along + ("x",)), P(along + ("x",), None)
    return jax.shard_map(
        on_device,
        mesh=fine,
        in_specs=(token, P("x", None), vec, mat, mat, mat, mat, vec, mat, mat, mat, token),
        out_specs=(token, token, vec, mat, mat, mat, mat, vec, mat, mat, mat),
        check_vma=False,
    )
```

time: 4920 us -> 897 us (0.18)
  waiting for transfers between devices: 4290 us -> 338 us
  blocking collectives: 157 us -> 0 us
  starting transfers between devices: 1.28 us -> 99 us
  local copies, waits for them, and re-layouts: 105 us -> 176 us
  matrix products: 229 us -> 159 us
    reduce_scatter x7 -> x0, waiting for transfers between devices: 3680 us -> none  [the longest x1 973 us: on_device(): lax.psum_scatter(grad_w_down, ('seq', 'fsdp'), scatter_dimension=0, tiled...]
    all_gather x9 -> x0, waiting for transfers between devices: 603 us -> none  [the longest x1 133 us: on_device(): lax.all_gather(w_up, ('seq', 'fsdp'), axis=0, tiled=True)]
    ppermute x0 -> x90, waiting for transfers between devices: none -> 338 us  [the longest x88 328 us: swap(): return lax.ppermute(a, axis, [(0, 1), (1, 0)])]
    unnamed x3 -> x0, blocking collectives: 114 us -> none
    ppermute x0 -> x90, starting transfers between devices: none -> 82.9 us  [the longest x88 75.9 us: swap(): return lax.ppermute(a, axis, [(0, 1), (1, 0)])]
    dot_general x36 -> x34, matrix products: 229 us -> 159 us  [the longest x12 115 us: dot(): return lax.dot_general(a, b, (dims, ((), ())), preferred_element_type=F32)]
    dynamic_slice x64 -> x3, local copies, waits for them, and re-layouts: 66.2 us -> 5.89 us  [reorder(): lax.dynamic_index_in_dim(blocks, p ^ me, 0, keepdims=False)]
  transfers between devices with their start and end apart: 16 -> 94, of which waited for: 13 -> 29; matrix products, arithmetic and copies ran while one was open for 7% -> 37% of each run, Pallas kernels for 0% -> 0%
where the time goes in v1:
time: 897 us; the launch traced here: 884 us
  waiting for transfers between devices  338 us (38%)
  local copies, waits for them, and re-layouts  176 us (20%)
  matrix products  159 us (18%)
  other arithmetic  110 us (12%)
  starting transfers between devices  99 us (11%)
    ppermute x88, waiting for transfers between devices, swap(): return lax.ppermute(a, axis, [(0, 1), (1, 0)])  328 us
    dot_general x12, matrix products, dot(): return lax.dot_general(a, b, (dims, ((), ())), preferred_element_type=F32)  115 us
    ppermute x88, starting transfers between devices, swap(): return lax.ppermute(a, axis, [(0, 1), (1, 0)])  75.9 us
    unnamed x278, local copies, waits for them, and re-layouts  63.9 us
  transfers between devices with their start and end apart: 94, of which 29 were waited for; matrix products, arithmetic and copies ran while one was open for 37% of the time, Pallas kernels for 0%

profile of v1, /device:TPU:0, one launch (start us, length us, event | category | flops | bytes accessed | tf_op | source)
XLA Modules:
  0.0 883.9 jit_solution(6759655922577701760)
XLA Ops:
  26.0 4.8 reshape.392
  32.6 4.5 reshape.393
  45.8 5.6 collective-permute-done.14
  53.7 4.8 all-to-all-start.1
  62.1 4.7 collective-permute-done.34
  68.7 5.5 collective-permute-done.8
  86.3 41.6 %collective-permute-done.9 = bf16[512,320]{1,0:T(8,128)(2,1)S(1)} collective-permute-done((bf16[512,320]{1,0:T(8,128)(2,1)S(1)}, bf16[512,320]{1,0:T(8,128)(2,1)S(1)}, u32[]{:S(2)}, u32[]{:S(2)}) %collective-permute-start.9) | collective-permute-done | bytes 327712 | tf_op jit(solution)/shard_map/ppermute | solution.py:36
  133.3 5.0 collective-permute-start.5
  142.8 11.7 %collective-permute-done.10 = bf16[512,320]{1,0:T(8,128)(2,1)S(1)} collective-permute-done((bf16[512,320]{1,0:T(8,128)(2,1)S(1)}, bf16[512,320]{1,0:T(8,128)(2,1)S(1)}, u32[]{:S(2)}, u32[]{:S(2)}) %collective-permute-start.10) | collective-permute-done | bytes 327712 | tf_op jit(solution)/shard_map/ppermute | solution.py:36
  175.5 7.6 stack.154
  195.1 5.0 convert_reduce_fusion
  203.9 5.5 collective-permute-start.11
  209.4 4.3 fusion.4
  245.4 9.2 %collective-permute-done.18 = bf16[128,2048]{1,0:T(8,128)(2,1)} collective-permute-done((bf16[128,2048]{1,0:T(8,128)(2,1)}, bf16[128,2048]{1,0:T(8,128)(2,1)}, u32[]{:S(2)}, u32[]{:S(2)}) %collective-permute-start.18) | collective-permute-done | bytes 524320 | tf_op jit(solution)/shard_map/ppermute | solution.py:36
  256.7 29.8 %collective-permute-done.21 = bf16[128,2048]{1,0:T(8,128)(2,1)S(1)} collective-permute-done((bf16[128,2048]{1,0:T(8,128)(2,1)}, bf16[128,2048]{1,0:T(8,128)(2,1)S(1)}, u32[]{:S(2)}, u32[]{:S(2)}) %collective-permute-start.21) | collective-permute-done | bytes 524320 | tf_op jit(solution)/shard_map/ppermute | solution.py:36
  295.8 13.4 %collective-permute-done.32 = bf16[512,1408]{1,0:T(8,128)(2,1)S(1)} collective-permute-done((bf16[512,1408]{1,0:T(8,128)(2,1)}, bf16[512,1408]{1,0:T(8,128)(2,1)S(1)}, u32[]{:S(2)}, u32[]{:S(2)}) %collective-permute-start.32) | collective-permute-done | bytes 1441824 | tf_op jit(solution)/shard_map/ppermute | solution.py:36
  311.5 20.1 %collective-permute-done.19 = bf16[256,2048]{1,0:T(8,128)(2,1)S(1)} collective-permute-done((bf16[256,2048]{1,0:T(8,128)(2,1)S(1)}, bf16[256,2048]{1,0:T(8,128)(2,1)S(1)}, u32[]{:S(2)}, u32[]{:S(2)}) %collective-permute-start.19) | collective-permute-done | bytes 1048608 | tf_op jit(solution)/shard_map/ppermute | solution.py:36
  344.1 17.8 %collective-permute-done.24 = bf16[256,2048]{1,0:T(8,128)(2,1)S(1)} collective-permute-done((bf16[256,2048]{1,0:T(8,128)(2,1)S(1)}, bf16[256,2048]{1,0:T(8,128)(2,1)S(1)}, u32[]{:S(2)}, u32[]{:S(2)}) %collective-permute-start.24) | collective-permute-done | bytes 1048608 | tf_op jit(solution)/shard_map/ppermute | solution.py:36
  369.9 6.1 collective-permute-done.28
  384.5 17.8 %fusion.112 = f32[2048,1408]{0,1:T(8,128)} fusion(bf16[2048,2048]{1,0:T(8,128)(2,1)} %constant_dynamic-update-slice_fusion.17, bf16[2048,1408]{1,0:T(8,128)(2,1)S(1)} %bitcast.332), kind=kOutput, calls=%fused_computation.372 | convolution fusion | flops 11811160064 | bytes 25690112 | tf_op jit(solution)/shard_map/dot_general | solution.py:20
  402.2 14.6 %multiply_convert_fusion.1 = (bf16[2048,704]{0,1:T(8,128)(2,1)S(1)}, bf16[2048,704]{0,1:T(8,128)(2,1)}, bf16[2048,704]{0,1:T(8,128)(2,1)S(1)}) fusion(f32[2048,1408]{0,1:T(8,128)} %fusion.112, bf16[2048,2048]{1,0:T(8,128)(2,1)} %constant_dynamic-update-slice_fusion.26, bf16[704,2048]{1,0:T(8,128)(2,1)S(1)} %bitcast.347), kind=kOutput, calls=%fused_computation.13 | convolution fusion | flops 5927206912 | bytes 31457280 | tf_op jit(solution)/shard_map/dot_general | solution.py:20
  416.8 11.9 %convolution_convert_fusion.5 = bf16[704,2048]{1,0:T(8,128)(2,1)} fusion(bf16[2048,704]{0,1:T(8,128)(2,1)S(1)} %get-tuple-element.70, bf16[2048,2048]{1,0:T(8,128)(2,1)} %constant_dynamic-update-slice_fusion.26), kind=kOutput, calls=%fused_computation.23 | convolution fusion | flops 5907021824 | bytes 14155776 | tf_op jit(solution)/shard_map/dot_general | solution.py:20
  428.7 9.1 %convolution_convert_fusion.2 = bf16[2048,2048]{1,0:T(8,128)(2,1)} fusion(bf16[2048,704]{0,1:T(8,128)(2,1)S(1)} %get-tuple-element.70, bf16[704,2048]{1,0:T(8,128)(2,1)S(1)} %bitcast.348), kind=kOutput, calls=%fused_computation.7 | convolution fusion | flops 5909774336 | bytes 14155776 | tf_op jit(solution)/shard_map/dot_general | solution.py:20
  437.8 18.1 %convolution_convert_fusion.4 = bf16[2048,1408]{1,0:T(8,128)(2,1)} fusion(bf16[2048,2048]{1,0:T(8,128)(2,1)} %constant_dynamic-update-slice_fusion.17, bf16[2048,704]{0,1:T(8,128)(2,1)} %get-tuple-element.69, bf16[2048,704]{0,1:T(8,128)(2,1)S(1)} %get-tuple-element.68), kind=kOutput, calls=%fused_computation.9 | convolution fusion | flops 11825577984 | bytes 19922944 | tf_op jit(solution)/shard_map/dot_general | solution.py:20
  456.0 17.7 %convolution_convert_fusion.1 = bf16[2048,2048]{1,0:T(8,128)(2,1)} fusion(bf16[2048,1408]{1,0:T(8,128)(2,1)S(1)} %bitcast.333, bf16[2048,704]{0,1:T(8,128)(2,1)} %get-tuple-element.69, bf16[2048,704]{0,1:T(8,128)(2,1)} %copy-done.101), kind=kOutput, calls=%fused_computation.6 | convolution fusion | flops 11826888704 | bytes 19922944 | tf_op jit(solution)/shard_map/dot_general | solution.py:20
  480.2 5.7 fusion.102
  503.1 7.6 collective-permute-done.40
  514.7 9.2 %collective-permute-done.56 = bf16[128,2048]{1,0:T(8,128)(2,1)S(1)} collective-permute-done((bf16[128,2048]{1,0:T(8,128)(2,1)S(1)}, bf16[128,2048]{1,0:T(8,128)(2,1)S(1)}, u32[]{:S(2)}, u32[]{:S(2)}) %collective-permute-start.56) | collective-permute-done | bytes 524320 | tf_op jit(solution)/shard_map/ppermute | solution.py:36
  525.8 10.2 %collective-permute-done.59 = bf16[128,2048]{1,0:T(8,128)(2,1)S(1)} collective-permute-done((bf16[128,2048]{1,0:T(8,128)(2,1)S(1)}, bf16[128,2048]{1,0:T(8,128)(2,1)S(1)}, u32[]{:S(2)}, u32[]{:S(2)}) %collective-permute-start.59) | collective-permute-done | bytes 524320 | tf_op jit(solution)/shard_map/ppermute | solution.py:36
  545.8 24.1 %collective-permute-done.41 = bf16[256,2048]{1,0:T(8,128)(2,1)S(1)} collective-permute-done((bf16[256,2048]{1,0:T(8,128)(2,1)S(1)}, bf16[256,2048]{1,0:T(8,128)(2,1)S(1)}, u32[]{:S(2)}, u32[]{:S(2)}) %collective-permute-start.41) | collective-permute-done | bytes 1048608 | tf_op jit(solution)/shard_map/ppermute | solution.py:36
  571.5 22.6 %collective-permute-done.57 = bf16[256,2048]{1,0:T(8,128)(2,1)S(1)} collective-permute-done((bf16[256,2048]{1,0:T(8,128)(2,1)S(1)}, bf16[256,2048]{1,0:T(8,128)(2,1)S(1)}, u32[]{:S(2)}, u32[]{:S(2)}) %collective-permute-start.57) | collective-permute-done | bytes 1048608 | tf_op jit(solution)/shard_map/ppermute | solution.py:36
  594.9 5.5 multiply_reduce_fusion.2
  608.1 24.5 %collective-permute-done.89 = bf16[176,2048]{1,0:T(8,128)(2,1)} collective-permute-done((bf16[176,2048]{1,0:T(8,128)(2,1)}, bf16[176,2048]{1,0:T(8,128)(2,1)}, u32[]{:S(2)}, u32[]{:S(2)}) %collective-permute-start.89) | collective-permute-done | bytes 720928 | tf_op jit(solution)/shard_map/ppermute | solution.py:36
  636.6 16.0 %collective-permute-done.64 = bf16[256,2048]{1,0:T(8,128)(2,1)} collective-permute-done((bf16[256,2048]{1,0:T(8,128)(2,1)}, bf16[256,2048]{1,0:T(8,128)(2,1)}, u32[]{:S(2)}, u32[]{:S(2)}) %collective-permute-start.64) | collective-permute-done | bytes 1048608 | tf_op jit(solution)/shard_map/ppermute | solution.py:36
  655.4 6.0 collective-permute-done.86
  665.3 4.3 all-to-all-start.3
  682.2 5.9 convolution_convert_fusion.7
  711.0 9.5 %collective-permute-done.69 = bf16[2,153,129]{2,1,0:T(8,128)(2,1)S(1)} collective-permute-done((bf16[2,153,129]{2,1,0:T(8,128)(2,1)S(1)}, bf16[2,153,129]{2,1,0:T(8,128)(2,1)S(1)}, u32[]{:S(2)}, u32[]{:S(2)}) %collective-permute-start.69) | collective-permute-done | bytes 78980 | tf_op jit(solution)/shard_map/ppermute | solution.py:163
  738.4 6.8 stack.183
  746.3 7.3 convolution_convert_fusion.6
  757.6 4.8 convolution_convert_fusion
  774.4 4.7 reshape.412
  785.7 4.7 reshape.414
  804.0 5.4 convert_add_fusion.5
  817.8 10.2 %collective-permute-done.80 = bf16[8,64,320]{2,1,0:T(8,128)(2,1)S(1)} collective-permute-done((bf16[8,64,320]{2,1,0:T(8,128)(2,1)S(1)}, bf16[8,64,320]{2,1,0:T(8,128)(2,1)S(1)}, u32[]{:S(2)}, u32[]{:S(2)}) %collective-permute-start.80) | collective-permute-done | bytes 327712 | tf_op jit(solution)/shard_map/ppermute | solution.py:36
  838.6 13.0 %collective-permute-done.76 = bf16[128,2048]{1,0:T(8,128)(2,1)S(1)} collective-permute-done((bf16[128,2048]{1,0:T(8,128)(2,1)}, bf16[128,2048]{1,0:T(8,128)(2,1)S(1)}, u32[]{:S(2)}, u32[]{:S(2)}) %collective-permute-start.76) | collective-permute-done | bytes 524320 | tf_op jit(solution)/shard_map/ppermute | solution.py:36
  869.2 4.5 collective-permute-done.74
  879.6 4.1 fusion.21
  (646 shorter events, 367.7 us)
Async XLA Ops:
  0.7 75.2 %collective-permute-start.1 = (bf16[256,2048]{1,0:T(8,128)(2,1)}, bf16[256,2048]{1,0:T(8,128)(2,1)}, u32[]{:S(2)}, u32[]{:S(2)}) collective-permute-start(bf16[256,2048]{1,0:T(8,128)(2,1)} %bitcast.316), channel_id=1, source_target_pairs={{0,4},{4,0},{1,5},{5,1},{2,6},{6,2},{3,7},{7,3},{8,12},{12,8},{9,1... | collective-permute-start | bytes 3145736 | tf_op jit(solution)/shard_map/ppermute | solution.py:36
  3.7 75.3 %collective-permute-start = (bf16[256,2048]{1,0:T(8,128)(2,1)}, bf16[256,2048]{1,0:T(8,128)(2,1)}, u32[]{:S(2)}, u32[]{:S(2)}) collective-permute-start(bf16[256,2048]{1,0:T(8,128)(2,1)} %bitcast.317), channel_id=1, source_target_pairs={{0,2},{2,0},{1,3},{3,1},{4,6},{6,4},{5,7},{7,5},{8,10},{10,8},{9,1... | collective-permute-start | bytes 3145736 | tf_op jit(solution)/shard_map/ppermute | solution.py:36
  3.7 38.2 %collective-permute-start.13 = (bf16[64,2048]{1,0:T(8,128)(2,1)}, bf16[64,2048]{1,0:T(8,128)(2,1)}, u32[]{:S(2)}, u32[]{:S(2)}) collective-permute-start(bf16[64,2048]{1,0:T(8,128)(2,1)} %param.20), channel_id=1, source_target_pairs={{0,16},{16,0},{1,17},{17,1},{2,18},{18,2},{3,19},{19,3},{4,20},{20... | collective-permute-start | bytes 786440 | tf_op jit(solution)/shard_map/ppermute | solution.py:36
  6.3 36.8 %collective-permute-start.12 = (bf16[64,2048]{1,0:T(8,128)(2,1)}, bf16[64,2048]{1,0:T(8,128)(2,1)}, u32[]{:S(2)}, u32[]{:S(2)}) collective-permute-start(bf16[64,2048]{1,0:T(8,128)(2,1)} %param.20), channel_id=1, source_target_pairs={{0,1},{1,0},{2,3},{3,2},{4,5},{5,4},{6,7},{7,6},{8,9},{9,8},{10,11... | collective-permute-start | bytes 786440 | tf_op jit(solution)/shard_map/ppermute | solution.py:36
  13.2 40.5 %all-to-all-start = ((bf16[8,64,320]{2,1,0:T(8,128)(2,1)}), bf16[8,64,320]{2,1,0:T(8,128)(2,1)S(1)}, u32[]{:S(2)}, u32[]{:S(2)}) async-start(bf16[8,64,320]{2,1,0:T(8,128)(2,1)} %pad_maximum_fusion.24), calls=%async_computation | async-start | bytes 786432 | tf_op jit(solution)/shard_map/all_to_all | solution.py:125
  16.7 41.8 %collective-permute-start.35 = (bf16[176,2048]{1,0:T(8,128)(2,1)}, bf16[176,2048]{1,0:T(8,128)(2,1)}, u32[]{:S(2)}, u32[]{:S(2)}) collective-permute-start(bf16[176,2048]{1,0:T(8,128)(2,1)} %param.24), channel_id=1, source_target_pairs={{0,16},{16,0},{1,17},{17,1},{2,18},{18,2},{3,19},{19,3},{4,20},{20... | collective-permute-start | bytes 2162696 | tf_op jit(solution)/shard_map/ppermute | solution.py:36
  51.3 77.1 %collective-permute-start.45 = (bf16[256,2048]{1,0:T(8,128)(2,1)}, bf16[256,2048]{1,0:T(8,128)(2,1)}, u32[]{:S(2)}, u32[]{:S(2)}) collective-permute-start(bf16[256,2048]{1,0:T(8,128)(2,1)} %bitcast.339), channel_id=1, source_target_pairs={{0,2},{2,0},{1,3},{3,1},{4,6},{6,4},{5,7},{7,5},{8,10},{10,8},{9,1... | collective-permute-start | bytes 3145736 | tf_op jit(solution)/shard_map/ppermute | solution.py:36
  53.7 189.7 %all-to-all-start.1 = ((bf16[8,64,1408]{2,1,0:T(8,128)(2,1)}), bf16[8,64,1408]{2,1,0:T(8,128)(2,1)}, u32[]{:S(2)}, u32[]{:S(2)}) async-start(bf16[8,64,1408]{2,1,0:T(8,128)(2,1)} %pad_maximum_fusion.10), calls=%async_computation.1 | async-start | bytes 2883584 | tf_op jit(solution)/shard_map/all_to_all | solution.py:125
  66.8 66.5 %collective-permute-start.3 = (bf16[256,2048]{1,0:T(8,128)(2,1)S(1)}, bf16[256,2048]{1,0:T(8,128)(2,1)S(1)}, u32[]{:S(2)}, u32[]{:S(2)}) collective-permute-start(bf16[256,2048]{1,0:T(8,128)(2,1)S(1)} %bitcast.318), channel_id=1, source_target_pairs={{0,8},{8,0},{1,9},{9,1},{2,10},{10,2},{3,11},{11,3},{4,12},{12,4},... | collective-permute-start | bytes 3145736 | tf_op jit(solution)/shard_map/ppermute | solution.py:36
  74.2 64.2 %collective-permute-start.46 = (bf16[256,2048]{1,0:T(8,128)(2,1)}, bf16[256,2048]{1,0:T(8,128)(2,1)S(1)}, u32[]{:S(2)}, u32[]{:S(2)}) collective-permute-start(bf16[256,2048]{1,0:T(8,128)(2,1)} %bitcast.340), channel_id=1, source_target_pairs={{0,4},{4,0},{1,5},{5,1},{2,6},{6,2},{3,7},{7,3},{8,12},{12,8},{9,1... | collective-permute-start | bytes 3145736 | tf_op jit(solution)/shard_map/ppermute | solution.py:36
  75.9 64.9 %collective-permute-start.48 = (bf16[256,2048]{1,0:T(8,128)(2,1)}, bf16[256,2048]{1,0:T(8,128)(2,1)S(1)}, u32[]{:S(2)}, u32[]{:S(2)}) collective-permute-start(bf16[256,2048]{1,0:T(8,128)(2,1)} %bitcast.341), channel_id=1, source_target_pairs={{0,8},{8,0},{1,9},{9,1},{2,10},{10,2},{3,11},{11,3},{4,12},{12,4},... | collective-permute-start | bytes 3145736 | tf_op jit(solution)/shard_map/ppermute | solution.py:36
  79.0 48.9 %collective-permute-start.9 = (bf16[512,320]{1,0:T(8,128)(2,1)S(1)}, bf16[512,320]{1,0:T(8,128)(2,1)S(1)}, u32[]{:S(2)}, u32[]{:S(2)}) collective-permute-start(bf16[512,320]{1,0:T(8,128)(2,1)S(1)} %bitcast.358), channel_id=1, source_target_pairs={{0,16},{16,0},{1,17},{17,1},{2,18},{18,2},{3,19},{19,3},{4,20},{20... | collective-permute-start | bytes 983048 | tf_op jit(solution)/shard_map/ppermute | solution.py:36
  140.8 92.3 %collective-permute-start.50 = (bf16[128,2048]{1,0:T(8,128)(2,1)}, bf16[128,2048]{1,0:T(8,128)(2,1)}, u32[]{:S(2)}, u32[]{:S(2)}) collective-permute-start(bf16[128,2048]{1,0:T(8,128)(2,1)} %slice.315), channel_id=1, source_target_pairs={{0,8},{8,0},{1,9},{9,1},{2,10},{10,2},{3,11},{11,3},{4,12},{12,4},... | collective-permute-start | bytes 1572872 | tf_op jit(solution)/shard_map/ppermute | solution.py:36
  160.3 72.8 %collective-permute-start.51 = (bf16[128,2048]{1,0:T(8,128)(2,1)}, bf16[128,2048]{1,0:T(8,128)(2,1)}, u32[]{:S(2)}, u32[]{:S(2)}) collective-permute-start(bf16[128,2048]{1,0:T(8,128)(2,1)} %slice.316), channel_id=1, source_target_pairs={{0,4},{4,0},{1,5},{5,1},{2,6},{6,2},{3,7},{7,3},{8,12},{12,8},{9,1... | collective-permute-start | bytes 1572872 | tf_op jit(solution)/shard_map/ppermute | solution.py:36
  235.9 53.2 %collective-permute-start.52 = (bf16[256,2048]{1,0:T(8,128)(2,1)}, bf16[256,2048]{1,0:T(8,128)(2,1)S(1)}, u32[]{:S(2)}, u32[]{:S(2)}) collective-permute-start(bf16[256,2048]{1,0:T(8,128)(2,1)} %pad_maximum_fusion.18), channel_id=1, source_target_pairs={{0,2},{2,0},{1,3},{3,1},{4,6},{6,4},{5,7},{7,5},{8,10},{10,8},{9,1... | collective-permute-start | bytes 3145736 | tf_op jit(solution)/shard_map/ppermute | solution.py:36
  243.4 65.8 %collective-permute-start.32 = (bf16[512,1408]{1,0:T(8,128)(2,1)}, bf16[512,1408]{1,0:T(8,128)(2,1)S(1)}, u32[]{:S(2)}, u32[]{:S(2)}) collective-permute-start(bf16[512,1408]{1,0:T(8,128)(2,1)} %bitcast.49), channel_id=1, source_target_pairs={{0,16},{16,0},{1,17},{17,1},{2,18},{18,2},{3,19},{19,3},{4,20},{20... | collective-permute-start | bytes 4325384 | tf_op jit(solution)/shard_map/ppermute | solution.py:36
  243.5 66.3 %collective-permute-start.31 = (bf16[512,1408]{1,0:T(8,128)(2,1)}, bf16[512,1408]{1,0:T(8,128)(2,1)S(1)}, u32[]{:S(2)}, u32[]{:S(2)}) collective-permute-start(bf16[512,1408]{1,0:T(8,128)(2,1)} %bitcast.49), channel_id=1, source_target_pairs={{0,1},{1,0},{2,3},{3,2},{4,5},{5,4},{6,7},{7,6},{8,9},{9,8},{10,11... | collective-permute-start | bytes 4325384 | tf_op jit(solution)/shard_map/ppermute | solution.py:36
  244.0 67.5 %collective-permute-start.15 = (bf16[256,2048]{1,0:T(8,128)(2,1)}, bf16[256,2048]{1,0:T(8,128)(2,1)S(1)}, u32[]{:S(2)}, u32[]{:S(2)}) collective-permute-start(bf16[256,2048]{1,0:T(8,128)(2,1)} %get-tuple-element.92), channel_id=1, source_target_pairs={{0,2},{2,0},{1,3},{3,1},{4,6},{6,4},{5,7},{7,5},{8,10},{10,8},{9,1... | collective-permute-start | bytes 3145736 | tf_op jit(solution)/shard_map/ppermute | solution.py:36
  254.7 31.8 %collective-permute-start.21 = (bf16[128,2048]{1,0:T(8,128)(2,1)}, bf16[128,2048]{1,0:T(8,128)(2,1)S(1)}, u32[]{:S(2)}, u32[]{:S(2)}) collective-permute-start(bf16[128,2048]{1,0:T(8,128)(2,1)} %get-tuple-element.141), channel_id=1, source_target_pairs={{0,8},{8,0},{1,9},{9,1},{2,10},{10,2},{3,11},{11,3},{4,12},{12,4},... | collective-permute-start | bytes 1572872 | tf_op jit(solution)/shard_map/ppermute | solution.py:36
  286.5 45.1 %collective-permute-start.19 = (bf16[256,2048]{1,0:T(8,128)(2,1)S(1)}, bf16[256,2048]{1,0:T(8,128)(2,1)S(1)}, u32[]{:S(2)}, u32[]{:S(2)}) collective-permute-start(bf16[256,2048]{1,0:T(8,128)(2,1)S(1)} %pad_maximum_fusion.13), channel_id=1, source_target_pairs={{0,8},{8,0},{1,9},{9,1},{2,10},{10,2},{3,11},{11,3},{4,12},{12,4},... | collective-permute-start | bytes 3145736 | tf_op jit(solution)/shard_map/ppermute | solution.py:36
  289.1 42.4 %collective-permute-start.22 = (bf16[256,2048]{1,0:T(8,128)(2,1)S(1)}, bf16[256,2048]{1,0:T(8,128)(2,1)S(1)}, u32[]{:S(2)}, u32[]{:S(2)}) collective-permute-start(bf16[256,2048]{1,0:T(8,128)(2,1)S(1)} %pad_maximum_fusion.14), channel_id=1, source_target_pairs={{0,4},{4,0},{1,5},{5,1},{2,6},{6,2},{3,7},{7,3},{8,12},{12,8},{9,1... | collective-permute-start | bytes 3145736 | tf_op jit(solution)/shard_map/ppermute | solution.py:36
  309.2 32.8 %collective-permute-start.33 = (bf16[512,1408]{1,0:T(8,128)(2,1)S(1)}, bf16[512,1408]{1,0:T(8,128)(2,1)S(1)}, u32[]{:S(2)}, u32[]{:S(2)}) collective-permute-start(bf16[512,1408]{1,0:T(8,128)(2,1)S(1)} %collective-permute-done.32), channel_id=1, source_target_pairs={{0,1},{1,0},{2,3},{3,2},{4,5},{5,4},{6,7},{7,6},{8,9},{9,8},{10,11... | collective-permute-start | bytes 4325384 | tf_op jit(solution)/shard_map/ppermute | solution.py:36
  476.6 61.1 %collective-permute-start.88 = (bf16[176,2048]{1,0:T(8,128)(2,1)}, bf16[176,2048]{1,0:T(8,128)(2,1)}, u32[]{:S(2)}, u32[]{:S(2)}) collective-permute-start(bf16[176,2048]{1,0:T(8,128)(2,1)} %get-tuple-element.102), channel_id=1, source_target_pairs={{0,1},{1,0},{2,3},{3,2},{4,5},{5,4},{6,7},{7,6},{8,9},{9,8},{10,11... | collective-permute-start | bytes 2162696 | tf_op jit(solution)/shard_map/ppermute | solution.py:36
  488.0 51.8 %collective-permute-start.85 = (bf16[8,64,1408]{2,1,0:T(8,128)(2,1)S(1)}, bf16[8,64,1408]{2,1,0:T(8,128)(2,1)S(1)}, u32[]{:S(2)}, u32[]{:S(2)}) collective-permute-start(bf16[8,64,1408]{2,1,0:T(8,128)(2,1)S(1)} %get-tuple-element.100), channel_id=1, source_target_pairs={{0,1},{1,0},{2,3},{3,2},{4,5},{5,4},{6,7},{7,6},{8,9},{9,8},{10,11... | collective-permute-start | bytes 4325384 | tf_op jit(solution)/shard_map/ppermute | solution.py:36
  496.2 43.3 %collective-permute-start.37 = (bf16[256,2048]{1,0:T(8,128)(2,1)}, bf16[256,2048]{1,0:T(8,128)(2,1)}, u32[]{:S(2)}, u32[]{:S(2)}) collective-permute-start(bf16[256,2048]{1,0:T(8,128)(2,1)} %get-tuple-element.85), channel_id=1, source_target_pairs={{0,2},{2,0},{1,3},{3,1},{4,6},{6,4},{5,7},{7,5},{8,10},{10,8},{9,1... | collective-permute-start | bytes 3145736 | tf_op jit(solution)/shard_map/ppermute | solution.py:36
  513.4 30.7 %collective-permute-start.53 = (bf16[256,2048]{1,0:T(8,128)(2,1)S(1)}, bf16[256,2048]{1,0:T(8,128)(2,1)S(1)}, u32[]{:S(2)}, u32[]{:S(2)}) collective-permute-start(bf16[256,2048]{1,0:T(8,128)(2,1)S(1)} %copy-done.66), channel_id=1, source_target_pairs={{0,2},{2,0},{1,3},{3,1},{4,6},{6,4},{5,7},{7,5},{8,10},{10,8},{9,1... | collective-permute-start | bytes 3145736 | tf_op jit(solution)/shard_map/ppermute | solution.py:36
  536.0 33.8 %collective-permute-start.41 = (bf16[256,2048]{1,0:T(8,128)(2,1)S(1)}, bf16[256,2048]{1,0:T(8,128)(2,1)S(1)}, u32[]{:S(2)}, u32[]{:S(2)}) collective-permute-start(bf16[256,2048]{1,0:T(8,128)(2,1)S(1)} %pad_maximum_fusion.16), channel_id=1, source_target_pairs={{0,8},{8,0},{1,9},{9,1},{2,10},{10,2},{3,11},{11,3},{4,12},{12,4},... | collective-permute-start | bytes 3145736 | tf_op jit(solution)/shard_map/ppermute | solution.py:36
  537.7 33.8 %collective-permute-start.44 = (bf16[256,2048]{1,0:T(8,128)(2,1)S(1)}, bf16[256,2048]{1,0:T(8,128)(2,1)S(1)}, u32[]{:S(2)}, u32[]{:S(2)}) collective-permute-start(bf16[256,2048]{1,0:T(8,128)(2,1)S(1)} %pad_maximum_fusion.17), channel_id=1, source_target_pairs={{0,4},{4,0},{1,5},{5,1},{2,6},{6,2},{3,7},{7,3},{8,12},{12,8},{9,1... | collective-permute-start | bytes 3145736 | tf_op jit(solution)/shard_map/ppermute | solution.py:36
  539.5 54.6 %collective-permute-start.57 = (bf16[256,2048]{1,0:T(8,128)(2,1)S(1)}, bf16[256,2048]{1,0:T(8,128)(2,1)S(1)}, u32[]{:S(2)}, u32[]{:S(2)}) collective-permute-start(bf16[256,2048]{1,0:T(8,128)(2,1)S(1)} %pad_maximum_fusion.19), channel_id=1, source_target_pairs={{0,8},{8,0},{1,9},{9,1},{2,10},{10,2},{3,11},{11,3},{4,12},{12,4},... | collective-permute-start | bytes 3145736 | tf_op jit(solution)/shard_map/ppermute | solution.py:36
  539.8 55.0 %collective-permute-start.60 = (bf16[256,2048]{1,0:T(8,128)(2,1)S(1)}, bf16[256,2048]{1,0:T(8,128)(2,1)S(1)}, u32[]{:S(2)}, u32[]{:S(2)}) collective-permute-start(bf16[256,2048]{1,0:T(8,128)(2,1)S(1)} %pad_maximum_fusion.20), channel_id=1, source_target_pairs={{0,4},{4,0},{1,5},{5,1},{2,6},{6,2},{3,7},{7,3},{8,12},{12,8},{9,1... | collective-permute-start | bytes 3145736 | tf_op jit(solution)/shard_map/ppermute | solution.py:36
  544.1 61.5 %collective-permute-start.87 = (bf16[176,2048]{1,0:T(8,128)(2,1)S(1)}, bf16[176,2048]{1,0:T(8,128)(2,1)}, u32[]{:S(2)}, u32[]{:S(2)}) collective-permute-start(bf16[176,2048]{1,0:T(8,128)(2,1)S(1)} %copy-done.71), channel_id=1, source_target_pairs={{0,1},{1,0},{2,3},{3,2},{4,5},{5,4},{6,7},{7,6},{8,9},{9,8},{10,11... | collective-permute-start | bytes 2162696 | tf_op jit(solution)/shard_map/ppermute | solution.py:36
  569.9 85.6 %collective-permute-start.84 = (bf16[8,64,1408]{2,1,0:T(8,128)(2,1)}, bf16[8,64,1408]{2,1,0:T(8,128)(2,1)}, u32[]{:S(2)}, u32[]{:S(2)}) collective-permute-start(bf16[8,64,1408]{2,1,0:T(8,128)(2,1)} %get-tuple-element.99), channel_id=1, source_target_pairs={{0,1},{1,0},{2,3},{3,2},{4,5},{5,4},{6,7},{7,6},{8,9},{9,8},{10,11... | collective-permute-start | bytes 4325384 | tf_op jit(solution)/shard_map/ppermute | solution.py:36
  571.5 61.1 %collective-permute-start.89 = (bf16[176,2048]{1,0:T(8,128)(2,1)}, bf16[176,2048]{1,0:T(8,128)(2,1)}, u32[]{:S(2)}, u32[]{:S(2)}) collective-permute-start(bf16[176,2048]{1,0:T(8,128)(2,1)} %fusion.29), channel_id=1, source_target_pairs={{0,16},{16,0},{1,17},{17,1},{2,18},{18,2},{3,19},{19,3},{4,20},{20... | collective-permute-start | bytes 2162696 | tf_op jit(solution)/shard_map/ppermute | solution.py:36
  594.2 67.3 %collective-permute-start.86 = (bf16[8,64,1408]{2,1,0:T(8,128)(2,1)}, bf16[8,64,1408]{2,1,0:T(8,128)(2,1)}, u32[]{:S(2)}, u32[]{:S(2)}) collective-permute-start(bf16[8,64,1408]{2,1,0:T(8,128)(2,1)} %fusion.1), channel_id=1, source_target_pairs={{0,16},{16,0},{1,17},{17,1},{2,18},{18,2},{3,19},{19,3},{4,20},{20... | collective-permute-start | bytes 4325384 | tf_op jit(solution)/shard_map/ppermute | solution.py:36
  603.8 31.6 %collective-permute-start.62 = (bf16[256,2048]{1,0:T(8,128)(2,1)}, bf16[256,2048]{1,0:T(8,128)(2,1)}, u32[]{:S(2)}, u32[]{:S(2)}) collective-permute-start(bf16[256,2048]{1,0:T(8,128)(2,1)} %get-tuple-element.60), channel_id=1, source_target_pairs={{0,4},{4,0},{1,5},{5,1},{2,6},{6,2},{3,7},{7,3},{8,12},{12,8},{9,1... | collective-permute-start | bytes 3145736 | tf_op jit(solution)/shard_map/ppermute | solution.py:36
  605.6 47.0 %collective-permute-start.64 = (bf16[256,2048]{1,0:T(8,128)(2,1)}, bf16[256,2048]{1,0:T(8,128)(2,1)}, u32[]{:S(2)}, u32[]{:S(2)}) collective-permute-start(bf16[256,2048]{1,0:T(8,128)(2,1)} %get-tuple-element.60), channel_id=1, source_target_pairs={{0,8},{8,0},{1,9},{9,1},{2,10},{10,2},{3,11},{11,3},{4,12},{12,4},... | collective-permute-start | bytes 3145736 | tf_op jit(solution)/shard_map/ppermute | solution.py:36
  632.6 37.3 %collective-permute-start.61 = (bf16[256,2048]{1,0:T(8,128)(2,1)}, bf16[256,2048]{1,0:T(8,128)(2,1)}, u32[]{:S(2)}, u32[]{:S(2)}) collective-permute-start(bf16[256,2048]{1,0:T(8,128)(2,1)} %get-tuple-element.60), channel_id=1, source_target_pairs={{0,2},{2,0},{1,3},{3,1},{4,6},{6,4},{5,7},{7,5},{8,10},{10,8},{9,1... | collective-permute-start | bytes 3145736 | tf_op jit(solution)/shard_map/ppermute | solution.py:36
  636.5 38.1 %collective-permute-start.66 = (bf16[128,2048]{1,0:T(8,128)(2,1)S(1)}, bf16[128,2048]{1,0:T(8,128)(2,1)S(1)}, u32[]{:S(2)}, u32[]{:S(2)}) collective-permute-start(bf16[128,2048]{1,0:T(8,128)(2,1)S(1)} %slice.323), channel_id=1, source_target_pairs={{0,8},{8,0},{1,9},{9,1},{2,10},{10,2},{3,11},{11,3},{4,12},{12,4},... | collective-permute-start | bytes 1572872 | tf_op jit(solution)/shard_map/ppermute | solution.py:36
  665.3 105.6 %all-to-all-start.3 = ((bf16[8,64,1408]{2,1,0:T(8,128)(2,1)}), bf16[8,64,1408]{2,1,0:T(8,128)(2,1)}, u32[]{:S(2)}, u32[]{:S(2)}) async-start(bf16[8,64,1408]{2,1,0:T(8,128)(2,1)} %fusion.3), calls=%async_computation.3 | async-start | bytes 2883584 | tf_op jit(solution)/shard_map/all_to_all | solution.py:136
  705.2 105.2 %collective-permute-start.82 = (bf16[64,2048]{1,0:T(8,128)(2,1)}, bf16[64,2048]{1,0:T(8,128)(2,1)}, u32[]{:S(2)}, u32[]{:S(2)}) collective-permute-start(bf16[64,2048]{1,0:T(8,128)(2,1)} %get-tuple-element.132), channel_id=1, source_target_pairs={{0,1},{1,0},{2,3},{3,2},{4,5},{5,4},{6,7},{7,6},{8,9},{9,8},{10,11... | collective-permute-start | bytes 786440 | tf_op jit(solution)/shard_map/ppermute | solution.py:36
  767.0 36.4 %collective-permute-start.71 = (bf16[256,2048]{1,0:T(8,128)(2,1)}, bf16[256,2048]{1,0:T(8,128)(2,1)}, u32[]{:S(2)}, u32[]{:S(2)}) collective-permute-start(bf16[256,2048]{1,0:T(8,128)(2,1)} %get-tuple-element.74), channel_id=1, source_target_pairs={{0,2},{2,0},{1,3},{3,1},{4,6},{6,4},{5,7},{7,5},{8,10},{10,8},{9,1... | collective-permute-start | bytes 3145736 | tf_op jit(solution)/shard_map/ppermute | solution.py:36
  767.1 36.8 %collective-permute-start.72 = (bf16[256,2048]{1,0:T(8,128)(2,1)}, bf16[256,2048]{1,0:T(8,128)(2,1)}, u32[]{:S(2)}, u32[]{:S(2)}) collective-permute-start(bf16[256,2048]{1,0:T(8,128)(2,1)} %get-tuple-element.73), channel_id=1, source_target_pairs={{0,2},{2,0},{1,3},{3,1},{4,6},{6,4},{5,7},{7,5},{8,10},{10,8},{9,1... | collective-permute-start | bytes 3145736 | tf_op jit(solution)/shard_map/ppermute | solution.py:36
  767.6 36.3 %collective-permute-start.75 = (bf16[256,2048]{1,0:T(8,128)(2,1)}, bf16[256,2048]{1,0:T(8,128)(2,1)}, u32[]{:S(2)}, u32[]{:S(2)}) collective-permute-start(bf16[256,2048]{1,0:T(8,128)(2,1)} %get-tuple-element.72), channel_id=1, source_target_pairs={{0,2},{2,0},{1,3},{3,1},{4,6},{6,4},{5,7},{7,5},{8,10},{10,8},{9,1... | collective-permute-start | bytes 3145736 | tf_op jit(solution)/shard_map/ppermute | solution.py:36
  770.5 30.1 %collective-permute-start.79 = (bf16[8,64,320]{2,1,0:T(8,128)(2,1)}, bf16[8,64,320]{2,1,0:T(8,128)(2,1)}, u32[]{:S(2)}, u32[]{:S(2)}) collective-permute-start(bf16[8,64,320]{2,1,0:T(8,128)(2,1)} %get-tuple-element.124), channel_id=1, source_target_pairs={{0,1},{1,0},{2,3},{3,2},{4,5},{5,4},{6,7},{7,6},{8,9},{9,8},{10,11... | collective-permute-start | bytes 983048 | tf_op jit(solution)/shard_map/ppermute | solution.py:36
  800.7 53.6 %collective-permute-start.81 = (bf16[64,2048]{1,0:T(8,128)(2,1)}, bf16[64,2048]{1,0:T(8,128)(2,1)}, u32[]{:S(2)}, u32[]{:S(2)}) collective-permute-start(bf16[64,2048]{1,0:T(8,128)(2,1)} %get-tuple-element.131), channel_id=1, source_target_pairs={{0,1},{1,0},{2,3},{3,2},{4,5},{5,4},{6,7},{7,6},{8,9},{9,8},{10,11... | collective-permute-start | bytes 786440 | tf_op jit(solution)/shard_map/ppermute | solution.py:36
  803.9 65.3 %collective-permute-start.70 = (bf16[256,2048]{1,0:T(8,128)(2,1)}, bf16[256,2048]{1,0:T(8,128)(2,1)S(1)}, u32[]{:S(2)}, u32[]{:S(2)}) collective-permute-start(bf16[256,2048]{1,0:T(8,128)(2,1)} %get-tuple-element.71), channel_id=1, source_target_pairs={{0,2},{2,0},{1,3},{3,1},{4,6},{6,4},{5,7},{7,5},{8,10},{10,8},{9,1... | collective-permute-start | bytes 3145736 | tf_op jit(solution)/shard_map/ppermute | solution.py:36
  817.8 36.5 %collective-permute-start.83 = (bf16[64,2048]{1,0:T(8,128)(2,1)}, bf16[64,2048]{1,0:T(8,128)(2,1)}, u32[]{:S(2)}, u32[]{:S(2)}) collective-permute-start(bf16[64,2048]{1,0:T(8,128)(2,1)} %fusion.65), channel_id=1, source_target_pairs={{0,16},{16,0},{1,17},{17,1},{2,18},{18,2},{3,19},{19,3},{4,20},{20... | collective-permute-start | bytes 786440 | tf_op jit(solution)/shard_map/ppermute | solution.py:36
  838.3 35.4 %collective-permute-start.74 = (bf16[256,2048]{1,0:T(8,128)(2,1)}, bf16[256,2048]{1,0:T(8,128)(2,1)}, u32[]{:S(2)}, u32[]{:S(2)}) collective-permute-start(bf16[256,2048]{1,0:T(8,128)(2,1)} %pad_maximum_fusion.22), channel_id=1, source_target_pairs={{0,8},{8,0},{1,9},{9,1},{2,10},{10,2},{3,11},{11,3},{4,12},{12,4},... | collective-permute-start | bytes 3145736 | tf_op jit(solution)/shard_map/ppermute | solution.py:36
  (154 other events, 1810.9 us)

commit v2 on v1

v2 whole, which is shorter than its diff:
```python
import functools

import jax
import jax.numpy as jnp
import numpy as np
from jax import lax
from jax.experimental import pallas as pl
from jax.experimental.pallas import tpu as pltpu
from jax.sharding import Mesh
from jax.sharding import PartitionSpec as P

H = 16
FD = 16
DV = 128
HP = 2
ROWS = DV + 2 * FD
WIDE = 384
QK = 2 * DV
LANE_R, LANE_ONE = 64, 65
FEAT = 256
SENT = 160
SEQS = 4
TP = ("l", "y", "c")
DP = ("h", "x")
EPS = 1e-5
F32, BF16 = jnp.float32, jnp.bfloat16


def dot(a, b, dims):
    return lax.dot_general(a, b, (dims, ((), ())), preferred_element_type=F32)


def mm(a, b):
    return dot(a, b, ((1,), (0,)))


def mm_nt(a, b):
    return dot(a, b, ((1,), (1,)))


def mm_tn(a, b):
    return dot(a, b, ((0,), (0,)))


def swap(a, axis):
    return lax.ppermute(a, axis, [(0, 1), (1, 0)])


class Order:
    def __init__(self, info):
        self.info = info

    def at(self, *values):
        flat, tree = jax.tree.flatten(values)
        got = lax.optimization_barrier((self.info, *flat))
        self.info = got[0]
        return jax.tree.unflatten(tree, got[1:])


SLOTS = ((0, 0, 256), (1, 0, 256), (2, 0, 256), (3, 0, 256), (4, 0, 256), (5, 0, 256))
SLOTS += ((6, 0, 128), (6, 128, 128), (7, 0, 128), (7, 128, 128))


def near_tokens(own):
    return [own, swap(own, "l"), swap(own, "y"), swap(own, "c")]


def far_tokens(near):
    own, from_l, from_y, _ = near
    half = own.shape[0] // 2
    return [swap(from_y[:half], "l"), swap(from_l[half:], "y"), swap(from_y, "c"), swap(from_l, "c")]


def last_tokens(far):
    return [swap(far[0], "c"), swap(far[1], "c")]


def in_slots(near, far, last):
    return [near[0], near[3], near[2], far[2], near[1], far[3], far[0], far[1], *last]


def far_cores(p):
    return [swap(p[8], "c"), swap(p[9], "c")]


def near_cores(p):
    return [swap(p[1], "c"), swap(p[3], "c"), swap(p[5], "c")]


def plus(*terms):
    return functools.reduce(jnp.add, [t.astype(F32) for t in terms]).astype(BF16)


def send_far(p, fars):
    return [swap(plus(p[6], fars[0]), "l"), swap(plus(p[7], fars[1]), "y")]


def send_first(p, nears):
    half = p[6].shape[0]
    return [swap(plus(p[2][half:], nears[1][half:]), "y"), swap(plus(p[4][:half], nears[2][:half]), "l")]


def send_second(p, nears, via):
    half = p[6].shape[0]
    y_a = plus(p[2][:half], nears[1][:half], via[0])
    l_b = plus(p[4][half:], nears[2][half:], via[1])
    return [swap(y_a, "y"), swap(l_b, "l")]


def terms(p, nears, first, second):
    return [p[0], nears[0], second[0], first[1], first[0], second[1]]


def flips(a):
    a = jnp.where(lax.axis_index("h") == 0, a, a[::-1])
    return jnp.where(lax.axis_index("x") == 0, a, a[:, ::-1])


def small_mesh():
    return lax.axis_size("h") == 2 and lax.axis_size("x") == 2


def over_both(a):
    if small_mesh():
        over_h = swap(a, "h")
        rel = [jnp.stack([a, swap(a, "x")]), jnp.stack([over_h, swap(over_h, "x")])]
        return flips(jnp.stack(rel))
    full = lax.all_gather(a, DP)
    return full.reshape((lax.axis_size("h"), lax.axis_size("x")) + a.shape)


def sum_both(parts):
    flat = parts.reshape((-1,) + parts.shape[2:])
    return lax.psum_scatter(flat, DP, scatter_dimension=0, tiled=False).astype(F32)


def cut(a, n):
    step = a.shape[0] // n
    return [a[i * step : (i + 1) * step] for i in range(n)]


def sub_head():
    return lax.axis_size(DP + TP) // H == 2 * lax.axis_size("x")


def split_heads(w, width):
    rows = w.shape[0]
    w = w.T
    if sub_head():
        w = w.reshape(2, HP, 2, 2, width, rows).transpose(2, 3, 0, 1, 4, 5)
    else:
        w = w.reshape(HP, 8, width, rows).transpose(1, 0, 2, 3)
    return w.reshape(8, HP, width, rows)


def join_heads(w, width):
    rows = w.shape[-1]
    if sub_head():
        w = w.reshape(2, 2, 2, HP, width, rows).transpose(2, 3, 0, 1, 4, 5)
    else:
        w = w.transpose(1, 0, 2, 3)
    return w.reshape(H * width, rows).T


def split_hidden(first, second):
    h, x = lax.axis_size("h"), lax.axis_size("x")
    w = jnp.concatenate([first, second], 0).T
    cols = w.shape[1]
    return w.reshape(h, 8, x, -1, cols).transpose(1, 0, 2, 3, 4).reshape(8, -1, cols)


def join_hidden(w):
    h, x = lax.axis_size("h"), lax.axis_size("x")
    cols = w.shape[-1]
    w = w.reshape(8, h, x, -1, cols).transpose(1, 0, 2, 3, 4).reshape(-1, cols).T
    return w[: cols // 2], w[cols // 2 :]


LAYOUT_HEADS = ((0, 0, 0, DV), (1, 0, DV, DV), (0, DV, QK, FD), (1, DV, QK + FD, FD))
LAYOUT_HEADS += ((0, DV + FD, QK + 2 * FD, FD), (1, DV + FD, QK + 3 * FD, FD))


def layout_hidden(n):
    return ((0, 0, 0, n), (1, 0, n, n))


def slabs_to_rows(full, layout, height):
    h, x, _, n, cols = full.shape
    pair = full.reshape(h, x, 8, n, 2, cols // 2).transpose(4, 3, 0, 2, 1, 5).reshape(2, n, -1)
    rows = [pair[m, src : src + count] for m, src, _, count in layout]
    have = sum(count for *_, count in layout)
    return jnp.concatenate(rows + [jnp.zeros((height - have, pair.shape[2]), BF16)], 0)


def unpack(info, chunks, layout, height):
    k = len(chunks[0])
    args = [c for piece in chunks for c in piece]
    return call(functools.partial(unpack_kernel, layout, k), [info, *args], [((height, 16 * 128), BF16)], vmem=20)[0]


def rows_to_slabs(rows, layout):
    h, x = lax.axis_size("h"), lax.axis_size("x")
    pair = [jnp.concatenate([rows[dst : dst + c] for m, _, dst, c in layout if m == k], 0) for k in (0, 1)]
    n = pair[0].shape[0]
    parts = jnp.stack(pair).reshape(2, n, h, 8, x, -1).transpose(2, 4, 3, 1, 0, 5)
    return parts.reshape(h, x, 8, n, -1)


def exchange(slabs):
    return lax.all_to_all(slabs, TP, 0, 0, tiled=True)


def out_rows_in(full):
    if sub_head():
        h, x, rows, d = full.shape
        full = lax.all_to_all(full.reshape(2, h // 2, x, rows, d), "c", 0, 0, tiled=True)
        full = full.transpose(1, 0, 2, 3, 4)
    return full.reshape(HP * DV, -1)


def out_rows_out(grad):
    h, x = lax.axis_size("h"), lax.axis_size("x")
    d = grad.shape[1]
    if sub_head():
        grad = grad.reshape(HP, 2, x, -1, d).transpose(1, 0, 2, 3, 4)
        grad = lax.all_to_all(grad, "c", 0, 0, tiled=True)
    return grad.reshape(h, x, -1, d)


def entering(total, reverse):
    n = lax.axis_size("h")
    got = jnp.zeros_like(total)
    for s in range(1, n):
        route = [(i + s, i) if reverse else (i, i + s) for i in range(n - s)]
        came = lax.ppermute(total, "h", route)
        got = came if s == 1 else (got.astype(F32) + came.astype(F32)).astype(BF16)
    return got


def feature_maps():
    maps = np.zeros((4, 2, 128, FEAT), np.float32)
    for kind in range(4):
        where = [kind * FD + i for i in range(FD)] + [LANE_ONE]
        size = [0.5] * FD + [1.0]
        col = 0
        for i in range(FD + 1):
            for j in range(i, FD + 1):
                maps[kind, 0, where[i], col] = size[i]
                maps[kind, 1, where[j], col] = size[j] * (0.5 if kind >= 2 and i == j < FD else 1.0)
                col += 1
    return maps


MAPS = feature_maps()


def lanes(shape):
    return lax.broadcasted_iota(jnp.int32, shape, len(shape) - 1)


def segments(info, places):
    end, found = 0, jnp.zeros(places.shape, jnp.int32)
    for i in range(SEQS):
        end = end + info[2 + i]
        found = found + (places >= end).astype(jnp.int32)
    return found


def long_bounds(info):
    start, end, best, total = 0, info[2], info[2], info[2]
    for i in range(1, SEQS):
        more = info[2 + i] > best
        start = jnp.where(more, total, start)
        total = total + info[2 + i]
        end = jnp.where(more, total, end)
        best = jnp.where(more, info[2 + i], best)
    return start, end


def crossing(info, base):
    start, end = long_bounds(info)
    places = base + lax.broadcasted_iota(jnp.int32, (256, 1), 0)
    return ((places >= start) & (places < end)).astype(F32)


def pair_mask(info, base):
    row = lax.broadcasted_iota(jnp.int32, (256, 256), 0)
    col = lax.broadcasted_iota(jnp.int32, (256, 256), 1)
    down = segments(info, base + lax.broadcasted_iota(jnp.int32, (256, 1), 0))
    across = segments(info, base + lax.broadcasted_iota(jnp.int32, (1, 256), 1))
    return ((down == across) & (row >= col)).astype(F32)


def maps_of(tile, maps, kind):
    return mm(tile, maps[kind, 0]), mm(tile, maps[kind, 1])


def feats_t(tile, maps_t, kind):
    return (mm_nt(maps_t[kind, 0], tile) * mm_nt(maps_t[kind, 1], tile)).astype(BF16)


def feats(tile, maps, kind):
    a, b = maps_of(tile, maps, kind)
    return (a * b).astype(BF16)


def with_ones(values):
    one = (lanes((256, 128)) == 0).astype(BF16)
    return jnp.concatenate([values, one], 1)


def head_mask(h):
    at = lanes((256, 128))
    return ((at >= h * FD) & (at < (h + 1) * FD)).astype(F32)


def keys_on_queries(tile):
    return pltpu.roll(tile, 128 - HP * FD, 1)


def load(refs, r):
    if r < 6:
        return refs[r][...]
    return jnp.concatenate([refs[2 * r - 6][...], refs[2 * r - 5][...]], 0)


def store(refs, r, value):
    if r < 6:
        refs[r][...] = value
    else:
        refs[2 * r - 6][...] = value[:128]
        refs[2 * r - 5][...] = value[128:]


def project_kernel(info, *refs):
    xs, (w, maps_t, tile_ref, val_ref, state_ref, sums) = refs[:10], refs[10:]
    me, first = info[0], info[1]
    sums[...] = jnp.zeros_like(sums)
    at = lanes((256, 128))
    for r in range(8):
        p = jnp.bitwise_xor(me, r)
        x = load(xs, r)
        wide = x.astype(F32)
        scale = lax.rsqrt(jnp.mean(wide * wide, 1, keepdims=True) + EPS)
        y = mm_nt(x, w[...]) * scale
        values = y[:, :QK].astype(BF16)
        tile = jnp.where(at == LANE_R, scale, jnp.where(at == LANE_ONE, 1.0, y[:, QK:]))
        tile_ref[p] = tile
        val_ref[p] = values
        cross = crossing(info, first + p * 256).astype(BF16)
        low = tile.astype(BF16)
        for h in range(HP):
            feat = feats_t(low, maps_t, 2 + h)
            sums[h] += mm(feat, with_ones(values[:, h * DV : (h + 1) * DV]) * cross)
    state_ref[...] = sums[:, :SENT].astype(BF16)


def attend_kernel(info, tile_ref, val_ref, enter, maps, maps_t, w, *refs):
    mixed_ref, den_ref, before_ref = refs[:3]
    outs, sums = refs[3:13], refs[13]
    me, first = info[0], info[1]
    sums[...] = jnp.zeros_like(sums)
    sums[:, :SENT] = enter[...].astype(F32)

    def step(p, carry):
        tile = tile_ref[p]
        low = tile.astype(BF16)
        keys = keys_on_queries(tile).astype(BF16)
        cross = crossing(info, first + p * 256)
        cross_low = cross.astype(BF16)
        mask = pair_mask(info, first + p * 256)
        den = jnp.zeros((256, 128), F32)
        for h in range(HP):
            flat = mm_nt((tile * (head_mask(h) * 0.25)).astype(BF16), keys)
            low_scores = ((1.0 + flat + 0.5 * flat * flat) * mask).astype(BF16)
            values = with_ones(val_ref[p, :, h * DV : (h + 1) * DV])
            state = sums[h].astype(BF16)
            before_ref[p, h] = state
            both = mm(low_scores, values) + cross * mm(feats(low, maps, h), state)
            here = both[:, DV : DV + 1]
            mixed_ref[p, :, h * DV : (h + 1) * DV] = (both[:, :DV] / here).astype(BF16)
            den = jnp.where(lanes((256, 128)) == h, here, den)
            sums[h] += mm(feats_t(low, maps_t, 2 + h), values * cross_low)
        den_ref[p] = den
        return carry

    lax.fori_loop(0, 8, step, 0, unroll=True)
    for r in range(8):
        store(outs, r, mm(mixed_ref[jnp.bitwise_xor(me, r)], w[...]).astype(BF16))


def back_state_kernel(info, *refs):
    dbs = refs[:10]
    w, mixed_ref, den_ref, tile_ref, maps_t, d_num_ref, d_den_ref, state_ref, sums = refs[10:]
    me, first = info[0], info[1]
    sums[...] = jnp.zeros_like(sums)
    at = lanes((256, 128))
    for r in range(8):
        p = jnp.bitwise_xor(me, r)
        d_attn = mm_nt(load(dbs, r), w[...])
        low = tile_ref[p].astype(BF16)
        cross = crossing(info, first + p * 256).astype(BF16)
        den = den_ref[p]
        d_den = jnp.zeros((256, 128), F32)
        for h in range(HP):
            cols = slice(h * DV, (h + 1) * DV)
            inv = 1.0 / den[:, h : h + 1]
            d_num = (d_attn[:, cols] * inv).astype(BF16)
            d_num_ref[p, :, cols] = d_num
            total = -jnp.sum(d_attn[:, cols] * mixed_ref[p, :, cols].astype(F32), 1, keepdims=True) * inv
            d_den = jnp.where(at == h, total, d_den)
            grad = jnp.concatenate([d_num, jnp.where(at == 0, total, 0.0).astype(BF16)], 1)
            sums[h] += mm(feats_t(low, maps_t, h), grad * cross)
        d_den_ref[p] = d_den
    state_ref[...] = sums[:, :SENT].astype(BF16)


def back_kernel(info, tile_ref, val_ref, d_num_ref, d_den_ref, before_ref, enter, maps, w, *refs):
    e_ref, outs, sums = refs[0], refs[1:11], refs[11]
    me, first = info[0], info[1]
    sums[...] = jnp.zeros_like(sums)
    sums[:, :SENT] = enter[...].astype(F32)
    at = lanes((256, 128))

    def through(d_feat, a, b, kind):
        return mm_nt((d_feat * b).astype(BF16), maps[kind, 0]) + mm_nt((d_feat * a).astype(BF16), maps[kind, 1])

    def step(i, carry):
        p = 7 - i
        tile = tile_ref[p]
        low = tile.astype(BF16)
        keys = keys_on_queries(tile)
        keys_low = keys.astype(BF16)
        cross = crossing(info, first + p * 256)
        cross_low = cross.astype(BF16)
        mask = pair_mask(info, first + p * 256)
        d_tile = jnp.zeros((256, 128), F32)
        d_keys = jnp.zeros((256, 128), F32)
        scale = tile[:, LANE_R : LANE_R + 1]
        for h in range(HP):
            cols = slice(h * DV, (h + 1) * DV)
            here = head_mask(h)
            flat = mm_nt((tile * (here * 0.25)).astype(BF16), keys_low)
            low_scores = ((1.0 + flat + 0.5 * flat * flat) * mask).astype(BF16)
            values = val_ref[p, :, cols]
            d_num = d_num_ref[p, :, cols]
            d_den = d_den_ref[p][:, h : h + 1]
            back = sums[h].astype(BF16)
            d_flat = ((mm_nt(d_num, values) + d_den) * mask * (0.25 + 0.25 * flat)).astype(BF16)
            qa, qb = maps_of(low, maps, h)
            ka, kb = maps_of(low, maps, 2 + h)
            grad = jnp.concatenate([d_num, jnp.where(at == 0, d_den, 0.0).astype(BF16)], 1)
            d_feat_q = mm_nt(grad, before_ref[p, h]) * cross
            d_feat_k = mm_nt(with_ones(values), back) * cross
            d_tile += mm(d_flat, (keys * here).astype(BF16)) + through(d_feat_q, qa, qb, h)
            d_tile += through(d_feat_k, ka, kb, 2 + h)
            d_keys += mm_tn(d_flat, (tile * here).astype(BF16))
            d_val = mm_tn(low_scores, d_num) + cross * mm((ka * kb).astype(BF16), back[:, :DV])
            e_ref[p, :, cols] = (d_val * scale).astype(BF16)
            sums[h] += mm_tn((qa * qb).astype(BF16), grad * cross_low)
        d_tile = jnp.where(at < 2 * HP * FD, d_tile + pltpu.roll(d_keys, HP * FD, 1), 0.0)
        e_ref[p, :, QK:] = (d_tile * scale).astype(BF16)
        return carry

    lax.fori_loop(0, 8, step, 0)
    for r in range(8):
        store(outs, r, mm(e_ref[jnp.bitwise_xor(me, r)], w[...]).astype(BF16))


def unpack_kernel(layout, k, info, *refs):
    pieces, out = [refs[i * k : (i + 1) * k] for i in range(4)], refs[4 * k]
    have = sum(count for *_, count in layout)
    if have < out.shape[0]:
        out[have:] = jnp.zeros((out.shape[0] - have, out.shape[1]), BF16)
    even = info[7] == 0
    each = 8 // k
    for dh in range(2):
        for s in range(8):
            near, far = pieces[dh][s // each][s % each], pieces[2 + dh][s // each][s % each]
            first, second = lax.select(even, near, far), lax.select(even, far, near)
            pair = [jnp.concatenate([first[:, c : c + 64], second[:, c : c + 64]], 1) for c in (0, 64)]
            at = pl.multiple_of((jnp.bitwise_xor(info[6], dh) * 8 + s) * 128, 128)
            for m, src, dst, count in layout:
                out[dst : dst + count, pl.ds(at, 128)] = pair[m][src : src + count]


def rows_kernel(k, info, *refs):
    pieces, out = [refs[i * k : (i + 1) * k] for i in range(4)], refs[4 * k]
    block = sum(c.shape[0] for c in pieces[0])
    even = info[7] == 0
    for dh in range(2):
        start = 0
        for c in range(k):
            near, far = pieces[dh][c][...], pieces[2 + dh][c][...]
            for x, value in enumerate((lax.select(even, near, far), lax.select(even, far, near))):
                at = (jnp.bitwise_xor(info[6], dh) * 2 + x) * block + start
                out[pl.ds(pl.multiple_of(at, 16), near.shape[0])] = value
            start += near.shape[0]


def total_kernel(groups, *refs):
    total, at = 0.0, 0
    for k in groups:
        term = [refs[at + c][...].astype(F32) for c in range(k)]
        total = total + (term[0] if k == 1 else jnp.concatenate(term, 0))
        at += k
    refs[-1][...] = total.astype(refs[-1].dtype)


def summed(pieces):
    total = pieces[0][...].astype(F32) + pieces[1][...].astype(F32)
    upper = pieces[2][...].astype(F32) + pieces[3][...].astype(F32)
    lower = pieces[4][...].astype(F32) + pieces[5][...].astype(F32)
    return total + jnp.concatenate([upper, lower], 0)


def scale_of(v):
    return lax.rsqrt(jnp.mean(v * v, 1, keepdims=True) + EPS)


def residual_kernel(x, *refs):
    resid = x[...].astype(F32) + summed(refs[:6])
    refs[6][...] = resid
    refs[7][...] = (resid * scale_of(resid)).astype(BF16)


def d_residual_kernel(dy, resid_ref, *refs):
    resid, d_n = resid_ref[...], summed(refs[:6])
    r = scale_of(resid)
    n = resid * r
    d = dy[...].astype(F32) + r * (d_n - n * jnp.mean(d_n * n, 1, keepdims=True))
    refs[6][...] = d
    refs[7][...] = d.astype(BF16)


def input_kernel(x_ref, d_resid, *refs):
    x, d_x = x_ref[...].astype(F32), summed(refs[:6])
    n = x * scale_of(x)
    refs[6][0] = d_resid[...] + d_x - n * jnp.mean(d_x * n, 1, keepdims=True)


def output_kernel(resid, *refs):
    refs[6][0] = resid[...] + summed(refs[:6])


def sort_by_x(info, zero, one):
    even = info[7] == 0
    return lax.select(even, zero, one), lax.select(even, one, zero)


def pack_tile(info, first, second):
    zero = jnp.concatenate([first[:, :64], second[:, :64]], 1)
    one = jnp.concatenate([first[:, 64:], second[:, 64:]], 1)
    return sort_by_x(info, zero, one)


def qkv_grads_kernel(info, *refs):
    xs, (e_ref, total) = refs[:10], (refs[10], refs[-1])
    me = info[0]
    for r in range(8):
        more = mm_tn(e_ref[jnp.bitwise_xor(me, r)], load(xs, r))
        total[...] = more if r == 0 else total[...] + more
    if len(refs) == 13:
        refs[11][...] = total[...].astype(BF16)
        return
    outs = refs[11:15]
    for dh in range(2):
        for s in range(8):
            at = pl.multiple_of((jnp.bitwise_xor(info[6], dh) * 8 + s) * 128, 128)
            tile = total[:, pl.ds(at, 128)].astype(BF16)
            pair = [
                jnp.concatenate([tile[dst : dst + c] for m, _, dst, c in LAYOUT_HEADS if m == k], 0) for k in (0, 1)
            ]
            outs[dh][s], outs[2 + dh][s] = pack_tile(info, *pair)


def out_grads_kernel(info, *refs):
    dbs, (mixed_ref, total) = refs[:10], (refs[10], refs[-1])
    me = info[0]
    for r in range(8):
        more = mm_tn(mixed_ref[jnp.bitwise_xor(me, r)], load(dbs, r))
        total[...] = more if r == 0 else total[...] + more
    if len(refs) == 13:
        refs[11][...] = total[...].astype(BF16)
        return
    outs = refs[11:15]
    for dh in range(2):
        at = pl.multiple_of(jnp.bitwise_xor(info[6], dh) * DV, DV)
        rows = total[pl.ds(at, DV), :].astype(BF16)
        outs[dh][...], outs[2 + dh][...] = sort_by_x(info, rows[:64], rows[64:])


def mlp_kernel(pieces, *refs):
    ns, dys, (w_gu, wd) = refs[:pieces], refs[pieces : 2 * pieces], refs[2 * pieces : 2 * pieces + 2]
    outs, dns = refs[2 * pieces + 2 : 3 * pieces + 2], refs[3 * pieces + 2 : 4 * pieces + 2]
    hid_ref, dg_ref, du_ref = refs[4 * pieces + 2 :]
    ff = wd.shape[0]
    at = 0
    for i in range(pieces):
        rows = ns[i].shape[0]
        n, dy = ns[i][...], dys[i][...]
        gate, up, d_hid = mm_nt(n, w_gu[:ff]), mm_nt(n, w_gu[ff:]), mm_nt(dy, wd[...])
        sig = 1.0 / (1.0 + jnp.exp(-gate))
        silu = gate * sig
        hid = (silu * up).astype(BF16)
        dg = (d_hid * up * sig * (1.0 + gate * (1.0 - sig))).astype(BF16)
        du = (d_hid * silu).astype(BF16)
        hid_ref[at : at + rows] = hid
        dg_ref[at : at + rows] = dg
        du_ref[at : at + rows] = du
        outs[i][...] = mm(hid, wd[...]).astype(BF16)
        dns[i][...] = (mm(dg, w_gu[:ff]) + mm(du, w_gu[ff:])).astype(BF16)
        at += rows


QUARTERS = ((0, 1), (2, 3), (4, 5), (6, 7, 8, 9))


def over_tokens(lefts, rights, scratch):
    @pl.when(pl.program_id(0) == 0)
    def _():
        for q in range(4):
            scratch[:, q * 512 : (q + 1) * 512] = lefts[q][...].T

    total = 0.0
    for q, at in enumerate(QUARTERS):
        total += mm(scratch[:, q * 512 : (q + 1) * 512], jnp.concatenate([rights[i][...] for i in at], 0))
    return total.astype(BF16)


def hidden_grads_kernel(info, *refs):
    ns, dgs, dus, (near, far, dg_t, du_t) = refs[:10], refs[10:14], refs[14:18], refs[18:]
    gate, up = over_tokens(dgs, ns, dg_t), over_tokens(dus, ns, du_t)
    for s in range(gate.shape[1] // 128):
        cols = slice(s * 128, (s + 1) * 128)
        near[s], far[s] = pack_tile(info, gate[:, cols], up[:, cols])


def down_grads_kernel(info, *refs):
    dys, hids, outs = refs[:10], refs[10:14], refs[14:18]
    grad = over_tokens(hids, dys, refs[18])
    rows = grad.shape[0] // 4
    cut = lambda i: grad[i * rows : (i + 1) * rows]
    even = info[6] == 0
    for k, (zero, one) in enumerate(((cut(0), cut(1)), (cut(2), cut(3)))):
        stays, goes = sort_by_x(info, zero, one)
        if k == 0:
            first = stays, goes
    for i in range(2):
        outs[2 * i][...] = lax.select(even, first[i], (stays, goes)[i])
        outs[2 * i + 1][...] = lax.select(even, (stays, goes)[i], first[i])


def plain_grads_kernel(info, *refs):
    rights, lefts, (out, left_t) = refs[:10], refs[10:14], refs[14:]
    out[...] = over_tokens(lefts, rights, left_t)


SMEM = pl.BlockSpec(memory_space=pltpu.SMEM)
VMEM = pl.BlockSpec(memory_space=pltpu.VMEM)


def call(kernel, args, outs, scratch=(), flops=0, vmem=24, grid=None):
    shapes = tuple(jax.ShapeDtypeStruct(s, t) for s, t in outs)
    moved = sum(a.size * a.dtype.itemsize for a in args) + sum(s.size * s.dtype.itemsize for s in shapes)
    if grid is None:
        grid = {
            "in_specs": [SMEM if a.dtype == jnp.int32 else VMEM for a in args],
            "out_specs": [VMEM] * len(outs),
            "scratch_shapes": list(scratch),
        }
    return pl.pallas_call(
        kernel,
        out_shape=shapes,
        compiler_params=pltpu.CompilerParams(vmem_limit_bytes=vmem << 20),
        cost_estimate=pl.CostEstimate(flops=flops, bytes_accessed=moved, transcendentals=0),
        **grid,
    )(*args)


STATE = pltpu.VMEM((HP, FEAT, 2 * DV), F32)
TOKENS = [((n, 2048), BF16) for _, _, n in SLOTS]


QUARTER_SLICES = (slice(0, 2), slice(2, 4), slice(4, 6), slice(6, 10))


def mlp(ns, dys, w_gu, wd):
    ff, d = wd.shape
    k = len(ns)
    blocks = [((n.shape[0], d), BF16) for n in ns]
    rows = sum(n.shape[0] for n in ns)
    got = call(
        functools.partial(mlp_kernel, k),
        [*ns, *dys, w_gu, wd],
        blocks + blocks + [((rows, ff), BF16)] * 3,
        flops=12 * rows * ff * d,
    )
    return got[:k], got[k : 2 * k], got[2 * k :]


CUT = 256


def tall(n, at=lambda i, info: i):
    return pl.BlockSpec((n, CUT), lambda i, info: (0, at(i, info)))


def whole(a):
    return pl.BlockSpec(a.shape, lambda i, info: (0, 0))


def scalar_grid(steps, in_specs, out_specs, scratch):
    return {
        "grid_spec": pltpu.PrefetchScalarGridSpec(
            num_scalar_prefetch=1, grid=(steps,), in_specs=in_specs, out_specs=out_specs, scratch_shapes=scratch
        )
    }


def turned(ff):
    return pltpu.VMEM((ff, 2048), BF16)


def plain_grads(info, rights, lefts):
    ff, d = lefts[0].shape[1], rights[0].shape[1]
    grid = scalar_grid(d // CUT, [tall(a.shape[0]) for a in rights] + [whole(a) for a in lefts], [tall(ff)], [turned(ff)])
    return call(plain_grads_kernel, [info, *rights, *lefts], [((ff, d), BF16)], grid=grid)[0]


def hidden_grads(info, ns, dgs, dus, dh):
    ff, d = dgs[0].shape[1], ns[0].shape[1]
    steps = d // 2 // CUT
    cols = lambda i, info: jnp.bitwise_xor(info[6], dh) * steps + i
    slab = pl.BlockSpec((CUT // 128, ff, 128), lambda i, info: (i, 0, 0))
    grid = scalar_grid(steps, [tall(a.shape[0], cols) for a in ns] + [whole(a) for a in [*dgs, *dus]], [slab] * 2, [turned(ff)] * 2)
    return call(
        hidden_grads_kernel,
        [info, *ns, *dgs, *dus],
        [((8, ff, 128), BF16)] * 2,
        flops=2 * 2048 * ff * d,
        grid=grid,
        vmem=36,
    )


def down_grads(info, dys, hids):
    ff, d = hids[0].shape[1], dys[0].shape[1]
    out = tall(ff // 4)
    grid = scalar_grid(d // CUT, [tall(a.shape[0]) for a in dys] + [whole(a) for a in hids], [out] * 4, [turned(ff)])
    shapes = [((ff // 4, d), BF16)] * 4
    return call(down_grads_kernel, [info, *dys, *hids], shapes, flops=2 * 2048 * ff * d, grid=grid)


def gained(gain, w):
    return (gain * w.astype(F32)).astype(BF16)


def head_slabs(gain, w_query, w_key, w_value):
    split = [split_heads(gained(gain, w), n) for w, n in ((w_value, DV), (w_query, FD), (w_key, FD))]
    return jnp.concatenate(split, 2).transpose(0, 2, 1, 3).reshape(8, ROWS, -1)


def project(info, xs, w_qkv, maps_t):
    size, d = 256, w_qkv.shape[1]
    return call(
        project_kernel,
        [info, *xs, w_qkv, maps_t],
        [((8, size, 128), F32), ((8, size, QK), BF16), ((HP, SENT, 2 * DV), BF16)],
        [STATE],
        flops=2 * 8 * size * d * WIDE,
    )


def attend(info, tile, values, enter, maps, maps_t, w_out):
    size, d = 256, w_out.shape[1]
    got = call(
        attend_kernel,
        [info, tile, values, enter, maps, maps_t, w_out],
        [((8, size, QK), BF16), ((8, size, 128), F32), ((8, HP, FEAT, 2 * DV), BF16)] + TOKENS,
        [STATE],
        flops=2 * 8 * size * d * QK,
    )
    return got[:3], got[3:]


def back_state(info, dbs, w_out, mixed, den, tile, maps_t):
    size, d = 256, w_out.shape[1]
    return call(
        back_state_kernel,
        [info, *dbs, w_out, mixed, den, tile, maps_t],
        [((8, size, QK), BF16), ((8, size, 128), F32), ((HP, SENT, 2 * DV), BF16)],
        [STATE],
        flops=2 * 8 * size * d * QK,
    )


def back(info, tile, values, d_num, d_den, before, later, maps, w_qkv):
    size, d = 256, w_qkv.shape[1]
    got = call(
        back_kernel,
        [info, tile, values, d_num, d_den, before, later, maps, w_qkv],
        [((8, size, WIDE), BF16)] + TOKENS,
        [STATE],
        flops=2 * 8 * size * d * WIDE,
        vmem=28,
    )
    return got[0], got[1:]


def qkv_grads(info, xs, e, packed):
    d = xs[0].shape[1]
    outs = [((8, ROWS, 128), BF16)] * 4 if packed else [((WIDE, d), BF16)]
    return call(qkv_grads_kernel, [info, *xs, e], outs, [pltpu.VMEM((WIDE, d), F32)], flops=2 * 2048 * d * WIDE)


def out_grads(info, dbs, mixed, packed):
    d = dbs[0].shape[1]
    outs = [((QK // 4, d), BF16)] * 4 if packed else [((QK, d), BF16)]
    return call(out_grads_kernel, [info, *dbs, mixed], outs, [pltpu.VMEM((QK, d), F32)], flops=2 * 2048 * d * QK)


def total(groups, shape, dtype):
    args = [c for g in groups for c in g]
    return call(functools.partial(total_kernel, [len(g) for g in groups]), args, [(shape, dtype)])[0]


def finish_residual(x, pieces):
    return call(residual_kernel, [x, *pieces], [(x.shape, F32), (x.shape, BF16)])


def finish_d_residual(dy, resid, pieces):
    return call(d_residual_kernel, [dy, resid, *pieces], [(dy.shape, F32), (dy.shape, BF16)])


def finish_input(x, d_resid, pieces):
    return call(input_kernel, [x, d_resid, *pieces], [((1,) + x.shape, F32)])[0]


def finish_output(resid, pieces):
    return call(output_kernel, [resid, *pieces], [((1,) + resid.shape, F32)])[0]


def gather_all(own):
    near = near_tokens(own)
    far = far_tokens(near)
    return in_slots(near, far, last_tokens(far))


def scatter_all(p):
    nears = near_cores(p)
    via = send_far(p, far_cores(p))
    return terms(p, nears, send_first(p, nears), send_second(p, nears, via))


def weight_grads(weights, gains, g_heads, g_hid):
    w_query, w_key, w_value, w_gate, w_up = weights
    g_gate, g_up = join_hidden(g_hid.astype(F32))
    g_heads = g_heads.astype(F32).reshape(8, ROWS, HP, -1).transpose(0, 2, 1, 3)
    g_value = join_heads(g_heads[:, :, :DV], DV)
    g_query = join_heads(g_heads[:, :, DV : DV + FD], FD)
    g_key = join_heads(g_heads[:, :, DV + FD :], FD)
    along = lambda w, g: jnp.sum(w.astype(F32) * g, -1)
    g_one = along(w_query, g_query) + along(w_key, g_key) + along(w_value, g_value)
    g_two = along(w_gate, g_gate) + along(w_up, g_up)
    return g_one, gains[0] * g_query, gains[0] * g_key, gains[0] * g_value, g_two, gains[1] * g_gate, gains[1] * g_up


def on_device(
    tokens, seq_lengths, norm_gain, w_query, w_key, w_value, w_out, mlp_gain, w_gate, w_up, w_down, cotangent
):
    x, dy = tokens[0], cotangent[0]
    gains = [g.astype(F32)[:, None] for g in (norm_gain, mlp_gain)]
    h, along_x = lax.axis_index("h"), lax.axis_index("x")
    place = jnp.stack([lax.axis_index(TP), h * 8 * x.shape[0]])
    info = jnp.concatenate([place, seq_lengths[0], jnp.stack([h, along_x])]).astype(jnp.int32)
    maps, maps_t = jnp.asarray(MAPS, BF16), jnp.asarray(MAPS.transpose(0, 1, 3, 2), BF16)
    small = small_mesh() and w_query.shape[0] == 64
    run = scheduled if small else plain
    block_out, input_grad, g_heads, g_out, g_hid, g_down = run(
        info, x, dy, gains, w_query, w_key, w_value, w_out, w_gate, w_up, w_down, maps, maps_t
    )
    g = weight_grads((w_query, w_key, w_value, w_gate, w_up), gains, g_heads, g_hid)
    return block_out, input_grad, *g[:4], g_out, *g[4:], g_down


def plain(info, x, dy, gains, w_query, w_key, w_value, w_out, w_gate, w_up, w_down, maps, maps_t):
    heads = over_both(exchange(head_slabs(gains[0], w_query, w_key, w_value)))
    w_qkv = slabs_to_rows(heads, LAYOUT_HEADS, WIDE)
    w_out_mine = out_rows_in(over_both(w_out))
    hid = over_both(exchange(split_hidden(gained(gains[1], w_gate), gained(gains[1], w_up))))
    wd = over_both(w_down).reshape(-1, x.shape[1])
    ff = wd.shape[0]
    w_gu = slabs_to_rows(hid, layout_hidden(ff), 2 * ff)
    xs = gather_all(x)
    tile, values, state = project(info, xs, w_qkv, maps_t)
    (mixed, den, before), p = attend(info, tile, values, entering(state, False), maps, maps_t, w_out_mine)
    resid, n_low = finish_residual(x, scatter_all(p))
    ns, dys = gather_all(n_low), gather_all(dy)
    ran = [mlp(ns[c], dys[c], w_gu, wd) for c in QUARTER_SLICES]
    hids, dgs, dus = [[r[2][i] for r in ran] for i in range(3)]
    block_out = finish_output(resid, scatter_all([b for r in ran for b in r[0]]))
    d_resid, d_low = finish_d_residual(dy, resid, scatter_all([b for r in ran for b in r[1]]))
    grads = jnp.concatenate([plain_grads(info, ns, dgs), plain_grads(info, ns, dus)], 0)
    g_hid = exchange(sum_both(rows_to_slabs(grads, layout_hidden(ff))).astype(BF16))
    g_down = sum_both(plain_grads(info, dys, hids).reshape(*hid.shape[:2], -1, x.shape[1]))
    dbs = gather_all(d_low)
    d_num, d_den, use = back_state(info, dbs, w_out_mine, mixed, den, tile, maps_t)
    e, p = back(info, tile, values, d_num, d_den, before, entering(use, True), maps, w_qkv)
    input_grad = finish_input(x, d_resid, scatter_all(p))
    g_out = sum_both(out_rows_out(out_grads(info, dbs, mixed, False)[0]))
    g_heads = exchange(sum_both(rows_to_slabs(qkv_grads(info, xs, e, False)[0], LAYOUT_HEADS)).astype(BF16))
    return block_out, input_grad, g_heads, g_out, g_hid, g_down


def scheduled(info, x, dy, gains, w_query, w_key, w_value, w_out, w_gate, w_up, w_down, maps, maps_t):
    d_model = x.shape[1]
    o = Order(info)

    near = near_tokens(x)
    out_h = swap(w_out, "h")
    heads = exchange(head_slabs(gains[0], w_query, w_key, w_value))
    heads, out_h = o.at(heads, out_h)
    hid = split_hidden(gained(gains[1], w_gate), gained(gains[1], w_up))
    heads_h, heads_x = swap(heads, "h"), swap(heads, "x")
    near, heads_h, heads_x, hid = o.at(near, heads_h, heads_x, hid)
    far = far_tokens(near)
    heads_hx = swap(heads_h, "x")
    d0, d1 = w_down[:96], w_down[96:]
    d0_h = swap(d0, "h")
    far, heads_hx, d0_h, hid = o.at(far, heads_hx, d0_h, hid)
    last = last_tokens(far)
    w_qkv = unpack(o.info, [[heads], [heads_h], [heads_x], [heads_hx]], LAYOUT_HEADS, WIDE)
    out_x, out_hx = swap(w_out, "x"), swap(out_h, "x")
    last, w_qkv, out_x, out_hx = o.at(last, w_qkv, out_x, out_hx)
    xs = in_slots(near, far, last)

    hid = exchange(hid)
    d1_h = swap(d1, "h")
    tile, values, state = project(o.info, xs, w_qkv, maps_t)
    tile, values, state, hid, d1_h = o.at(tile, values, state, hid, d1_h)
    enter = entering(state, False)
    d0_x, d1_x = swap(d0, "x"), swap(d1, "x")
    w_out_mine = call(
        functools.partial(rows_kernel, 1), [o.info, w_out, out_h, out_x, out_hx], [((QK, d_model), BF16)]
    )[0]
    enter, d0_x, d1_x, w_out_mine = o.at(enter, d0_x, d1_x, w_out_mine)
    dy_near = near_tokens(dy)
    u = cut(hid, 4)
    u_h, u_x, u_hx = [None] * 4, [None] * 4, [None] * 4
    u_h[0] = swap(u[0], "h")
    d0_hx, d1_hx = swap(d0_h, "x"), swap(d1_h, "x")
    (mixed, den, before), p = attend(o.info, tile, values, enter, maps, maps_t, w_out_mine)
    p, mixed, den, before, u_h[0], d0_hx, d1_hx = o.at(p, mixed, den, before, u_h[0], d0_hx, d1_hx)
    fars = far_cores(p)
    u_x[0] = swap(u[0], "x")
    fars, dy_near, u_x[0] = o.at(fars, dy_near, u_x[0])
    via = send_far(p, fars)
    nears = near_cores(p)
    u_h[1], u_x[1], u_hx[0] = swap(u[1], "h"), swap(u[1], "x"), swap(u_h[0], "x")
    via, nears, u_h[1], u_x[1], u_hx[0] = o.at(via, nears, u_h[1], u_x[1], u_hx[0])
    first = send_first(p, nears)
    u_h[2], u_x[2], u_hx[1] = swap(u[2], "h"), swap(u[2], "x"), swap(u_h[1], "x")
    first, u_h[2], u_x[2], u_hx[1] = o.at(first, u_h[2], u_x[2], u_hx[1])
    second = send_second(p, nears, via)
    u_h[3], u_x[3], u_hx[2] = swap(u[3], "h"), swap(u[3], "x"), swap(u_h[2], "x")
    wd = call(
        functools.partial(rows_kernel, 2),
        [o.info, d0, d1, d0_h, d1_h, d0_x, d1_x, d0_hx, d1_hx],
        [((4 * w_down.shape[0], d_model), BF16)],
    )[0]
    ff = wd.shape[0]
    second, u_h[3], u_x[3], u_hx[2], wd = o.at(second, u_h[3], u_x[3], u_hx[2], wd)
    resid, n_low = finish_residual(x, terms(p, nears, first, second))
    resid, n_low = o.at(resid, n_low)

    near = near_tokens(n_low)
    u_hx[3] = swap(u_h[3], "x")
    w_gu = unpack(o.info, [u, u_h, u_x, u_hx], layout_hidden(ff), 2 * ff)
    near, w_gu = o.at(near, w_gu)
    far = far_tokens(near)
    quarter = lambda i, ns, dys: mlp(ns[QUARTER_SLICES[i]], dys[QUARTER_SLICES[i]], w_gu, wd)
    ns, dys = in_slots(near, far, [None] * 2), in_slots(dy_near, [None] * 4, [None] * 2)
    ran = [quarter(0, ns, dys)]
    far, ran = o.at(far, ran)
    last = last_tokens(far)
    dy_far = far_tokens(dy_near)
    ns, dys = in_slots(near, far, last), in_slots(dy_near, dy_far, [None] * 2)
    dy_ready = dy_far[2:]
    last, dy_ready = o.at(last, dy_ready)
    dy_far = dy_far[:2] + dy_ready
    ns, dys = in_slots(near, far, last), in_slots(dy_near, dy_far, [None] * 2)
    ran.append(quarter(1, ns, dys))
    ran, dy_far = o.at(ran, dy_far)
    dy_last = last_tokens(dy_far)
    dys = in_slots(dy_near, dy_far, dy_last)
    ran.append(quarter(2, ns, dys))
    ran, dy_last = o.at(ran, dy_last)
    dys = in_slots(dy_near, dy_far, dy_last)
    p = [b for r in ran for b in r[1]]
    nears = near_cores(p)
    ran.append(quarter(3, ns, dys))
    nears, ran = o.at(nears, ran)
    p = [b for r in ran for b in r[1]]
    outs = [b for r in ran for b in r[0]]
    hids, dgs, dus = [[r[2][i] for r in ran] for i in range(3)]
    fars = far_cores(p)
    fars, = o.at(fars)
    via = send_far(p, fars)
    near_1, far_1 = hidden_grads(o.info, ns, dgs, dus, 1)
    via, near_1, far_1 = o.at(via, near_1, far_1)
    first = send_first(p, nears)
    near_0, far_0 = hidden_grads(o.info, ns, dgs, dus, 0)
    f1, f0 = cut(far_1, 2), cut(far_0, 2)
    f1[0] = swap(f1[0], "x")
    first, near_0, far_0, f1[0] = o.at(first, near_0, far_0, f1[0])
    second = send_second(p, nears, via)
    f1[1] = swap(f1[1], "x")
    n1 = cut(near_1, 2)
    go = cut(plus(n1[0], f1[0]), 2)
    came = [swap(go[0], "h")]
    down = down_grads(o.info, dys, hids)
    second, f1[1], came, down = o.at(second, f1[1], came, down)
    d_resid, d_low = finish_d_residual(dy, resid, terms(p, nears, first, second))
    d_resid, d_low = o.at(d_resid, d_low)

    near = near_tokens(d_low)
    came.append(swap(go[1], "h"))
    go += cut(plus(n1[1], f1[1]), 2)
    down_f1 = swap(down[3], "x")
    near, came, go, down_f1 = o.at(near, came, go, down_f1)
    far = far_tokens(near)
    f0[0] = swap(f0[0], "x")
    came.append(swap(go[2], "h"))
    o_nears = near_cores(outs)
    far, f0[0], came, o_nears = o.at(far, f0[0], came, o_nears)
    last = last_tokens(far)
    o_fars = far_cores(outs)
    last, o_fars = o.at(last, o_fars)
    dbs = in_slots(near, far, last)
    f0[1] = swap(f0[1], "x")
    came.append(swap(go[3], "h"))
    o_via = send_far(outs, o_fars)
    d_num, d_den, use = back_state(o.info, dbs, w_out_mine, mixed, den, tile, maps_t)
    d_num, d_den, use, f0[1], came, o_via = o.at(d_num, d_den, use, f0[1], came, o_via)
    later = entering(use, True)
    o_first = send_first(outs, o_nears)
    down_f0 = swap(down[2], "x")
    g_hid = total([[near_0], f0, came], near_0.shape, BF16)
    out_n0, out_n1, out_f0, out_f1 = out_grads(o.info, dbs, mixed, True)
    later, o_first, down_f0, g_hid, out_f0, out_f1 = o.at(later, o_first, down_f0, g_hid, out_f0, out_f1)
    down_go = plus(down[1], down_f1)
    down_came = [swap(down_go[:96], "h")]
    g_hid = exchange(g_hid)
    e, p = back(o.info, tile, values, d_num, d_den, before, later, maps, w_qkv)
    e, p, down_came, g_hid = o.at(e, p, down_came, g_hid)
    nears, fars = near_cores(p), far_cores(p)
    nears, fars = o.at(nears, fars)
    via = send_far(p, fars)
    down_came.append(swap(down_go[96:], "h"))
    out_f1, out_f0 = swap(out_f1, "x"), swap(out_f0, "x")
    head_n0, head_n1, head_f0, head_f1 = qkv_grads(o.info, xs, e, True)
    via, down_came, out_f1, out_f0, head_f0, head_f1 = o.at(via, down_came, out_f1, out_f0, head_f0, head_f1)
    first = send_first(p, nears)
    head_f1 = swap(head_f1, "x")
    out_came = swap(plus(out_n1, out_f1), "h")
    first, head_f1, out_came = o.at(first, head_f1, out_came)
    second = send_second(p, nears, via)
    head_came = swap(plus(head_n1, head_f1), "h")
    head_f0 = swap(head_f0, "x")
    g_down = total([[down[0]], [down_f0], down_came], w_down.shape, F32)
    g_out = total([[out_n0], [out_f0], [out_came]], w_out.shape, F32)
    second, head_came, head_f0 = o.at(second, head_came, head_f0)
    g_heads = exchange(total([[head_n0], [head_f0], [head_came]], head_n0.shape, BF16))
    o_second = send_second(outs, o_nears, o_via)
    input_grad = finish_input(x, d_resid, terms(p, nears, first, second))
    block_out = finish_output(resid, terms(outs, o_nears, o_first, o_second))
    return block_out, input_grad, g_heads, g_out, g_hid, g_down


def solution(mesh):
    seq, fsdp = mesh.shape["seq"], mesh.shape["fsdp"]
    fine = Mesh(mesh.devices.reshape(seq // 8, 2, 2, 2, fsdp), ("h", "l", "y", "c", "x"))
    along = ("h", "l", "y", "c")
    token, vec, mat = P("x", along, None), P(along + ("x",)), P(along + ("x",), None)
    return jax.shard_map(
        on_device,
        mesh=fine,
        in_specs=(token, P("x", None), vec, mat, mat, mat, mat, vec, mat, mat, mat, token),
        out_specs=(token, token, vec, mat, mat, mat, mat, vec, mat, mat, mat),
        check_vma=False,
    )
```

time: 897 us -> 763 us (0.85)
  Pallas kernels: 0 us -> 170 us
  matrix products: 159 us -> 0 us
  other arithmetic: 110 us -> 29.7 us
  waiting for transfers between devices: 338 us -> 282 us
  local copies, waits for them, and re-layouts: 176 us -> 134 us
  starting transfers between devices: 99 us -> 137 us
    pallas_call x0 -> x25, Pallas kernels: none -> 170 us  [call(): pl.pallas_call(kernel, out_shape=shapes, compiler_params=pltpu.CompilerPa...]
    dot_general x34 -> x0, matrix products: 159 us -> none  [the longest x12 115 us: dot(): return lax.dot_general(a, b, (dims, ((), ())), preferred_element_type=F32)]
    ppermute x88 -> x122, waiting for transfers between devices: 328 us -> 257 us  [swap(): return lax.ppermute(a, axis, [(0, 1), (1, 0)])]
    unnamed x278 -> x447, local copies, waits for them, and re-layouts: 63.9 us -> 120 us
    ppermute x88 -> x122, starting transfers between devices: 75.9 us -> 116 us  [swap(): return lax.ppermute(a, axis, [(0, 1), (1, 0)])]
    reshape x17 -> x2, local copies, waits for them, and re-layouts: 40.5 us -> 1 us  [the longest x1 0.93 us: head_slabs(): return jnp.concatenate(split, 2).transpose(0, 2, 1, 3).reshape(8, ROWS, -1)]
    another operation x8 -> x0, local copies, waits for them, and re-layouts: 25.3 us -> none  [the longest x4 14.4 us: reorder(): jnp.stack([lax.dynamic_index_in_dim(blocks, p ^ me, 0, keepdims=False) fo...]
    add x11 -> x2, other arithmetic: 20 us -> 1.03 us  [the longest x1 0.51 us: weight_grads(): along(w_query, g_query) + along(w_key, g_key) + along(w_value, g_value)]
  transfers between devices with their start and end apart: 94 -> 128, of which waited for: 29 -> 46; matrix products, arithmetic and copies ran while one was open for 37% -> 6% of each run, Pallas kernels for 0% -> 22%
where the time goes in v2:
time: 763 us; the launch traced here: 756 us
  waiting for transfers between devices  282 us (37%)
  Pallas kernels  170 us (22%)
  starting transfers between devices  137 us (18%)
  local copies, waits for them, and re-layouts  134 us (18%)
  other arithmetic  29.7 us (4%)
    ppermute x122, waiting for transfers between devices, swap(): return lax.ppermute(a, axis, [(0, 1), (1, 0)])  257 us
    pallas_call x25, Pallas kernels, call(): pl.pallas_call(kernel, out_shape=shapes, compiler_params=pltpu.CompilerPa...  170 us
    unnamed x447, local copies, waits for them, and re-layouts  120 us
    ppermute x122, starting transfers between devices, swap(): return lax.ppermute(a, axis, [(0, 1), (1, 0)])  116 us
    ppermute x2, waiting for transfers between devices, entering(): came = lax.ppermute(total, 'h', route)  23.4 us
    all_to_all x4, starting transfers between devices, exchange(): return lax.all_to_all(slabs, TP, 0, 0, tiled=True)  17.3 us
    convert_element_type x21, other arithmetic, plus(): functools.reduce(jnp.add, [t.astype(F32) for t in terms]).astype(BF16)  15.5 us
  transfers between devices with their start and end apart: 128, of which 46 were waited for; matrix products, arithmetic and copies ran while one was open for 6% of the time, Pallas kernels for 22%

profile of v2, /device:TPU:0, one launch (start us, length us, event | category | flops | bytes accessed | tf_op | source)
XLA Modules:
  0.0 755.7 jit_solution(15233020804436853649)
XLA Ops:
  10.5 3.6 all-to-all-start
  20.7 3.9 fusion
  24.7 12.9 %collective-permute-done.refs_1_ = bf16[64,2048]{1,0:T(8,128)(2,1)} collective-permute-done((bf16[64,2048]{1,0:T(8,128)(2,1)}, bf16[64,2048]{1,0:T(8,128)(2,1)}, u32[]{:S(2)}, u32[]{:S(2)}) %collective-permute-start) | collective-permute-done | bytes 262176 | tf_op jit(solution)/shard_map/ppermute | solution.py:46
  47.3 9.1 %collective-permute-done.4.refs_1_ = bf16[8,160,128]{2,1,0:T(8,128)(2,1)S(1)} collective-permute-done((bf16[8,160,128]{2,1,0:T(8,128)(2,1)S(1)}, bf16[8,160,128]{2,1,0:T(8,128)(2,1)S(1)}, u32[]{:S(2)}, u32[]{:S(2)}) %collective-permute-start.4) | collective-permute-done | bytes 327712 | tf_op jit(solution)/shard_map/ppermute | solution.py:46
  60.2 3.7 collective-permute-start.6
  64.0 14.8 %collective-permute-done.11.refs_2_ = bf16[96,2048]{1,0:T(8,128)(2,1)S(1)} collective-permute-done((bf16[96,2048]{1,0:T(8,128)(2,1)S(1)}, bf16[96,2048]{1,0:T(8,128)(2,1)S(1)}, u32[]{:S(2)}, u32[]{:S(2)}) %collective-permute-start.11) | collective-permute-done | bytes 393248 | tf_op jit(solution)/shard_map/ppermute | solution.py:46
  79.3 8.3 %collective-permute-done.10.refs_3_ = bf16[8,160,128]{2,1,0:T(8,128)(2,1)S(1)} collective-permute-done((bf16[8,160,128]{2,1,0:T(8,128)(2,1)S(1)}, bf16[8,160,128]{2,1,0:T(8,128)(2,1)S(1)}, u32[]{:S(2)}, u32[]{:S(2)}) %collective-permute-start.10) | collective-permute-done | bytes 327712 | tf_op jit(solution)/shard_map/ppermute | solution.py:46
  89.6 4.5 all-to-all-start.1
  98.2 5.7 collective-permute-done.14.refs_2_
  104.7 4.9 collective-permute-done.15.refs_3_
  121.4 10.4 %shard_map.222 = (f32[8,256,128]{2,1,0:T(8,128)S(1)}, bf16[8,256,256]{2,1,0:T(8,128)(2,1)S(1)}, bf16[2,160,256]{2,1,0:T(8,128)(2,1)S(1)}) custom-call(s32[8]{0:T(128)S(1)} %concatenate.9.info, bf16[256,2048]{1,0:T(8,128)(2,1)S(1)} %bitcast.81, bf16[256,2048]{1,0:T(8,128)(2,1)S(1)} %copy-done.100, bf16[256,2048]{1,0:T(8,128)(2,1)S(1)} %copy-done.91, ...), custom_call_target="tpu_custom_call" | custom-call | flops 3221225472 | bytes 12746784 | tf_op jit(solution)/shard_map/pallas_call | solution.py:672
  142.6 23.4 %collective-permute-done.17.enter = bf16[2,160,256]{2,1,0:T(8,128)(2,1)S(1)} collective-permute-done((bf16[2,160,256]{2,1,0:T(8,128)(2,1)}, bf16[2,160,256]{2,1,0:T(8,128)(2,1)S(1)}, u32[]{:S(2)}, u32[]{:S(2)}) %collective-permute-start.17) | collective-permute-done | bytes 163872 | tf_op jit(solution)/shard_map/ppermute | solution.py:235
  167.9 9.3 %shard_map.224 = (bf16[8,256,256]{2,1,0:T(8,128)(2,1)S(1)}, f32[8,256,128]{2,1,0:T(8,128)S(1)}, bf16[8,2,256,256]{3,2,1,0:T(8,128)(2,1)S(1)}, bf16[256,2048]{1,0...) custom-call(s32[8]{0:T(128)S(1)} %concatenate.9.info, ...), custom_call_target="tpu_custom_call" | custom-call | flops 2147483648 | bytes 16941088 | tf_op jit(solution)/shard_map/pallas_call | solution.py:672
  183.1 6.0 collective-permute-done.28.refs_8_
  189.8 6.1 collective-permute-done.35.refs_9_
  197.4 8.1 %collective-permute-done.36.refs_12_ = bf16[2,704,128]{2,1,0:T(8,128)(2,1)S(1)} collective-permute-done((bf16[2,704,128]{2,1,0:T(8,128)(2,1)S(1)}, bf16[2,704,128]{2,1,0:T(8,128)(2,1)S(1)}, u32[]{:S(2)}, u32[]{:S(2)}) %collective-permute-start.36) | collective-permute-done | bytes 360480 | tf_op jit(solution)/shard_map/ppermute | solution.py:46
  206.0 4.0 collective-permute-done.29
  210.7 6.9 collective-permute-done.30
  225.9 12.4 %collective-permute-done.39.refs_6_ = bf16[2,704,128]{2,1,0:T(8,128)(2,1)S(1)} collective-permute-done((bf16[2,704,128]{2,1,0:T(8,128)(2,1)S(1)}, bf16[2,704,128]{2,1,0:T(8,128)(2,1)S(1)}, u32[]{:S(2)}, u32[]{:S(2)}) %collective-permute-start.39) | collective-permute-done | bytes 360480 | tf_op jit(solution)/shard_map/ppermute | solution.py:46
  241.1 4.3 collective-permute-start.44
  248.5 5.7 collective-permute-done.44.refs_7_
  262.7 8.9 %collective-permute-done.50.refs_15_ = bf16[2,704,128]{2,1,0:T(8,128)(2,1)S(1)} collective-permute-done((bf16[2,704,128]{2,1,0:T(8,128)(2,1)S(1)}, bf16[2,704,128]{2,1,0:T(8,128)(2,1)S(1)}, u32[]{:S(2)}, u32[]{:S(2)}) %collective-permute-start.50) | collective-permute-done | bytes 360480 | tf_op jit(solution)/shard_map/ppermute | solution.py:46
  274.3 10.3 %collective-permute-done.48.refs_0_.refs_2_ = bf16[256,2048]{1,0:T(8,128)(2,1)S(1)} collective-permute-done((bf16[256,2048]{1,0:T(8,128)(2,1)S(1)}, bf16[256,2048]{1,0:T(8,128)(2,1)S(1)}, u32[]{:S(2)}, u32[]{:S(2)}) %collective-permute-start.48) | collective-permute-done | bytes 1048608 | tf_op jit(solution)/shard_map/ppermute | solution.py:46
  287.5 11.8 %collective-permute-done.52.refs_1_.refs_7_ = bf16[128,2048]{1,0:T(8,128)(2,1)S(1)} collective-permute-done((bf16[128,2048]{1,0:T(8,128)(2,1)S(1)}, bf16[128,2048]{1,0:T(8,128)(2,1)S(1)}, u32[]{:S(2)}, u32[]{:S(2)}) %collective-permute-start.52) | collective-permute-done | bytes 524320 | tf_op jit(solution)/shard_map/ppermute | solution.py:46
  299.9 11.8 %shard_map.228 = (bf16[256,2048]{1,0:T(8,128)(2,1)S(1)}, bf16[256,2048]{1,0:T(8,128)(2,1)S(1)}, bf16[256,2048]{1,0:T(8,128)(2,1)S(1)}, bf16[256,2048]{1,0:T(8,12...) custom-call(bf16[256,2048]{1,0:T(8,128)(2,1)S(1)} %get-tuple-element.484.refs_, ...), custom_call_target="tpu_custom_call" | custom-call | flops 8858370048 | bytes 19202048 | tf_op jit(solution)/shard_map/pallas_call | solution.py:672
  318.9 12.3 %shard_map.229 = (bf16[256,2048]{1,0:T(8,128)(2,1)S(1)}, bf16[256,2048]{1,0:T(8,128)(2,1)S(1)}, bf16[256,2048]{1,0:T(8,128)(2,1)S(1)}, bf16[256,2048]{1,0:T(8,12...) custom-call(bf16[256,2048]{1,0:T(8,128)(2,1)S(1)} %collective-permute-done.48., ...), custom_call_target="tpu_custom_call" | custom-call | flops 8858370048 | bytes 19202048 | tf_op jit(solution)/shard_map/pallas_call | solution.py:672
  336.5 10.8 %shard_map.230 = (bf16[256,2048]{1,0:T(8,128)(2,1)S(1)}, bf16[256,2048]{1,0:T(8,128)(2,1)S(1)}, bf16[256,2048]{1,0:T(8,128)(2,1)S(1)}, bf16[256,2048]{1,0:T(8,12...) custom-call(bf16[256,2048]{1,0:T(8,128)(2,1)S(1)} %collective-permute-done.47., ...), custom_call_target="tpu_custom_call" | custom-call | flops 8858370048 | bytes 19202048 | tf_op jit(solution)/shard_map/pallas_call | solution.py:672
  353.9 16.3 %shard_map.231 = (bf16[128,2048]{1,0:T(8,128)(2,1)S(1)}, bf16[128,2048]{1,0:T(8,128)(2,1)S(1)}, bf16[128,2048]{1,0:T(8,128)(2,1)S(1)}, bf16[128,2048]{1,0:T(8,12...) custom-call(bf16[128,2048]{1,0:T(8,128)(2,1)S(1)} %collective-permut, ...), custom_call_target="tpu_custom_call" | custom-call | flops 8858370048 | bytes 19202048 | tf_op jit(solution)/shard_map/pallas_call | solution.py:672
  397.5 17.1 %shard_map.232 = (bf16[8,704,128]{2,1,0:T(8,128)(2,1)S(1)}, bf16[8,704,128]{2,1,0:T(8,128)(2,1)S(1)}) custom-call(s32[8]{0:T(128)S(1)} %concatenate.9.info, bf16[256,2048]{1,0:T(8,128)(2,1)S(1)} %copy-done.115, bf16[256,2048]{1,0:T(8,128)(2,1)S(1)} %copy-done.118, bf16[256,2048]{1,0:T(8,128)(2,1)S(1)} %copy-done.96, bf16[256,2048]{1,0:T(8,128)(2,1)S(1)} %copy-done.125, ...), custom_call_target="tpu_custom_call" | custom-call | flops 5905580032 | bytes 17039392 | tf_op jit(solution)/shard_map/pallas_call | solution.py:672
  426.0 16.8 %shard_map.233 = (bf16[8,704,128]{2,1,0:T(8,128)(2,1)S(1)}, bf16[8,704,128]{2,1,0:T(8,128)(2,1)S(1)}) custom-call(s32[8]{0:T(128)S(1)} %concatenate.9.info, bf16[256,2048]{1,0:T(8,128)(2,1)S(1)} %copy-done.116, bf16[256,2048]{1,0:T(8,128)(2,1)S(1)} %copy-done.119, bf16[256,2048]{1,0:T(8,128)(2,1)S(1)} %copy-done.96, bf16[256,2048]{1,0:T(8,128)(2,1)S(1)} %copy-done.125, ...), custom_call_target="tpu_custom_call" | custom-call | flops 5905580032 | bytes 17039392 | tf_op jit(solution)/shard_map/pallas_call | solution.py:672
  444.6 3.6 collective-permute-done.71.refs_3_
  460.6 11.6 %shard_map.234 = (bf16[176,2048]{1,0:T(8,128)(2,1)S(1)}, bf16[176,2048]{1,0:T(8,128)(2,1)S(1)}, bf16[176,2048]{1,0:T(8,128)(2,1)S(1)}, bf16[176,2048]{1,0:T(8,128)(2,1)S(1)}) custom-call(s32[8]{0:T(128)S(1)} %concatenate.9.info, bf16[256,2048]{1,0:T(8,128)(2,1)S(1)} %bitcast.89, bf16[256,2048]{1,0:T(8,128)(2,1)} %collective-permute-done.27.refs_3_.refs_1_, ...), custom_call_target="tpu_custom_call" | custom-call | flops 5905580032 | bytes 14155808 | tf_op jit(solution)/shard_map/pallas_call | solution.py:672
  479.9 15.7 %collective-permute-done.80.refs_4_ = bf16[2,704,128]{2,1,0:T(8,128)(2,1)S(1)} collective-permute-done((bf16[2,704,128]{2,1,0:T(8,128)(2,1)S(1)}, bf16[2,704,128]{2,1,0:T(8,128)(2,1)S(1)}, u32[]{:S(2)}, u32[]{:S(2)}) %collective-permute-start.80) | collective-permute-done | bytes 360480 | tf_op jit(solution)/shard_map/ppermute | solution.py:46
  497.0 5.3 collective-permute-done.78.refs_2_
  503.2 8.4 %collective-permute-done.77.refs_4_ = bf16[256,2048]{1,0:T(8,128)(2,1)S(1)} collective-permute-done((bf16[256,2048]{1,0:T(8,128)(2,1)S(1)}, bf16[256,2048]{1,0:T(8,128)(2,1)S(1)}, u32[]{:S(2)}, u32[]{:S(2)}) %collective-permute-start.77) | collective-permute-done | bytes 1048608 | tf_op jit(solution)/shard_map/ppermute | solution.py:46
  513.9 5.8 collective-permute-done.86.refs_1_
  521.6 15.4 %collective-permute-done.87.refs_5_ = bf16[2,704,128]{2,1,0:T(8,128)(2,1)S(1)} collective-permute-done((bf16[2,704,128]{2,1,0:T(8,128)(2,1)S(1)}, bf16[2,704,128]{2,1,0:T(8,128)(2,1)S(1)}, u32[]{:S(2)}, u32[]{:S(2)}) %collective-permute-start.87) | collective-permute-done | bytes 360480 | tf_op jit(solution)/shard_map/ppermute | solution.py:46
  546.6 6.8 shard_map.236
  553.4 3.8 collective-permute-done.95.refs_2_
  557.2 4.9 collective-permute-done.96.refs_6_
  579.7 3.9 collective-permute-done.102.refs_3_
  584.4 5.0 all-to-all-start.2
  598.4 18.3 %shard_map.240 = (bf16[8,256,384]{2,1,0:T(8,128)(2,1)S(1)}, bf16[256,2048]{1,0:T(8,128)(2,1)S(1)}, bf16[256,2048]{1,0:T(8,128)(2,1)S(1)}, bf16[256,2048]{1,0:T(8...) custom-call(s32[8]{0:T(128)S(1)} %concatenate.9.info, ...), custom_call_target="tpu_custom_call" | custom-call | flops 3221225472 | bytes 18513952 | tf_op jit(solution)/shard_map/pallas_call | solution.py:672
  628.6 5.2 collective-permute-done.109
  651.3 5.5 shard_map.241
  667.5 11.6 %collective-permute-done.121.refs_2_ = bf16[64,2048]{1,0:T(8,128)(2,1)S(1)} collective-permute-done((bf16[64,2048]{1,0:T(8,128)(2,1)S(1)}, bf16[64,2048]{1,0:T(8,128)(2,1)S(1)}, u32[]{:S(2)}, u32[]{:S(2)}) %collective-permute-start.121) | collective-permute-done | bytes 262176 | tf_op jit(solution)/shard_map/ppermute | solution.py:46
  689.0 22.7 %collective-permute-done.117.refs_5_ = bf16[128,2048]{1,0:T(8,128)(2,1)S(1)} collective-permute-done((bf16[128,2048]{1,0:T(8,128)(2,1)S(1)}, bf16[128,2048]{1,0:T(8,128)(2,1)S(1)}, u32[]{:S(2)}, u32[]{:S(2)}) %collective-permute-start.117) | collective-permute-done | bytes 524320 | tf_op jit(solution)/shard_map/ppermute | solution.py:46
  714.3 4.3 all-to-all-start.3
  (743 shorter events, 311.0 us)
Async XLA Ops:
  0.6 55.8 %collective-permute-start.3 = (bf16[256,2048]{1,0:T(8,128)(2,1)}, bf16[256,2048]{1,0:T(8,128)(2,1)S(1)}, u32[]{:S(2)}, u32[]{:S(2)}) collective-permute-start(bf16[256,2048]{1,0:T(8,128)(2,1)} %bitcast.78), channel_id=1, source_target_pairs={{0,2},{2,0},{1,3},{3,1},{4,6},{6,4},{5,7},{7,5},{8,10},{10,8},{9,1... | collective-permute-start | bytes 3145736 | tf_op jit(solution)/shard_map/ppermute | solution.py:46
  1.2 56.4 %collective-permute-start.2 = (bf16[256,2048]{1,0:T(8,128)(2,1)}, bf16[256,2048]{1,0:T(8,128)(2,1)S(1)}, u32[]{:S(2)}, u32[]{:S(2)}) collective-permute-start(bf16[256,2048]{1,0:T(8,128)(2,1)} %bitcast.79), channel_id=1, source_target_pairs={{0,4},{4,0},{1,5},{5,1},{2,6},{6,2},{3,7},{7,3},{8,12},{12,8},{9,1... | collective-permute-start | bytes 3145736 | tf_op jit(solution)/shard_map/ppermute | solution.py:46
  3.8 53.8 %collective-permute-start.1 = (bf16[256,2048]{1,0:T(8,128)(2,1)}, bf16[256,2048]{1,0:T(8,128)(2,1)}, u32[]{:S(2)}, u32[]{:S(2)}) collective-permute-start(bf16[256,2048]{1,0:T(8,128)(2,1)} %bitcast.80), channel_id=1, source_target_pairs={{0,8},{8,0},{1,9},{9,1},{2,10},{10,2},{3,11},{11,3},{4,12},{12,4},... | collective-permute-start | bytes 3145736 | tf_op jit(solution)/shard_map/ppermute | solution.py:46
  10.5 27.8 %all-to-all-start = ((bf16[8,160,128]{2,1,0:T(8,128)(2,1)}), bf16[8,160,128]{2,1,0:T(8,128)(2,1)S(1)}, u32[]{:S(2)}, u32[]{:S(2)}) async-start(bf16[8,160,128]{2,1,0:T(8,128)(2,1)} %copy.55), calls=%async_computation | async-start | bytes 655360 | tf_op jit(solution)/shard_map/all_to_all | solution.py:210
  57.5 30.0 %collective-permute-start.8 = (bf16[256,2048]{1,0:T(8,128)(2,1)S(1)}, bf16[256,2048]{1,0:T(8,128)(2,1)S(1)}, u32[]{:S(2)}, u32[]{:S(2)}) collective-permute-start(bf16[256,2048]{1,0:T(8,128)(2,1)S(1)} %collective-permute-done.2.refs_2_), channel_id=1, source_target_pairs={{0,2},{2,0},{1,3},{3,1},{4,6},{6,4},{5,7},{7,5},{8,10},{10,8},{9,1... | collective-permute-start | bytes 3145736 | tf_op jit(solution)/shard_map/ppermute | solution.py:46
  57.6 31.0 %collective-permute-start.9 = (bf16[256,2048]{1,0:T(8,128)(2,1)}, bf16[256,2048]{1,0:T(8,128)(2,1)S(1)}, u32[]{:S(2)}, u32[]{:S(2)}) collective-permute-start(bf16[256,2048]{1,0:T(8,128)(2,1)} %collective-permute-done.1.refs_4_), channel_id=1, source_target_pairs={{0,2},{2,0},{1,3},{3,1},{4,6},{6,4},{5,7},{7,5},{8,10},{10,8},{9,1... | collective-permute-start | bytes 3145736 | tf_op jit(solution)/shard_map/ppermute | solution.py:46
  59.4 28.2 %collective-permute-start.7 = (bf16[128,2048]{1,0:T(8,128)(2,1)S(1)}, bf16[128,2048]{1,0:T(8,128)(2,1)}, u32[]{:S(2)}, u32[]{:S(2)}) collective-permute-start(bf16[128,2048]{1,0:T(8,128)(2,1)S(1)} %slice.190), channel_id=1, source_target_pairs={{0,4},{4,0},{1,5},{5,1},{2,6},{6,2},{3,7},{7,3},{8,12},{12,8},{9,1... | collective-permute-start | bytes 1572872 | tf_op jit(solution)/shard_map/ppermute | solution.py:46
  60.2 27.3 %collective-permute-start.6 = (bf16[128,2048]{1,0:T(8,128)(2,1)S(1)}, bf16[128,2048]{1,0:T(8,128)(2,1)}, u32[]{:S(2)}, u32[]{:S(2)}) collective-permute-start(bf16[128,2048]{1,0:T(8,128)(2,1)S(1)} %slice.189), channel_id=1, source_target_pairs={{0,8},{8,0},{1,9},{9,1},{2,10},{10,2},{3,11},{11,3},{4,12},{12,4},... | collective-permute-start | bytes 1572872 | tf_op jit(solution)/shard_map/ppermute | solution.py:46
  89.6 47.6 %all-to-all-start.1 = ((bf16[8,704,128]{2,1,0:T(8,128)(2,1)}), bf16[8,704,128]{2,1,0:T(8,128)(2,1)}, u32[]{:S(2)}, u32[]{:S(2)}) async-start(bf16[8,704,128]{2,1,0:T(8,128)(2,1)} %bitcast.94), calls=%async_computation.1 | async-start | bytes 2883584 | tf_op jit(solution)/shard_map/all_to_all | solution.py:210
  96.7 42.1 %collective-permute-start.18 = (bf16[96,2048]{1,0:T(8,128)(2,1)S(1)}, bf16[96,2048]{1,0:T(8,128)(2,1)}, u32[]{:S(2)}, u32[]{:S(2)}) collective-permute-start(bf16[96,2048]{1,0:T(8,128)(2,1)S(1)} %slice.191.refs_0_), channel_id=1, source_target_pairs={{0,1},{1,0},{2,3},{3,2},{4,5},{5,4},{6,7},{7,6},{8,9},{9,8},{10,11... | collective-permute-start | bytes 1179656 | tf_op jit(solution)/shard_map/ppermute | solution.py:46
  104.7 29.8 %collective-permute-start.16 = (bf16[80,2048]{1,0:T(8,128)(2,1)S(1)}, bf16[80,2048]{1,0:T(8,128)(2,1)S(1)}, u32[]{:S(2)}, u32[]{:S(2)}) collective-permute-start(bf16[80,2048]{1,0:T(8,128)(2,1)S(1)} %slice.192.refs_1_), channel_id=1, source_target_pairs={{0,16},{16,0},{1,17},{17,1},{2,18},{18,2},{3,19},{19,3},{4,20},{20... | collective-permute-start | bytes 983048 | tf_op jit(solution)/shard_map/ppermute | solution.py:46
  110.3 26.9 %collective-permute-start.19 = (bf16[80,2048]{1,0:T(8,128)(2,1)S(1)}, bf16[80,2048]{1,0:T(8,128)(2,1)}, u32[]{:S(2)}, u32[]{:S(2)}) collective-permute-start(bf16[80,2048]{1,0:T(8,128)(2,1)S(1)} %slice.192.refs_1_), channel_id=1, source_target_pairs={{0,1},{1,0},{2,3},{3,2},{4,5},{5,4},{6,7},{7,6},{8,9},{9,8},{10,11... | collective-permute-start | bytes 983048 | tf_op jit(solution)/shard_map/ppermute | solution.py:46
  114.8 63.0 %collective-permute-start.27 = (bf16[256,2048]{1,0:T(8,128)(2,1)S(1)}, bf16[256,2048]{1,0:T(8,128)(2,1)}, u32[]{:S(2)}, u32[]{:S(2)}) collective-permute-start(bf16[256,2048]{1,0:T(8,128)(2,1)S(1)} %bitcast.85), channel_id=1, source_target_pairs={{0,2},{2,0},{1,3},{3,1},{4,6},{6,4},{5,7},{7,5},{8,10},{10,8},{9,1... | collective-permute-start | bytes 3145736 | tf_op jit(solution)/shard_map/ppermute | solution.py:46
  114.9 27.6 %collective-permute-start.21 = (bf16[96,2048]{1,0:T(8,128)(2,1)S(1)}, bf16[96,2048]{1,0:T(8,128)(2,1)}, u32[]{:S(2)}, u32[]{:S(2)}) collective-permute-start(bf16[96,2048]{1,0:T(8,128)(2,1)S(1)} %collective-permute-done.11.refs_2_), channel_id=1, source_target_pairs={{0,1},{1,0},{2,3},{3,2},{4,5},{5,4},{6,7},{7,6},{8,9},{9,8},{10,11... | collective-permute-start | bytes 1179656 | tf_op jit(solution)/shard_map/ppermute | solution.py:46
  135.2 43.9 %collective-permute-start.26 = (bf16[256,2048]{1,0:T(8,128)(2,1)S(1)}, bf16[256,2048]{1,0:T(8,128)(2,1)}, u32[]{:S(2)}, u32[]{:S(2)}) collective-permute-start(bf16[256,2048]{1,0:T(8,128)(2,1)S(1)} %bitcast.86), channel_id=1, source_target_pairs={{0,4},{4,0},{1,5},{5,1},{2,6},{6,2},{3,7},{7,3},{8,12},{12,8},{9,1... | collective-permute-start | bytes 3145736 | tf_op jit(solution)/shard_map/ppermute | solution.py:46
  137.2 42.6 %collective-permute-start.25 = (bf16[256,2048]{1,0:T(8,128)(2,1)S(1)}, bf16[256,2048]{1,0:T(8,128)(2,1)S(1)}, u32[]{:S(2)}, u32[]{:S(2)}) collective-permute-start(bf16[256,2048]{1,0:T(8,128)(2,1)S(1)} %bitcast.87), channel_id=1, source_target_pairs={{0,8},{8,0},{1,9},{9,1},{2,10},{10,2},{3,11},{11,3},{4,12},{12,4},... | collective-permute-start | bytes 3145736 | tf_op jit(solution)/shard_map/ppermute | solution.py:46
  138.8 27.2 %collective-permute-start.17 = (bf16[2,160,256]{2,1,0:T(8,128)(2,1)}, bf16[2,160,256]{2,1,0:T(8,128)(2,1)S(1)}, u32[]{:S(2)}, u32[]{:S(2)}) collective-permute-start(bf16[2,160,256]{2,1,0:T(8,128)(2,1)} %copy-done.165), channel_id=1, source_target_pairs={{0,16},{1,17},{2,18},{3,19},{4,20},{5,21},{6,22},{7,23},{8,24},{9,... | collective-permute-start | bytes 491528 | tf_op jit(solution)/shard_map/ppermute | solution.py:235
  142.5 34.7 %collective-permute-start.20 = (bf16[2,704,128]{2,1,0:T(8,128)(2,1)S(1)}, bf16[2,704,128]{2,1,0:T(8,128)(2,1)S(1)}, u32[]{:S(2)}, u32[]{:S(2)}) collective-permute-start(bf16[2,704,128]{2,1,0:T(8,128)(2,1)S(1)} %get-tuple-element.810.refs_0_), channel_id=1, source_target_pairs={{0,16},{16,0},{1,17},{17,1},{2,18},{18,2},{3,19},{19,3},{4,20},{20... | collective-permute-start | bytes 1081352 | tf_op jit(solution)/shard_map/ppermute | solution.py:46
  189.0 28.6 %collective-permute-start.31 = (bf16[256,2048]{1,0:T(8,128)(2,1)S(1)}, bf16[256,2048]{1,0:T(8,128)(2,1)S(1)}, u32[]{:S(2)}, u32[]{:S(2)}) collective-permute-start(bf16[256,2048]{1,0:T(8,128)(2,1)S(1)} %get-tuple-element.443), channel_id=1, source_target_pairs={{0,2},{2,0},{1,3},{3,1},{4,6},{6,4},{5,7},{7,5},{8,10},{10,8},{9,1... | collective-permute-start | bytes 3145736 | tf_op jit(solution)/shard_map/ppermute | solution.py:46
  189.1 28.6 %collective-permute-start.32 = (bf16[256,2048]{1,0:T(8,128)(2,1)S(1)}, bf16[256,2048]{1,0:T(8,128)(2,1)S(1)}, u32[]{:S(2)}, u32[]{:S(2)}) collective-permute-start(bf16[256,2048]{1,0:T(8,128)(2,1)S(1)} %get-tuple-element.444), channel_id=1, source_target_pairs={{0,2},{2,0},{1,3},{3,1},{4,6},{6,4},{5,7},{7,5},{8,10},{10,8},{9,1... | collective-permute-start | bytes 3145736 | tf_op jit(solution)/shard_map/ppermute | solution.py:46
  189.6 28.0 %collective-permute-start.33 = (bf16[256,2048]{1,0:T(8,128)(2,1)S(1)}, bf16[256,2048]{1,0:T(8,128)(2,1)S(1)}, u32[]{:S(2)}, u32[]{:S(2)}) collective-permute-start(bf16[256,2048]{1,0:T(8,128)(2,1)S(1)} %get-tuple-element.445), channel_id=1, source_target_pairs={{0,2},{2,0},{1,3},{3,1},{4,6},{6,4},{5,7},{7,5},{8,10},{10,8},{9,1... | collective-permute-start | bytes 3145736 | tf_op jit(solution)/shard_map/ppermute | solution.py:46
  218.7 26.7 %collective-permute-start.37 = (bf16[128,2048]{1,0:T(8,128)(2,1)S(1)}, bf16[128,2048]{1,0:T(8,128)(2,1)S(1)}, u32[]{:S(2)}, u32[]{:S(2)}) collective-permute-start(bf16[128,2048]{1,0:T(8,128)(2,1)S(1)} %get-tuple-element.802), channel_id=1, source_target_pairs={{0,4},{4,0},{1,5},{5,1},{2,6},{6,2},{3,7},{7,3},{8,12},{12,8},{9,1... | collective-permute-start | bytes 1572872 | tf_op jit(solution)/shard_map/ppermute | solution.py:46
  223.9 32.2 %collective-permute-start.43 = (bf16[128,2048]{1,0:T(8,128)(2,1)S(1)}, bf16[128,2048]{1,0:T(8,128)(2,1)S(1)}, u32[]{:S(2)}, u32[]{:S(2)}) collective-permute-start(bf16[128,2048]{1,0:T(8,128)(2,1)S(1)} %get-tuple-element.799), channel_id=1, source_target_pairs={{0,8},{8,0},{1,9},{9,1},{2,10},{10,2},{3,11},{11,3},{4,12},{12,4},... | collective-permute-start | bytes 1572872 | tf_op jit(solution)/shard_map/ppermute | solution.py:46
  257.3 27.3 %collective-permute-start.48 = (bf16[256,2048]{1,0:T(8,128)(2,1)S(1)}, bf16[256,2048]{1,0:T(8,128)(2,1)S(1)}, u32[]{:S(2)}, u32[]{:S(2)}) collective-permute-start(bf16[256,2048]{1,0:T(8,128)(2,1)S(1)} %get-tuple-element.484.refs_0_), channel_id=1, source_target_pairs={{0,4},{4,0},{1,5},{5,1},{2,6},{6,2},{3,7},{7,3},{8,12},{12,8},{9,1... | collective-permute-start | bytes 3145736 | tf_op jit(solution)/shard_map/ppermute | solution.py:46
  260.8 25.2 %collective-permute-start.47 = (bf16[256,2048]{1,0:T(8,128)(2,1)S(1)}, bf16[256,2048]{1,0:T(8,128)(2,1)S(1)}, u32[]{:S(2)}, u32[]{:S(2)}) collective-permute-start(bf16[256,2048]{1,0:T(8,128)(2,1)S(1)} %get-tuple-element.484.refs_0_), channel_id=1, source_target_pairs={{0,8},{8,0},{1,9},{9,1},{2,10},{10,2},{3,11},{11,3},{4,12},{12,4},... | collective-permute-start | bytes 3145736 | tf_op jit(solution)/shard_map/ppermute | solution.py:46
  286.5 28.0 %collective-permute-start.53 = (bf16[256,2048]{1,0:T(8,128)(2,1)S(1)}, bf16[256,2048]{1,0:T(8,128)(2,1)S(1)}, u32[]{:S(2)}, u32[]{:S(2)}) collective-permute-start(bf16[256,2048]{1,0:T(8,128)(2,1)S(1)} %collective-permute-done.48.refs_0_.refs_2_), channel_id=1, source_target_pairs={{0,2},{2,0},{1,3},{3,1},{4,6},{6,4},{5,7},{7,5},{8,10},{10,8},{9,1... | collective-permute-start | bytes 3145736 | tf_op jit(solution)/shard_map/ppermute | solution.py:46
  286.5 28.1 %collective-permute-start.54 = (bf16[256,2048]{1,0:T(8,128)(2,1)S(1)}, bf16[256,2048]{1,0:T(8,128)(2,1)S(1)}, u32[]{:S(2)}, u32[]{:S(2)}) collective-permute-start(bf16[256,2048]{1,0:T(8,128)(2,1)S(1)} %collective-permute-done.47.refs_0_.refs_4_), channel_id=1, source_target_pairs={{0,2},{2,0},{1,3},{3,1},{4,6},{6,4},{5,7},{7,5},{8,10},{10,8},{9,1... | collective-permute-start | bytes 3145736 | tf_op jit(solution)/shard_map/ppermute | solution.py:46
  287.0 31.1 %collective-permute-start.57 = (bf16[256,2048]{1,0:T(8,128)(2,1)}, bf16[256,2048]{1,0:T(8,128)(2,1)S(1)}, u32[]{:S(2)}, u32[]{:S(2)}) collective-permute-start(bf16[256,2048]{1,0:T(8,128)(2,1)} %collective-permute-done.26.refs_2_), channel_id=1, source_target_pairs={{0,2},{2,0},{1,3},{3,1},{4,6},{6,4},{5,7},{7,5},{8,10},{10,8},{9,1... | collective-permute-start | bytes 3145736 | tf_op jit(solution)/shard_map/ppermute | solution.py:46
  287.0 31.9 %collective-permute-start.58 = (bf16[256,2048]{1,0:T(8,128)(2,1)S(1)}, bf16[256,2048]{1,0:T(8,128)(2,1)S(1)}, u32[]{:S(2)}, u32[]{:S(2)}) collective-permute-start(bf16[256,2048]{1,0:T(8,128)(2,1)S(1)} %collective-permute-done.25.refs_2_.refs_4_), channel_id=1, source_target_pairs={{0,2},{2,0},{1,3},{3,1},{4,6},{6,4},{5,7},{7,5},{8,10},{10,8},{9,1... | collective-permute-start | bytes 3145736 | tf_op jit(solution)/shard_map/ppermute | solution.py:46
  377.6 37.0 %collective-permute-start.69 = (bf16[128,2048]{1,0:T(8,128)(2,1)}, bf16[128,2048]{1,0:T(8,128)(2,1)S(1)}, u32[]{:S(2)}, u32[]{:S(2)}) collective-permute-start(bf16[128,2048]{1,0:T(8,128)(2,1)} %add_convert_fusion.19), channel_id=1, source_target_pairs={{0,4},{4,0},{1,5},{5,1},{2,6},{6,2},{3,7},{7,3},{8,12},{12,8},{9,1... | collective-permute-start | bytes 1572872 | tf_op jit(solution)/shard_map/ppermute | solution.py:46
  380.0 34.6 %collective-permute-start.68 = (bf16[128,2048]{1,0:T(8,128)(2,1)}, bf16[128,2048]{1,0:T(8,128)(2,1)S(1)}, u32[]{:S(2)}, u32[]{:S(2)}) collective-permute-start(bf16[128,2048]{1,0:T(8,128)(2,1)} %add_convert_fusion.20), channel_id=1, source_target_pairs={{0,8},{8,0},{1,9},{9,1},{2,10},{10,2},{3,11},{11,3},{4,12},{12,4},... | collective-permute-start | bytes 1572872 | tf_op jit(solution)/shard_map/ppermute | solution.py:46
  418.0 54.3 %collective-permute-start.73 = (bf16[128,2048]{1,0:T(8,128)(2,1)}, bf16[128,2048]{1,0:T(8,128)(2,1)S(1)}, u32[]{:S(2)}, u32[]{:S(2)}) collective-permute-start(bf16[128,2048]{1,0:T(8,128)(2,1)} %get-tuple-element.797), channel_id=1, source_target_pairs={{0,4},{4,0},{1,5},{5,1},{2,6},{6,2},{3,7},{7,3},{8,12},{12,8},{9,1... | collective-permute-start | bytes 1572872 | tf_op jit(solution)/shard_map/ppermute | solution.py:46
  420.0 28.2 %collective-permute-start.72 = (bf16[4,704,128]{2,1,0:T(8,128)(2,1)}, bf16[4,704,128]{2,1,0:T(8,128)(2,1)}, u32[]{:S(2)}, u32[]{:S(2)}) collective-permute-start(bf16[4,704,128]{2,1,0:T(8,128)(2,1)} %get-tuple-element.806), channel_id=1, source_target_pairs={{0,1},{1,0},{2,3},{3,2},{4,5},{5,4},{6,7},{7,6},{8,9},{9,8},{10,11... | collective-permute-start | bytes 2162696 | tf_op jit(solution)/shard_map/ppermute | solution.py:46
  424.0 48.3 %collective-permute-start.74 = (bf16[128,2048]{1,0:T(8,128)(2,1)}, bf16[128,2048]{1,0:T(8,128)(2,1)S(1)}, u32[]{:S(2)}, u32[]{:S(2)}) collective-permute-start(bf16[128,2048]{1,0:T(8,128)(2,1)} %get-tuple-element.795), channel_id=1, source_target_pairs={{0,8},{8,0},{1,9},{9,1},{2,10},{10,2},{3,11},{11,3},{4,12},{12,4},... | collective-permute-start | bytes 1572872 | tf_op jit(solution)/shard_map/ppermute | solution.py:46
  443.1 30.1 %collective-permute-start.75 = (bf16[4,704,128]{2,1,0:T(8,128)(2,1)}, bf16[4,704,128]{2,1,0:T(8,128)(2,1)S(1)}, u32[]{:S(2)}, u32[]{:S(2)}) collective-permute-start(bf16[4,704,128]{2,1,0:T(8,128)(2,1)} %get-tuple-element.805), channel_id=1, source_target_pairs={{0,1},{1,0},{2,3},{3,2},{4,5},{5,4},{6,7},{7,6},{8,9},{9,8},{10,11... | collective-permute-start | bytes 2162696 | tf_op jit(solution)/shard_map/ppermute | solution.py:46
  477.1 25.2 %collective-permute-start.78 = (bf16[256,2048]{1,0:T(8,128)(2,1)S(1)}, bf16[256,2048]{1,0:T(8,128)(2,1)S(1)}, u32[]{:S(2)}, u32[]{:S(2)}) collective-permute-start(bf16[256,2048]{1,0:T(8,128)(2,1)S(1)} %get-tuple-element.656.refs_0_), channel_id=1, source_target_pairs={{0,4},{4,0},{1,5},{5,1},{2,6},{6,2},{3,7},{7,3},{8,12},{12,8},{9,1... | collective-permute-start | bytes 3145736 | tf_op jit(solution)/shard_map/ppermute | solution.py:46
  479.3 32.3 %collective-permute-start.77 = (bf16[256,2048]{1,0:T(8,128)(2,1)S(1)}, bf16[256,2048]{1,0:T(8,128)(2,1)S(1)}, u32[]{:S(2)}, u32[]{:S(2)}) collective-permute-start(bf16[256,2048]{1,0:T(8,128)(2,1)S(1)} %get-tuple-element.656.refs_0_), channel_id=1, source_target_pairs={{0,8},{8,0},{1,9},{9,1},{2,10},{10,2},{3,11},{11,3},{4,12},{12,4},... | collective-permute-start | bytes 3145736 | tf_op jit(solution)/shard_map/ppermute | solution.py:46
  511.6 26.0 %collective-permute-start.84 = (bf16[256,2048]{1,0:T(8,128)(2,1)S(1)}, bf16[256,2048]{1,0:T(8,128)(2,1)S(1)}, u32[]{:S(2)}, u32[]{:S(2)}) collective-permute-start(bf16[256,2048]{1,0:T(8,128)(2,1)S(1)} %collective-permute-done.78.refs_2_), channel_id=1, source_target_pairs={{0,2},{2,0},{1,3},{3,1},{4,6},{6,4},{5,7},{7,5},{8,10},{10,8},{9,1... | collective-permute-start | bytes 3145736 | tf_op jit(solution)/shard_map/ppermute | solution.py:46
  512.6 25.0 %collective-permute-start.85 = (bf16[256,2048]{1,0:T(8,128)(2,1)S(1)}, bf16[256,2048]{1,0:T(8,128)(2,1)S(1)}, u32[]{:S(2)}, u32[]{:S(2)}) collective-permute-start(bf16[256,2048]{1,0:T(8,128)(2,1)S(1)} %collective-permute-done.77.refs_4_), channel_id=1, source_target_pairs={{0,2},{2,0},{1,3},{3,1},{4,6},{6,4},{5,7},{7,5},{8,10},{10,8},{9,1... | collective-permute-start | bytes 3145736 | tf_op jit(solution)/shard_map/ppermute | solution.py:46
  545.6 31.8 %collective-permute-start.103 = (bf16[176,2048]{1,0:T(8,128)(2,1)S(1)}, bf16[176,2048]{1,0:T(8,128)(2,1)S(1)}, u32[]{:S(2)}, u32[]{:S(2)}) collective-permute-start(bf16[176,2048]{1,0:T(8,128)(2,1)S(1)} %get-tuple-element.680), channel_id=1, source_target_pairs={{0,1},{1,0},{2,3},{3,2},{4,5},{5,4},{6,7},{7,6},{8,9},{9,8},{10,11... | collective-permute-start | bytes 2162696 | tf_op jit(solution)/shard_map/ppermute | solution.py:46
  584.4 42.6 %all-to-all-start.2 = ((bf16[8,704,128]{2,1,0:T(8,128)(2,1)}), bf16[8,704,128]{2,1,0:T(8,128)(2,1)}, u32[]{:S(2)}, u32[]{:S(2)}) async-start(bf16[8,704,128]{2,1,0:T(8,128)(2,1)} %shard_map.237), calls=%async_computation.2 | async-start | bytes 2883584 | tf_op jit(solution)/shard_map/all_to_all | solution.py:210
  592.1 34.9 %collective-permute-start.105 = (bf16[96,2048]{1,0:T(8,128)(2,1)S(1)}, bf16[96,2048]{1,0:T(8,128)(2,1)S(1)}, u32[]{:S(2)}, u32[]{:S(2)}) collective-permute-start(bf16[96,2048]{1,0:T(8,128)(2,1)S(1)} %slice.256), channel_id=1, source_target_pairs={{0,16},{16,0},{1,17},{17,1},{2,18},{18,2},{3,19},{19,3},{4,20},{20... | collective-permute-start | bytes 1179656 | tf_op jit(solution)/shard_map/ppermute | solution.py:46
  679.8 38.8 %collective-permute-start.99 = (bf16[128,2048]{1,0:T(8,128)(2,1)}, bf16[128,2048]{1,0:T(8,128)(2,1)}, u32[]{:S(2)}, u32[]{:S(2)}) collective-permute-start(bf16[128,2048]{1,0:T(8,128)(2,1)} %get-tuple-element.794), channel_id=1, source_target_pairs={{0,4},{4,0},{1,5},{5,1},{2,6},{6,2},{3,7},{7,3},{8,12},{12,8},{9,1... | collective-permute-start | bytes 1572872 | tf_op jit(solution)/shard_map/ppermute | solution.py:46
  681.1 37.5 %collective-permute-start.104 = (bf16[128,2048]{1,0:T(8,128)(2,1)}, bf16[128,2048]{1,0:T(8,128)(2,1)}, u32[]{:S(2)}, u32[]{:S(2)}) collective-permute-start(bf16[128,2048]{1,0:T(8,128)(2,1)} %get-tuple-element.791), channel_id=1, source_target_pairs={{0,8},{8,0},{1,9},{9,1},{2,10},{10,2},{3,11},{11,3},{4,12},{12,4},... | collective-permute-start | bytes 1572872 | tf_op jit(solution)/shard_map/ppermute | solution.py:46
  684.1 27.7 %collective-permute-start.117 = (bf16[128,2048]{1,0:T(8,128)(2,1)S(1)}, bf16[128,2048]{1,0:T(8,128)(2,1)S(1)}, u32[]{:S(2)}, u32[]{:S(2)}) collective-permute-start(bf16[128,2048]{1,0:T(8,128)(2,1)S(1)} %get-tuple-element.788), channel_id=1, source_target_pairs={{0,8},{8,0},{1,9},{9,1},{2,10},{10,2},{3,11},{11,3},{4,12},{12,4},... | collective-permute-start | bytes 1572872 | tf_op jit(solution)/shard_map/ppermute | solution.py:46
  684.9 27.7 %collective-permute-start.116 = (bf16[128,2048]{1,0:T(8,128)(2,1)S(1)}, bf16[128,2048]{1,0:T(8,128)(2,1)S(1)}, u32[]{:S(2)}, u32[]{:S(2)}) collective-permute-start(bf16[128,2048]{1,0:T(8,128)(2,1)S(1)} %get-tuple-element.790), channel_id=1, source_target_pairs={{0,4},{4,0},{1,5},{5,1},{2,6},{6,2},{3,7},{7,3},{8,12},{12,8},{9,1... | collective-permute-start | bytes 1572872 | tf_op jit(solution)/shard_map/ppermute | solution.py:46
  685.6 27.8 %collective-permute-start.122 = (bf16[8,160,128]{2,1,0:T(8,128)(2,1)S(1)}, bf16[8,160,128]{2,1,0:T(8,128)(2,1)S(1)}, u32[]{:S(2)}, u32[]{:S(2)}) collective-permute-start(bf16[8,160,128]{2,1,0:T(8,128)(2,1)S(1)} %add_convert_fusion.27), channel_id=1, source_target_pairs={{0,16},{16,0},{1,17},{17,1},{2,18},{18,2},{3,19},{19,3},{4,20},{20... | collective-permute-start | bytes 983048 | tf_op jit(solution)/shard_map/ppermute | solution.py:46
  714.3 35.8 %all-to-all-start.3 = ((bf16[8,160,128]{2,1,0:T(8,128)(2,1)}), bf16[8,160,128]{2,1,0:T(8,128)(2,1)}, u32[]{:S(2)}, u32[]{:S(2)}) async-start(bf16[8,160,128]{2,1,0:T(8,128)(2,1)} %shard_map.243), calls=%async_computation.3 | async-start | bytes 655360 | tf_op jit(solution)/shard_map/all_to_all | solution.py:210
  (299 other events, 3055.5 us)

commit v3 on v2

v3 whole, which is shorter than its diff:
```python
import functools

import jax
import jax.numpy as jnp
import numpy as np
from jax import lax
from jax.experimental import pallas as pl
from jax.experimental.pallas import tpu as pltpu
from jax.sharding import Mesh
from jax.sharding import PartitionSpec as P

H = 16
FD = 16
DV = 128
HP = 2
ROWS = DV + 2 * FD
WIDE = 384
QK = 2 * DV
LANE_R, LANE_ONE = 64, 65
FEAT = 256
SENT = 160
SEQS = 4
TP = ("l", "y", "c")
DP = ("h", "x")
EPS = 1e-5
F32, BF16 = jnp.float32, jnp.bfloat16


def dot(a, b, dims):
    return lax.dot_general(a, b, (dims, ((), ())), preferred_element_type=F32)


def mm(a, b):
    return dot(a, b, ((1,), (0,)))


def mm_nt(a, b):
    return dot(a, b, ((1,), (1,)))


def mm_tn(a, b):
    return dot(a, b, ((0,), (0,)))


def swap(a, axis):
    return lax.ppermute(a, axis, [(0, 1), (1, 0)])


class Order:
    def __init__(self, mark):
        self.mark = mark

    def at(self, *values):
        flat, tree = jax.tree.flatten(values)
        got = lax.optimization_barrier((self.mark, *flat))
        self.mark = got[0]
        return jax.tree.unflatten(tree, got[1:])


SLOTS = ((0, 0, 256), (1, 0, 256), (2, 0, 256), (3, 0, 256), (4, 0, 256), (5, 0, 256))
SLOTS += ((6, 0, 128), (6, 128, 128), (7, 0, 128), (7, 128, 128))


def near_tokens(own, a):
    return [own, swap(own, a), swap(own, "y"), swap(own, "c")]


def chips_near(own, a):
    return [own, swap(own, a), swap(own, "y"), None]


def chip_far(near, a):
    _, from_a, from_y, _ = near
    half = from_a.shape[0] // 2
    return [swap(from_y[:half], a), swap(from_a[half:], "y")]


def cores_of(near):
    return [swap(near[2], "c"), swap(near[1], "c")]


def far_tokens(near, a):
    return chip_far(near, a) + cores_of(near)


def last_tokens(far):
    return [swap(far[0], "c"), swap(far[1], "c")]


def in_slots(near, far, last):
    return [near[0], near[3], near[2], far[2], near[1], far[3], far[0], far[1], *last]


def far_cores(p):
    return [swap(p[8], "c"), swap(p[9], "c")]


def near_cores(p):
    return [swap(p[1], "c"), swap(p[3], "c"), swap(p[5], "c")]


def plus(*terms):
    return functools.reduce(jnp.add, [t.astype(F32) for t in terms]).astype(BF16)


def send_far(p, fars, a):
    return [swap(plus(p[6], fars[0]), a), swap(plus(p[7], fars[1]), "y")]


def send_first(p, nears, a):
    half = p[6].shape[0]
    return [swap(plus(p[2][half:], nears[1][half:]), "y"), swap(plus(p[4][:half], nears[2][:half]), a)]


def send_second(p, nears, via, a):
    half = p[6].shape[0]
    y_a = plus(p[2][:half], nears[1][:half], via[0])
    a_b = plus(p[4][half:], nears[2][half:], via[1])
    return [swap(y_a, "y"), swap(a_b, a)]


def terms(p, nears, first, second):
    return [p[0], nears[0], second[0], first[1], first[0], second[1]]


def over_both(a):
    full = lax.all_gather(a, DP)
    return full.reshape((lax.axis_size("h"), lax.axis_size("x")) + a.shape)


def sum_both(parts):
    flat = parts.reshape((-1,) + parts.shape[2:])
    return lax.psum_scatter(flat, DP, scatter_dimension=0, tiled=False).astype(F32)


def sub_head():
    return lax.axis_size(DP + TP) // H == 2 * lax.axis_size("x")


def split_heads(w, width):
    rows = w.shape[0]
    w = w.T
    if sub_head():
        w = w.reshape(2, HP, 2, 2, width, rows).transpose(2, 3, 0, 1, 4, 5)
    else:
        w = w.reshape(HP, 8, width, rows).transpose(1, 0, 2, 3)
    return w.reshape(8, HP, width, rows)


def join_heads(w, width):
    rows = w.shape[-1]
    if sub_head():
        w = w.reshape(2, 2, 2, HP, width, rows).transpose(2, 3, 0, 1, 4, 5)
    else:
        w = w.transpose(1, 0, 2, 3)
    return w.reshape(H * width, rows).T


def split_hidden(first, second):
    h, x = lax.axis_size("h"), lax.axis_size("x")
    w = jnp.concatenate([first, second], 0).T
    cols = w.shape[1]
    return w.reshape(h, 8, x, -1, cols).transpose(1, 0, 2, 3, 4).reshape(8, -1, cols)


def join_hidden(w):
    h, x = lax.axis_size("h"), lax.axis_size("x")
    cols = w.shape[-1]
    w = w.reshape(8, h, x, -1, cols).transpose(1, 0, 2, 3, 4).reshape(-1, cols).T
    return w[: cols // 2], w[cols // 2 :]


LAYOUT_HEADS = ((0, 0, 0, DV), (1, 0, DV, DV), (0, DV, QK, FD), (1, DV, QK + FD, FD))
LAYOUT_HEADS += ((0, DV + FD, QK + 2 * FD, FD), (1, DV + FD, QK + 3 * FD, FD))


def layout_hidden(n):
    return ((0, 0, 0, n), (1, 0, n, n))


def slabs_to_rows(full, layout, height):
    h, x, _, n, cols = full.shape
    pair = full.reshape(h, x, 8, n, 2, cols // 2).transpose(4, 3, 0, 2, 1, 5).reshape(2, n, -1)
    rows = [pair[m, src : src + count] for m, src, _, count in layout]
    have = sum(count for *_, count in layout)
    return jnp.concatenate(rows + [jnp.zeros((height - have, pair.shape[2]), BF16)], 0)


def rows_to_slabs(rows, layout):
    h, x = lax.axis_size("h"), lax.axis_size("x")
    pair = [jnp.concatenate([rows[dst : dst + c] for m, _, dst, c in layout if m == k], 0) for k in (0, 1)]
    n = pair[0].shape[0]
    parts = jnp.stack(pair).reshape(2, n, h, 8, x, -1).transpose(2, 4, 3, 1, 0, 5)
    return parts.reshape(h, x, 8, n, -1)


def exchange(slabs, axes):
    return lax.all_to_all(slabs, axes, 0, 0, tiled=True)


def out_rows_in(full):
    if sub_head():
        h, x, rows, d = full.shape
        full = lax.all_to_all(full.reshape(2, h // 2, x, rows, d), "c", 0, 0, tiled=True)
        full = full.transpose(1, 0, 2, 3, 4)
    return full.reshape(HP * DV, -1)


def out_rows_out(grad):
    h, x = lax.axis_size("h"), lax.axis_size("x")
    d = grad.shape[1]
    if sub_head():
        grad = grad.reshape(HP, 2, x, -1, d).transpose(1, 0, 2, 3, 4)
        grad = lax.all_to_all(grad, "c", 0, 0, tiled=True)
    return grad.reshape(h, x, -1, d)


def turn(a, k):
    return lax.ppermute(a, "z", [(i, (i + k) % 4) for i in range(4)])


def ring(a):
    return [a] + [turn(a, k) for k in (1, 2, 3)]


def ring_sum(pieces):
    return [pieces[0]] + [turn(pieces[k], k) for k in (1, 2, 3)]


def line_gather(a):
    return lax.all_gather(a, "z")


def line_sum(parts):
    return lax.psum_scatter(parts, "z", scatter_dimension=0, tiled=False)


def entering(total, reverse):
    n = lax.axis_size("h")
    got = jnp.zeros_like(total)
    for s in range(1, n):
        route = [(i + s, i) if reverse else (i, i + s) for i in range(n - s)]
        came = lax.ppermute(total, "h", route)
        got = came if s == 1 else (got.astype(F32) + came.astype(F32)).astype(BF16)
    return got


def entering_line(total, reverse):
    return [turn(total, -k if reverse else k) for k in (1, 2, 3)]


def feature_maps():
    maps = np.zeros((4, 2, 128, FEAT), np.float32)
    for kind in range(4):
        where = [kind * FD + i for i in range(FD)] + [LANE_ONE]
        size = [0.5] * FD + [1.0]
        col = 0
        for i in range(FD + 1):
            for j in range(i, FD + 1):
                maps[kind, 0, where[i], col] = size[i]
                maps[kind, 1, where[j], col] = size[j] * (0.5 if kind >= 2 and i == j < FD else 1.0)
                col += 1
    return maps


MAPS = feature_maps()


def lanes(shape):
    return lax.broadcasted_iota(jnp.int32, shape, len(shape) - 1)


def where_is(info, groups, p):
    each = 8 // groups
    g = p // each if groups > 1 else 0
    return g, info[1] + (p - g * each) * 256


def lengths_of(info, g):
    return [info[4 + SEQS * g + i] for i in range(SEQS)]


def segments(info, g, places):
    end, found = 0, jnp.zeros(places.shape, jnp.int32)
    for length in lengths_of(info, g):
        end = end + length
        found = found + (places >= end).astype(jnp.int32)
    return found


def crossing(info, g, base):
    lengths = lengths_of(info, g)
    start, end, best, total = 0, lengths[0], lengths[0], lengths[0]
    for length in lengths[1:]:
        more = length > best
        start = jnp.where(more, total, start)
        total = total + length
        end = jnp.where(more, total, end)
        best = jnp.where(more, length, best)
    places = base + lax.broadcasted_iota(jnp.int32, (256, 1), 0)
    return ((places >= start) & (places < end)).astype(F32)


def pair_mask(info, g, base):
    row = lax.broadcasted_iota(jnp.int32, (256, 256), 0)
    col = lax.broadcasted_iota(jnp.int32, (256, 256), 1)
    down = segments(info, g, base + lax.broadcasted_iota(jnp.int32, (256, 1), 0))
    across = segments(info, g, base + lax.broadcasted_iota(jnp.int32, (1, 256), 1))
    return ((down == across) & (row >= col)).astype(F32)


def to_send(total):
    row = total[:, DV:].T[:1]
    at = lax.broadcasted_iota(jnp.int32, (SENT, DV), 0)
    return jnp.where(at == 156, row[:, :DV], jnp.where(at == 157, row[:, DV:], total[:SENT, :DV]))


def from_sent(sent):
    at = lax.broadcasted_iota(jnp.int32, (SENT, DV), 0)
    state = jnp.concatenate([jnp.where(at < 153, sent, 0.0), jnp.zeros((FEAT - SENT, DV), F32)], 0)
    row = jnp.concatenate([sent[156:157], sent[157:158]], 1)
    den = jnp.broadcast_to(row, (DV, FEAT)).T
    return jnp.concatenate([state, jnp.where(lanes((FEAT, DV)) == 0, den, 0.0)], 1)


def send_sums(sums, state_ref, groups, before):
    for g in range(groups):
        for h in range(HP):
            total = to_send(sums[g, h])
            if before is not None:
                total = total + before[g, h].astype(F32)
            state_ref[g, h] = total.astype(BF16)


def start_sums(info, sums, enter, groups, reverse):
    count = enter.shape[0] // groups
    for g in range(groups):
        for h in range(HP):
            came = 0.0
            for i in range(count):
                there = (info[2] + i + 1 <= 3 if reverse else info[2] - i - 1 >= 0) if count > 1 else True
                came = came + jnp.where(there, enter[i * groups + g, h].astype(F32), 0.0)
            sums[g, h] = from_sent(came)


def maps_of(tile, maps, kind):
    return mm(tile, maps[kind, 0]), mm(tile, maps[kind, 1])


def feats_t(tile, maps_t, kind):
    return (mm_nt(maps_t[kind, 0], tile) * mm_nt(maps_t[kind, 1], tile)).astype(BF16)


def feats(tile, maps, kind):
    a, b = maps_of(tile, maps, kind)
    return (a * b).astype(BF16)


def with_ones(values):
    one = (lanes((256, 128)) == 0).astype(BF16)
    return jnp.concatenate([values, one], 1)


def head_mask(h):
    at = lanes((256, 128))
    return ((at >= h * FD) & (at < (h + 1) * FD)).astype(F32)


def keys_on_queries(tile):
    return pltpu.roll(tile, 128 - HP * FD, 1)


def store(refs, r, value):
    if r < 6:
        refs[r][...] = value
        refs[r].leave()
    else:
        for i in range(2):
            refs[2 * r - 6 + i][...] = value[i * 128 : (i + 1) * 128]
            refs[2 * r - 6 + i].leave()


NEAR, FAR = tuple(range(6)), (6, 7)


def project_kernel(groups, slots, info, w, xs, maps_t, *refs):
    before = refs[0] if len(refs) == 5 else None
    tile_ref, val_ref, state_ref, sums = refs[-4:]
    sums[...] = jnp.zeros_like(sums)
    at = lanes((256, 128))
    for i, r in enumerate(slots):
        g, base = where_is(info, groups, jnp.bitwise_xor(info[0], r))
        x = xs.rows(i * 256, 256)
        wide = x.astype(F32)
        scale = lax.rsqrt(jnp.mean(wide * wide, 1, keepdims=True) + EPS)
        y = mm_nt(x, w[...]) * scale
        values = y[:, :QK].astype(BF16)
        tile = jnp.where(at == LANE_R, scale, jnp.where(at == LANE_ONE, 1.0, y[:, QK:]))
        tile_ref[i] = tile
        val_ref[i] = values
        cross = crossing(info, g, base).astype(BF16)
        low = tile.astype(BF16)
        for h in range(HP):
            feat = feats_t(low, maps_t, 2 + h)
            sums[g, h] += mm(feat, with_ones(values[:, h * DV : (h + 1) * DV]) * cross)
    tile_ref.leave()
    val_ref.leave()
    send_sums(sums, state_ref, groups, before)


def attend_kernel(groups, info, tile_ref, val_ref, enter, maps, maps_t, w, *refs):
    mixed_ref, den_ref, before_ref = refs[:3]
    outs, sums = refs[3:13], refs[13]
    start_sums(info, sums, enter, groups, False)
    for arrival in (tile_ref, val_ref, maps, maps_t):
        arrival.ready()

    def step(p, carry):
        r = jnp.bitwise_xor(info[0], p)
        tile = tile_ref[r]
        low = tile.astype(BF16)
        keys = keys_on_queries(tile).astype(BF16)
        g, base = where_is(info, groups, p)
        cross = crossing(info, g, base)
        cross_low = cross.astype(BF16)
        mask = pair_mask(info, g, base)
        den = jnp.zeros((256, 128), F32)
        for h in range(HP):
            flat = mm_nt((tile * (head_mask(h) * 0.25)).astype(BF16), keys)
            low_scores = ((1.0 + flat + 0.5 * flat * flat) * mask).astype(BF16)
            values = with_ones(val_ref[r, :, h * DV : (h + 1) * DV])
            state = sums[g, h].astype(BF16)
            before_ref[r, h] = state
            both = mm(low_scores, values) + cross * mm(feats(low, maps, h), state)
            here = both[:, DV : DV + 1]
            mixed_ref[r, :, h * DV : (h + 1) * DV] = (both[:, :DV] / here).astype(BF16)
            den = jnp.where(lanes((256, 128)) == h, here, den)
            sums[g, h] += mm(feats_t(low, maps_t, 2 + h), values * cross_low)
        den_ref[r] = den
        return carry

    lax.fori_loop(0, 8, step, 0, unroll=True)
    for out in refs[:3]:
        out.leave()
    for r in range(8):
        store(outs, r, mm(mixed_ref[r], w[...]).astype(BF16))


def back_state_kernel(groups, slots, info, w, tile_ref, den_ref, mixed_ref, maps_t, dbs, *refs):
    before = refs[0] if len(refs) == 5 else None
    d_num_ref, d_den_ref, state_ref, sums = refs[-4:]
    sums[...] = jnp.zeros_like(sums)
    at = lanes((256, 128))
    for i, r in enumerate(slots):
        g, base = where_is(info, groups, jnp.bitwise_xor(info[0], r))
        d_attn = mm_nt(dbs.rows(i * 256, 256), w[...])
        low = tile_ref[r].astype(BF16)
        cross = crossing(info, g, base).astype(BF16)
        den = den_ref[r]
        d_den = jnp.zeros((256, 128), F32)
        for h in range(HP):
            cols = slice(h * DV, (h + 1) * DV)
            inv = 1.0 / den[:, h : h + 1]
            d_num = (d_attn[:, cols] * inv).astype(BF16)
            d_num_ref[i, :, cols] = d_num
            total = -jnp.sum(d_attn[:, cols] * mixed_ref[r, :, cols].astype(F32), 1, keepdims=True) * inv
            d_den = jnp.where(at == h, total, d_den)
            grad = jnp.concatenate([d_num, jnp.where(at == 0, total, 0.0).astype(BF16)], 1)
            sums[g, h] += mm(feats_t(low, maps_t, h), grad * cross)
        d_den_ref[i] = d_den
    d_num_ref.leave()
    d_den_ref.leave()
    send_sums(sums, state_ref, groups, before)


def back_kernel(groups, info, tile_ref, val_ref, d_num_ref, d_den_ref, before_ref, enter, maps, w, *refs):
    e_ref, outs, sums = refs[0], refs[1:11], refs[11]
    start_sums(info, sums, enter, groups, True)
    for arrival in (tile_ref, val_ref, d_num_ref, d_den_ref, before_ref, maps):
        arrival.ready()
    at = lanes((256, 128))

    def through(d_feat, a, b, kind):
        return mm_nt((d_feat * b).astype(BF16), maps[kind, 0]) + mm_nt((d_feat * a).astype(BF16), maps[kind, 1])

    def step(i, carry):
        p = 7 - i
        r = jnp.bitwise_xor(info[0], p)
        tile = tile_ref[r]
        low = tile.astype(BF16)
        keys = keys_on_queries(tile)
        keys_low = keys.astype(BF16)
        g, base = where_is(info, groups, p)
        cross = crossing(info, g, base)
        cross_low = cross.astype(BF16)
        mask = pair_mask(info, g, base)
        d_tile = jnp.zeros((256, 128), F32)
        d_keys = jnp.zeros((256, 128), F32)
        scale = tile[:, LANE_R : LANE_R + 1]
        for h in range(HP):
            cols = slice(h * DV, (h + 1) * DV)
            here = head_mask(h)
            flat = mm_nt((tile * (here * 0.25)).astype(BF16), keys_low)
            low_scores = ((1.0 + flat + 0.5 * flat * flat) * mask).astype(BF16)
            values = val_ref[r, :, cols]
            d_num = d_num_ref[r, :, cols]
            d_den = d_den_ref[r][:, h : h + 1]
            back = sums[g, h].astype(BF16)
            d_flat = ((mm_nt(d_num, values) + d_den) * mask * (0.25 + 0.25 * flat)).astype(BF16)
            qa, qb = maps_of(low, maps, h)
            ka, kb = maps_of(low, maps, 2 + h)
            grad = jnp.concatenate([d_num, jnp.where(at == 0, d_den, 0.0).astype(BF16)], 1)
            d_feat_q = mm_nt(grad, before_ref[r, h]) * cross
            d_feat_k = mm_nt(with_ones(values), back) * cross
            d_tile += mm(d_flat, (keys * here).astype(BF16)) + through(d_feat_q, qa, qb, h)
            d_tile += through(d_feat_k, ka, kb, 2 + h)
            d_keys += mm_tn(d_flat, (tile * here).astype(BF16))
            d_val = mm_tn(low_scores, d_num) + cross * mm((ka * kb).astype(BF16), back[:, :DV])
            e_ref[r, :, cols] = (d_val * scale).astype(BF16)
            sums[g, h] += mm_tn((qa * qb).astype(BF16), grad * cross_low)
        d_tile = jnp.where(at < 2 * HP * FD, d_tile + pltpu.roll(d_keys, HP * FD, 1), 0.0)
        e_ref[r, :, QK:] = (d_tile * scale).astype(BF16)
        return carry

    lax.fori_loop(0, 8, step, 0)
    e_ref.leave()
    for r in range(8):
        store(outs, r, mm(e_ref[r], w[...]).astype(BF16))


def unpack_kernel(layout, turned_by, info, *refs):
    out = refs[-1]
    have = sum(count for *_, count in layout)
    if have < out.shape[0]:
        out[have:] = jnp.zeros((out.shape[0] - have, out.shape[1]), BF16)
    for k in range(4):
        z = jnp.bitwise_and(info[2] - k, 3) if turned_by else k
        for yc in range(4):
            first, second = (refs[k][yc], refs[k][4 + yc]) if turned_by else (refs[0][k, yc], refs[0][k, 4 + yc])
            pair = pack_tile(first, second)
            at = pl.multiple_of((z * 4 + yc) * 128, 128) if turned_by else (k * 4 + yc) * 128
            for m, src, dst, count in layout:
                out[dst : dst + count, pl.ds(at, 128)] = pair[m][src : src + count]


def sort_heads_kernel(info, halves, mine, other):
    halves.ready()
    for k in range(HP):
        mine[k] = halves[info[3] * 2 + k]
        other[k] = halves[(1 - info[3]) * 2 + k]


def join_halves_kernel(info, mine, other, out):
    for k in range(HP):
        out[pl.ds(pl.multiple_of(k * DV + info[3] * 64, 64), 64)] = mine[k]
        out[pl.ds(pl.multiple_of(k * DV + (1 - info[3]) * 64, 64), 64)] = other[k]


def by_step_kernel(info, mine, other, out):
    mine.ready(), other.ready()
    for k in range(4):
        z = jnp.bitwise_and(info[2] + k, 3)
        out[k] = lax.select(z // 2 == info[3], mine[z % 2], other[z % 2])


def total_kernel(groups, *refs):
    total, at = 0.0, 0
    for k in groups:
        term = [refs[at + c][...].astype(F32) for c in range(k)]
        total = total + (term[0] if k == 1 else jnp.concatenate(term, 0))
        at += k
    refs[-1][...] = total.astype(refs[-1].dtype)


def summed(pieces):
    total = pieces[0][...].astype(F32) + pieces[1][...].astype(F32)
    upper = pieces[2][...].astype(F32) + pieces[3][...].astype(F32)
    lower = pieces[4][...].astype(F32) + pieces[5][...].astype(F32)
    return total + jnp.concatenate([upper, lower], 0)


def scale_of(v):
    return lax.rsqrt(jnp.mean(v * v, 1, keepdims=True) + EPS)


def residual_kernel(x, *refs):
    resid = x[...].astype(F32) + summed(refs[:6])
    refs[6][...] = resid
    refs[7][...] = (resid * scale_of(resid)).astype(BF16)


def d_residual_kernel(dy, resid_ref, *refs):
    resid, d_n = resid_ref[...], summed(refs[:6])
    r = scale_of(resid)
    n = resid * r
    d = dy[...].astype(F32) + r * (d_n - n * jnp.mean(d_n * n, 1, keepdims=True))
    refs[6][...] = d
    refs[7][...] = d.astype(BF16)


def input_kernel(x_ref, d_resid, *refs):
    x, d_x = x_ref[...].astype(F32), summed(refs[:6])
    n = x * scale_of(x)
    refs[6][0] = d_resid[...] + d_x - n * jnp.mean(d_x * n, 1, keepdims=True)


def output_kernel(resid, *refs):
    refs[6][0] = resid[...] + summed(refs[:6])


def pack_tile(first, second):
    return [jnp.concatenate([first[:, c : c + 64], second[:, c : c + 64]], 1) for c in (0, 64)]


def over_blocks(info, left, rights, total):
    for r in range(8):
        more = mm_tn(left[r], rights.rows(r * 256, 256))
        total[...] = more if r == 0 else total[...] + more


def qkv_grads_kernel(info, e_ref, xs, out, total):
    over_blocks(info, e_ref, xs, total)
    if len(out.shape) == 2:
        out[...] = total[...].astype(BF16)
        return
    for k in range(4):
        z = jnp.bitwise_and(info[2] + k, 3)
        for yc in range(4):
            tile = total[:, pl.ds(pl.multiple_of((z * 4 + yc) * 128, 128), 128)].astype(BF16)
            pair = [
                jnp.concatenate([tile[dst : dst + c] for m, _, dst, c in LAYOUT_HEADS if m == i], 0) for i in (0, 1)
            ]
            out[k, yc], out[k, 4 + yc] = pack_tile(*pair)


def out_grads_kernel(info, mixed_ref, dbs, *refs):
    outs, total = refs[:-1], refs[-1]
    over_blocks(info, mixed_ref, dbs, total)
    if len(outs) == 1:
        outs[0][...] = total[...].astype(BF16)
        return
    for i in range(HP):
        for out, half in ((outs[0], info[3]), (outs[1], 1 - info[3])):
            out[i] = total[pl.ds(pl.multiple_of(i * DV + half * 64, 64), 64), :].astype(BF16)


def mlp_kernel(sizes, info, ns, w_gu, dys, wd, *refs):
    k = len(sizes)
    outs, dns, (hid_ref, dg_ref, du_ref) = refs[:k], refs[k : 2 * k], refs[2 * k :]
    ff, rows = wd.shape[0], 256
    starts = [sum(sizes[:i]) for i in range(len(sizes))]

    def put(refs, at, value):
        for ref, start, size in zip(refs, starts, sizes):
            if at <= start < at + rows:
                ref[...] = value[start - at : start - at + size]
                ref.leave()

    for at in range(0, sum(sizes), rows):
        n, dy = ns.rows(at, rows), dys.rows(at, rows)
        gate, up, d_hid = mm_nt(n, w_gu[:ff]), mm_nt(n, w_gu[ff:]), mm_nt(dy, wd[...])
        sig = 1.0 / (1.0 + jnp.exp(-gate))
        silu = gate * sig
        hid = (silu * up).astype(BF16)
        dg = (d_hid * up * sig * (1.0 + gate * (1.0 - sig))).astype(BF16)
        du = (d_hid * silu).astype(BF16)
        hid_ref[at : at + rows] = hid
        dg_ref[at : at + rows] = dg
        du_ref[at : at + rows] = du
        if at + rows == sum(sizes):
            for ref in (hid_ref, dg_ref, du_ref):
                ref.leave()
        put(dns, at, (mm(dg, w_gu[:ff]) + mm(du, w_gu[ff:])).astype(BF16))
        put(outs, at, mm(hid, wd[...]).astype(BF16))


def turn_over(left, scratch):
    for q in range(0, 2048, 512):
        scratch[:, q : q + 512] = left.rows(q, 512).T


def hidden_grads_kernel(info, dgs, dus, ns, out, dg_t, du_t):
    turn_over(dgs, dg_t)
    turn_over(dus, du_t)
    right = ns.ready()

    def step(i, carry):
        tile = right[:, pl.ds(pl.multiple_of(i * 256, 256), 256)]
        gate, up = mm(dg_t[...], tile).astype(BF16), mm(du_t[...], tile).astype(BF16)
        for j in range(2):
            cols = slice(j * 128, (j + 1) * 128)
            for x, slab in enumerate(pack_tile(gate[:, cols], up[:, cols])):
                out[(i // 2) * 8 + x * 4 + (i % 2) * 2 + j] = slab
        return carry

    lax.fori_loop(0, 8, step, 0)


def plain_grads_kernel(info, lefts, rights, out, left_t):
    turn_over(lefts, left_t)
    right = rights.ready()

    def step(i, carry):
        cols = pl.ds(pl.multiple_of(i * 256, 256), 256)
        out[:, cols] = mm(left_t[...], right[:, cols]).astype(BF16)
        return carry

    lax.fori_loop(0, out.shape[1] // 256, step, 0)


class Arriving:
    def __init__(self, parts, buf, sems, first):
        self.buf, self.shape, self.copies, row = buf, buf.shape, [], 0
        for i, part in enumerate(parts):
            rows = buf if len(parts) == 1 else buf.at[pl.ds(row, part.shape[0])]
            copy = pltpu.make_async_copy(part, rows, sems.at[first + i])
            copy.start()
            self.copies.append([row, part.shape[0], copy])
            row += part.shape[0]

    def ready(self, start=None, stop=None):
        for entry in list(self.copies):
            if start is None or (entry[0] < stop and start < entry[0] + entry[1]):
                entry[2].wait()
                self.copies.remove(entry)
        return self.buf

    def rows(self, start, count):
        return self.ready(start, start + count)[start : start + count]

    def __getitem__(self, at):
        return self.ready()[at]


class Leaving:
    def __init__(self, out, buf, sem):
        self.buf, self.shape, self.dtype = buf, buf.shape, buf.dtype
        self.copy, self.left = pltpu.make_async_copy(buf, out, sem), False

    def __getitem__(self, at):
        return self.buf[at]

    def __setitem__(self, at, value):
        self.buf[at] = value

    def leave(self):
        if not self.left:
            self.copy.start()
            self.left = True


def call(kernel, args, outs, scratch=(), flops=0, vmem=40):
    shapes = tuple(jax.ShapeDtypeStruct(s, t) for s, t in outs)
    flat = [a for arg in args for a in (arg if isinstance(arg, list) else [arg])]
    moved = sum(a.size * a.dtype.itemsize for a in flat) + sum(s.size * s.dtype.itemsize for s in shapes)
    groups = [arg if isinstance(arg, list) else [arg] for arg in args]
    large = [g for g in groups if g[0].dtype != jnp.int32]
    bufs = [pltpu.VMEM((sum(a.shape[0] for a in g),) + g[0].shape[1:], g[0].dtype) for g in large]
    n_in = sum(len(g) for g in large)

    def body(*refs):
        refs = list(refs)
        take = lambda n: [refs.pop(0) for _ in range(n)]
        ins, results, in_bufs, out_bufs = take(len(flat)), take(len(outs)), take(len(large)), take(len(outs))
        mine, (in_sems, out_sems) = take(len(scratch)), refs
        given, at, sem, buf = [], 0, 0, 0
        for g in groups:
            parts = ins[at : at + len(g)]
            at += len(g)
            if g[0].dtype == jnp.int32:
                given.append(parts[0])
                continue
            given.append(Arriving(parts, in_bufs[buf], in_sems, sem))
            sem, buf = sem + len(g), buf + 1
        going = [Leaving(r, b, out_sems.at[i]) for i, (r, b) in enumerate(zip(results, out_bufs))]
        kernel(*given, *going, *mine)
        for out in going:
            out.leave()
        for out in going:
            out.copy.wait()
        for arrival in given:
            if isinstance(arrival, Arriving):
                arrival.ready()

    return pl.pallas_call(
        body,
        out_shape=tuple(pltpu.HBM(s, t) for s, t in outs),
        in_specs=[pl.BlockSpec(memory_space=pltpu.SMEM if a.dtype == jnp.int32 else pltpu.HBM) for a in flat],
        out_specs=[pl.BlockSpec(memory_space=pltpu.HBM)] * len(outs),
        scratch_shapes=[
            *bufs,
            *[pltpu.VMEM(s, t) for s, t in outs],
            *scratch,
            pltpu.SemaphoreType.DMA((max(n_in, 1),)),
            pltpu.SemaphoreType.DMA((len(outs),)),
        ],
        compiler_params=pltpu.CompilerParams(vmem_limit_bytes=vmem << 20),
        cost_estimate=pl.CostEstimate(flops=flops, bytes_accessed=moved, transcendentals=0),
    )(*[a if a.dtype == jnp.int32 else pltpu.with_memory_space_constraint(a, pltpu.HBM) for a in flat])


def state_scratch(groups):
    return pltpu.VMEM((groups, HP, FEAT, 2 * DV), F32)


TOKENS = [((n, 2048), BF16) for _, _, n in SLOTS]


OWN, NEXT, LAST = slice(0, 2), slice(2, 6), slice(6, 10)


def mlp(info, ns, dys, w_gu, wd):
    ff, d = wd.shape
    sizes = [n.shape[0] for n in ns]
    blocks = [((n, d), BF16) for n in sizes]
    rows, k = sum(sizes), len(ns)
    got = call(
        functools.partial(mlp_kernel, sizes),
        [info, list(ns), w_gu, list(dys), wd],
        blocks + blocks + [((rows, ff), BF16)] * 3,
        flops=12 * rows * ff * d,
    )
    return got[:k], got[k : 2 * k], got[2 * k :]


def turned(ff):
    return pltpu.VMEM((ff, 2048), BF16)


def plain_grads(info, rights, lefts):
    ff, d = lefts[0].shape[1], rights[0].shape[1]
    shapes, flops = [((ff, d), BF16)], 2 * 2048 * ff * d
    return call(plain_grads_kernel, [info, list(lefts), list(rights)], shapes, [turned(ff)], flops, 32)[0]


def hidden_grads(info, ns, dgs, dus):
    ff, d = dgs[0].shape[1], ns[0].shape[1]
    args, shapes = [info, list(dgs), list(dus), list(ns)], [((d // 64, ff, 128), BF16)]
    got = call(hidden_grads_kernel, args, shapes, [turned(ff)] * 2, 4 * 2048 * ff * d, 36)[0]
    return got.reshape(4, 8, ff, 128)


def down_grads(info, dys, hids):
    return plain_grads(info, dys, hids).reshape(4, -1, dys[0].shape[1])


def gained(gain, w):
    return (gain * w.astype(F32)).astype(BF16)


def head_slabs(split, gain, w_query, w_key, w_value):
    parts = [split(gained(gain, w), n) for w, n in ((w_value, DV), (w_query, FD), (w_key, FD))]
    return jnp.concatenate(parts, 2).transpose(0, 2, 1, 3).reshape(8, ROWS, -1)


def project(groups, slots, info, xs, w_qkv, maps_t, before=None):
    size, d, n = 256, w_qkv.shape[1], len(slots)
    return call(
        functools.partial(project_kernel, groups, slots),
        [info, w_qkv, list(xs), maps_t] + ([] if before is None else [before]),
        [((n, size, 128), F32), ((n, size, QK), BF16), ((groups, HP, SENT, DV), BF16)],
        [state_scratch(groups)],
        flops=2 * n * size * d * WIDE,
    )


def attend(groups, info, tile, values, enter, maps, maps_t, w_out):
    size, d = 256, w_out.shape[1]
    got = call(
        functools.partial(attend_kernel, groups),
        [info, tile, values, enter, maps, maps_t, w_out],
        [((8, size, QK), BF16), ((8, size, 128), F32), ((8, HP, FEAT, 2 * DV), BF16)] + TOKENS,
        [state_scratch(groups)],
        flops=2 * 8 * size * d * QK,
    )
    return got[:3], got[3:]


def back_state(groups, slots, info, dbs, w_out, mixed, den, tile, maps_t, before=None):
    size, d, n = 256, w_out.shape[1], len(slots)
    return call(
        functools.partial(back_state_kernel, groups, slots),
        [info, w_out, tile, den, mixed, maps_t, list(dbs)] + ([] if before is None else [before]),
        [((n, size, QK), BF16), ((n, size, 128), F32), ((groups, HP, SENT, DV), BF16)],
        [state_scratch(groups)],
        flops=2 * n * size * d * QK,
    )


def back(groups, info, tile, values, d_num, d_den, before, later, maps, w_qkv):
    size, d = 256, w_qkv.shape[1]
    got = call(
        functools.partial(back_kernel, groups),
        [info, tile, values, d_num, d_den, before, later, maps, w_qkv],
        [((8, size, WIDE), BF16)] + TOKENS,
        [state_scratch(groups)],
        flops=2 * 8 * size * d * WIDE,
        vmem=28,
    )
    return got[0], got[1:]


def qkv_grads(info, xs, e, packed):
    d = xs[0].shape[1]
    outs = [((4, 8, ROWS, 128) if packed else (WIDE, d), BF16)]
    return call(qkv_grads_kernel, [info, e, list(xs)], outs, [pltpu.VMEM((WIDE, d), F32)], flops=2 * 2048 * d * WIDE)[0]


def out_grads(info, dbs, mixed, packed):
    d = dbs[0].shape[1]
    outs = [((HP, 64, d), BF16)] * 2 if packed else [((QK, d), BF16)]
    return call(out_grads_kernel, [info, mixed, list(dbs)], outs, [pltpu.VMEM((QK, d), F32)], flops=2 * 2048 * d * QK)


def unpack(info, pieces, layout, height):
    turned_by = len(pieces) > 1
    kernel = functools.partial(unpack_kernel, layout, turned_by)
    return call(kernel, [info, *pieces], [((height, 16 * 128), BF16)])[0]


def total(groups, shape, dtype):
    args = [c for g in groups for c in g]
    return call(functools.partial(total_kernel, [len(g) for g in groups]), args, [(shape, dtype)])[0]


def finish_residual(x, pieces):
    return call(residual_kernel, [x, *pieces], [(x.shape, F32), (x.shape, BF16)])


def finish_d_residual(dy, resid, pieces):
    return call(d_residual_kernel, [dy, resid, *pieces], [(dy.shape, F32), (dy.shape, BF16)])


def finish_input(x, d_resid, pieces):
    return call(input_kernel, [x, d_resid, *pieces], [((1,) + x.shape, F32)])[0]


def finish_output(resid, pieces):
    return call(output_kernel, [resid, *pieces], [((1,) + resid.shape, F32)])[0]


def gather_all(own, a):
    near = near_tokens(own, a)
    far = far_tokens(near, a)
    return in_slots(near, far, last_tokens(far))


def scatter_all(p, a):
    nears = near_cores(p)
    via = send_far(p, far_cores(p), a)
    return terms(p, nears, send_first(p, nears, a), send_second(p, nears, via, a))


def weight_grads(weights, gains, grads):
    g_query, g_key, g_value, g_gate, g_up = grads
    along = [jnp.sum(w.astype(F32) * g, -1) for w, g in zip(weights, grads)]
    one, two = along[0] + along[1] + along[2], along[3] + along[4]
    return one, gains[0] * g_query, gains[0] * g_key, gains[0] * g_value, two, gains[1] * g_gate, gains[1] * g_up


def split_of_heads(join, g_heads):
    g = g_heads.astype(F32).reshape(8, ROWS, HP, -1).transpose(0, 2, 1, 3)
    return join(g[:, :, DV : DV + FD], FD), join(g[:, :, DV + FD :], FD), join(g[:, :, :DV], DV)


def on_device(
    run, tokens, seq_lengths, norm_gain, w_query, w_key, w_value, w_out, mlp_gain, w_gate, w_up, w_down, cotangent
):
    gains = [g.astype(F32)[:, None] for g in (norm_gain, mlp_gain)]
    maps, maps_t = jnp.asarray(MAPS, BF16), jnp.asarray(MAPS.transpose(0, 1, 3, 2), BF16)
    weights = (w_query, w_key, w_value, w_gate, w_up)
    block_out, input_grad, grads, g_out, g_down = run(
        tokens[0], cotangent[0], seq_lengths, gains, weights, w_out, w_down, maps, maps_t
    )
    g = weight_grads(weights, gains, grads)
    return block_out, input_grad, *g[:4], g_out, *g[4:], g_down


def plain(x, dy, lengths, gains, weights, w_out, w_down, maps, maps_t):
    w_query, w_key, w_value, w_gate, w_up = weights
    place = jnp.stack([lax.axis_index(TP), lax.axis_index("h") * 8 * x.shape[0], 0, 0])
    info = jnp.concatenate([place.astype(jnp.int32), lengths[0]])
    heads = over_both(exchange(head_slabs(split_heads, gains[0], w_query, w_key, w_value), TP))
    w_qkv = slabs_to_rows(heads, LAYOUT_HEADS, WIDE)
    w_out_mine = out_rows_in(over_both(w_out))
    hid = over_both(exchange(split_hidden(gained(gains[1], w_gate), gained(gains[1], w_up)), TP))
    wd = over_both(w_down).reshape(-1, x.shape[1])
    ff = wd.shape[0]
    w_gu = slabs_to_rows(hid, layout_hidden(ff), 2 * ff)
    xs = gather_all(x, "l")
    tile, values, state = project(1, NEAR + FAR, info, xs, w_qkv, maps_t)
    (mixed, den, before), p = attend(1, info, tile, values, entering(state, False), maps, maps_t, w_out_mine)
    resid, n_low = finish_residual(x, scatter_all(p, "l"))
    ns, dys = gather_all(n_low, "l"), gather_all(dy, "l")
    ran = [mlp(info, ns[c], dys[c], w_gu, wd) for c in (OWN, NEXT, LAST)]
    hids, dgs, dus = [[r[2][i] for r in ran] for i in range(3)]
    block_out = finish_output(resid, scatter_all([b for r in ran for b in r[0]], "l"))
    d_resid, d_low = finish_d_residual(dy, resid, scatter_all([b for r in ran for b in r[1]], "l"))
    grads = jnp.concatenate([plain_grads(info, ns, dgs), plain_grads(info, ns, dus)], 0)
    g_hid = exchange(sum_both(rows_to_slabs(grads, layout_hidden(ff))).astype(BF16), TP)
    g_down = sum_both(plain_grads(info, dys, hids).reshape(*hid.shape[:2], -1, x.shape[1]))
    dbs = gather_all(d_low, "l")
    d_num, d_den, use = back_state(1, NEAR + FAR, info, dbs, w_out_mine, mixed, den, tile, maps_t)
    e, p = back(1, info, tile, values, d_num, d_den, before, entering(use, True), maps, w_qkv)
    input_grad = finish_input(x, d_resid, scatter_all(p, "l"))
    g_out = sum_both(out_rows_out(out_grads(info, dbs, mixed, False)[0]))
    g_heads = exchange(sum_both(rows_to_slabs(qkv_grads(info, xs, e, False), LAYOUT_HEADS)).astype(BF16), TP)
    grads = (*split_of_heads(join_heads, g_heads), *join_hidden(g_hid.astype(F32)))
    return block_out, input_grad, grads, g_out, g_down


EIGHT = ("x", "y", "c")


def split_heads_z(w, width):
    rows = w.shape[0]
    return w.T.reshape(2, HP, 4, width, rows).transpose(0, 2, 1, 3, 4).reshape(8, HP, width, rows)


def join_heads_z(w, width):
    rows = w.shape[-1]
    return w.reshape(2, 4, HP, width, rows).transpose(0, 2, 1, 3, 4).reshape(H * width, rows).T


def split_hidden_z(first, second):
    w = jnp.concatenate([first, second], 0).T.reshape(4, 4, 2, -1, 128)
    return w.transpose(2, 1, 0, 3, 4).reshape(8, -1, 128)


def join_hidden_z(w):
    w = w.reshape(2, 4, 4, -1, 128).transpose(2, 1, 0, 3, 4).reshape(-1, 128).T
    return w[:64], w[64:]


def scheduled(x, dy, lengths, gains, weights, w_out, w_down, maps, maps_t):
    w_query, w_key, w_value, w_gate, w_up = weights
    d_model = x.shape[1]
    z, my_x = lax.axis_index("z"), lax.axis_index("x")
    place = jnp.stack([lax.axis_index(EIGHT), z * 4 * x.shape[0], z, my_x]).astype(jnp.int32)
    o = Order(place)
    ax = "x"

    low = jnp.concatenate([lengths[0] % 256, lengths[0] // 256]).astype(BF16)
    low = jnp.broadcast_to(jnp.pad(low, (0, 120)), (8, 16, 128))
    heads = jnp.concatenate([head_slabs(split_heads_z, gains[0], w_query, w_key, w_value), low], 1)
    halves = line_gather(w_out)
    heads = exchange(heads, EIGHT)
    heads, x_sent, w_gate, w_up = o.at(heads, x, w_gate, w_up)
    near = chips_near(x_sent, ax)
    sent = heads[::4, ROWS, :8].astype(jnp.int32)
    info = jnp.concatenate([place, (sent[:, :4] + 256 * sent[:, 4:]).reshape(-1)])
    heads = ring(heads)
    hid = split_hidden_z(gained(gains[1], w_gate), gained(gains[1], w_up))
    heads, near, hid, x_sent, halves = o.at(heads, near, hid, x_sent, halves)
    cores = cores_of(near)
    near[3] = swap(x_sent, "c")
    wd = line_gather(w_down)
    w_qkv = unpack(info, heads, LAYOUT_HEADS, WIDE)
    near[3], cores, w_qkv = o.at(near[3], cores, w_qkv)
    far = chip_far(near, ax)
    xs = in_slots(near, far + cores, [None] * 2)
    one = project(2, NEAR, info, xs[:6], w_qkv, maps_t)
    one, far, hid = o.at(one, far, hid)
    last = last_tokens(far)
    hid = exchange(hid, EIGHT)
    w_out_near, w_out_far = call(sort_heads_kernel, [info, halves], [((HP, 64, d_model), BF16)] * 2)
    last, w_out_near, w_out_far = o.at(last, w_out_near, w_out_far)
    xs = in_slots(near, far + cores, last)

    two = project(2, FAR, info, xs[6:], w_qkv, maps_t, one[2])
    two, = o.at(two)
    tile, values = [one[0], two[0]], [one[1], two[1]]
    enter = entering_line(two[2], False)
    w_out_other = swap(w_out_far, "x")
    enter, w_out_other, wd, hid = o.at(enter, w_out_other, wd, hid)
    hid = line_gather(hid)
    w_out_mine = call(join_halves_kernel, [info, w_out_near, w_out_other], [((QK, d_model), BF16)])[0]
    (mixed, den, before), p = attend(2, info, tile, values, enter, maps, maps_t, w_out_mine)
    p, mixed, den, before = o.at(p, mixed, den, before)
    fars, nears = far_cores(p), near_cores(p)
    fars, nears = o.at(fars, nears)
    via = send_far(p, fars, ax)
    via, = o.at(via)
    first = send_first(p, nears, ax)
    first, = o.at(first)
    second = send_second(p, nears, via, ax)
    second, = o.at(second)
    resid, n_low = finish_residual(x, terms(p, nears, first, second))
    resid, n_low = o.at(resid, n_low)

    near = near_tokens(n_low, ax)
    dy_core = swap(dy, "c")
    near, dy_core = o.at(near, dy_core)
    far = chip_far(near, ax)
    wd = wd.reshape(-1, d_model)
    ff = wd.shape[0]
    w_gu = unpack(info, [hid], layout_hidden(ff), 2 * ff)
    ns, dys = in_slots(near, [None] * 4, [None] * 2), [dy, dy_core]
    run = lambda c: mlp(info, ns[c], dys[c], w_gu, wd)
    far, w_gu, dy, wd = o.at(far, w_gu, dy, wd)
    dy_near = chips_near(dy, ax)
    ran = [run(OWN)]
    cores = cores_of(near)
    ran, cores, dy_near = o.at(ran, cores, dy_near)
    dy_near[3] = dy_core
    dy_cores = cores_of(dy_near)
    last = last_tokens(far)
    dy_cores, last = o.at(dy_cores, last)
    dy_far = chip_far(dy_near, ax)
    ns, dys = in_slots(near, far + cores, last), in_slots(dy_near, dy_far + dy_cores, [None] * 2)
    ran.append(run(NEXT))
    ran, dy_far = o.at(ran, dy_far)
    dy_last = last_tokens(dy_far)
    dy_last, = o.at(dy_last)
    p = [b for r in ran for b in r[1]]
    nears = near_cores(p)
    ns, dys = in_slots(near, far + cores, last), in_slots(dy_near, dy_far + dy_cores, dy_last)
    ran.append(run(LAST))
    ran, nears = o.at(ran, nears)
    p = [b for r in ran for b in r[1]]
    outs = [b for r in ran for b in r[0]]
    parts = lambda i: [r[2][i] for r in ran]
    fars = far_cores(p)
    fars, outs = o.at(fars, outs)
    via = send_far(p, fars, ax)
    g_down = down_grads(info, dys, parts(0))
    via, g_down = o.at(via, g_down)
    g_down = line_sum(g_down)
    first = send_first(p, nears, ax)
    first, = o.at(first)
    second = send_second(p, nears, via, ax)
    second, = o.at(second)
    d_resid, d_low = finish_d_residual(dy, resid, terms(p, nears, first, second))
    d_resid, d_low = o.at(d_resid, d_low)

    near = near_tokens(d_low, ax)
    g_hid = hidden_grads(info, ns, parts(1), parts(2))
    near, g_hid = o.at(near, g_hid)
    cores = cores_of(near)
    cores, g_down, g_hid = o.at(cores, g_down, g_hid)
    g_hid = line_sum(g_hid)
    far = chip_far(near, ax)
    dbs = in_slots(near, far + cores, [None] * 2)
    one = back_state(2, NEAR, info, dbs[:6], w_out_mine, mixed, den, tile, maps_t)
    one, far = o.at(one, far)
    last = last_tokens(far)
    last, outs = o.at(last, outs)
    o_nears, o_fars = near_cores(outs), far_cores(outs)
    dbs = in_slots(near, far + cores, last)
    two = back_state(2, FAR, info, dbs[6:], w_out_mine, mixed, den, tile, maps_t, one[2])
    two, o_nears, o_fars = o.at(two, o_nears, o_fars)
    d_num, d_den = [one[0], two[0]], [one[1], two[1]]
    later = entering_line(two[2], True)
    out_near, out_far = out_grads(info, dbs, mixed, True)
    o_via = send_far(outs, o_fars, ax)
    later, out_far, o_via = o.at(later, out_far, o_via)
    out_other = swap(out_far, "x")
    o_first = send_first(outs, o_nears, ax)
    o_second = send_second(outs, o_nears, o_via, ax)
    e, p = back(2, info, tile, values, d_num, d_den, before, later, maps, w_qkv)
    e, p, out_other, o_first, o_second = o.at(e, p, out_other, o_first, o_second)
    steps = lambda a: [a[i] for i in range(4)]
    nears, fars = near_cores(p), far_cores(p)
    head_g = qkv_grads(info, xs, e, True)
    nears, fars, head_g = o.at(nears, fars, head_g)
    heads = ring_sum(steps(head_g))
    via = send_far(p, fars, ax)
    op = call(by_step_kernel, [info, out_near, out_other], [((4, 64, d_model), BF16)])[0]
    via, heads[1], heads[3], op, g_hid = o.at(via, heads[1], heads[3], op, g_hid)
    first = send_first(p, nears, ax)
    g_hid = exchange(g_hid, EIGHT)
    block_out = finish_output(resid, terms(outs, o_nears, o_first, o_second))
    first, heads[2], block_out = o.at(first, heads[2], block_out)
    second = send_second(p, nears, via, ax)
    g_heads = exchange(total([[a] for a in heads], heads[0].shape, BF16), EIGHT)
    op = ring_sum(steps(op))
    g_hid = join_hidden_z(g_hid.astype(F32))
    second, g_heads, g_hid = o.at(second, g_heads, g_hid)
    input_grad = finish_input(x, d_resid, terms(p, nears, first, second))
    g_out = total([[a] for a in op], w_out.shape, F32)
    grads = (*split_of_heads(join_heads_z, g_heads), *g_hid)
    return block_out, input_grad, grads, g_out, g_down.astype(F32)


def solution(mesh):
    seq, fsdp = mesh.shape["seq"], mesh.shape["fsdp"]
    if (seq, fsdp) == (16, 2):
        shape, along, run = (4, 2, 2, 2), ("z", "y", "c"), scheduled
    else:
        shape, along, run = (seq // 8, 2, 2, 2, fsdp), ("h", "l", "y", "c"), plain
    fine = Mesh(mesh.devices.reshape(shape), along + ("x",))
    token, vec, mat = P("x", along, None), P(along + ("x",)), P(along + ("x",), None)
    return jax.shard_map(
        functools.partial(on_device, run),
        mesh=fine,
        in_specs=(token, P("x", None), vec, mat, mat, mat, mat, vec, mat, mat, mat, token),
        out_specs=(token, token, vec, mat, mat, mat, mat, vec, mat, mat, mat),
        check_vma=False,
    )
```

time: 763 us -> 658 us (0.86)
  local copies, waits for them, and re-layouts: 134 us -> 35.3 us
  Pallas kernels: 170 us -> 235 us
  waiting for transfers between devices: 282 us -> 227 us
  starting transfers between devices: 137 us -> 103 us
  between operations: 2.85 us -> 15.7 us
    ppermute x122 -> x82, waiting for transfers between devices: 257 us -> 109 us  [swap(): return lax.ppermute(a, axis, [(0, 1), (1, 0)])]
    unnamed x447 -> x178, local copies, waits for them, and re-layouts: 120 us -> 20.1 us
    ppermute x2 -> x15, waiting for transfers between devices: 23.4 us -> 98.3 us  [turn(): return lax.ppermute(a, 'z', [(i, (i + k) % 4) for i in range(4)])]
    pallas_call x25 -> x24, Pallas kernels: 170 us -> 235 us  [call(): pl.pallas_call(body, out_shape=tuple((pltpu.HBM(s, t) for s, t in outs)),...]
    ppermute x122 -> x82, starting transfers between devices: 116 us -> 60.5 us  [swap(): return lax.ppermute(a, axis, [(0, 1), (1, 0)])]
    ppermute x2 -> x15, starting transfers between devices: 3.61 us -> 26 us  [turn(): return lax.ppermute(a, 'z', [(i, (i + k) % 4) for i in range(4)])]
    all_gather x0 -> x3, waiting for transfers between devices: none -> 8.65 us  [line_gather(): return lax.all_gather(a, 'z')]
    all_to_all x4, waiting for transfers between devices: 0.76 us -> 9.2 us  [exchange(): return lax.all_to_all(slabs, axes, 0, 0, tiled=True)]
  transfers between devices with their start and end apart: 128 -> 106, of which waited for: 46 -> 39; matrix products, arithmetic and copies ran while one was open for 6% -> 6% of each run, Pallas kernels for 22% -> 36%
where the time goes in v3:
time: 658 us; the launch traced here: 646 us
  Pallas kernels  235 us (36%)
  waiting for transfers between devices  227 us (34%)
  starting transfers between devices  103 us (16%)
  local copies, waits for them, and re-layouts  35.3 us (5%)
  other arithmetic  30.4 us (5%)
  between operations  15.7 us (2%)
    pallas_call x24, Pallas kernels, call(): pl.pallas_call(body, out_shape=tuple((pltpu.HBM(s, t) for s, t in outs)),...  235 us
    ppermute x82, waiting for transfers between devices, swap(): return lax.ppermute(a, axis, [(0, 1), (1, 0)])  109 us
    ppermute x15, waiting for transfers between devices, turn(): return lax.ppermute(a, 'z', [(i, (i + k) % 4) for i in range(4)])  98.3 us
    ppermute x82, starting transfers between devices, swap(): return lax.ppermute(a, axis, [(0, 1), (1, 0)])  60.5 us
    ppermute x15, starting transfers between devices, turn(): return lax.ppermute(a, 'z', [(i, (i + k) % 4) for i in range(4)])  26 us
    unnamed x178, local copies, waits for them, and re-layouts  20.1 us
    convert_element_type x16, other arithmetic, plus(): functools.reduce(jnp.add, [t.astype(F32) for t in terms]).astype(BF16)  16.7 us
    all_to_all x4, starting transfers between devices, exchange(): return lax.all_to_all(slabs, axes, 0, 0, tiled=True)  15.8 us
  transfers between devices with their start and end apart: 106, of which 39 were waited for; matrix products, arithmetic and copies ran while one was open for 6% of the time, Pallas kernels for 36%

profile of v3, /device:TPU:0, one launch (start us, length us, event | category | flops | bytes accessed | tf_op | source)
XLA Modules:
  0.0 646.1 jit_solution(12653542686073860947)
XLA Ops:
  13.4 5.2 all-to-all-start
  19.4 6.3 all-to-all-done.refs_1_
  38.5 8.2 %collective-permute-done.refs_2_ = bf16[8,176,128]{2,1,0:T(8,128)(2,1)} collective-permute-done((bf16[8,176,128]{2,1,0:T(8,128)(2,1)S(1)}, bf16[8,176,128]{2,1,0:T(8,128)(2,1)}, u32[]{:S(2)}, u32[]{:S(2)}) %collective-permute-start) | collective-permute-done | bytes 360480 | tf_op jit(solution)/shard_map/ppermute | solution.py:219
  46.6 17.2 %collective-permute-done.1.refs_3_ = bf16[8,176,128]{2,1,0:T(8,128)(2,1)} collective-permute-done((bf16[8,176,128]{2,1,0:T(8,128)(2,1)S(1)}, bf16[8,176,128]{2,1,0:T(8,128)(2,1)}, u32[]{:S(2)}, u32[]{:S(2)}) %collective-permute-start.1) | collective-permute-done | bytes 360480 | tf_op jit(solution)/shard_map/ppermute | solution.py:219
  70.0 3.4 shard_map.221.refs_1_.refs_14_
  73.5 11.7 %shard_map.222 = (f32[6,256,128]{2,1,0:T(8,128)}, bf16[6,256,256]{2,1,0:T(8,128)(2,1)}, bf16[2,2,160,128]{3,2,1,0:T(8,128)(2,1)}) custom-call(s32[12]{0:T(128)S(1)} %concatenate.20.refs_0_, bf16[384,2048]{1,0:T(8,128)(2,1)} %shard_map.221.refs_1_.refs_14_, bf16[256,2048]{1,0:T(8,128)(2,1)} %bitcast.18.refs_2_.refs_0_, ...), custom_call_target="tpu_custom_call" | custom-call | flops 2415919104 | bytes 10125360 | tf_op jit(solution)/shard_map/pallas_call | solution.py:785
  85.2 3.6 all-to-all-start.1
  94.4 6.0 shard_map.224
  100.5 8.0 %collective-permute-start.12 = (bf16[2,2,160,128]{3,2,1,0:T(8,128)(2,1)}, bf16[2,2,160,128]{3,2,1,0:T(8,128)(2,1)S(1)}, u32[]{:S(2)}, u32[]{:S(2)}) collective-permute-start(bf16[2,2,160,128]{3,2,1,0:T(8,128)(2,1)} %get-tuple-element.383), channel_id=1, source_target_pairs={{0,8},{8,16},{16,24},{24,0},{1,9},{9,17},{17,25},{25,1},{2,10},{10... | collective-permute-start | bytes 491528 | tf_op jit(solution)/shard_map/ppermute | solution.py:219
  111.0 7.1 %collective-permute-done.12.refs_5_ = bf16[2,2,160,128]{3,2,1,0:T(8,128)(2,1)S(1)} collective-permute-done((bf16[2,2,160,128]{3,2,1,0:T(8,128)(2,1)}, bf16[2,2,160,128]{3,2,1,0:T(8,128)(2,1)S(1)}, u32[]{:S(2)}, u32[]{:S(2)}) %collective-permute-start.12) | collective-permute-done | bytes 163872 | tf_op jit(solution)/shard_map/ppermute | solution.py:219
  118.1 11.6 %collective-permute-done.13.refs_6_ = bf16[2,2,160,128]{3,2,1,0:T(8,128)(2,1)S(1)} collective-permute-done((bf16[2,2,160,128]{3,2,1,0:T(8,128)(2,1)}, bf16[2,2,160,128]{3,2,1,0:T(8,128)(2,1)S(1)}, u32[]{:S(2)}, u32[]{:S(2)}) %collective-permute-start.13) | collective-permute-done | bytes 163872 | tf_op jit(solution)/shard_map/ppermute | solution.py:219
  135.7 13.7 %shard_map.226 = (bf16[8,256,256]{2,1,0:T(8,128)(2,1)}, f32[8,256,128]{2,1,0:T(8,128)}, bf16[8,2,256,256]{3,2,1,0:T(8,128)(2,1)}, bf16[256,2048]{1,0:T(8,128)(2,...) custom-call(s32[12]{0:T(128)S(1)} %concatenate.20.refs_0_, ...), custom_call_target="tpu_custom_call" | custom-call | flops 2147483648 | bytes 17268784 | tf_op jit(solution)/shard_map/pallas_call | solution.py:785
  150.5 5.5 collective-permute-done.16
  163.0 9.5 %collective-permute-done.21 = bf16[128,2048]{1,0:T(8,128)(2,1)S(1)} collective-permute-done((bf16[128,2048]{1,0:T(8,128)(2,1)S(1)}, bf16[128,2048]{1,0:T(8,128)(2,1)S(1)}, u32[]{:S(2)}, u32[]{:S(2)}) %collective-permute-start.21) | collective-permute-done | bytes 524320 | tf_op jit(solution)/shard_map/ppermute | solution.py:46
  180.4 10.3 %collective-permute-done.25.refs_3_ = bf16[128,2048]{1,0:T(8,128)(2,1)S(1)} collective-permute-done((bf16[128,2048]{1,0:T(8,128)(2,1)S(1)}, bf16[128,2048]{1,0:T(8,128)(2,1)S(1)}, u32[]{:S(2)}, u32[]{:S(2)}) %collective-permute-start.25) | collective-permute-done | bytes 524320 | tf_op jit(solution)/shard_map/ppermute | solution.py:46
  192.7 7.2 %collective-permute-done.23.refs_5_ = bf16[128,2048]{1,0:T(8,128)(2,1)S(1)} collective-permute-done((bf16[128,2048]{1,0:T(8,128)(2,1)S(1)}, bf16[128,2048]{1,0:T(8,128)(2,1)S(1)}, u32[]{:S(2)}, u32[]{:S(2)}) %collective-permute-start.23) | collective-permute-done | bytes 524320 | tf_op jit(solution)/shard_map/ppermute | solution.py:46
  202.5 5.0 shard_map.227
  208.4 22.4 %collective-permute-done.27.refs_3_.refs_11_ = bf16[256,2048]{1,0:T(8,128)(2,1)S(1)} collective-permute-done((bf16[256,2048]{1,0:T(8,128)(2,1)}, bf16[256,2048]{1,0:T(8,128)(2,1)S(1)}, u32[]{:S(2)}, u32[]{:S(2)}) %collective-permute-start.27) | collective-permute-done | bytes 1048608 | tf_op jit(solution)/shard_map/ppermute | solution.py:46
  235.2 5.7 all-gather.11.cloned.1.call-done
  240.9 7.6 %shard_map.228.refs_3_.refs_5_ = bf16[1408,2048]{1,0:T(8,128)(2,1)} custom-call(s32[12]{0:T(128)S(1)} %concatenate.20.refs_0_, bf16[4,8,704,128]{3,2,1,0:T(8,128)(2,1)} %bitcast.113), custom_call_target="tpu_custom_call" | custom-call | bytes 11534384 | tf_op jit(solution)/shard_map/pallas_call | solution.py:785
  251.5 17.0 %shard_map.229 = (bf16[256,2048]{1,0:T(8,128)(2,1)}, bf16[256,2048]{1,0:T(8,128)(2,1)}, bf16[256,2048]{1,0:T(8,128)(2,1)}, bf16[256,2048]{1,0:T(8,128)(2,1)}, bf...) custom-call(s32[12]{0:T(128)S(1)} %concatenate.20.refs_0_, ...), custom_call_target="tpu_custom_call" | custom-call | flops 8858370048 | bytes 19202096 | tf_op jit(solution)/shard_map/pallas_call | solution.py:785
  268.6 5.1 collective-permute-done.35.refs_8_
  282.8 29.4 %shard_map.230 = (bf16[256,2048]{1,0:T(8,128)(2,1)}, bf16[256,2048]{1,0:T(8,128)(2,1)}, bf16[256,2048]{1,0:T(8,128)(2,1)}, bf16[256,2048]{1,0:T(8,128)(2,1)}, bf...) custom-call(s32[12]{0:T(128)S(1)} %concatenate.20.refs_0_, ...), custom_call_target="tpu_custom_call" | custom-call | flops 17716740096 | bytes 29753392 | tf_op jit(solution)/shard_map/pallas_call | solution.py:785
  316.6 17.1 %shard_map.231 = (bf16[128,2048]{1,0:T(8,128)(2,1)}, bf16[128,2048]{1,0:T(8,128)(2,1)}, bf16[128,2048]{1,0:T(8,128)(2,1)}, bf16[128,2048]{1,0:T(8,128)(2,1)}, bf...) custom-call(s32[12]{0:T(128)S(1)} %concatenate.20.refs_0_, ...), custom_call_target="tpu_custom_call" | custom-call | flops 8858370048 | bytes 19202096 | tf_op jit(solution)/shard_map/pallas_call | solution.py:785
  341.3 13.9 %shard_map.232 = bf16[704,2048]{1,0:T(8,128)(2,1)} custom-call(s32[12]{0:T(128)S(1)} %concatenate.20.refs_0_, bf16[512,704]{1,0:T(8,128)(2,1)} %get-tuple-element.543.refs_1_, bf16[1024,704]{1,0:T(8,128)(2,1)} %get-tuple-element.544.refs_2_, bf16[512,704]{1,0:T(8,128)(2,1)} %get-tuple-element.545.refs_3_, bf16[256,2048]{1,0:T(8,128)(2,1)} %bitcast.123, ...), custom_call_target="tpu_custom_call" | custom-call | flops 5905580032 | bytes 14155824 | tf_op jit(solution)/shard_map/pallas_call | solution.py:785
  364.3 9.1 %collective-permute-done.52.refs_4_ = bf16[128,2048]{1,0:T(8,128)(2,1)S(1)} collective-permute-done((bf16[128,2048]{1,0:T(8,128)(2,1)S(1)}, bf16[128,2048]{1,0:T(8,128)(2,1)S(1)}, u32[]{:S(2)}, u32[]{:S(2)}) %collective-permute-start.52) | collective-permute-done | bytes 524320 | tf_op jit(solution)/shard_map/ppermute | solution.py:46
  375.6 7.5 %collective-permute-done.54.refs_6_ = bf16[128,2048]{1,0:T(8,128)(2,1)S(1)} collective-permute-done((bf16[128,2048]{1,0:T(8,128)(2,1)S(1)}, bf16[128,2048]{1,0:T(8,128)(2,1)S(1)}, u32[]{:S(2)}, u32[]{:S(2)}) %collective-permute-start.54) | collective-permute-done | bytes 524320 | tf_op jit(solution)/shard_map/ppermute | solution.py:46
  385.8 6.6 %shard_map.233 = (f32[256,2048]{1,0:T(8,128)}, bf16[256,2048]{1,0:T(8,128)(2,1)}) custom-call(bf16[256,2048]{1,0:T(8,128)(2,1)} %bitcast.124, f32[256,2048]{1,0:T(8,128)} %get-tuple-element.442.refs_1_.refs_0_, bf16[256,2048]{1,0:T(8,128)(2,1)} %get-tuple-element.521.refs_2_, bf16[256,2048]{1,0:T(8,128)(2,1)} %copy-done.19, bf16[128,2048]{1,0:T(8,128)(2,1)} %copy-done.31, ...), custom_call_target="tpu_custom_call" | custom-call | bytes 10485760 | tf_op jit(solution)/shard_map/pallas_call | solution.py:785
  395.4 22.8 %shard_map.234 = bf16[32,704,128]{2,1,0:T(8,128)(2,1)} custom-call(s32[12]{0:T(128)S(1)} %concatenate.20.refs_0_, bf16[512,704]{1,0:T(8,128)(2,1)} %get-tuple-element.556.refs_1_, bf16[1024,704]{1,0:T(8,128)(2,1)} %get-tuple-element.557.refs_2_, bf16[512,704]{1,0:T(8,128)(2,1)} %get-tuple-element.558.refs_3_, bf16[512,704]{1,0:T(8,128)(2,1)} %get-tuple-element.559.refs_4_, ...), custom_call_target="tpu_custom_call" | custom-call | flops 11811160064 | bytes 19922992 | tf_op jit(solution)/shard_map/pallas_call | solution.py:785
  424.2 13.5 %shard_map.235 = (bf16[6,256,256]{2,1,0:T(8,128)(2,1)}, f32[6,256,128]{2,1,0:T(8,128)}, bf16[2,2,160,128]{3,2,1,0:T(8,128)(2,1)}) custom-call(s32[12]{0:T(128)S(1)} %concatenate.20.refs_0_, bf16[256,2048]{1,0:T(8,128)(2,1)} %shard_map.225.refs_10_.refs_1_, f32[6,256,128]{2,1,0:T(8,128)} %get-tuple-element.364.refs_1_.refs_2_, ...), custom_call_target="tpu_custom_call" | custom-call | flops 1610612736 | bytes 12746800 | tf_op jit(solution)/shard_map/pallas_call | solution.py:785
  441.7 7.4 %shard_map.236 = (bf16[2,256,256]{2,1,0:T(8,128)(2,1)}, f32[2,256,128]{2,1,0:T(8,128)}, bf16[2,2,160,128]{3,2,1,0:T(8,128)(2,1)}) custom-call(s32[12]{0:T(128)S(1)} %concatenate.20.refs_0_, bf16[256,2048]{1,0:T(8,128)(2,1)} %shard_map.225.refs_10_.refs_1_, f32[6,256,128]{2,1,0:T(8,128)} %get-tuple-element.364.refs_1_.refs_2_, ...), custom_call_target="tpu_custom_call" | custom-call | flops 536870912 | bytes 7667760 | tf_op jit(solution)/shard_map/pallas_call | solution.py:785
  454.7 6.1 shard_map.237
  460.8 3.4 collective-permute-done.70.refs_10_
  464.2 20.9 %collective-permute-done.71.refs_11_ = bf16[2,2,160,128]{3,2,1,0:T(8,128)(2,1)S(1)} collective-permute-done((bf16[2,2,160,128]{3,2,1,0:T(8,128)(2,1)S(1)}, bf16[2,2,160,128]{3,2,1,0:T(8,128)(2,1)S(1)}, u32[]{:S(2)}, u32[]{:S(2)}) %collective-permute-start.71) | collective-permute-done | bytes 163872 | tf_op jit(solution)/shard_map/ppermute | solution.py:219
  491.5 22.8 %shard_map.238 = (bf16[8,256,384]{2,1,0:T(8,128)(2,1)}, bf16[256,2048]{1,0:T(8,128)(2,1)}, bf16[256,2048]{1,0:T(8,128)(2,1)}, bf16[256,2048]{1,0:T(8,128)(2,1)},...) custom-call(s32[12]{0:T(128)S(1)} %concatenate.20.refs_0_, ...), custom_call_target="tpu_custom_call" | custom-call | flops 3221225472 | bytes 18841648 | tf_op jit(solution)/shard_map/pallas_call | solution.py:785
  514.4 7.3 %collective-permute-done.79.refs_6_ = bf16[128,2048]{1,0:T(8,128)(2,1)S(1)} collective-permute-done((bf16[128,2048]{1,0:T(8,128)(2,1)S(1)}, bf16[128,2048]{1,0:T(8,128)(2,1)S(1)}, u32[]{:S(2)}, u32[]{:S(2)}) %collective-permute-start.79) | collective-permute-done | bytes 524320 | tf_op jit(solution)/shard_map/ppermute | solution.py:46
  522.8 8.6 %shard_map.239 = bf16[4,8,160,128]{3,2,1,0:T(8,128)(2,1)} custom-call(s32[12]{0:T(128)S(1)} %concatenate.20.refs_0_, bf16[8,256,384]{2,1,0:T(8,128)(2,1)} %get-tuple-element.634.refs_1_, bf16[256,2048]{1,0:T(8,128)(2,1)} %bitcast.18.refs_2_.refs_0_, bf16[256,2048]{1,0:T(8,128)(2,1)} %collective-permute-done.5.refs_3_, ...), custom_call_target="tpu_custom_call" | custom-call | flops 3221225472 | bytes 11272240 | tf_op jit(solution)/shard_map/pallas_call | solution.py:785
  541.0 5.7 collective-permute-done.90.refs_1_
  546.7 6.4 collective-permute-done.91.refs_3_
  558.4 3.6 all-to-all-start.3
  563.5 3.1 add_convert_fusion
  579.2 4.5 shard_map.240
  583.7 15.2 %collective-permute-done.95.refs_2_ = bf16[64,2048]{1,0:T(8,128)(2,1)} collective-permute-done((bf16[64,2048]{1,0:T(8,128)(2,1)}, bf16[64,2048]{1,0:T(8,128)(2,1)}, u32[]{:S(2)}, u32[]{:S(2)}) %collective-permute-start.95) | collective-permute-done | bytes 262176 | tf_op jit(solution)/shard_map/ppermute | solution.py:219
  607.4 3.4 all-to-all-start.2
  611.4 3.4 fusion.10
  621.8 6.0 broadcast_multiply_fusion
  627.7 3.1 copy.91
  633.8 5.6 shard_map.243
  (438 shorter events, 176.7 us)
Async XLA Ops:
  7.2 56.7 %all-gather.7.cloned.1.call-start = ((), (), s32[]{:S(2)}) async-start(), calls=%async_computation.8 | async-start | bytes 1310720 | tf_op jit(solution)/shard_map/all_gather | solution.py:231
  18.6 114.2 %all-gather.9.cloned.1.call-start = ((), (), s32[]{:S(2)}) async-start(), calls=%async_computation.9 | async-start | bytes 3604480 | tf_op jit(solution)/shard_map/all_gather | solution.py:231
  25.7 20.9 %collective-permute-start = (bf16[8,176,128]{2,1,0:T(8,128)(2,1)S(1)}, bf16[8,176,128]{2,1,0:T(8,128)(2,1)}, u32[]{:S(2)}, u32[]{:S(2)}) collective-permute-start(bf16[8,176,128]{2,1,0:T(8,128)(2,1)S(1)} %all-to-all-done.refs_1_), channel_id=1, source_target_pairs={{0,8},{8,16},{16,24},{24,0},{1,9},{9,17},{17,25},{25,1},{2,10},{10... | collective-permute-start | bytes 1081352 | tf_op jit(solution)/shard_map/ppermute | solution.py:219
  27.3 36.5 %collective-permute-start.1 = (bf16[8,176,128]{2,1,0:T(8,128)(2,1)S(1)}, bf16[8,176,128]{2,1,0:T(8,128)(2,1)}, u32[]{:S(2)}, u32[]{:S(2)}) collective-permute-start(bf16[8,176,128]{2,1,0:T(8,128)(2,1)S(1)} %all-to-all-done.refs_1_), channel_id=1, source_target_pairs={{0,16},{8,24},{16,0},{24,8},{1,17},{9,25},{17,1},{25,9},{2,18},{10... | collective-permute-start | bytes 1081352 | tf_op jit(solution)/shard_map/ppermute | solution.py:219
  29.9 33.9 %collective-permute-start.2 = (bf16[8,176,128]{2,1,0:T(8,128)(2,1)S(1)}, bf16[8,176,128]{2,1,0:T(8,128)(2,1)}, u32[]{:S(2)}, u32[]{:S(2)}) collective-permute-start(bf16[8,176,128]{2,1,0:T(8,128)(2,1)S(1)} %all-to-all-done.refs_1_), channel_id=1, source_target_pairs={{0,24},{8,0},{16,8},{24,16},{1,25},{9,1},{17,9},{25,17},{2,26},{10... | collective-permute-start | bytes 1081352 | tf_op jit(solution)/shard_map/ppermute | solution.py:219
  31.2 32.6 %collective-permute-start.3 = (bf16[256,2048]{1,0:T(8,128)(2,1)}, bf16[256,2048]{1,0:T(8,128)(2,1)}, u32[]{:S(2)}, u32[]{:S(2)}) collective-permute-start(bf16[256,2048]{1,0:T(8,128)(2,1)} %bitcast.18.refs_2_.refs_0_), channel_id=1, source_target_pairs={{0,1},{1,0},{2,3},{3,2},{4,5},{5,4},{6,7},{7,6},{8,9},{9,8},{10,11... | collective-permute-start | bytes 3145736 | tf_op jit(solution)/shard_map/ppermute | solution.py:46
  32.7 31.2 %collective-permute-start.4 = (bf16[256,2048]{1,0:T(8,128)(2,1)}, bf16[256,2048]{1,0:T(8,128)(2,1)}, u32[]{:S(2)}, u32[]{:S(2)}) collective-permute-start(bf16[256,2048]{1,0:T(8,128)(2,1)} %bitcast.18.refs_2_.refs_0_), channel_id=1, source_target_pairs={{0,4},{4,0},{1,5},{5,1},{2,6},{6,2},{3,7},{7,3},{8,12},{12,8},{9,1... | collective-permute-start | bytes 3145736 | tf_op jit(solution)/shard_map/ppermute | solution.py:46
  85.2 44.6 %all-to-all-start.1 = ((bf16[8,704,128]{2,1,0:T(8,128)(2,1)}), bf16[8,704,128]{2,1,0:T(8,128)(2,1)S(1)}, u32[]{:S(2)}, u32[]{:S(2)}) async-start(bf16[8,704,128]{2,1,0:T(8,128)(2,1)} %bitcast.23), calls=%async_computation.1 | async-start | bytes 2883584 | tf_op jit(solution)/shard_map/all_to_all | solution.py:198
  88.8 152.1 %all-gather.11.cloned.1.call-start = ((), (), s32[]{:S(2)}) async-start(), calls=%async_computation.10 | async-start | bytes 7208960 | tf_op jit(solution)/shard_map/all_gather | solution.py:231
  92.4 37.3 %collective-permute-start.15 = (bf16[2,64,2048]{2,1,0:T(8,128)(2,1)}, bf16[2,64,2048]{2,1,0:T(8,128)(2,1)}, u32[]{:S(2)}, u32[]{:S(2)}) collective-permute-start(bf16[2,64,2048]{2,1,0:T(8,128)(2,1)} %get-tuple-element.384), channel_id=1, source_target_pairs={{0,1},{1,0},{2,3},{3,2},{4,5},{5,4},{6,7},{7,6},{8,9},{9,8},{10,11... | collective-permute-start | bytes 1572872 | tf_op jit(solution)/shard_map/ppermute | solution.py:46
  108.5 21.2 %collective-permute-start.13 = (bf16[2,2,160,128]{3,2,1,0:T(8,128)(2,1)}, bf16[2,2,160,128]{3,2,1,0:T(8,128)(2,1)S(1)}, u32[]{:S(2)}, u32[]{:S(2)}) collective-permute-start(bf16[2,2,160,128]{3,2,1,0:T(8,128)(2,1)} %get-tuple-element.383), channel_id=1, source_target_pairs={{0,16},{8,24},{16,0},{24,8},{1,17},{9,25},{17,1},{25,9},{2,18},{10... | collective-permute-start | bytes 491528 | tf_op jit(solution)/shard_map/ppermute | solution.py:219
  132.8 290.0 %reduce-scatter.3.cloned.1.call-start = ((), (), s32[]{:S(2)}) async-start(), calls=%async_computation.6 | async-start | bytes 3604480 | tf_op jit(solution)/shard_map/reduce_scatter | solution.py:235
  178.1 21.8 %collective-permute-start.23 = (bf16[128,2048]{1,0:T(8,128)(2,1)S(1)}, bf16[128,2048]{1,0:T(8,128)(2,1)S(1)}, u32[]{:S(2)}, u32[]{:S(2)}) collective-permute-start(bf16[128,2048]{1,0:T(8,128)(2,1)S(1)} %get-tuple-element.724), channel_id=1, source_target_pairs={{0,4},{4,0},{1,5},{5,1},{2,6},{6,2},{3,7},{7,3},{8,12},{12,8},{9,1... | collective-permute-start | bytes 1572872 | tf_op jit(solution)/shard_map/ppermute | solution.py:46
  178.7 23.0 %collective-permute-start.24 = (bf16[128,2048]{1,0:T(8,128)(2,1)S(1)}, bf16[128,2048]{1,0:T(8,128)(2,1)S(1)}, u32[]{:S(2)}, u32[]{:S(2)}) collective-permute-start(bf16[128,2048]{1,0:T(8,128)(2,1)S(1)} %get-tuple-element.722), channel_id=1, source_target_pairs={{0,1},{1,0},{2,3},{3,2},{4,5},{5,4},{6,7},{7,6},{8,9},{9,8},{10,11... | collective-permute-start | bytes 1572872 | tf_op jit(solution)/shard_map/ppermute | solution.py:46
  180.4 28.0 %collective-permute-start.30 = (bf16[256,2048]{1,0:T(8,128)(2,1)S(1)}, bf16[256,2048]{1,0:T(8,128)(2,1)S(1)}, u32[]{:S(2)}, u32[]{:S(2)}) collective-permute-start(bf16[256,2048]{1,0:T(8,128)(2,1)S(1)} %bitcast.125), channel_id=1, source_target_pairs={{0,2},{2,0},{1,3},{3,1},{4,6},{6,4},{5,7},{7,5},{8,10},{10,8},{9,1... | collective-permute-start | bytes 3145736 | tf_op jit(solution)/shard_map/ppermute | solution.py:46
  207.5 23.3 %collective-permute-start.27 = (bf16[256,2048]{1,0:T(8,128)(2,1)}, bf16[256,2048]{1,0:T(8,128)(2,1)S(1)}, u32[]{:S(2)}, u32[]{:S(2)}) collective-permute-start(bf16[256,2048]{1,0:T(8,128)(2,1)} %get-tuple-element.444.refs_1_.refs_7_), channel_id=1, source_target_pairs={{0,1},{1,0},{2,3},{3,2},{4,5},{5,4},{6,7},{7,6},{8,9},{9,8},{10,11... | collective-permute-start | bytes 3145736 | tf_op jit(solution)/shard_map/ppermute | solution.py:46
  207.9 23.1 %collective-permute-start.28 = (bf16[256,2048]{1,0:T(8,128)(2,1)}, bf16[256,2048]{1,0:T(8,128)(2,1)}, u32[]{:S(2)}, u32[]{:S(2)}) collective-permute-start(bf16[256,2048]{1,0:T(8,128)(2,1)} %get-tuple-element.444.refs_1_.refs_7_), channel_id=1, source_target_pairs={{0,4},{4,0},{1,5},{5,1},{2,6},{6,2},{3,7},{7,3},{8,12},{12,8},{9,1... | collective-permute-start | bytes 3145736 | tf_op jit(solution)/shard_map/ppermute | solution.py:46
  208.4 22.6 %collective-permute-start.29 = (bf16[256,2048]{1,0:T(8,128)(2,1)}, bf16[256,2048]{1,0:T(8,128)(2,1)}, u32[]{:S(2)}, u32[]{:S(2)}) collective-permute-start(bf16[256,2048]{1,0:T(8,128)(2,1)} %get-tuple-element.444.refs_1_.refs_7_), channel_id=1, source_target_pairs={{0,2},{2,0},{1,3},{3,1},{4,6},{6,4},{5,7},{7,5},{8,10},{10,8},{9,1... | collective-permute-start | bytes 3145736 | tf_op jit(solution)/shard_map/ppermute | solution.py:46
  234.7 33.8 %collective-permute-start.33 = (bf16[256,2048]{1,0:T(8,128)(2,1)}, bf16[256,2048]{1,0:T(8,128)(2,1)}, u32[]{:S(2)}, u32[]{:S(2)}) collective-permute-start(bf16[256,2048]{1,0:T(8,128)(2,1)} %collective-permute-done.28.refs_1_.refs_9_), channel_id=1, source_target_pairs={{0,2},{2,0},{1,3},{3,1},{4,6},{6,4},{5,7},{7,5},{8,10},{10,8},{9,1... | collective-permute-start | bytes 3145736 | tf_op jit(solution)/shard_map/ppermute | solution.py:46
  234.7 33.8 %collective-permute-start.34 = (bf16[256,2048]{1,0:T(8,128)(2,1)S(1)}, bf16[256,2048]{1,0:T(8,128)(2,1)}, u32[]{:S(2)}, u32[]{:S(2)}) collective-permute-start(bf16[256,2048]{1,0:T(8,128)(2,1)S(1)} %collective-permute-done.27.refs_3_.refs_11_), channel_id=1, source_target_pairs={{0,2},{2,0},{1,3},{3,1},{4,6},{6,4},{5,7},{7,5},{8,10},{10,8},{9,1... | collective-permute-start | bytes 3145736 | tf_op jit(solution)/shard_map/ppermute | solution.py:46
  248.5 25.2 %collective-permute-start.35 = (bf16[256,2048]{1,0:T(8,128)(2,1)S(1)}, bf16[256,2048]{1,0:T(8,128)(2,1)S(1)}, u32[]{:S(2)}, u32[]{:S(2)}) collective-permute-start(bf16[256,2048]{1,0:T(8,128)(2,1)S(1)} %bitcast.126), channel_id=1, source_target_pairs={{0,1},{1,0},{2,3},{3,2},{4,5},{5,4},{6,7},{7,6},{8,9},{9,8},{10,11... | collective-permute-start | bytes 3145736 | tf_op jit(solution)/shard_map/ppermute | solution.py:46
  250.0 24.8 %collective-permute-start.36 = (bf16[256,2048]{1,0:T(8,128)(2,1)S(1)}, bf16[256,2048]{1,0:T(8,128)(2,1)S(1)}, u32[]{:S(2)}, u32[]{:S(2)}) collective-permute-start(bf16[256,2048]{1,0:T(8,128)(2,1)S(1)} %bitcast.127), channel_id=1, source_target_pairs={{0,4},{4,0},{1,5},{5,1},{2,6},{6,2},{3,7},{7,3},{8,12},{12,8},{9,1... | collective-permute-start | bytes 3145736 | tf_op jit(solution)/shard_map/ppermute | solution.py:46
  276.0 36.3 %collective-permute-start.41 = (bf16[128,2048]{1,0:T(8,128)(2,1)S(1)}, bf16[128,2048]{1,0:T(8,128)(2,1)S(1)}, u32[]{:S(2)}, u32[]{:S(2)}) collective-permute-start(bf16[128,2048]{1,0:T(8,128)(2,1)S(1)} %slice.183), channel_id=1, source_target_pairs={{0,1},{1,0},{2,3},{3,2},{4,5},{5,4},{6,7},{7,6},{8,9},{9,8},{10,11... | collective-permute-start | bytes 1572872 | tf_op jit(solution)/shard_map/ppermute | solution.py:46
  279.2 33.0 %collective-permute-start.42 = (bf16[128,2048]{1,0:T(8,128)(2,1)S(1)}, bf16[128,2048]{1,0:T(8,128)(2,1)S(1)}, u32[]{:S(2)}, u32[]{:S(2)}) collective-permute-start(bf16[128,2048]{1,0:T(8,128)(2,1)S(1)} %slice.184), channel_id=1, source_target_pairs={{0,4},{4,0},{1,5},{5,1},{2,6},{6,2},{3,7},{7,3},{8,12},{12,8},{9,1... | collective-permute-start | bytes 1572872 | tf_op jit(solution)/shard_map/ppermute | solution.py:46
  312.9 20.8 %collective-permute-start.45 = (bf16[256,2048]{1,0:T(8,128)(2,1)S(1)}, bf16[256,2048]{1,0:T(8,128)(2,1)S(1)}, u32[]{:S(2)}, u32[]{:S(2)}) collective-permute-start(bf16[256,2048]{1,0:T(8,128)(2,1)S(1)} %copy-done.67), channel_id=1, source_target_pairs={{0,2},{2,0},{1,3},{3,1},{4,6},{6,4},{5,7},{7,5},{8,10},{10,8},{9,1... | collective-permute-start | bytes 3145736 | tf_op jit(solution)/shard_map/ppermute | solution.py:46
  356.1 197.7 %reduce-scatter.5.cloned.1.call-start = ((), (), s32[]{:S(2)}) async-start(), calls=%async_computation.7 | async-start | bytes 7208960 | tf_op jit(solution)/shard_map/reduce_scatter | solution.py:235
  362.2 20.9 %collective-permute-start.54 = (bf16[128,2048]{1,0:T(8,128)(2,1)S(1)}, bf16[128,2048]{1,0:T(8,128)(2,1)S(1)}, u32[]{:S(2)}, u32[]{:S(2)}) collective-permute-start(bf16[128,2048]{1,0:T(8,128)(2,1)S(1)} %get-tuple-element.720), channel_id=1, source_target_pairs={{0,4},{4,0},{1,5},{5,1},{2,6},{6,2},{3,7},{7,3},{8,12},{12,8},{9,1... | collective-permute-start | bytes 1572872 | tf_op jit(solution)/shard_map/ppermute | solution.py:46
  363.7 21.3 %collective-permute-start.55 = (bf16[128,2048]{1,0:T(8,128)(2,1)S(1)}, bf16[128,2048]{1,0:T(8,128)(2,1)S(1)}, u32[]{:S(2)}, u32[]{:S(2)}) collective-permute-start(bf16[128,2048]{1,0:T(8,128)(2,1)S(1)} %get-tuple-element.718), channel_id=1, source_target_pairs={{0,1},{1,0},{2,3},{3,2},{4,5},{5,4},{6,7},{7,6},{8,9},{9,8},{10,11... | collective-permute-start | bytes 1572872 | tf_op jit(solution)/shard_map/ppermute | solution.py:46
  392.4 25.8 %collective-permute-start.56 = (bf16[256,2048]{1,0:T(8,128)(2,1)}, bf16[256,2048]{1,0:T(8,128)(2,1)S(1)}, u32[]{:S(2)}, u32[]{:S(2)}) collective-permute-start(bf16[256,2048]{1,0:T(8,128)(2,1)} %get-tuple-element.562.refs_7_.refs_2_), channel_id=1, source_target_pairs={{0,1},{1,0},{2,3},{3,2},{4,5},{5,4},{6,7},{7,6},{8,9},{9,8},{10,11... | collective-permute-start | bytes 3145736 | tf_op jit(solution)/shard_map/ppermute | solution.py:46
  393.9 24.3 %collective-permute-start.57 = (bf16[256,2048]{1,0:T(8,128)(2,1)}, bf16[256,2048]{1,0:T(8,128)(2,1)S(1)}, u32[]{:S(2)}, u32[]{:S(2)}) collective-permute-start(bf16[256,2048]{1,0:T(8,128)(2,1)} %get-tuple-element.562.refs_7_.refs_2_), channel_id=1, source_target_pairs={{0,4},{4,0},{1,5},{5,1},{2,6},{6,2},{3,7},{7,3},{8,12},{12,8},{9,1... | collective-permute-start | bytes 3145736 | tf_op jit(solution)/shard_map/ppermute | solution.py:46
  395.4 22.8 %collective-permute-start.58 = (bf16[256,2048]{1,0:T(8,128)(2,1)}, bf16[256,2048]{1,0:T(8,128)(2,1)S(1)}, u32[]{:S(2)}, u32[]{:S(2)}) collective-permute-start(bf16[256,2048]{1,0:T(8,128)(2,1)} %get-tuple-element.562.refs_7_.refs_2_), channel_id=1, source_target_pairs={{0,2},{2,0},{1,3},{3,1},{4,6},{6,4},{5,7},{7,5},{8,10},{10,8},{9,1... | collective-permute-start | bytes 3145736 | tf_op jit(solution)/shard_map/ppermute | solution.py:46
  449.3 35.9 %collective-permute-start.73 = (bf16[128,2048]{1,0:T(8,128)(2,1)S(1)}, bf16[128,2048]{1,0:T(8,128)(2,1)S(1)}, u32[]{:S(2)}, u32[]{:S(2)}) collective-permute-start(bf16[128,2048]{1,0:T(8,128)(2,1)S(1)} %add_convert_fusion.11), channel_id=1, source_target_pairs={{0,1},{1,0},{2,3},{3,2},{4,5},{5,4},{6,7},{7,6},{8,9},{9,8},{10,11... | collective-permute-start | bytes 1572872 | tf_op jit(solution)/shard_map/ppermute | solution.py:46
  451.1 34.0 %collective-permute-start.74 = (bf16[128,2048]{1,0:T(8,128)(2,1)S(1)}, bf16[128,2048]{1,0:T(8,128)(2,1)S(1)}, u32[]{:S(2)}, u32[]{:S(2)}) collective-permute-start(bf16[128,2048]{1,0:T(8,128)(2,1)S(1)} %add_convert_fusion.10), channel_id=1, source_target_pairs={{0,4},{4,0},{1,5},{5,1},{2,6},{6,2},{3,7},{7,3},{8,12},{12,8},{9,1... | collective-permute-start | bytes 1572872 | tf_op jit(solution)/shard_map/ppermute | solution.py:46
  452.7 32.5 %collective-permute-start.71 = (bf16[2,2,160,128]{3,2,1,0:T(8,128)(2,1)S(1)}, bf16[2,2,160,128]{3,2,1,0:T(8,128)(2,1)S(1)}, u32[]{:S(2)}, u32[]{:S(2)}) collective-permute-start(bf16[2,2,160,128]{3,2,1,0:T(8,128)(2,1)S(1)} %copy-done.79), channel_id=1, source_target_pairs={{0,16},{8,24},{16,0},{24,8},{1,17},{9,25},{17,1},{25,9},{2,18},{10... | collective-permute-start | bytes 491528 | tf_op jit(solution)/shard_map/ppermute | solution.py:219
  452.7 32.5 %collective-permute-start.72 = (bf16[2,2,160,128]{3,2,1,0:T(8,128)(2,1)S(1)}, bf16[2,2,160,128]{3,2,1,0:T(8,128)(2,1)S(1)}, u32[]{:S(2)}, u32[]{:S(2)}) collective-permute-start(bf16[2,2,160,128]{3,2,1,0:T(8,128)(2,1)S(1)} %copy-done.79), channel_id=1, source_target_pairs={{0,8},{8,16},{16,24},{24,0},{1,9},{9,17},{17,25},{25,1},{2,10},{10... | collective-permute-start | bytes 491528 | tf_op jit(solution)/shard_map/ppermute | solution.py:219
  485.2 29.2 %collective-permute-start.75 = (bf16[2,64,2048]{2,1,0:T(8,128)(2,1)}, bf16[2,64,2048]{2,1,0:T(8,128)(2,1)S(1)}, u32[]{:S(2)}, u32[]{:S(2)}) collective-permute-start(bf16[2,64,2048]{2,1,0:T(8,128)(2,1)} %get-tuple-element.621), channel_id=1, source_target_pairs={{0,1},{1,0},{2,3},{3,2},{4,5},{5,4},{6,7},{7,6},{8,9},{9,8},{10,11... | collective-permute-start | bytes 1572872 | tf_op jit(solution)/shard_map/ppermute | solution.py:46
  486.8 27.5 %collective-permute-start.76 = (bf16[128,2048]{1,0:T(8,128)(2,1)S(1)}, bf16[128,2048]{1,0:T(8,128)(2,1)S(1)}, u32[]{:S(2)}, u32[]{:S(2)}) collective-permute-start(bf16[128,2048]{1,0:T(8,128)(2,1)S(1)} %get-tuple-element.717), channel_id=1, source_target_pairs={{0,4},{4,0},{1,5},{5,1},{2,6},{6,2},{3,7},{7,3},{8,12},{12,8},{9,1... | collective-permute-start | bytes 1572872 | tf_op jit(solution)/shard_map/ppermute | solution.py:46
  488.6 25.8 %collective-permute-start.77 = (bf16[128,2048]{1,0:T(8,128)(2,1)S(1)}, bf16[128,2048]{1,0:T(8,128)(2,1)S(1)}, u32[]{:S(2)}, u32[]{:S(2)}) collective-permute-start(bf16[128,2048]{1,0:T(8,128)(2,1)S(1)} %get-tuple-element.715), channel_id=1, source_target_pairs={{0,1},{1,0},{2,3},{3,2},{4,5},{5,4},{6,7},{7,6},{8,9},{9,8},{10,11... | collective-permute-start | bytes 1572872 | tf_op jit(solution)/shard_map/ppermute | solution.py:46
  489.8 24.6 %collective-permute-start.78 = (bf16[128,2048]{1,0:T(8,128)(2,1)S(1)}, bf16[128,2048]{1,0:T(8,128)(2,1)S(1)}, u32[]{:S(2)}, u32[]{:S(2)}) collective-permute-start(bf16[128,2048]{1,0:T(8,128)(2,1)S(1)} %get-tuple-element.716), channel_id=1, source_target_pairs={{0,4},{4,0},{1,5},{5,1},{2,6},{6,2},{3,7},{7,3},{8,12},{12,8},{9,1... | collective-permute-start | bytes 1572872 | tf_op jit(solution)/shard_map/ppermute | solution.py:46
  490.4 31.4 %collective-permute-start.79 = (bf16[128,2048]{1,0:T(8,128)(2,1)S(1)}, bf16[128,2048]{1,0:T(8,128)(2,1)S(1)}, u32[]{:S(2)}, u32[]{:S(2)}) collective-permute-start(bf16[128,2048]{1,0:T(8,128)(2,1)S(1)} %get-tuple-element.714), channel_id=1, source_target_pairs={{0,1},{1,0},{2,3},{3,2},{4,5},{5,4},{6,7},{7,6},{8,9},{9,8},{10,11... | collective-permute-start | bytes 1572872 | tf_op jit(solution)/shard_map/ppermute | solution.py:46
  531.6 21.5 %collective-permute-start.88 = (bf16[128,2048]{1,0:T(8,128)(2,1)S(1)}, bf16[128,2048]{1,0:T(8,128)(2,1)}, u32[]{:S(2)}, u32[]{:S(2)}) collective-permute-start(bf16[128,2048]{1,0:T(8,128)(2,1)S(1)} %add_convert_fusion.3), channel_id=1, source_target_pairs={{0,1},{1,0},{2,3},{3,2},{4,5},{5,4},{6,7},{7,6},{8,9},{9,8},{10,11... | collective-permute-start | bytes 1572872 | tf_op jit(solution)/shard_map/ppermute | solution.py:46
  532.3 21.5 %collective-permute-start.89 = (bf16[128,2048]{1,0:T(8,128)(2,1)S(1)}, bf16[128,2048]{1,0:T(8,128)(2,1)S(1)}, u32[]{:S(2)}, u32[]{:S(2)}) collective-permute-start(bf16[128,2048]{1,0:T(8,128)(2,1)S(1)} %add_convert_fusion.2), channel_id=1, source_target_pairs={{0,4},{4,0},{1,5},{5,1},{2,6},{6,2},{3,7},{7,3},{8,12},{12,8},{9,1... | collective-permute-start | bytes 1572872 | tf_op jit(solution)/shard_map/ppermute | solution.py:46
  557.1 48.1 %collective-permute-start.85 = (bf16[128,2048]{1,0:T(8,128)(2,1)}, bf16[128,2048]{1,0:T(8,128)(2,1)}, u32[]{:S(2)}, u32[]{:S(2)}) collective-permute-start(bf16[128,2048]{1,0:T(8,128)(2,1)} %get-tuple-element.713), channel_id=1, source_target_pairs={{0,4},{4,0},{1,5},{5,1},{2,6},{6,2},{3,7},{7,3},{8,12},{12,8},{9,1... | collective-permute-start | bytes 1572872 | tf_op jit(solution)/shard_map/ppermute | solution.py:46
  558.4 49.0 %all-to-all-start.3 = ((bf16[8,704,128]{2,1,0:T(8,128)(2,1)}), bf16[8,704,128]{2,1,0:T(8,128)(2,1)S(1)}, u32[]{:S(2)}, u32[]{:S(2)}) async-start(bf16[8,704,128]{2,1,0:T(8,128)(2,1)} %bitcast.121), calls=%async_computation.5 | async-start | bytes 2883584 | tf_op jit(solution)/shard_map/all_to_all | solution.py:198
  566.6 38.7 %collective-permute-start.86 = (bf16[128,2048]{1,0:T(8,128)(2,1)}, bf16[128,2048]{1,0:T(8,128)(2,1)}, u32[]{:S(2)}, u32[]{:S(2)}) collective-permute-start(bf16[128,2048]{1,0:T(8,128)(2,1)} %get-tuple-element.711), channel_id=1, source_target_pairs={{0,1},{1,0},{2,3},{3,2},{4,5},{5,4},{6,7},{7,6},{8,9},{9,8},{10,11... | collective-permute-start | bytes 1572872 | tf_op jit(solution)/shard_map/ppermute | solution.py:46
  568.5 36.7 %collective-permute-start.87 = (bf16[8,160,128]{2,1,0:T(8,128)(2,1)S(1)}, bf16[8,160,128]{2,1,0:T(8,128)(2,1)}, u32[]{:S(2)}, u32[]{:S(2)}) collective-permute-start(bf16[8,160,128]{2,1,0:T(8,128)(2,1)S(1)} %get-tuple-element.729), channel_id=1, source_target_pairs={{0,16},{8,24},{16,0},{24,8},{1,17},{9,25},{17,1},{25,9},{2,18},{10... | collective-permute-start | bytes 983048 | tf_op jit(solution)/shard_map/ppermute | solution.py:219
  570.0 28.8 %collective-permute-start.95 = (bf16[64,2048]{1,0:T(8,128)(2,1)}, bf16[64,2048]{1,0:T(8,128)(2,1)}, u32[]{:S(2)}, u32[]{:S(2)}) collective-permute-start(bf16[64,2048]{1,0:T(8,128)(2,1)} %get-tuple-element.731), channel_id=1, source_target_pairs={{0,16},{8,24},{16,0},{24,8},{1,17},{9,25},{17,1},{25,9},{2,18},{10... | collective-permute-start | bytes 786440 | tf_op jit(solution)/shard_map/ppermute | solution.py:219
  574.0 26.4 %collective-permute-start.96 = (bf16[64,2048]{1,0:T(8,128)(2,1)}, bf16[64,2048]{1,0:T(8,128)(2,1)}, u32[]{:S(2)}, u32[]{:S(2)}) collective-permute-start(bf16[64,2048]{1,0:T(8,128)(2,1)} %get-tuple-element.730), channel_id=1, source_target_pairs={{0,24},{8,0},{16,8},{24,16},{1,25},{9,1},{17,9},{25,17},{2,26},{10... | collective-permute-start | bytes 786440 | tf_op jit(solution)/shard_map/ppermute | solution.py:219
  (143 other events, 1432.0 us)
Sparse Core Ops, SparseCore 0:
  9.6 51.6 all-gather.6
  62.8 69.9 all-gather.8
  134.9 105.9 all-gather.10
  356.2 53.4 reduce-scatter.2
  422.9 109.1 reduce-scatter.4

commit v4 on v3

--- a/solution.py
+++ b/solution.py
@@ -556,11 +556,52 @@
         out[pl.ds(pl.multiple_of(k * DV + (1 - info[3]) * 64, 64), 64)] = other[k]
 
 
-def by_step_kernel(info, mine, other, out):
+def by_z_kernel(info, mine, other, out):
     mine.ready(), other.ready()
-    for k in range(4):
-        z = jnp.bitwise_and(info[2] + k, 3)
-        out[k] = lax.select(z // 2 == info[3], mine[z % 2], other[z % 2])
+    for z in range(4):
+        out[z] = lax.select(info[3] == z // 2, mine[z % 2], other[z % 2])
+
+
+def hidden_out_kernel(slabs, w_gate, w_up, gain, gate_ref, up_ref, gain_ref, rows):
+    part = slabs.shape[1] // 4
+    for z in range(4):
+        for yc in range(4):
+            for x in range(2):
+                at = ((z * 4 + yc) * 2 + x) * part
+                rows[at : at + part] = slabs[x * 4 + yc, z * part : (z + 1) * part]
+    scale, added = gain[...], jnp.zeros((64, 128), F32)
+    for c in range(rows.shape[0] // 128):
+        cols = slice(c * 128, (c + 1) * 128)
+        both = rows[cols, :].astype(F32).T
+        gate, up = both[:64], both[64:]
+        added += gate * w_gate[:, cols].astype(F32) + up * w_up[:, cols].astype(F32)
+        gate_ref[:, cols] = gate * scale
+        up_ref[:, cols] = up * scale
+    gain_ref[...] = jnp.broadcast_to(jnp.sum(added, 1, keepdims=True), (64, 128))
+
+
+def heads_out_kernel(slabs, w_query, w_key, w_value, gain, query_ref, key_ref, value_ref, gain_ref, rows):
+    scale, added = gain[...], jnp.zeros((64, 128), F32)
+    rows[...] = jnp.zeros_like(rows)
+    for x in range(2):
+        for yc in range(4):
+            slab = slabs[x * 4 + yc].astype(F32)
+            both = slab[:DV].T
+            for k in range(HP):
+                head = (x * HP + k) * 4 + yc
+                lanes_of = slice(k * 64, (k + 1) * 64)
+                value, cols = both[lanes_of], slice(head * DV, (head + 1) * DV)
+                added += value * w_value[:, cols].astype(F32)
+                value_ref[:, cols] = value * scale
+                for i in range(2):
+                    start = DV + i * FD
+                    rows[i, head * FD : (head + 1) * FD, :64] = slab[start : start + FD, lanes_of]
+    total = jnp.sum(added, 1, keepdims=True)
+    for i, (out, w) in enumerate(((query_ref, w_query), (key_ref, w_key))):
+        grad = rows[i].T[:64]
+        total += jnp.sum(grad * w[...].astype(F32), 1, keepdims=True)
+        out[...] = grad * scale
+    gain_ref[...] = jnp.broadcast_to(total, (64, 128))
 
 
 def total_kernel(groups, *refs):
@@ -939,6 +980,20 @@
     return call(output_kernel, [resid, *pieces], [((1,) + resid.shape, F32)])[0]
 
 
+def hidden_out(slabs, w_gate, w_up, gain):
+    ff = w_gate.shape[1]
+    outs = [((64, ff), F32), ((64, ff), F32), ((64, 128), F32)]
+    gate, up, one = call(hidden_out_kernel, [slabs, w_gate, w_up, gain], outs, [pltpu.VMEM((ff, 128), BF16)])
+    return one[:, 0], gate, up
+
+
+def heads_out(slabs, w_query, w_key, w_value, gain):
+    outs = [(w.shape, F32) for w in (w_query, w_key, w_value)] + [((64, 128), F32)]
+    scratch = [pltpu.VMEM((2, H * FD, 128), F32)]
+    query, key, value, one = call(heads_out_kernel, [slabs, w_query, w_key, w_value, gain], outs, scratch)
+    return one[:, 0], query, key, value
+
+
 def gather_all(own, a):
     near = near_tokens(own, a)
     far = far_tokens(near, a)
@@ -969,10 +1024,9 @@
     gains = [g.astype(F32)[:, None] for g in (norm_gain, mlp_gain)]
     maps, maps_t = jnp.asarray(MAPS, BF16), jnp.asarray(MAPS.transpose(0, 1, 3, 2), BF16)
     weights = (w_query, w_key, w_value, w_gate, w_up)
-    block_out, input_grad, grads, g_out, g_down = run(
+    block_out, input_grad, g, g_out, g_down = run(
         tokens[0], cotangent[0], seq_lengths, gains, weights, w_out, w_down, maps, maps_t
     )
-    g = weight_grads(weights, gains, grads)
     return block_out, input_grad, *g[:4], g_out, *g[4:], g_down
 
 
@@ -1006,7 +1060,7 @@
     g_out = sum_both(out_rows_out(out_grads(info, dbs, mixed, False)[0]))
     g_heads = exchange(sum_both(rows_to_slabs(qkv_grads(info, xs, e, False), LAYOUT_HEADS)).astype(BF16), TP)
     grads = (*split_of_heads(join_heads, g_heads), *join_hidden(g_hid.astype(F32)))
-    return block_out, input_grad, grads, g_out, g_down
+    return block_out, input_grad, weight_grads(weights, gains, grads), g_out, g_down
 
 
 EIGHT = ("x", "y", "c")
@@ -1017,19 +1071,9 @@
     return w.T.reshape(2, HP, 4, width, rows).transpose(0, 2, 1, 3, 4).reshape(8, HP, width, rows)
 
 
-def join_heads_z(w, width):
-    rows = w.shape[-1]
-    return w.reshape(2, 4, HP, width, rows).transpose(0, 2, 1, 3, 4).reshape(H * width, rows).T
-
-
 def split_hidden_z(first, second):
     w = jnp.concatenate([first, second], 0).T.reshape(4, 4, 2, -1, 128)
     return w.transpose(2, 1, 0, 3, 4).reshape(8, -1, 128)
-
-
-def join_hidden_z(w):
-    w = w.reshape(2, 4, 4, -1, 128).transpose(2, 1, 0, 3, 4).reshape(-1, 128).T
-    return w[:64], w[64:]
 
 
 def scheduled(x, dy, lengths, gains, weights, w_out, w_down, maps, maps_t):
@@ -1072,49 +1116,44 @@
     tile, values = [one[0], two[0]], [one[1], two[1]]
     enter = entering_line(two[2], False)
     w_out_other = swap(w_out_far, "x")
-    enter, w_out_other, wd, hid = o.at(enter, w_out_other, wd, hid)
+    enter, w_out_other, wd, hid, dy = o.at(enter, w_out_other, wd, hid, dy)
     hid = line_gather(hid)
     w_out_mine = call(join_halves_kernel, [info, w_out_near, w_out_other], [((QK, d_model), BF16)])[0]
+    dy_near = near_tokens(dy, ax)
     (mixed, den, before), p = attend(2, info, tile, values, enter, maps, maps_t, w_out_mine)
     p, mixed, den, before = o.at(p, mixed, den, before)
-    fars, nears = far_cores(p), near_cores(p)
-    fars, nears = o.at(fars, nears)
+    fars = far_cores(p)
+    fars, dy_near = o.at(fars, dy_near)
     via = send_far(p, fars, ax)
-    via, = o.at(via)
+    nears = near_cores(p)
+    via, nears = o.at(via, nears)
     first = send_first(p, nears, ax)
     first, = o.at(first)
     second = send_second(p, nears, via, ax)
-    second, = o.at(second)
+    dy_cores = cores_of(dy_near)
+    second, dy_cores = o.at(second, dy_cores)
     resid, n_low = finish_residual(x, terms(p, nears, first, second))
     resid, n_low = o.at(resid, n_low)
 
     near = near_tokens(n_low, ax)
-    dy_core = swap(dy, "c")
-    near, dy_core = o.at(near, dy_core)
-    far = chip_far(near, ax)
+    near, = o.at(near)
+    far, cores = chip_far(near, ax), cores_of(near)
     wd = wd.reshape(-1, d_model)
     ff = wd.shape[0]
     w_gu = unpack(info, [hid], layout_hidden(ff), 2 * ff)
-    ns, dys = in_slots(near, [None] * 4, [None] * 2), [dy, dy_core]
+    ns, dys = in_slots(near, far + cores, [None] * 2), [dy_near[0], dy_near[3]]
     run = lambda c: mlp(info, ns[c], dys[c], w_gu, wd)
-    far, w_gu, dy, wd = o.at(far, w_gu, dy, wd)
-    dy_near = chips_near(dy, ax)
+    far, cores, w_gu, dy_near = o.at(far, cores, w_gu, dy_near)
+    last, dy_far = last_tokens(far), chip_far(dy_near, ax)
     ran = [run(OWN)]
-    cores = cores_of(near)
-    ran, cores, dy_near = o.at(ran, cores, dy_near)
-    dy_near[3] = dy_core
-    dy_cores = cores_of(dy_near)
-    last = last_tokens(far)
-    dy_cores, last = o.at(dy_cores, last)
-    dy_far = chip_far(dy_near, ax)
+    ran, last, dy_far = o.at(ran, last, dy_far)
     ns, dys = in_slots(near, far + cores, last), in_slots(dy_near, dy_far + dy_cores, [None] * 2)
+    dy_last = last_tokens(dy_far)
     ran.append(run(NEXT))
-    ran, dy_far = o.at(ran, dy_far)
-    dy_last = last_tokens(dy_far)
-    dy_last, = o.at(dy_last)
+    ran, dy_last = o.at(ran, dy_last)
+    ns, dys = in_slots(near, far + cores, last), in_slots(dy_near, dy_far + dy_cores, dy_last)
     p = [b for r in ran for b in r[1]]
     nears = near_cores(p)
-    ns, dys = in_slots(near, far + cores, last), in_slots(dy_near, dy_far + dy_cores, dy_last)
     ran.append(run(LAST))
     ran, nears = o.at(ran, nears)
     p = [b for r in ran for b in r[1]]
@@ -1165,21 +1204,20 @@
     nears, fars, head_g = o.at(nears, fars, head_g)
     heads = ring_sum(steps(head_g))
     via = send_far(p, fars, ax)
-    op = call(by_step_kernel, [info, out_near, out_other], [((4, 64, d_model), BF16)])[0]
-    via, heads[1], heads[3], op, g_hid = o.at(via, heads[1], heads[3], op, g_hid)
+    g_hid = exchange(g_hid, EIGHT)
+    g_out = call(by_z_kernel, [info, out_near, out_other], [((4, 64, d_model), BF16)])[0]
+    via, heads[1:3], g_hid, g_out = o.at(via, heads[1:3], g_hid, g_out)
     first = send_first(p, nears, ax)
-    g_hid = exchange(g_hid, EIGHT)
+    hid_out = hidden_out(g_hid, w_gate, w_up, gains[1])
+    first, heads[3], hid_out, g_out = o.at(first, heads[3], hid_out, g_out)
+    g_out = line_sum(g_out)
+    g_heads = exchange(total([[a] for a in heads], heads[0].shape, BF16), EIGHT)
+    second = send_second(p, nears, via, ax)
     block_out = finish_output(resid, terms(outs, o_nears, o_first, o_second))
-    first, heads[2], block_out = o.at(first, heads[2], block_out)
-    second = send_second(p, nears, via, ax)
-    g_heads = exchange(total([[a] for a in heads], heads[0].shape, BF16), EIGHT)
-    op = ring_sum(steps(op))
-    g_hid = join_hidden_z(g_hid.astype(F32))
-    second, g_heads, g_hid = o.at(second, g_heads, g_hid)
+    second, g_heads, block_out = o.at(second, g_heads, block_out)
     input_grad = finish_input(x, d_resid, terms(p, nears, first, second))
-    g_out = total([[a] for a in op], w_out.shape, F32)
-    grads = (*split_of_heads(join_heads_z, g_heads), *g_hid)
-    return block_out, input_grad, grads, g_out, g_down.astype(F32)
+    head_out = heads_out(g_heads, w_query, w_key, w_value, gains[0])
+    return block_out, input_grad, (*head_out, *hid_out), g_out.astype(F32), g_down.astype(F32)
 
 
 def solution(mesh):

time: 658 us -> 623 us (0.947)
  local copies, waits for them, and re-layouts: 35.3 us -> 18.4 us
  waiting for transfers between devices: 227 us -> 216 us
    unnamed x178 -> x170, local copies, waits for them, and re-layouts: 20.1 us -> 7.18 us
    mul x3 -> x0, other arithmetic: 7.03 us -> none  [the longest x1 5.96 us: weight_grads(): gains[1] * g_up]
    ppermute x15 -> x12, waiting for transfers between devices: 98.3 us -> 93 us  [turn(): return lax.ppermute(a, 'z', [(i, (i + k) % 4) for i in range(4)])]
    ppermute x15 -> x12, starting transfers between devices: 26 us -> 30 us  [turn(): return lax.ppermute(a, 'z', [(i, (i + k) % 4) for i in range(4)])]
    pallas_call x24 -> x25, Pallas kernels: 235 us -> 239 us  [call(): pl.pallas_call(body, out_shape=tuple((pltpu.HBM(s, t) for s, t in outs)),...]
  transfers between devices with their start and end apart: 106 -> 104, of which waited for: 39 -> 41; matrix products, arithmetic and copies ran while one was open for 6% -> 5% of each run, Pallas kernels for 36% -> 39%
where the time goes in v4:
time: 623 us; the launch traced here: 614 us
  Pallas kernels  239 us (38%)
  waiting for transfers between devices  216 us (35%)
  starting transfers between devices  101 us (16%)
  other arithmetic  25 us (4%)
  local copies, waits for them, and re-layouts  18.4 us (3%)
  between operations  15.9 us (3%)
    pallas_call x25, Pallas kernels, call(): pl.pallas_call(body, out_shape=tuple((pltpu.HBM(s, t) for s, t in outs)),...  239 us
    ppermute x82, waiting for transfers between devices, swap(): return lax.ppermute(a, axis, [(0, 1), (1, 0)])  105 us
    ppermute x12, waiting for transfers between devices, turn(): return lax.ppermute(a, 'z', [(i, (i + k) % 4) for i in range(4)])  93 us
    ppermute x82, starting transfers between devices, swap(): return lax.ppermute(a, axis, [(0, 1), (1, 0)])  54.3 us
    ppermute x12, starting transfers between devices, turn(): return lax.ppermute(a, 'z', [(i, (i + k) % 4) for i in range(4)])  30 us
    convert_element_type x16, other arithmetic, plus(): functools.reduce(jnp.add, [t.astype(F32) for t in terms]).astype(BF16)  18.8 us
    all_to_all x4, starting transfers between devices, exchange(): return lax.all_to_all(slabs, axes, 0, 0, tiled=True)  15.9 us
  transfers between devices with their start and end apart: 104, of which 41 were waited for; matrix products, arithmetic and copies ran while one was open for 5% of the time, Pallas kernels for 39%

profile of v4, /device:TPU:0, one launch (start us, length us, event | category | flops | bytes accessed | tf_op | source)
XLA Modules:
  0.0 614.2 jit_solution(12855855501385153383)
XLA Ops:
  11.9 5.2 all-to-all-start
  17.8 6.4 %all-to-all-done.refs_1_ = bf16[8,176,128]{2,1,0:T(8,128)(2,1)S(1)} async-done(((bf16[8,176,128]{2,1,0:T(8,128)(2,1)}), bf16[8,176,128]{2,1,0:T(8,128)(2,1)S(1)}, u32[]{:S(2)}, u32[]{:S(2)}) %all-to-all-start) | async-done | bytes 360480 | tf_op jit(solution)/shard_map/all_to_all | solution.py:198
  34.2 10.8 %collective-permute-done.refs_2_ = bf16[8,176,128]{2,1,0:T(8,128)(2,1)} collective-permute-done((bf16[8,176,128]{2,1,0:T(8,128)(2,1)S(1)}, bf16[8,176,128]{2,1,0:T(8,128)(2,1)}, u32[]{:S(2)}, u32[]{:S(2)}) %collective-permute-start) | collective-permute-done | bytes 360480 | tf_op jit(solution)/shard_map/ppermute | solution.py:219
  45.1 18.7 %collective-permute-done.1.refs_3_ = bf16[8,176,128]{2,1,0:T(8,128)(2,1)} collective-permute-done((bf16[8,176,128]{2,1,0:T(8,128)(2,1)S(1)}, bf16[8,176,128]{2,1,0:T(8,128)(2,1)}, u32[]{:S(2)}, u32[]{:S(2)}) %collective-permute-start.1) | collective-permute-done | bytes 360480 | tf_op jit(solution)/shard_map/ppermute | solution.py:219
  70.0 3.4 shard_map.221.refs_1_.refs_14_
  73.5 11.7 %shard_map.222 = (f32[6,256,128]{2,1,0:T(8,128)}, bf16[6,256,256]{2,1,0:T(8,128)(2,1)}, bf16[2,2,160,128]{3,2,1,0:T(8,128)(2,1)}) custom-call(s32[12]{0:T(128)S(1)} %concatenate.20.refs_0_, bf16[384,2048]{1,0:T(8,128)(2,1)} %shard_map.221.refs_1_.refs_14_, bf16[256,2048]{1,0:T(8,128)(2,1)} %bitcast.18.refs_2_.refs_0_, ...), custom_call_target="tpu_custom_call" | custom-call | flops 2415919104 | bytes 10125360 | tf_op jit(solution)/shard_map/pallas_call | solution.py:826
  85.2 3.6 all-to-all-start.1
  94.4 6.0 shard_map.224
  100.5 8.2 %collective-permute-start.12 = (bf16[2,2,160,128]{3,2,1,0:T(8,128)(2,1)}, bf16[2,2,160,128]{3,2,1,0:T(8,128)(2,1)S(1)}, u32[]{:S(2)}, u32[]{:S(2)}) collective-permute-start(bf16[2,2,160,128]{3,2,1,0:T(8,128)(2,1)} %get-tuple-element.393), channel_id=1, source_target_pairs={{0,8},{8,16},{16,24},{24,0},{1,9},{9,17},{17,25},{25,1},{2,10},{10... | collective-permute-start | bytes 491528 | tf_op jit(solution)/shard_map/ppermute | solution.py:219
  111.1 7.1 %collective-permute-done.12.refs_5_ = bf16[2,2,160,128]{3,2,1,0:T(8,128)(2,1)S(1)} collective-permute-done((bf16[2,2,160,128]{3,2,1,0:T(8,128)(2,1)}, bf16[2,2,160,128]{3,2,1,0:T(8,128)(2,1)S(1)}, u32[]{:S(2)}, u32[]{:S(2)}) %collective-permute-start.12) | collective-permute-done | bytes 163872 | tf_op jit(solution)/shard_map/ppermute | solution.py:219
  118.2 11.7 %collective-permute-done.13.refs_6_ = bf16[2,2,160,128]{3,2,1,0:T(8,128)(2,1)S(1)} collective-permute-done((bf16[2,2,160,128]{3,2,1,0:T(8,128)(2,1)}, bf16[2,2,160,128]{3,2,1,0:T(8,128)(2,1)S(1)}, u32[]{:S(2)}, u32[]{:S(2)}) %collective-permute-start.13) | collective-permute-done | bytes 163872 | tf_op jit(solution)/shard_map/ppermute | solution.py:219
  130.0 3.9 all-gather.9.cloned.1.call-done
  139.8 14.1 %shard_map.226 = (bf16[8,256,256]{2,1,0:T(8,128)(2,1)}, f32[8,256,128]{2,1,0:T(8,128)}, bf16[8,2,256,256]{3,2,1,0:T(8,128)(2,1)}, bf16[256,2048]{1,0:T(8,128)(2,...) custom-call(s32[12]{0:T(128)S(1)} %concatenate.20.refs_0_, ...), custom_call_target="tpu_custom_call" | custom-call | flops 2147483648 | bytes 17268784 | tf_op jit(solution)/shard_map/pallas_call | solution.py:826
  163.5 10.9 %collective-permute-done.21 = bf16[128,2048]{1,0:T(8,128)(2,1)S(1)} collective-permute-done((bf16[128,2048]{1,0:T(8,128)(2,1)S(1)}, bf16[128,2048]{1,0:T(8,128)(2,1)S(1)}, u32[]{:S(2)}, u32[]{:S(2)}) %collective-permute-start.21) | collective-permute-done | bytes 524320 | tf_op jit(solution)/shard_map/ppermute | solution.py:46
  180.1 11.2 %collective-permute-done.26.refs_5_ = bf16[128,2048]{1,0:T(8,128)(2,1)S(1)} collective-permute-done((bf16[128,2048]{1,0:T(8,128)(2,1)S(1)}, bf16[128,2048]{1,0:T(8,128)(2,1)S(1)}, u32[]{:S(2)}, u32[]{:S(2)}) %collective-permute-start.26) | collective-permute-done | bytes 524320 | tf_op jit(solution)/shard_map/ppermute | solution.py:46
  193.8 7.0 %collective-permute-done.28.refs_3_ = bf16[128,2048]{1,0:T(8,128)(2,1)S(1)} collective-permute-done((bf16[128,2048]{1,0:T(8,128)(2,1)S(1)}, bf16[128,2048]{1,0:T(8,128)(2,1)S(1)}, u32[]{:S(2)}, u32[]{:S(2)}) %collective-permute-start.28) | collective-permute-done | bytes 524320 | tf_op jit(solution)/shard_map/ppermute | solution.py:46
  200.8 3.3 collective-permute-done.29.refs_6_
  204.9 4.8 shard_map.227
  210.9 22.3 %collective-permute-done.32.refs_3_.refs_11_ = bf16[256,2048]{1,0:T(8,128)(2,1)S(1)} collective-permute-done((bf16[256,2048]{1,0:T(8,128)(2,1)}, bf16[256,2048]{1,0:T(8,128)(2,1)S(1)}, u32[]{:S(2)}, u32[]{:S(2)}) %collective-permute-start.32) | collective-permute-done | bytes 1048608 | tf_op jit(solution)/shard_map/ppermute | solution.py:46
  237.5 4.2 all-gather.11.cloned.1.call-done
  241.7 7.5 %shard_map.228.refs_3_.refs_5_ = bf16[1408,2048]{1,0:T(8,128)(2,1)} custom-call(s32[12]{0:T(128)S(1)} %concatenate.20.refs_0_, bf16[4,8,704,128]{3,2,1,0:T(8,128)(2,1)} %bitcast.75), custom_call_target="tpu_custom_call" | custom-call | bytes 11534384 | tf_op jit(solution)/shard_map/pallas_call | solution.py:826
  253.0 17.0 %shard_map.229 = (bf16[256,2048]{1,0:T(8,128)(2,1)}, bf16[256,2048]{1,0:T(8,128)(2,1)}, bf16[256,2048]{1,0:T(8,128)(2,1)}, bf16[256,2048]{1,0:T(8,128)(2,1)}, bf...) custom-call(s32[12]{0:T(128)S(1)} %concatenate.20.refs_0_, ...), custom_call_target="tpu_custom_call" | custom-call | flops 8858370048 | bytes 19202096 | tf_op jit(solution)/shard_map/pallas_call | solution.py:826
  270.7 29.5 %shard_map.230 = (bf16[256,2048]{1,0:T(8,128)(2,1)}, bf16[256,2048]{1,0:T(8,128)(2,1)}, bf16[256,2048]{1,0:T(8,128)(2,1)}, bf16[256,2048]{1,0:T(8,128)(2,1)}, bf...) custom-call(s32[12]{0:T(128)S(1)} %concatenate.20.refs_0_, ...), custom_call_target="tpu_custom_call" | custom-call | flops 17716740096 | bytes 29753392 | tf_op jit(solution)/shard_map/pallas_call | solution.py:826
  301.1 17.1 %shard_map.231 = (bf16[128,2048]{1,0:T(8,128)(2,1)}, bf16[128,2048]{1,0:T(8,128)(2,1)}, bf16[128,2048]{1,0:T(8,128)(2,1)}, bf16[128,2048]{1,0:T(8,128)(2,1)}, bf...) custom-call(s32[12]{0:T(128)S(1)} %concatenate.20.refs_0_, ...), custom_call_target="tpu_custom_call" | custom-call | flops 8858370048 | bytes 19202096 | tf_op jit(solution)/shard_map/pallas_call | solution.py:826
  325.9 13.9 %shard_map.232 = bf16[704,2048]{1,0:T(8,128)(2,1)} custom-call(s32[12]{0:T(128)S(1)} %concatenate.20.refs_0_, bf16[512,704]{1,0:T(8,128)(2,1)} %get-tuple-element.553.refs_1_, bf16[1024,704]{1,0:T(8,128)(2,1)} %get-tuple-element.554.refs_2_, bf16[512,704]{1,0:T(8,128)(2,1)} %get-tuple-element.555.refs_3_, bf16[256,2048]{1,0:T(8,128)(2,1)} %bitcast.81, ...), custom_call_target="tpu_custom_call" | custom-call | flops 5905580032 | bytes 14155824 | tf_op jit(solution)/shard_map/pallas_call | solution.py:826
  348.6 9.2 %collective-permute-done.52.refs_4_ = bf16[128,2048]{1,0:T(8,128)(2,1)S(1)} collective-permute-done((bf16[128,2048]{1,0:T(8,128)(2,1)S(1)}, bf16[128,2048]{1,0:T(8,128)(2,1)S(1)}, u32[]{:S(2)}, u32[]{:S(2)}) %collective-permute-start.52) | collective-permute-done | bytes 524320 | tf_op jit(solution)/shard_map/ppermute | solution.py:46
  359.8 7.9 %collective-permute-done.54.refs_6_ = bf16[128,2048]{1,0:T(8,128)(2,1)S(1)} collective-permute-done((bf16[128,2048]{1,0:T(8,128)(2,1)S(1)}, bf16[128,2048]{1,0:T(8,128)(2,1)S(1)}, u32[]{:S(2)}, u32[]{:S(2)}) %collective-permute-start.54) | collective-permute-done | bytes 524320 | tf_op jit(solution)/shard_map/ppermute | solution.py:46
  370.1 6.5 %shard_map.233 = (f32[256,2048]{1,0:T(8,128)}, bf16[256,2048]{1,0:T(8,128)(2,1)}) custom-call(bf16[256,2048]{1,0:T(8,128)(2,1)} %bitcast.82, f32[256,2048]{1,0:T(8,128)} %get-tuple-element.447.refs_1_.refs_0_, bf16[256,2048]{1,0:T(8,128)(2,1)} %get-tuple-element.531.refs_2_, bf16[256,2048]{1,0:T(8,128)(2,1)} %copy-done.20, bf16[128,2048]{1,0:T(8,128)(2,1)} %copy-done.30, ...), custom_call_target="tpu_custom_call" | custom-call | bytes 10485760 | tf_op jit(solution)/shard_map/pallas_call | solution.py:826
  378.9 22.6 %shard_map.234 = bf16[32,704,128]{2,1,0:T(8,128)(2,1)} custom-call(s32[12]{0:T(128)S(1)} %concatenate.20.refs_0_, bf16[512,704]{1,0:T(8,128)(2,1)} %get-tuple-element.567.refs_1_, bf16[1024,704]{1,0:T(8,128)(2,1)} %get-tuple-element.568.refs_2_, bf16[512,704]{1,0:T(8,128)(2,1)} %get-tuple-element.569.refs_3_, bf16[512,704]{1,0:T(8,128)(2,1)} %get-tuple-element.570.refs_4_, ...), custom_call_target="tpu_custom_call" | custom-call | flops 11811160064 | bytes 19922992 | tf_op jit(solution)/shard_map/pallas_call | solution.py:826
  408.6 12.7 %shard_map.235 = (bf16[6,256,256]{2,1,0:T(8,128)(2,1)}, f32[6,256,128]{2,1,0:T(8,128)}, bf16[2,2,160,128]{3,2,1,0:T(8,128)(2,1)}) custom-call(s32[12]{0:T(128)S(1)} %concatenate.20.refs_0_, bf16[256,2048]{1,0:T(8,128)(2,1)} %shard_map.225.refs_10_.refs_1_, f32[6,256,128]{2,1,0:T(8,128)} %get-tuple-element.374.refs_1_.refs_2_, ...), custom_call_target="tpu_custom_call" | custom-call | flops 1610612736 | bytes 12746800 | tf_op jit(solution)/shard_map/pallas_call | solution.py:826
  425.7 7.3 %shard_map.236 = (bf16[2,256,256]{2,1,0:T(8,128)(2,1)}, f32[2,256,128]{2,1,0:T(8,128)}, bf16[2,2,160,128]{3,2,1,0:T(8,128)(2,1)}) custom-call(s32[12]{0:T(128)S(1)} %concatenate.20.refs_0_, bf16[256,2048]{1,0:T(8,128)(2,1)} %shard_map.225.refs_10_.refs_1_, f32[6,256,128]{2,1,0:T(8,128)} %get-tuple-element.374.refs_1_.refs_2_, ...), custom_call_target="tpu_custom_call" | custom-call | flops 536870912 | bytes 7667760 | tf_op jit(solution)/shard_map/pallas_call | solution.py:826
  435.4 4.1 collective-permute-start.70
  440.8 6.1 shard_map.237
  446.9 4.4 collective-permute-done.70.refs_10_
  451.3 22.4 %collective-permute-done.71.refs_11_ = bf16[2,2,160,128]{3,2,1,0:T(8,128)(2,1)S(1)} collective-permute-done((bf16[2,2,160,128]{3,2,1,0:T(8,128)(2,1)S(1)}, bf16[2,2,160,128]{3,2,1,0:T(8,128)(2,1)S(1)}, u32[]{:S(2)}, u32[]{:S(2)}) %collective-permute-start.71) | collective-permute-done | bytes 163872 | tf_op jit(solution)/shard_map/ppermute | solution.py:219
  480.5 22.8 %shard_map.238 = (bf16[8,256,384]{2,1,0:T(8,128)(2,1)}, bf16[256,2048]{1,0:T(8,128)(2,1)}, bf16[256,2048]{1,0:T(8,128)(2,1)}, bf16[256,2048]{1,0:T(8,128)(2,1)},...) custom-call(s32[12]{0:T(128)S(1)} %concatenate.20.refs_0_, ...), custom_call_target="tpu_custom_call" | custom-call | flops 3221225472 | bytes 18841648 | tf_op jit(solution)/shard_map/pallas_call | solution.py:826
  503.3 6.8 %collective-permute-done.79.refs_6_ = bf16[128,2048]{1,0:T(8,128)(2,1)} collective-permute-done((bf16[128,2048]{1,0:T(8,128)(2,1)S(1)}, bf16[128,2048]{1,0:T(8,128)(2,1)}, u32[]{:S(2)}, u32[]{:S(2)}) %collective-permute-start.79) | collective-permute-done | bytes 524320 | tf_op jit(solution)/shard_map/ppermute | solution.py:46
  511.1 8.5 %shard_map.239 = bf16[4,8,160,128]{3,2,1,0:T(8,128)(2,1)} custom-call(s32[12]{0:T(128)S(1)} %concatenate.20.refs_0_, bf16[8,256,384]{2,1,0:T(8,128)(2,1)} %get-tuple-element.645.refs_1_, bf16[256,2048]{1,0:T(8,128)(2,1)} %bitcast.18.refs_2_.refs_0_, bf16[256,2048]{1,0:T(8,128)(2,1)} %collective-permute-done.5.refs_3_, ...), custom_call_target="tpu_custom_call" | custom-call | flops 3221225472 | bytes 11272240 | tf_op jit(solution)/shard_map/pallas_call | solution.py:826
  520.5 3.7 all-to-all-start.2
  533.0 4.6 collective-permute-start.87
  540.5 5.6 collective-permute-done.87.refs_1_
  546.1 12.3 %collective-permute-done.88.refs_2_ = bf16[8,160,128]{2,1,0:T(8,128)(2,1)} collective-permute-done((bf16[8,160,128]{2,1,0:T(8,128)(2,1)}, bf16[8,160,128]{2,1,0:T(8,128)(2,1)}, u32[]{:S(2)}, u32[]{:S(2)}) %collective-permute-start.88) | collective-permute-done | bytes 327712 | tf_op jit(solution)/shard_map/ppermute | solution.py:219
  558.4 3.3 add_convert_fusion.1
  565.3 3.9 collective-permute-start.93
  569.9 4.2 shard_map.241
  582.7 3.4 all-to-all-start.3
  588.1 4.5 shard_map.243
  599.1 5.6 shard_map.244
  (418 shorter events, 146.5 us)
Async XLA Ops:
  7.2 56.7 %all-gather.7.cloned.1.call-start = ((), (), s32[]{:S(2)}) async-start(), calls=%async_computation.10 | async-start | bytes 1310720 | tf_op jit(solution)/shard_map/all_gather | solution.py:231
  17.1 116.8 %all-gather.9.cloned.1.call-start = ((), (), s32[]{:S(2)}) async-start(), calls=%async_computation.11 | async-start | bytes 3604480 | tf_op jit(solution)/shard_map/all_gather | solution.py:231
  24.2 20.9 %collective-permute-start = (bf16[8,176,128]{2,1,0:T(8,128)(2,1)S(1)}, bf16[8,176,128]{2,1,0:T(8,128)(2,1)}, u32[]{:S(2)}, u32[]{:S(2)}) collective-permute-start(bf16[8,176,128]{2,1,0:T(8,128)(2,1)S(1)} %all-to-all-done.refs_1_), channel_id=1, source_target_pairs={{0,8},{8,16},{16,24},{24,0},{1,9},{9,17},{17,25},{25,1},{2,10},{10... | collective-permute-start | bytes 1081352 | tf_op jit(solution)/shard_map/ppermute | solution.py:219
  25.8 38.0 %collective-permute-start.1 = (bf16[8,176,128]{2,1,0:T(8,128)(2,1)S(1)}, bf16[8,176,128]{2,1,0:T(8,128)(2,1)}, u32[]{:S(2)}, u32[]{:S(2)}) collective-permute-start(bf16[8,176,128]{2,1,0:T(8,128)(2,1)S(1)} %all-to-all-done.refs_1_), channel_id=1, source_target_pairs={{0,16},{8,24},{16,0},{24,8},{1,17},{9,25},{17,1},{25,9},{2,18},{10... | collective-permute-start | bytes 1081352 | tf_op jit(solution)/shard_map/ppermute | solution.py:219
  28.4 35.5 %collective-permute-start.2 = (bf16[8,176,128]{2,1,0:T(8,128)(2,1)S(1)}, bf16[8,176,128]{2,1,0:T(8,128)(2,1)}, u32[]{:S(2)}, u32[]{:S(2)}) collective-permute-start(bf16[8,176,128]{2,1,0:T(8,128)(2,1)S(1)} %all-to-all-done.refs_1_), channel_id=1, source_target_pairs={{0,24},{8,0},{16,8},{24,16},{1,25},{9,1},{17,9},{25,17},{2,26},{10... | collective-permute-start | bytes 1081352 | tf_op jit(solution)/shard_map/ppermute | solution.py:219
  29.7 34.1 %collective-permute-start.3 = (bf16[256,2048]{1,0:T(8,128)(2,1)}, bf16[256,2048]{1,0:T(8,128)(2,1)}, u32[]{:S(2)}, u32[]{:S(2)}) collective-permute-start(bf16[256,2048]{1,0:T(8,128)(2,1)} %bitcast.18.refs_2_.refs_0_), channel_id=1, source_target_pairs={{0,1},{1,0},{2,3},{3,2},{4,5},{5,4},{6,7},{7,6},{8,9},{9,8},{10,11... | collective-permute-start | bytes 3145736 | tf_op jit(solution)/shard_map/ppermute | solution.py:46
  31.1 32.7 %collective-permute-start.4 = (bf16[256,2048]{1,0:T(8,128)(2,1)}, bf16[256,2048]{1,0:T(8,128)(2,1)}, u32[]{:S(2)}, u32[]{:S(2)}) collective-permute-start(bf16[256,2048]{1,0:T(8,128)(2,1)} %bitcast.18.refs_2_.refs_0_), channel_id=1, source_target_pairs={{0,4},{4,0},{1,5},{5,1},{2,6},{6,2},{3,7},{7,3},{8,12},{12,8},{9,1... | collective-permute-start | bytes 3145736 | tf_op jit(solution)/shard_map/ppermute | solution.py:46
  66.7 18.5 %collective-permute-start.8 = (bf16[128,2048]{1,0:T(8,128)(2,1)S(1)}, bf16[128,2048]{1,0:T(8,128)(2,1)S(1)}, u32[]{:S(2)}, u32[]{:S(2)}) collective-permute-start(bf16[128,2048]{1,0:T(8,128)(2,1)S(1)} %slice.150), channel_id=1, source_target_pairs={{0,1},{1,0},{2,3},{3,2},{4,5},{5,4},{6,7},{7,6},{8,9},{9,8},{10,11... | collective-permute-start | bytes 1572872 | tf_op jit(solution)/shard_map/ppermute | solution.py:46
  85.2 44.7 %all-to-all-start.1 = ((bf16[8,704,128]{2,1,0:T(8,128)(2,1)}), bf16[8,704,128]{2,1,0:T(8,128)(2,1)S(1)}, u32[]{:S(2)}, u32[]{:S(2)}) async-start(bf16[8,704,128]{2,1,0:T(8,128)(2,1)} %bitcast.23), calls=%async_computation.1 | async-start | bytes 2883584 | tf_op jit(solution)/shard_map/all_to_all | solution.py:198
  88.8 152.9 %all-gather.11.cloned.1.call-start = ((), (), s32[]{:S(2)}) async-start(), calls=%async_computation.12 | async-start | bytes 7208960 | tf_op jit(solution)/shard_map/all_gather | solution.py:231
  92.5 37.5 %collective-permute-start.15 = (bf16[2,64,2048]{2,1,0:T(8,128)(2,1)}, bf16[2,64,2048]{2,1,0:T(8,128)(2,1)S(1)}, u32[]{:S(2)}, u32[]{:S(2)}) collective-permute-start(bf16[2,64,2048]{2,1,0:T(8,128)(2,1)} %get-tuple-element.394), channel_id=1, source_target_pairs={{0,1},{1,0},{2,3},{3,2},{4,5},{5,4},{6,7},{7,6},{8,9},{9,8},{10,11... | collective-permute-start | bytes 1572872 | tf_op jit(solution)/shard_map/ppermute | solution.py:46
  108.7 21.3 %collective-permute-start.13 = (bf16[2,2,160,128]{3,2,1,0:T(8,128)(2,1)}, bf16[2,2,160,128]{3,2,1,0:T(8,128)(2,1)S(1)}, u32[]{:S(2)}, u32[]{:S(2)}) collective-permute-start(bf16[2,2,160,128]{3,2,1,0:T(8,128)(2,1)} %get-tuple-element.393), channel_id=1, source_target_pairs={{0,16},{8,24},{16,0},{24,8},{1,17},{9,25},{17,1},{25,9},{2,18},{10... | collective-permute-start | bytes 491528 | tf_op jit(solution)/shard_map/ppermute | solution.py:219
  110.0 19.9 %collective-permute-start.14 = (bf16[2,2,160,128]{3,2,1,0:T(8,128)(2,1)}, bf16[2,2,160,128]{3,2,1,0:T(8,128)(2,1)S(1)}, u32[]{:S(2)}, u32[]{:S(2)}) collective-permute-start(bf16[2,2,160,128]{3,2,1,0:T(8,128)(2,1)} %get-tuple-element.393), channel_id=1, source_target_pairs={{0,24},{8,0},{16,8},{24,16},{1,25},{9,1},{17,9},{25,17},{2,26},{10... | collective-permute-start | bytes 491528 | tf_op jit(solution)/shard_map/ppermute | solution.py:219
  133.8 272.4 %reduce-scatter.4.cloned.1.call-start = ((), (), s32[]{:S(2)}) async-start(), calls=%async_computation.7 | async-start | bytes 3604480 | tf_op jit(solution)/shard_map/reduce_scatter | solution.py:235
  133.9 24.5 %collective-permute-start.18 = (bf16[256,2048]{1,0:T(8,128)(2,1)S(1)}, bf16[256,2048]{1,0:T(8,128)(2,1)S(1)}, u32[]{:S(2)}, u32[]{:S(2)}) collective-permute-start(bf16[256,2048]{1,0:T(8,128)(2,1)S(1)} %bitcast.83), channel_id=1, source_target_pairs={{0,1},{1,0},{2,3},{3,2},{4,5},{5,4},{6,7},{7,6},{8,9},{9,8},{10,11... | collective-permute-start | bytes 3145736 | tf_op jit(solution)/shard_map/ppermute | solution.py:46
  135.5 24.1 %collective-permute-start.19 = (bf16[256,2048]{1,0:T(8,128)(2,1)S(1)}, bf16[256,2048]{1,0:T(8,128)(2,1)S(1)}, u32[]{:S(2)}, u32[]{:S(2)}) collective-permute-start(bf16[256,2048]{1,0:T(8,128)(2,1)S(1)} %bitcast.84), channel_id=1, source_target_pairs={{0,4},{4,0},{1,5},{5,1},{2,6},{6,2},{3,7},{7,3},{8,12},{12,8},{9,1... | collective-permute-start | bytes 3145736 | tf_op jit(solution)/shard_map/ppermute | solution.py:46
  136.9 22.7 %collective-permute-start.20 = (bf16[256,2048]{1,0:T(8,128)(2,1)S(1)}, bf16[256,2048]{1,0:T(8,128)(2,1)S(1)}, u32[]{:S(2)}, u32[]{:S(2)}) collective-permute-start(bf16[256,2048]{1,0:T(8,128)(2,1)S(1)} %bitcast.85), channel_id=1, source_target_pairs={{0,2},{2,0},{1,3},{3,1},{4,6},{6,4},{5,7},{7,5},{8,10},{10,8},{9,1... | collective-permute-start | bytes 3145736 | tf_op jit(solution)/shard_map/ppermute | solution.py:46
  177.9 26.2 %collective-permute-start.30 = (bf16[256,2048]{1,0:T(8,128)(2,1)S(1)}, bf16[256,2048]{1,0:T(8,128)(2,1)S(1)}, u32[]{:S(2)}, u32[]{:S(2)}) collective-permute-start(bf16[256,2048]{1,0:T(8,128)(2,1)S(1)} %collective-permute-done.19.refs_6_), channel_id=1, source_target_pairs={{0,2},{2,0},{1,3},{3,1},{4,6},{6,4},{5,7},{7,5},{8,10},{10,8},{9,1... | collective-permute-start | bytes 3145736 | tf_op jit(solution)/shard_map/ppermute | solution.py:46
  177.9 26.2 %collective-permute-start.31 = (bf16[256,2048]{1,0:T(8,128)(2,1)S(1)}, bf16[256,2048]{1,0:T(8,128)(2,1)}, u32[]{:S(2)}, u32[]{:S(2)}) collective-permute-start(bf16[256,2048]{1,0:T(8,128)(2,1)S(1)} %collective-permute-done.18.refs_8_), channel_id=1, source_target_pairs={{0,2},{2,0},{1,3},{3,1},{4,6},{6,4},{5,7},{7,5},{8,10},{10,8},{9,1... | collective-permute-start | bytes 3145736 | tf_op jit(solution)/shard_map/ppermute | solution.py:46
  179.5 21.3 %collective-permute-start.28 = (bf16[128,2048]{1,0:T(8,128)(2,1)S(1)}, bf16[128,2048]{1,0:T(8,128)(2,1)S(1)}, u32[]{:S(2)}, u32[]{:S(2)}) collective-permute-start(bf16[128,2048]{1,0:T(8,128)(2,1)S(1)} %get-tuple-element.706), channel_id=1, source_target_pairs={{0,4},{4,0},{1,5},{5,1},{2,6},{6,2},{3,7},{7,3},{8,12},{12,8},{9,1... | collective-permute-start | bytes 1572872 | tf_op jit(solution)/shard_map/ppermute | solution.py:46
  209.7 23.5 %collective-permute-start.32 = (bf16[256,2048]{1,0:T(8,128)(2,1)}, bf16[256,2048]{1,0:T(8,128)(2,1)S(1)}, u32[]{:S(2)}, u32[]{:S(2)}) collective-permute-start(bf16[256,2048]{1,0:T(8,128)(2,1)} %get-tuple-element.457.refs_1_.refs_7_), channel_id=1, source_target_pairs={{0,1},{1,0},{2,3},{3,2},{4,5},{5,4},{6,7},{7,6},{8,9},{9,8},{10,11... | collective-permute-start | bytes 3145736 | tf_op jit(solution)/shard_map/ppermute | solution.py:46
  210.3 23.2 %collective-permute-start.33 = (bf16[256,2048]{1,0:T(8,128)(2,1)}, bf16[256,2048]{1,0:T(8,128)(2,1)}, u32[]{:S(2)}, u32[]{:S(2)}) collective-permute-start(bf16[256,2048]{1,0:T(8,128)(2,1)} %get-tuple-element.457.refs_1_.refs_7_), channel_id=1, source_target_pairs={{0,4},{4,0},{1,5},{5,1},{2,6},{6,2},{3,7},{7,3},{8,12},{12,8},{9,1... | collective-permute-start | bytes 3145736 | tf_op jit(solution)/shard_map/ppermute | solution.py:46
  210.9 22.6 %collective-permute-start.34 = (bf16[256,2048]{1,0:T(8,128)(2,1)}, bf16[256,2048]{1,0:T(8,128)(2,1)S(1)}, u32[]{:S(2)}, u32[]{:S(2)}) collective-permute-start(bf16[256,2048]{1,0:T(8,128)(2,1)} %get-tuple-element.457.refs_1_.refs_7_), channel_id=1, source_target_pairs={{0,2},{2,0},{1,3},{3,1},{4,6},{6,4},{5,7},{7,5},{8,10},{10,8},{9,1... | collective-permute-start | bytes 3145736 | tf_op jit(solution)/shard_map/ppermute | solution.py:46
  251.4 18.6 %collective-permute-start.39 = (bf16[128,2048]{1,0:T(8,128)(2,1)}, bf16[128,2048]{1,0:T(8,128)(2,1)S(1)}, u32[]{:S(2)}, u32[]{:S(2)}) collective-permute-start(bf16[128,2048]{1,0:T(8,128)(2,1)} %collective-permute-done.35.refs_1_.refs_13_), channel_id=1, source_target_pairs={{0,2},{2,0},{1,3},{3,1},{4,6},{6,4},{5,7},{7,5},{8,10},{10,8},{9,1... | collective-permute-start | bytes 1572872 | tf_op jit(solution)/shard_map/ppermute | solution.py:46
  251.4 18.7 %collective-permute-start.40 = (bf16[128,2048]{1,0:T(8,128)(2,1)}, bf16[128,2048]{1,0:T(8,128)(2,1)S(1)}, u32[]{:S(2)}, u32[]{:S(2)}) collective-permute-start(bf16[128,2048]{1,0:T(8,128)(2,1)} %collective-permute-done.36.refs_2_.refs_14_), channel_id=1, source_target_pairs={{0,2},{2,0},{1,3},{3,1},{4,6},{6,4},{5,7},{7,5},{8,10},{10,8},{9,1... | collective-permute-start | bytes 1572872 | tf_op jit(solution)/shard_map/ppermute | solution.py:46
  251.9 18.1 %collective-permute-start.41 = (bf16[128,2048]{1,0:T(8,128)(2,1)S(1)}, bf16[128,2048]{1,0:T(8,128)(2,1)S(1)}, u32[]{:S(2)}, u32[]{:S(2)}) collective-permute-start(bf16[128,2048]{1,0:T(8,128)(2,1)S(1)} %slice.162), channel_id=1, source_target_pairs={{0,1},{1,0},{2,3},{3,2},{4,5},{5,4},{6,7},{7,6},{8,9},{9,8},{10,11... | collective-permute-start | bytes 1572872 | tf_op jit(solution)/shard_map/ppermute | solution.py:46
  270.1 30.1 %collective-permute-start.43 = (bf16[128,2048]{1,0:T(8,128)(2,1)S(1)}, bf16[128,2048]{1,0:T(8,128)(2,1)S(1)}, u32[]{:S(2)}, u32[]{:S(2)}) collective-permute-start(bf16[128,2048]{1,0:T(8,128)(2,1)S(1)} %collective-permute-done.41.refs_6_.refs_10_), channel_id=1, source_target_pairs={{0,2},{2,0},{1,3},{3,1},{4,6},{6,4},{5,7},{7,5},{8,10},{10,8},{9,1... | collective-permute-start | bytes 1572872 | tf_op jit(solution)/shard_map/ppermute | solution.py:46
  270.2 30.0 %collective-permute-start.44 = (bf16[128,2048]{1,0:T(8,128)(2,1)S(1)}, bf16[128,2048]{1,0:T(8,128)(2,1)S(1)}, u32[]{:S(2)}, u32[]{:S(2)}) collective-permute-start(bf16[128,2048]{1,0:T(8,128)(2,1)S(1)} %collective-permute-done.42.refs_7_.refs_11_), channel_id=1, source_target_pairs={{0,2},{2,0},{1,3},{3,1},{4,6},{6,4},{5,7},{7,5},{8,10},{10,8},{9,1... | collective-permute-start | bytes 1572872 | tf_op jit(solution)/shard_map/ppermute | solution.py:46
  339.9 180.6 %reduce-scatter.6.cloned.1.call-start = ((), (), s32[]{:S(2)}) async-start(), calls=%async_computation.8 | async-start | bytes 7208960 | tf_op jit(solution)/shard_map/reduce_scatter | solution.py:235
  345.4 22.2 %collective-permute-start.54 = (bf16[128,2048]{1,0:T(8,128)(2,1)S(1)}, bf16[128,2048]{1,0:T(8,128)(2,1)S(1)}, u32[]{:S(2)}, u32[]{:S(2)}) collective-permute-start(bf16[128,2048]{1,0:T(8,128)(2,1)S(1)} %get-tuple-element.701), channel_id=1, source_target_pairs={{0,4},{4,0},{1,5},{5,1},{2,6},{6,2},{3,7},{7,3},{8,12},{12,8},{9,1... | collective-permute-start | bytes 1572872 | tf_op jit(solution)/shard_map/ppermute | solution.py:46
  347.1 22.1 %collective-permute-start.55 = (bf16[128,2048]{1,0:T(8,128)(2,1)S(1)}, bf16[128,2048]{1,0:T(8,128)(2,1)S(1)}, u32[]{:S(2)}, u32[]{:S(2)}) collective-permute-start(bf16[128,2048]{1,0:T(8,128)(2,1)S(1)} %get-tuple-element.699), channel_id=1, source_target_pairs={{0,1},{1,0},{2,3},{3,2},{4,5},{5,4},{6,7},{7,6},{8,9},{9,8},{10,11... | collective-permute-start | bytes 1572872 | tf_op jit(solution)/shard_map/ppermute | solution.py:46
  376.5 25.0 %collective-permute-start.56 = (bf16[256,2048]{1,0:T(8,128)(2,1)}, bf16[256,2048]{1,0:T(8,128)(2,1)S(1)}, u32[]{:S(2)}, u32[]{:S(2)}) collective-permute-start(bf16[256,2048]{1,0:T(8,128)(2,1)} %get-tuple-element.573.refs_7_.refs_2_), channel_id=1, source_target_pairs={{0,1},{1,0},{2,3},{3,2},{4,5},{5,4},{6,7},{7,6},{8,9},{9,8},{10,11... | collective-permute-start | bytes 3145736 | tf_op jit(solution)/shard_map/ppermute | solution.py:46
  377.2 24.3 %collective-permute-start.57 = (bf16[256,2048]{1,0:T(8,128)(2,1)}, bf16[256,2048]{1,0:T(8,128)(2,1)S(1)}, u32[]{:S(2)}, u32[]{:S(2)}) collective-permute-start(bf16[256,2048]{1,0:T(8,128)(2,1)} %get-tuple-element.573.refs_7_.refs_2_), channel_id=1, source_target_pairs={{0,4},{4,0},{1,5},{5,1},{2,6},{6,2},{3,7},{7,3},{8,12},{12,8},{9,1... | collective-permute-start | bytes 3145736 | tf_op jit(solution)/shard_map/ppermute | solution.py:46
  378.9 22.6 %collective-permute-start.58 = (bf16[256,2048]{1,0:T(8,128)(2,1)}, bf16[256,2048]{1,0:T(8,128)(2,1)S(1)}, u32[]{:S(2)}, u32[]{:S(2)}) collective-permute-start(bf16[256,2048]{1,0:T(8,128)(2,1)} %get-tuple-element.573.refs_7_.refs_2_), channel_id=1, source_target_pairs={{0,2},{2,0},{1,3},{3,1},{4,6},{6,4},{5,7},{7,5},{8,10},{10,8},{9,1... | collective-permute-start | bytes 3145736 | tf_op jit(solution)/shard_map/ppermute | solution.py:46
  433.2 40.5 %collective-permute-start.73 = (bf16[128,2048]{1,0:T(8,128)(2,1)S(1)}, bf16[128,2048]{1,0:T(8,128)(2,1)S(1)}, u32[]{:S(2)}, u32[]{:S(2)}) collective-permute-start(bf16[128,2048]{1,0:T(8,128)(2,1)S(1)} %add_convert_fusion.11), channel_id=1, source_target_pairs={{0,1},{1,0},{2,3},{3,2},{4,5},{5,4},{6,7},{7,6},{8,9},{9,8},{10,11... | collective-permute-start | bytes 1572872 | tf_op jit(solution)/shard_map/ppermute | solution.py:46
  434.4 39.3 %collective-permute-start.74 = (bf16[128,2048]{1,0:T(8,128)(2,1)S(1)}, bf16[128,2048]{1,0:T(8,128)(2,1)S(1)}, u32[]{:S(2)}, u32[]{:S(2)}) collective-permute-start(bf16[128,2048]{1,0:T(8,128)(2,1)S(1)} %add_convert_fusion.10), channel_id=1, source_target_pairs={{0,4},{4,0},{1,5},{5,1},{2,6},{6,2},{3,7},{7,3},{8,12},{12,8},{9,1... | collective-permute-start | bytes 1572872 | tf_op jit(solution)/shard_map/ppermute | solution.py:46
  439.5 34.2 %collective-permute-start.71 = (bf16[2,2,160,128]{3,2,1,0:T(8,128)(2,1)S(1)}, bf16[2,2,160,128]{3,2,1,0:T(8,128)(2,1)S(1)}, u32[]{:S(2)}, u32[]{:S(2)}) collective-permute-start(bf16[2,2,160,128]{3,2,1,0:T(8,128)(2,1)S(1)} %copy-done.79), channel_id=1, source_target_pairs={{0,16},{8,24},{16,0},{24,8},{1,17},{9,25},{17,1},{25,9},{2,18},{10... | collective-permute-start | bytes 491528 | tf_op jit(solution)/shard_map/ppermute | solution.py:219
  440.8 32.9 %collective-permute-start.72 = (bf16[2,2,160,128]{3,2,1,0:T(8,128)(2,1)S(1)}, bf16[2,2,160,128]{3,2,1,0:T(8,128)(2,1)S(1)}, u32[]{:S(2)}, u32[]{:S(2)}) collective-permute-start(bf16[2,2,160,128]{3,2,1,0:T(8,128)(2,1)S(1)} %copy-done.79), channel_id=1, source_target_pairs={{0,8},{8,16},{16,24},{24,0},{1,9},{9,17},{17,25},{25,1},{2,10},{10... | collective-permute-start | bytes 491528 | tf_op jit(solution)/shard_map/ppermute | solution.py:219
  473.7 29.5 %collective-permute-start.75 = (bf16[2,64,2048]{2,1,0:T(8,128)(2,1)}, bf16[2,64,2048]{2,1,0:T(8,128)(2,1)S(1)}, u32[]{:S(2)}, u32[]{:S(2)}) collective-permute-start(bf16[2,64,2048]{2,1,0:T(8,128)(2,1)} %get-tuple-element.632), channel_id=1, source_target_pairs={{0,1},{1,0},{2,3},{3,2},{4,5},{5,4},{6,7},{7,6},{8,9},{9,8},{10,11... | collective-permute-start | bytes 1572872 | tf_op jit(solution)/shard_map/ppermute | solution.py:46
  475.8 27.5 %collective-permute-start.76 = (bf16[128,2048]{1,0:T(8,128)(2,1)S(1)}, bf16[128,2048]{1,0:T(8,128)(2,1)}, u32[]{:S(2)}, u32[]{:S(2)}) collective-permute-start(bf16[128,2048]{1,0:T(8,128)(2,1)S(1)} %get-tuple-element.698), channel_id=1, source_target_pairs={{0,4},{4,0},{1,5},{5,1},{2,6},{6,2},{3,7},{7,3},{8,12},{12,8},{9,1... | collective-permute-start | bytes 1572872 | tf_op jit(solution)/shard_map/ppermute | solution.py:46
  477.5 25.8 %collective-permute-start.77 = (bf16[128,2048]{1,0:T(8,128)(2,1)S(1)}, bf16[128,2048]{1,0:T(8,128)(2,1)}, u32[]{:S(2)}, u32[]{:S(2)}) collective-permute-start(bf16[128,2048]{1,0:T(8,128)(2,1)S(1)} %get-tuple-element.696), channel_id=1, source_target_pairs={{0,1},{1,0},{2,3},{3,2},{4,5},{5,4},{6,7},{7,6},{8,9},{9,8},{10,11... | collective-permute-start | bytes 1572872 | tf_op jit(solution)/shard_map/ppermute | solution.py:46
  478.3 25.0 %collective-permute-start.78 = (bf16[128,2048]{1,0:T(8,128)(2,1)S(1)}, bf16[128,2048]{1,0:T(8,128)(2,1)}, u32[]{:S(2)}, u32[]{:S(2)}) collective-permute-start(bf16[128,2048]{1,0:T(8,128)(2,1)S(1)} %get-tuple-element.697), channel_id=1, source_target_pairs={{0,4},{4,0},{1,5},{5,1},{2,6},{6,2},{3,7},{7,3},{8,12},{12,8},{9,1... | collective-permute-start | bytes 1572872 | tf_op jit(solution)/shard_map/ppermute | solution.py:46
  479.0 31.1 %collective-permute-start.79 = (bf16[128,2048]{1,0:T(8,128)(2,1)S(1)}, bf16[128,2048]{1,0:T(8,128)(2,1)}, u32[]{:S(2)}, u32[]{:S(2)}) collective-permute-start(bf16[128,2048]{1,0:T(8,128)(2,1)S(1)} %get-tuple-element.695), channel_id=1, source_target_pairs={{0,1},{1,0},{2,3},{3,2},{4,5},{5,4},{6,7},{7,6},{8,9},{9,8},{10,11... | collective-permute-start | bytes 1572872 | tf_op jit(solution)/shard_map/ppermute | solution.py:46
  520.5 37.8 %all-to-all-start.2 = ((bf16[8,704,128]{2,1,0:T(8,128)(2,1)}), bf16[8,704,128]{2,1,0:T(8,128)(2,1)S(1)}, u32[]{:S(2)}, u32[]{:S(2)}) async-start(bf16[8,704,128]{2,1,0:T(8,128)(2,1)} %bitcast.79), calls=%async_computation.4 | async-start | bytes 2883584 | tf_op jit(solution)/shard_map/all_to_all | solution.py:198
  524.3 81.1 %reduce-scatter.8.cloned.1.call-start = ((), (), s32[]{:S(2)}) async-start(), calls=%async_computation.9 | async-start | bytes 1310720 | tf_op jit(solution)/shard_map/reduce_scatter | solution.py:235
  526.5 31.8 %collective-permute-start.85 = (bf16[128,2048]{1,0:T(8,128)(2,1)}, bf16[128,2048]{1,0:T(8,128)(2,1)}, u32[]{:S(2)}, u32[]{:S(2)}) collective-permute-start(bf16[128,2048]{1,0:T(8,128)(2,1)} %add_convert_fusion.5), channel_id=1, source_target_pairs={{0,1},{1,0},{2,3},{3,2},{4,5},{5,4},{6,7},{7,6},{8,9},{9,8},{10,11... | collective-permute-start | bytes 1572872 | tf_op jit(solution)/shard_map/ppermute | solution.py:46
  530.5 27.9 %collective-permute-start.86 = (bf16[128,2048]{1,0:T(8,128)(2,1)}, bf16[128,2048]{1,0:T(8,128)(2,1)}, u32[]{:S(2)}, u32[]{:S(2)}) collective-permute-start(bf16[128,2048]{1,0:T(8,128)(2,1)} %add_convert_fusion.4), channel_id=1, source_target_pairs={{0,4},{4,0},{1,5},{5,1},{2,6},{6,2},{3,7},{7,3},{8,12},{12,8},{9,1... | collective-permute-start | bytes 1572872 | tf_op jit(solution)/shard_map/ppermute | solution.py:46
  537.6 20.7 %collective-permute-start.88 = (bf16[8,160,128]{2,1,0:T(8,128)(2,1)}, bf16[8,160,128]{2,1,0:T(8,128)(2,1)}, u32[]{:S(2)}, u32[]{:S(2)}) collective-permute-start(bf16[8,160,128]{2,1,0:T(8,128)(2,1)} %get-tuple-element.709), channel_id=1, source_target_pairs={{0,16},{8,24},{16,0},{24,8},{1,17},{9,25},{17,1},{25,9},{2,18},{10... | collective-permute-start | bytes 983048 | tf_op jit(solution)/shard_map/ppermute | solution.py:219
  (141 other events, 1589.4 us)
Sparse Core Ops, SparseCore 0:
  9.6 52.4 all-gather.6
  63.6 70.1 all-gather.8
  136.0 105.6 all-gather.10
  340.0 56.0 reduce-scatter.3
  406.3 113.6 reduce-scatter.5
  578.6 26.1 reduce-scatter.7

commit v5 on v4

--- a/solution.py
+++ b/solution.py
@@ -246,7 +246,10 @@
 
 
 def entering_line(total, reverse):
-    return [turn(total, -k if reverse else k) for k in (1, 2, 3)]
+    z, sign = lax.axis_index("z"), -1 if reverse else 1
+    one = turn(total, sign)
+    there = z < 3 if reverse else z > 0
+    return [one, turn(plus(total, jnp.where(there, one, 0)), 2 * sign)]
 
 
 def feature_maps():

time: 623 us -> 617 us (level)
  waiting for transfers between devices: 216 us -> 207 us
    all_gather x3, waiting for transfers between devices: 8.04 us -> 1.65 us  [line_gather(): return lax.all_gather(a, 'z')]
    ppermute x12 -> x10, waiting for transfers between devices: 93 us -> 87.5 us  [turn(): return lax.ppermute(a, 'z', [(i, (i + k) % 4) for i in range(4)])]
    convert_element_type x16 -> x18, other arithmetic: 18.8 us -> 21.5 us  [plus(): functools.reduce(jnp.add, [t.astype(F32) for t in terms]).astype(BF16)]
    ppermute x12 -> x10, starting transfers between devices: 30 us -> 27.6 us  [turn(): return lax.ppermute(a, 'z', [(i, (i + k) % 4) for i in range(4)])]
  transfers between devices with their start and end apart: 104 -> 102, of which waited for: 41 -> 40; matrix products, arithmetic and copies ran while one was open for 5% -> 5% of each run, Pallas kernels for 39% -> 39%
where the time goes in v5:
time: 617 us; the launch traced here: 608 us
  Pallas kernels  240 us (39%)
  waiting for transfers between devices  207 us (34%)
  starting transfers between devices  97.6 us (16%)
  other arithmetic  27.7 us (4%)
  local copies, waits for them, and re-layouts  20.2 us (3%)
  between operations  15.9 us (3%)
    pallas_call x25, Pallas kernels, call(): pl.pallas_call(body, out_shape=tuple((pltpu.HBM(s, t) for s, t in outs)),...  240 us
    ppermute x82, waiting for transfers between devices, swap(): return lax.ppermute(a, axis, [(0, 1), (1, 0)])  109 us
    ppermute x10, waiting for transfers between devices, turn(): return lax.ppermute(a, 'z', [(i, (i + k) % 4) for i in range(4)])  87.5 us
    ppermute x82, starting transfers between devices, swap(): return lax.ppermute(a, axis, [(0, 1), (1, 0)])  53.7 us
    ppermute x10, starting transfers between devices, turn(): return lax.ppermute(a, 'z', [(i, (i + k) % 4) for i in range(4)])  27.6 us
    convert_element_type x18, other arithmetic, plus(): functools.reduce(jnp.add, [t.astype(F32) for t in terms]).astype(BF16)  21.5 us
    all_to_all x4, starting transfers between devices, exchange(): return lax.all_to_all(slabs, axes, 0, 0, tiled=True)  15.9 us
  transfers between devices with their start and end apart: 102, of which 40 were waited for; matrix products, arithmetic and copies ran while one was open for 5% of the time, Pallas kernels for 39%

profile of v5, /device:TPU:0, one launch (start us, length us, event | category | flops | bytes accessed | tf_op | source)
XLA Modules:
  0.0 608.3 jit_solution(4395806203605804732)
XLA Ops:
  11.9 5.2 all-to-all-start
  17.8 6.4 %all-to-all-done.refs_1_ = bf16[8,176,128]{2,1,0:T(8,128)(2,1)S(1)} async-done(((bf16[8,176,128]{2,1,0:T(8,128)(2,1)}), bf16[8,176,128]{2,1,0:T(8,128)(2,1)S(1)}, u32[]{:S(2)}, u32[]{:S(2)}) %all-to-all-start) | async-done | bytes 360480 | tf_op jit(solution)/shard_map/all_to_all | solution.py:198
  34.2 10.8 %collective-permute-done.refs_2_ = bf16[8,176,128]{2,1,0:T(8,128)(2,1)} collective-permute-done((bf16[8,176,128]{2,1,0:T(8,128)(2,1)S(1)}, bf16[8,176,128]{2,1,0:T(8,128)(2,1)}, u32[]{:S(2)}, u32[]{:S(2)}) %collective-permute-start) | collective-permute-done | bytes 360480 | tf_op jit(solution)/shard_map/ppermute | solution.py:219
  45.1 18.7 %collective-permute-done.1.refs_3_ = bf16[8,176,128]{2,1,0:T(8,128)(2,1)} collective-permute-done((bf16[8,176,128]{2,1,0:T(8,128)(2,1)S(1)}, bf16[8,176,128]{2,1,0:T(8,128)(2,1)}, u32[]{:S(2)}, u32[]{:S(2)}) %collective-permute-start.1) | collective-permute-done | bytes 360480 | tf_op jit(solution)/shard_map/ppermute | solution.py:219
  70.0 3.4 shard_map.221.refs_1_.refs_13_
  73.5 11.7 %shard_map.222 = (f32[6,256,128]{2,1,0:T(8,128)}, bf16[6,256,256]{2,1,0:T(8,128)(2,1)}, bf16[2,2,160,128]{3,2,1,0:T(8,128)(2,1)}) custom-call(s32[12]{0:T(128)S(1)} %concatenate.20.refs_0_, bf16[384,2048]{1,0:T(8,128)(2,1)} %shard_map.221.refs_1_.refs_13_, bf16[256,2048]{1,0:T(8,128)(2,1)} %bitcast.18.refs_2_.refs_0_, ...), custom_call_target="tpu_custom_call" | custom-call | flops 2415919104 | bytes 10125360 | tf_op jit(solution)/shard_map/pallas_call | solution.py:829
  85.2 3.6 all-to-all-start.1
  93.5 6.0 shard_map.224
  99.5 8.2 %collective-permute-start.12 = (bf16[2,2,160,128]{3,2,1,0:T(8,128)(2,1)}, bf16[2,2,160,128]{3,2,1,0:T(8,128)(2,1)S(1)}, u32[]{:S(2)}, u32[]{:S(2)}) collective-permute-start(bf16[2,2,160,128]{3,2,1,0:T(8,128)(2,1)} %get-tuple-element.391), channel_id=1, source_target_pairs={{0,8},{8,16},{16,24},{24,0},{1,9},{9,17},{17,25},{25,1},{2,10},{10... | collective-permute-start | bytes 491528 | tf_op jit(solution)/shard_map/ppermute | solution.py:219
  109.6 7.6 %collective-permute-done.12.refs_5_ = bf16[2,2,160,128]{3,2,1,0:T(8,128)(2,1)S(1)} collective-permute-done((bf16[2,2,160,128]{3,2,1,0:T(8,128)(2,1)}, bf16[2,2,160,128]{3,2,1,0:T(8,128)(2,1)S(1)}, u32[]{:S(2)}, u32[]{:S(2)}) %collective-permute-start.12) | collective-permute-done | bytes 163872 | tf_op jit(solution)/shard_map/ppermute | solution.py:219
  118.2 4.0 collective-permute-start.13
  122.3 9.3 %collective-permute-done.13.refs_6_ = bf16[2,2,160,128]{3,2,1,0:T(8,128)(2,1)S(1)} collective-permute-done((bf16[2,2,160,128]{3,2,1,0:T(8,128)(2,1)S(1)}, bf16[2,2,160,128]{3,2,1,0:T(8,128)(2,1)S(1)}, u32[]{:S(2)}, u32[]{:S(2)}) %collective-permute-start.13) | collective-permute-done | bytes 163872 | tf_op jit(solution)/shard_map/ppermute | solution.py:219
  138.6 14.1 %shard_map.226 = (bf16[8,256,256]{2,1,0:T(8,128)(2,1)}, f32[8,256,128]{2,1,0:T(8,128)}, bf16[8,2,256,256]{3,2,1,0:T(8,128)(2,1)}, bf16[256,2048]{1,0:T(8,128)(2,...) custom-call(s32[12]{0:T(128)S(1)} %concatenate.20.refs_0_, ...), custom_call_target="tpu_custom_call" | custom-call | flops 2147483648 | bytes 17104944 | tf_op jit(solution)/shard_map/pallas_call | solution.py:829
  162.9 10.9 %collective-permute-done.20 = bf16[128,2048]{1,0:T(8,128)(2,1)S(1)} collective-permute-done((bf16[128,2048]{1,0:T(8,128)(2,1)S(1)}, bf16[128,2048]{1,0:T(8,128)(2,1)S(1)}, u32[]{:S(2)}, u32[]{:S(2)}) %collective-permute-start.20) | collective-permute-done | bytes 524320 | tf_op jit(solution)/shard_map/ppermute | solution.py:46
  179.6 11.1 %collective-permute-done.25.refs_5_ = bf16[128,2048]{1,0:T(8,128)(2,1)S(1)} collective-permute-done((bf16[128,2048]{1,0:T(8,128)(2,1)S(1)}, bf16[128,2048]{1,0:T(8,128)(2,1)S(1)}, u32[]{:S(2)}, u32[]{:S(2)}) %collective-permute-start.25) | collective-permute-done | bytes 524320 | tf_op jit(solution)/shard_map/ppermute | solution.py:46
  193.2 6.9 %collective-permute-done.27.refs_3_ = bf16[128,2048]{1,0:T(8,128)(2,1)S(1)} collective-permute-done((bf16[128,2048]{1,0:T(8,128)(2,1)S(1)}, bf16[128,2048]{1,0:T(8,128)(2,1)S(1)}, u32[]{:S(2)}, u32[]{:S(2)}) %collective-permute-start.27) | collective-permute-done | bytes 524320 | tf_op jit(solution)/shard_map/ppermute | solution.py:46
  200.1 3.4 collective-permute-done.28.refs_6_
  204.3 5.0 shard_map.227
  210.6 22.2 %collective-permute-done.31.refs_3_.refs_11_ = bf16[256,2048]{1,0:T(8,128)(2,1)S(1)} collective-permute-done((bf16[256,2048]{1,0:T(8,128)(2,1)}, bf16[256,2048]{1,0:T(8,128)(2,1)S(1)}, u32[]{:S(2)}, u32[]{:S(2)}) %collective-permute-start.31) | collective-permute-done | bytes 1048608 | tf_op jit(solution)/shard_map/ppermute | solution.py:46
  238.8 7.5 %shard_map.228.refs_3_.refs_5_ = bf16[1408,2048]{1,0:T(8,128)(2,1)} custom-call(s32[12]{0:T(128)S(1)} %concatenate.20.refs_0_, bf16[4,8,704,128]{3,2,1,0:T(8,128)(2,1)} %bitcast.75), custom_call_target="tpu_custom_call" | custom-call | bytes 11534384 | tf_op jit(solution)/shard_map/pallas_call | solution.py:829
  246.3 3.5 collective-permute-done.34.refs_1_.refs_13_
  252.6 17.0 %shard_map.229 = (bf16[256,2048]{1,0:T(8,128)(2,1)}, bf16[256,2048]{1,0:T(8,128)(2,1)}, bf16[256,2048]{1,0:T(8,128)(2,1)}, bf16[256,2048]{1,0:T(8,128)(2,1)}, bf...) custom-call(s32[12]{0:T(128)S(1)} %concatenate.20.refs_0_, ...), custom_call_target="tpu_custom_call" | custom-call | flops 8858370048 | bytes 19202096 | tf_op jit(solution)/shard_map/pallas_call | solution.py:829
  270.3 29.4 %shard_map.230 = (bf16[256,2048]{1,0:T(8,128)(2,1)}, bf16[256,2048]{1,0:T(8,128)(2,1)}, bf16[256,2048]{1,0:T(8,128)(2,1)}, bf16[256,2048]{1,0:T(8,128)(2,1)}, bf...) custom-call(s32[12]{0:T(128)S(1)} %concatenate.20.refs_0_, ...), custom_call_target="tpu_custom_call" | custom-call | flops 17716740096 | bytes 29753392 | tf_op jit(solution)/shard_map/pallas_call | solution.py:829
  300.8 17.1 %shard_map.231 = (bf16[128,2048]{1,0:T(8,128)(2,1)}, bf16[128,2048]{1,0:T(8,128)(2,1)}, bf16[128,2048]{1,0:T(8,128)(2,1)}, bf16[128,2048]{1,0:T(8,128)(2,1)}, bf...) custom-call(s32[12]{0:T(128)S(1)} %concatenate.20.refs_0_, ...), custom_call_target="tpu_custom_call" | custom-call | flops 8858370048 | bytes 19202096 | tf_op jit(solution)/shard_map/pallas_call | solution.py:829
  325.6 13.9 %shard_map.232 = bf16[704,2048]{1,0:T(8,128)(2,1)} custom-call(s32[12]{0:T(128)S(1)} %concatenate.20.refs_0_, bf16[512,704]{1,0:T(8,128)(2,1)} %get-tuple-element.550.refs_1_, bf16[1024,704]{1,0:T(8,128)(2,1)} %get-tuple-element.551.refs_2_, bf16[512,704]{1,0:T(8,128)(2,1)} %get-tuple-element.552.refs_3_, bf16[256,2048]{1,0:T(8,128)(2,1)} %bitcast.81, ...), custom_call_target="tpu_custom_call" | custom-call | flops 5905580032 | bytes 14155824 | tf_op jit(solution)/shard_map/pallas_call | solution.py:829
  348.4 9.1 %collective-permute-done.51.refs_4_ = bf16[128,2048]{1,0:T(8,128)(2,1)S(1)} collective-permute-done((bf16[128,2048]{1,0:T(8,128)(2,1)S(1)}, bf16[128,2048]{1,0:T(8,128)(2,1)S(1)}, u32[]{:S(2)}, u32[]{:S(2)}) %collective-permute-start.51) | collective-permute-done | bytes 524320 | tf_op jit(solution)/shard_map/ppermute | solution.py:46
  359.6 7.8 %collective-permute-done.53.refs_6_ = bf16[128,2048]{1,0:T(8,128)(2,1)S(1)} collective-permute-done((bf16[128,2048]{1,0:T(8,128)(2,1)S(1)}, bf16[128,2048]{1,0:T(8,128)(2,1)S(1)}, u32[]{:S(2)}, u32[]{:S(2)}) %collective-permute-start.53) | collective-permute-done | bytes 524320 | tf_op jit(solution)/shard_map/ppermute | solution.py:46
  369.7 6.5 %shard_map.233 = (f32[256,2048]{1,0:T(8,128)}, bf16[256,2048]{1,0:T(8,128)(2,1)}) custom-call(bf16[256,2048]{1,0:T(8,128)(2,1)} %bitcast.82, f32[256,2048]{1,0:T(8,128)} %get-tuple-element.444.refs_1_.refs_0_, bf16[256,2048]{1,0:T(8,128)(2,1)} %get-tuple-element.528.refs_2_, bf16[256,2048]{1,0:T(8,128)(2,1)} %copy-done.20, bf16[128,2048]{1,0:T(8,128)(2,1)} %copy-done.30, ...), custom_call_target="tpu_custom_call" | custom-call | bytes 10485760 | tf_op jit(solution)/shard_map/pallas_call | solution.py:829
  378.5 22.7 %shard_map.234 = bf16[32,704,128]{2,1,0:T(8,128)(2,1)} custom-call(s32[12]{0:T(128)S(1)} %concatenate.20.refs_0_, bf16[512,704]{1,0:T(8,128)(2,1)} %get-tuple-element.564.refs_1_, bf16[1024,704]{1,0:T(8,128)(2,1)} %get-tuple-element.565.refs_2_, bf16[512,704]{1,0:T(8,128)(2,1)} %get-tuple-element.566.refs_3_, bf16[512,704]{1,0:T(8,128)(2,1)} %get-tuple-element.567.refs_4_, ...), custom_call_target="tpu_custom_call" | custom-call | flops 11811160064 | bytes 19922992 | tf_op jit(solution)/shard_map/pallas_call | solution.py:829
  401.9 2.9 collective-permute-done.58.refs_10_.refs_5_
  408.0 13.4 %shard_map.235 = (bf16[6,256,256]{2,1,0:T(8,128)(2,1)}, f32[6,256,128]{2,1,0:T(8,128)}, bf16[2,2,160,128]{3,2,1,0:T(8,128)(2,1)}) custom-call(s32[12]{0:T(128)S(1)} %concatenate.20.refs_0_, bf16[256,2048]{1,0:T(8,128)(2,1)} %shard_map.225.refs_9_.refs_1_, f32[6,256,128]{2,1,0:T(8,128)} %get-tuple-element.372.refs_1_.refs_2_, ...), custom_call_target="tpu_custom_call" | custom-call | flops 1610612736 | bytes 12746800 | tf_op jit(solution)/shard_map/pallas_call | solution.py:829
  425.4 7.3 %shard_map.236 = (bf16[2,256,256]{2,1,0:T(8,128)(2,1)}, f32[2,256,128]{2,1,0:T(8,128)}, bf16[2,2,160,128]{3,2,1,0:T(8,128)(2,1)}) custom-call(s32[12]{0:T(128)S(1)} %concatenate.20.refs_0_, bf16[256,2048]{1,0:T(8,128)(2,1)} %shard_map.225.refs_9_.refs_1_, f32[6,256,128]{2,1,0:T(8,128)} %get-tuple-element.372.refs_1_.refs_2_, ...), custom_call_target="tpu_custom_call" | custom-call | flops 536870912 | bytes 7667760 | tf_op jit(solution)/shard_map/pallas_call | solution.py:829
  438.2 9.2 %collective-permute-done.69.refs_10_ = bf16[2,2,160,128]{3,2,1,0:T(8,128)(2,1)S(1)} collective-permute-done((bf16[2,2,160,128]{3,2,1,0:T(8,128)(2,1)}, bf16[2,2,160,128]{3,2,1,0:T(8,128)(2,1)S(1)}, u32[]{:S(2)}, u32[]{:S(2)}) %collective-permute-start.69) | collective-permute-done | bytes 163872 | tf_op jit(solution)/shard_map/ppermute | solution.py:219
  447.6 6.1 shard_map.237
  453.7 13.7 %collective-permute-done.70.refs_11_ = bf16[2,2,160,128]{3,2,1,0:T(8,128)(2,1)S(1)} collective-permute-done((bf16[2,2,160,128]{3,2,1,0:T(8,128)(2,1)S(1)}, bf16[2,2,160,128]{3,2,1,0:T(8,128)(2,1)S(1)}, u32[]{:S(2)}, u32[]{:S(2)}) %collective-permute-start.70) | collective-permute-done | bytes 163872 | tf_op jit(solution)/shard_map/ppermute | solution.py:219
  473.8 22.5 %shard_map.238 = (bf16[8,256,384]{2,1,0:T(8,128)(2,1)}, bf16[256,2048]{1,0:T(8,128)(2,1)}, bf16[256,2048]{1,0:T(8,128)(2,1)}, bf16[256,2048]{1,0:T(8,128)(2,1)},...) custom-call(s32[12]{0:T(128)S(1)} %concatenate.20.refs_0_, ...), custom_call_target="tpu_custom_call" | custom-call | flops 3221225472 | bytes 18677808 | tf_op jit(solution)/shard_map/pallas_call | solution.py:829
  496.4 7.8 %collective-permute-done.77.refs_6_ = bf16[128,2048]{1,0:T(8,128)(2,1)} collective-permute-done((bf16[128,2048]{1,0:T(8,128)(2,1)S(1)}, bf16[128,2048]{1,0:T(8,128)(2,1)}, u32[]{:S(2)}, u32[]{:S(2)}) %collective-permute-start.77) | collective-permute-done | bytes 524320 | tf_op jit(solution)/shard_map/ppermute | solution.py:46
  505.2 8.5 %shard_map.239 = bf16[4,8,160,128]{3,2,1,0:T(8,128)(2,1)} custom-call(s32[12]{0:T(128)S(1)} %concatenate.20.refs_0_, bf16[8,256,384]{2,1,0:T(8,128)(2,1)} %get-tuple-element.641.refs_1_, bf16[256,2048]{1,0:T(8,128)(2,1)} %bitcast.18.refs_2_.refs_0_, bf16[256,2048]{1,0:T(8,128)(2,1)} %collective-permute-done.5.refs_3_, ...), custom_call_target="tpu_custom_call" | custom-call | flops 3221225472 | bytes 11272240 | tf_op jit(solution)/shard_map/pallas_call | solution.py:829
  514.6 3.7 all-to-all-start.2
  527.1 4.3 collective-permute-start.85
  534.3 5.6 collective-permute-done.85.refs_1_
  539.9 12.5 %collective-permute-done.86.refs_2_ = bf16[8,160,128]{2,1,0:T(8,128)(2,1)} collective-permute-done((bf16[8,160,128]{2,1,0:T(8,128)(2,1)}, bf16[8,160,128]{2,1,0:T(8,128)(2,1)}, u32[]{:S(2)}, u32[]{:S(2)}) %collective-permute-start.86) | collective-permute-done | bytes 327712 | tf_op jit(solution)/shard_map/ppermute | solution.py:219
  552.5 3.3 add_convert_fusion.1
  559.4 3.5 collective-permute-start.91
  563.6 4.2 shard_map.241
  576.8 3.4 all-to-all-start.3
  582.2 4.5 shard_map.243
  593.2 5.6 shard_map.244
  (412 shorter events, 146.9 us)
Async XLA Ops:
  7.2 56.7 %all-gather.7.cloned.1.call-start = ((), (), s32[]{:S(2)}) async-start(), calls=%async_computation.10 | async-start | bytes 1310720 | tf_op jit(solution)/shard_map/all_gather | solution.py:231
  17.1 114.6 %all-gather.9.cloned.1.call-start = ((), (), s32[]{:S(2)}) async-start(), calls=%async_computation.11 | async-start | bytes 3604480 | tf_op jit(solution)/shard_map/all_gather | solution.py:231
  24.2 20.9 %collective-permute-start = (bf16[8,176,128]{2,1,0:T(8,128)(2,1)S(1)}, bf16[8,176,128]{2,1,0:T(8,128)(2,1)}, u32[]{:S(2)}, u32[]{:S(2)}) collective-permute-start(bf16[8,176,128]{2,1,0:T(8,128)(2,1)S(1)} %all-to-all-done.refs_1_), channel_id=1, source_target_pairs={{0,8},{8,16},{16,24},{24,0},{1,9},{9,17},{17,25},{25,1},{2,10},{10... | collective-permute-start | bytes 1081352 | tf_op jit(solution)/shard_map/ppermute | solution.py:219
  25.8 38.0 %collective-permute-start.1 = (bf16[8,176,128]{2,1,0:T(8,128)(2,1)S(1)}, bf16[8,176,128]{2,1,0:T(8,128)(2,1)}, u32[]{:S(2)}, u32[]{:S(2)}) collective-permute-start(bf16[8,176,128]{2,1,0:T(8,128)(2,1)S(1)} %all-to-all-done.refs_1_), channel_id=1, source_target_pairs={{0,16},{8,24},{16,0},{24,8},{1,17},{9,25},{17,1},{25,9},{2,18},{10... | collective-permute-start | bytes 1081352 | tf_op jit(solution)/shard_map/ppermute | solution.py:219
  28.4 35.5 %collective-permute-start.2 = (bf16[8,176,128]{2,1,0:T(8,128)(2,1)S(1)}, bf16[8,176,128]{2,1,0:T(8,128)(2,1)}, u32[]{:S(2)}, u32[]{:S(2)}) collective-permute-start(bf16[8,176,128]{2,1,0:T(8,128)(2,1)S(1)} %all-to-all-done.refs_1_), channel_id=1, source_target_pairs={{0,24},{8,0},{16,8},{24,16},{1,25},{9,1},{17,9},{25,17},{2,26},{10... | collective-permute-start | bytes 1081352 | tf_op jit(solution)/shard_map/ppermute | solution.py:219
  29.7 34.1 %collective-permute-start.3 = (bf16[256,2048]{1,0:T(8,128)(2,1)}, bf16[256,2048]{1,0:T(8,128)(2,1)}, u32[]{:S(2)}, u32[]{:S(2)}) collective-permute-start(bf16[256,2048]{1,0:T(8,128)(2,1)} %bitcast.18.refs_2_.refs_0_), channel_id=1, source_target_pairs={{0,1},{1,0},{2,3},{3,2},{4,5},{5,4},{6,7},{7,6},{8,9},{9,8},{10,11... | collective-permute-start | bytes 3145736 | tf_op jit(solution)/shard_map/ppermute | solution.py:46
  31.1 32.7 %collective-permute-start.4 = (bf16[256,2048]{1,0:T(8,128)(2,1)}, bf16[256,2048]{1,0:T(8,128)(2,1)}, u32[]{:S(2)}, u32[]{:S(2)}) collective-permute-start(bf16[256,2048]{1,0:T(8,128)(2,1)} %bitcast.18.refs_2_.refs_0_), channel_id=1, source_target_pairs={{0,4},{4,0},{1,5},{5,1},{2,6},{6,2},{3,7},{7,3},{8,12},{12,8},{9,1... | collective-permute-start | bytes 3145736 | tf_op jit(solution)/shard_map/ppermute | solution.py:46
  66.7 18.5 %collective-permute-start.8 = (bf16[128,2048]{1,0:T(8,128)(2,1)S(1)}, bf16[128,2048]{1,0:T(8,128)(2,1)S(1)}, u32[]{:S(2)}, u32[]{:S(2)}) collective-permute-start(bf16[128,2048]{1,0:T(8,128)(2,1)S(1)} %slice.150), channel_id=1, source_target_pairs={{0,1},{1,0},{2,3},{3,2},{4,5},{5,4},{6,7},{7,6},{8,9},{9,8},{10,11... | collective-permute-start | bytes 1572872 | tf_op jit(solution)/shard_map/ppermute | solution.py:46
  85.2 46.4 %all-to-all-start.1 = ((bf16[8,704,128]{2,1,0:T(8,128)(2,1)}), bf16[8,704,128]{2,1,0:T(8,128)(2,1)S(1)}, u32[]{:S(2)}, u32[]{:S(2)}) async-start(bf16[8,704,128]{2,1,0:T(8,128)(2,1)} %bitcast.23), calls=%async_computation.1 | async-start | bytes 2883584 | tf_op jit(solution)/shard_map/all_to_all | solution.py:198
  88.8 150.0 %all-gather.11.cloned.1.call-start = ((), (), s32[]{:S(2)}) async-start(), calls=%async_computation.12 | async-start | bytes 7208960 | tf_op jit(solution)/shard_map/all_gather | solution.py:231
  107.7 23.8 %collective-permute-start.14 = (bf16[2,64,2048]{2,1,0:T(8,128)(2,1)}, bf16[2,64,2048]{2,1,0:T(8,128)(2,1)S(1)}, u32[]{:S(2)}, u32[]{:S(2)}) collective-permute-start(bf16[2,64,2048]{2,1,0:T(8,128)(2,1)} %get-tuple-element.392), channel_id=1, source_target_pairs={{0,1},{1,0},{2,3},{3,2},{4,5},{5,4},{6,7},{7,6},{8,9},{9,8},{10,11... | collective-permute-start | bytes 1572872 | tf_op jit(solution)/shard_map/ppermute | solution.py:46
  132.7 273.0 %reduce-scatter.4.cloned.1.call-start = ((), (), s32[]{:S(2)}) async-start(), calls=%async_computation.7 | async-start | bytes 3604480 | tf_op jit(solution)/shard_map/reduce_scatter | solution.py:235
  132.8 25.0 %collective-permute-start.17 = (bf16[256,2048]{1,0:T(8,128)(2,1)S(1)}, bf16[256,2048]{1,0:T(8,128)(2,1)S(1)}, u32[]{:S(2)}, u32[]{:S(2)}) collective-permute-start(bf16[256,2048]{1,0:T(8,128)(2,1)S(1)} %bitcast.83), channel_id=1, source_target_pairs={{0,1},{1,0},{2,3},{3,2},{4,5},{5,4},{6,7},{7,6},{8,9},{9,8},{10,11... | collective-permute-start | bytes 3145736 | tf_op jit(solution)/shard_map/ppermute | solution.py:46
  134.3 24.6 %collective-permute-start.18 = (bf16[256,2048]{1,0:T(8,128)(2,1)S(1)}, bf16[256,2048]{1,0:T(8,128)(2,1)S(1)}, u32[]{:S(2)}, u32[]{:S(2)}) collective-permute-start(bf16[256,2048]{1,0:T(8,128)(2,1)S(1)} %bitcast.84), channel_id=1, source_target_pairs={{0,4},{4,0},{1,5},{5,1},{2,6},{6,2},{3,7},{7,3},{8,12},{12,8},{9,1... | collective-permute-start | bytes 3145736 | tf_op jit(solution)/shard_map/ppermute | solution.py:46
  135.8 23.2 %collective-permute-start.19 = (bf16[256,2048]{1,0:T(8,128)(2,1)S(1)}, bf16[256,2048]{1,0:T(8,128)(2,1)S(1)}, u32[]{:S(2)}, u32[]{:S(2)}) collective-permute-start(bf16[256,2048]{1,0:T(8,128)(2,1)S(1)} %bitcast.85), channel_id=1, source_target_pairs={{0,2},{2,0},{1,3},{3,1},{4,6},{6,4},{5,7},{7,5},{8,10},{10,8},{9,1... | collective-permute-start | bytes 3145736 | tf_op jit(solution)/shard_map/ppermute | solution.py:46
  177.3 26.2 %collective-permute-start.29 = (bf16[256,2048]{1,0:T(8,128)(2,1)S(1)}, bf16[256,2048]{1,0:T(8,128)(2,1)S(1)}, u32[]{:S(2)}, u32[]{:S(2)}) collective-permute-start(bf16[256,2048]{1,0:T(8,128)(2,1)S(1)} %collective-permute-done.18.refs_6_), channel_id=1, source_target_pairs={{0,2},{2,0},{1,3},{3,1},{4,6},{6,4},{5,7},{7,5},{8,10},{10,8},{9,1... | collective-permute-start | bytes 3145736 | tf_op jit(solution)/shard_map/ppermute | solution.py:46
  177.3 26.2 %collective-permute-start.30 = (bf16[256,2048]{1,0:T(8,128)(2,1)S(1)}, bf16[256,2048]{1,0:T(8,128)(2,1)}, u32[]{:S(2)}, u32[]{:S(2)}) collective-permute-start(bf16[256,2048]{1,0:T(8,128)(2,1)S(1)} %collective-permute-done.17.refs_8_), channel_id=1, source_target_pairs={{0,2},{2,0},{1,3},{3,1},{4,6},{6,4},{5,7},{7,5},{8,10},{10,8},{9,1... | collective-permute-start | bytes 3145736 | tf_op jit(solution)/shard_map/ppermute | solution.py:46
  178.9 21.1 %collective-permute-start.27 = (bf16[128,2048]{1,0:T(8,128)(2,1)S(1)}, bf16[128,2048]{1,0:T(8,128)(2,1)S(1)}, u32[]{:S(2)}, u32[]{:S(2)}) collective-permute-start(bf16[128,2048]{1,0:T(8,128)(2,1)S(1)} %get-tuple-element.702), channel_id=1, source_target_pairs={{0,4},{4,0},{1,5},{5,1},{2,6},{6,2},{3,7},{7,3},{8,12},{12,8},{9,1... | collective-permute-start | bytes 1572872 | tf_op jit(solution)/shard_map/ppermute | solution.py:46
  209.3 23.5 %collective-permute-start.31 = (bf16[256,2048]{1,0:T(8,128)(2,1)}, bf16[256,2048]{1,0:T(8,128)(2,1)S(1)}, u32[]{:S(2)}, u32[]{:S(2)}) collective-permute-start(bf16[256,2048]{1,0:T(8,128)(2,1)} %get-tuple-element.454.refs_1_.refs_7_), channel_id=1, source_target_pairs={{0,1},{1,0},{2,3},{3,2},{4,5},{5,4},{6,7},{7,6},{8,9},{9,8},{10,11... | collective-permute-start | bytes 3145736 | tf_op jit(solution)/shard_map/ppermute | solution.py:46
  210.0 23.2 %collective-permute-start.32 = (bf16[256,2048]{1,0:T(8,128)(2,1)}, bf16[256,2048]{1,0:T(8,128)(2,1)}, u32[]{:S(2)}, u32[]{:S(2)}) collective-permute-start(bf16[256,2048]{1,0:T(8,128)(2,1)} %get-tuple-element.454.refs_1_.refs_7_), channel_id=1, source_target_pairs={{0,4},{4,0},{1,5},{5,1},{2,6},{6,2},{3,7},{7,3},{8,12},{12,8},{9,1... | collective-permute-start | bytes 3145736 | tf_op jit(solution)/shard_map/ppermute | solution.py:46
  210.6 22.6 %collective-permute-start.33 = (bf16[256,2048]{1,0:T(8,128)(2,1)}, bf16[256,2048]{1,0:T(8,128)(2,1)S(1)}, u32[]{:S(2)}, u32[]{:S(2)}) collective-permute-start(bf16[256,2048]{1,0:T(8,128)(2,1)} %get-tuple-element.454.refs_1_.refs_7_), channel_id=1, source_target_pairs={{0,2},{2,0},{1,3},{3,1},{4,6},{6,4},{5,7},{7,5},{8,10},{10,8},{9,1... | collective-permute-start | bytes 3145736 | tf_op jit(solution)/shard_map/ppermute | solution.py:46
  233.2 17.9 %collective-permute-start.36 = (bf16[256,2048]{1,0:T(8,128)(2,1)}, bf16[256,2048]{1,0:T(8,128)(2,1)}, u32[]{:S(2)}, u32[]{:S(2)}) collective-permute-start(bf16[256,2048]{1,0:T(8,128)(2,1)} %collective-permute-done.32.refs_1_.refs_9_), channel_id=1, source_target_pairs={{0,2},{2,0},{1,3},{3,1},{4,6},{6,4},{5,7},{7,5},{8,10},{10,8},{9,1... | collective-permute-start | bytes 3145736 | tf_op jit(solution)/shard_map/ppermute | solution.py:46
  251.0 18.6 %collective-permute-start.38 = (bf16[128,2048]{1,0:T(8,128)(2,1)}, bf16[128,2048]{1,0:T(8,128)(2,1)S(1)}, u32[]{:S(2)}, u32[]{:S(2)}) collective-permute-start(bf16[128,2048]{1,0:T(8,128)(2,1)} %collective-permute-done.34.refs_1_.refs_13_), channel_id=1, source_target_pairs={{0,2},{2,0},{1,3},{3,1},{4,6},{6,4},{5,7},{7,5},{8,10},{10,8},{9,1... | collective-permute-start | bytes 1572872 | tf_op jit(solution)/shard_map/ppermute | solution.py:46
  251.0 18.6 %collective-permute-start.39 = (bf16[128,2048]{1,0:T(8,128)(2,1)}, bf16[128,2048]{1,0:T(8,128)(2,1)S(1)}, u32[]{:S(2)}, u32[]{:S(2)}) collective-permute-start(bf16[128,2048]{1,0:T(8,128)(2,1)} %collective-permute-done.35.refs_2_.refs_14_), channel_id=1, source_target_pairs={{0,2},{2,0},{1,3},{3,1},{4,6},{6,4},{5,7},{7,5},{8,10},{10,8},{9,1... | collective-permute-start | bytes 1572872 | tf_op jit(solution)/shard_map/ppermute | solution.py:46
  251.6 18.1 %collective-permute-start.40 = (bf16[128,2048]{1,0:T(8,128)(2,1)S(1)}, bf16[128,2048]{1,0:T(8,128)(2,1)S(1)}, u32[]{:S(2)}, u32[]{:S(2)}) collective-permute-start(bf16[128,2048]{1,0:T(8,128)(2,1)S(1)} %slice.162), channel_id=1, source_target_pairs={{0,1},{1,0},{2,3},{3,2},{4,5},{5,4},{6,7},{7,6},{8,9},{9,8},{10,11... | collective-permute-start | bytes 1572872 | tf_op jit(solution)/shard_map/ppermute | solution.py:46
  269.7 30.1 %collective-permute-start.42 = (bf16[128,2048]{1,0:T(8,128)(2,1)S(1)}, bf16[128,2048]{1,0:T(8,128)(2,1)S(1)}, u32[]{:S(2)}, u32[]{:S(2)}) collective-permute-start(bf16[128,2048]{1,0:T(8,128)(2,1)S(1)} %collective-permute-done.40.refs_6_.refs_10_), channel_id=1, source_target_pairs={{0,2},{2,0},{1,3},{3,1},{4,6},{6,4},{5,7},{7,5},{8,10},{10,8},{9,1... | collective-permute-start | bytes 1572872 | tf_op jit(solution)/shard_map/ppermute | solution.py:46
  269.8 30.0 %collective-permute-start.43 = (bf16[128,2048]{1,0:T(8,128)(2,1)S(1)}, bf16[128,2048]{1,0:T(8,128)(2,1)S(1)}, u32[]{:S(2)}, u32[]{:S(2)}) collective-permute-start(bf16[128,2048]{1,0:T(8,128)(2,1)S(1)} %collective-permute-done.41.refs_7_.refs_11_), channel_id=1, source_target_pairs={{0,2},{2,0},{1,3},{3,1},{4,6},{6,4},{5,7},{7,5},{8,10},{10,8},{9,1... | collective-permute-start | bytes 1572872 | tf_op jit(solution)/shard_map/ppermute | solution.py:46
  299.9 18.0 %collective-permute-start.44 = (bf16[256,2048]{1,0:T(8,128)(2,1)S(1)}, bf16[256,2048]{1,0:T(8,128)(2,1)S(1)}, u32[]{:S(2)}, u32[]{:S(2)}) collective-permute-start(bf16[256,2048]{1,0:T(8,128)(2,1)S(1)} %copy-done.70), channel_id=1, source_target_pairs={{0,2},{2,0},{1,3},{3,1},{4,6},{6,4},{5,7},{7,5},{8,10},{10,8},{9,1... | collective-permute-start | bytes 3145736 | tf_op jit(solution)/shard_map/ppermute | solution.py:46
  300.0 17.9 %collective-permute-start.45 = (bf16[256,2048]{1,0:T(8,128)(2,1)}, bf16[256,2048]{1,0:T(8,128)(2,1)S(1)}, u32[]{:S(2)}, u32[]{:S(2)}) collective-permute-start(bf16[256,2048]{1,0:T(8,128)(2,1)} %get-tuple-element.507), channel_id=1, source_target_pairs={{0,2},{2,0},{1,3},{3,1},{4,6},{6,4},{5,7},{7,5},{8,10},{10,8},{9,1... | collective-permute-start | bytes 3145736 | tf_op jit(solution)/shard_map/ppermute | solution.py:46
  339.6 175.0 %reduce-scatter.6.cloned.1.call-start = ((), (), s32[]{:S(2)}) async-start(), calls=%async_computation.8 | async-start | bytes 7208960 | tf_op jit(solution)/shard_map/reduce_scatter | solution.py:235
  345.1 22.3 %collective-permute-start.53 = (bf16[128,2048]{1,0:T(8,128)(2,1)S(1)}, bf16[128,2048]{1,0:T(8,128)(2,1)S(1)}, u32[]{:S(2)}, u32[]{:S(2)}) collective-permute-start(bf16[128,2048]{1,0:T(8,128)(2,1)S(1)} %get-tuple-element.697), channel_id=1, source_target_pairs={{0,4},{4,0},{1,5},{5,1},{2,6},{6,2},{3,7},{7,3},{8,12},{12,8},{9,1... | collective-permute-start | bytes 1572872 | tf_op jit(solution)/shard_map/ppermute | solution.py:46
  346.8 22.2 %collective-permute-start.54 = (bf16[128,2048]{1,0:T(8,128)(2,1)S(1)}, bf16[128,2048]{1,0:T(8,128)(2,1)S(1)}, u32[]{:S(2)}, u32[]{:S(2)}) collective-permute-start(bf16[128,2048]{1,0:T(8,128)(2,1)S(1)} %get-tuple-element.695), channel_id=1, source_target_pairs={{0,1},{1,0},{2,3},{3,2},{4,5},{5,4},{6,7},{7,6},{8,9},{9,8},{10,11... | collective-permute-start | bytes 1572872 | tf_op jit(solution)/shard_map/ppermute | solution.py:46
  376.3 24.9 %collective-permute-start.55 = (bf16[256,2048]{1,0:T(8,128)(2,1)}, bf16[256,2048]{1,0:T(8,128)(2,1)S(1)}, u32[]{:S(2)}, u32[]{:S(2)}) collective-permute-start(bf16[256,2048]{1,0:T(8,128)(2,1)} %get-tuple-element.570.refs_7_.refs_2_), channel_id=1, source_target_pairs={{0,1},{1,0},{2,3},{3,2},{4,5},{5,4},{6,7},{7,6},{8,9},{9,8},{10,11... | collective-permute-start | bytes 3145736 | tf_op jit(solution)/shard_map/ppermute | solution.py:46
  376.8 24.4 %collective-permute-start.56 = (bf16[256,2048]{1,0:T(8,128)(2,1)}, bf16[256,2048]{1,0:T(8,128)(2,1)S(1)}, u32[]{:S(2)}, u32[]{:S(2)}) collective-permute-start(bf16[256,2048]{1,0:T(8,128)(2,1)} %get-tuple-element.570.refs_7_.refs_2_), channel_id=1, source_target_pairs={{0,4},{4,0},{1,5},{5,1},{2,6},{6,2},{3,7},{7,3},{8,12},{12,8},{9,1... | collective-permute-start | bytes 3145736 | tf_op jit(solution)/shard_map/ppermute | solution.py:46
  378.5 22.7 %collective-permute-start.57 = (bf16[256,2048]{1,0:T(8,128)(2,1)}, bf16[256,2048]{1,0:T(8,128)(2,1)S(1)}, u32[]{:S(2)}, u32[]{:S(2)}) collective-permute-start(bf16[256,2048]{1,0:T(8,128)(2,1)} %get-tuple-element.570.refs_7_.refs_2_), channel_id=1, source_target_pairs={{0,2},{2,0},{1,3},{3,1},{4,6},{6,4},{5,7},{7,5},{8,10},{10,8},{9,1... | collective-permute-start | bytes 3145736 | tf_op jit(solution)/shard_map/ppermute | solution.py:46
  435.6 31.8 %collective-permute-start.71 = (bf16[128,2048]{1,0:T(8,128)(2,1)}, bf16[128,2048]{1,0:T(8,128)(2,1)S(1)}, u32[]{:S(2)}, u32[]{:S(2)}) collective-permute-start(bf16[128,2048]{1,0:T(8,128)(2,1)} %add_convert_fusion.11), channel_id=1, source_target_pairs={{0,1},{1,0},{2,3},{3,2},{4,5},{5,4},{6,7},{7,6},{8,9},{9,8},{10,11... | collective-permute-start | bytes 1572872 | tf_op jit(solution)/shard_map/ppermute | solution.py:46
  437.3 30.1 %collective-permute-start.72 = (bf16[128,2048]{1,0:T(8,128)(2,1)}, bf16[128,2048]{1,0:T(8,128)(2,1)S(1)}, u32[]{:S(2)}, u32[]{:S(2)}) collective-permute-start(bf16[128,2048]{1,0:T(8,128)(2,1)} %add_convert_fusion.10), channel_id=1, source_target_pairs={{0,4},{4,0},{1,5},{5,1},{2,6},{6,2},{3,7},{7,3},{8,12},{12,8},{9,1... | collective-permute-start | bytes 1572872 | tf_op jit(solution)/shard_map/ppermute | solution.py:46
  447.5 19.9 %collective-permute-start.70 = (bf16[2,2,160,128]{3,2,1,0:T(8,128)(2,1)S(1)}, bf16[2,2,160,128]{3,2,1,0:T(8,128)(2,1)S(1)}, u32[]{:S(2)}, u32[]{:S(2)}) collective-permute-start(bf16[2,2,160,128]{3,2,1,0:T(8,128)(2,1)S(1)} %add_convert_fusion.24), channel_id=1, source_target_pairs={{0,16},{8,24},{16,0},{24,8},{1,17},{9,25},{17,1},{25,9},{2,18},{10... | collective-permute-start | bytes 491528 | tf_op jit(solution)/shard_map/ppermute | solution.py:219
  467.4 28.9 %collective-permute-start.73 = (bf16[2,64,2048]{2,1,0:T(8,128)(2,1)}, bf16[2,64,2048]{2,1,0:T(8,128)(2,1)S(1)}, u32[]{:S(2)}, u32[]{:S(2)}) collective-permute-start(bf16[2,64,2048]{2,1,0:T(8,128)(2,1)} %get-tuple-element.628), channel_id=1, source_target_pairs={{0,1},{1,0},{2,3},{3,2},{4,5},{5,4},{6,7},{7,6},{8,9},{9,8},{10,11... | collective-permute-start | bytes 1572872 | tf_op jit(solution)/shard_map/ppermute | solution.py:46
  469.1 27.2 %collective-permute-start.74 = (bf16[128,2048]{1,0:T(8,128)(2,1)S(1)}, bf16[128,2048]{1,0:T(8,128)(2,1)}, u32[]{:S(2)}, u32[]{:S(2)}) collective-permute-start(bf16[128,2048]{1,0:T(8,128)(2,1)S(1)} %get-tuple-element.694), channel_id=1, source_target_pairs={{0,4},{4,0},{1,5},{5,1},{2,6},{6,2},{3,7},{7,3},{8,12},{12,8},{9,1... | collective-permute-start | bytes 1572872 | tf_op jit(solution)/shard_map/ppermute | solution.py:46
  470.9 25.5 %collective-permute-start.75 = (bf16[128,2048]{1,0:T(8,128)(2,1)S(1)}, bf16[128,2048]{1,0:T(8,128)(2,1)}, u32[]{:S(2)}, u32[]{:S(2)}) collective-permute-start(bf16[128,2048]{1,0:T(8,128)(2,1)S(1)} %get-tuple-element.692), channel_id=1, source_target_pairs={{0,1},{1,0},{2,3},{3,2},{4,5},{5,4},{6,7},{7,6},{8,9},{9,8},{10,11... | collective-permute-start | bytes 1572872 | tf_op jit(solution)/shard_map/ppermute | solution.py:46
  472.0 24.4 %collective-permute-start.76 = (bf16[128,2048]{1,0:T(8,128)(2,1)S(1)}, bf16[128,2048]{1,0:T(8,128)(2,1)}, u32[]{:S(2)}, u32[]{:S(2)}) collective-permute-start(bf16[128,2048]{1,0:T(8,128)(2,1)S(1)} %get-tuple-element.693), channel_id=1, source_target_pairs={{0,4},{4,0},{1,5},{5,1},{2,6},{6,2},{3,7},{7,3},{8,12},{12,8},{9,1... | collective-permute-start | bytes 1572872 | tf_op jit(solution)/shard_map/ppermute | solution.py:46
  472.6 31.6 %collective-permute-start.77 = (bf16[128,2048]{1,0:T(8,128)(2,1)S(1)}, bf16[128,2048]{1,0:T(8,128)(2,1)}, u32[]{:S(2)}, u32[]{:S(2)}) collective-permute-start(bf16[128,2048]{1,0:T(8,128)(2,1)S(1)} %get-tuple-element.691), channel_id=1, source_target_pairs={{0,1},{1,0},{2,3},{3,2},{4,5},{5,4},{6,7},{7,6},{8,9},{9,8},{10,11... | collective-permute-start | bytes 1572872 | tf_op jit(solution)/shard_map/ppermute | solution.py:46
  514.6 37.8 %all-to-all-start.2 = ((bf16[8,704,128]{2,1,0:T(8,128)(2,1)}), bf16[8,704,128]{2,1,0:T(8,128)(2,1)S(1)}, u32[]{:S(2)}, u32[]{:S(2)}) async-start(bf16[8,704,128]{2,1,0:T(8,128)(2,1)} %bitcast.79), calls=%async_computation.4 | async-start | bytes 2883584 | tf_op jit(solution)/shard_map/all_to_all | solution.py:198
  518.3 81.1 %reduce-scatter.8.cloned.1.call-start = ((), (), s32[]{:S(2)}) async-start(), calls=%async_computation.9 | async-start | bytes 1310720 | tf_op jit(solution)/shard_map/reduce_scatter | solution.py:235
  520.6 31.8 %collective-permute-start.83 = (bf16[128,2048]{1,0:T(8,128)(2,1)}, bf16[128,2048]{1,0:T(8,128)(2,1)}, u32[]{:S(2)}, u32[]{:S(2)}) collective-permute-start(bf16[128,2048]{1,0:T(8,128)(2,1)} %add_convert_fusion.5), channel_id=1, source_target_pairs={{0,1},{1,0},{2,3},{3,2},{4,5},{5,4},{6,7},{7,6},{8,9},{9,8},{10,11... | collective-permute-start | bytes 1572872 | tf_op jit(solution)/shard_map/ppermute | solution.py:46
  524.5 27.9 %collective-permute-start.84 = (bf16[128,2048]{1,0:T(8,128)(2,1)}, bf16[128,2048]{1,0:T(8,128)(2,1)}, u32[]{:S(2)}, u32[]{:S(2)}) collective-permute-start(bf16[128,2048]{1,0:T(8,128)(2,1)} %add_convert_fusion.4), channel_id=1, source_target_pairs={{0,4},{4,0},{1,5},{5,1},{2,6},{6,2},{3,7},{7,3},{8,12},{12,8},{9,1... | collective-permute-start | bytes 1572872 | tf_op jit(solution)/shard_map/ppermute | solution.py:46
  531.4 21.0 %collective-permute-start.86 = (bf16[8,160,128]{2,1,0:T(8,128)(2,1)}, bf16[8,160,128]{2,1,0:T(8,128)(2,1)}, u32[]{:S(2)}, u32[]{:S(2)}) collective-permute-start(bf16[8,160,128]{2,1,0:T(8,128)(2,1)} %get-tuple-element.705), channel_id=1, source_target_pairs={{0,16},{8,24},{16,0},{24,8},{1,17},{9,25},{17,1},{25,9},{2,18},{10... | collective-permute-start | bytes 983048 | tf_op jit(solution)/shard_map/ppermute | solution.py:219
  (137 other events, 1511.5 us)
Sparse Core Ops, SparseCore 0:
  9.6 52.4 all-gather.6
  63.6 66.1 all-gather.8
  132.9 105.8 all-gather.10
  339.7 53.8 reduce-scatter.3
  405.9 107.8 reduce-scatter.5
  572.7 25.8 reduce-scatter.7
